TPU v7x, 32 devices: a whole 2x2x4 slice. The times are simulated.
32 devices in a mesh: row: 8 (over z, x), col: 4 (over y, core).
Axes of the slice: x: 2, y: 2, z: 4, core: 2. Of those that a mesh axis runs over, the one named last changes fastest.
Arguments:
- basis_now: float32 [8192, 128], P(('row', 'col')), may hold values from -6 to 6
- basis_prev: float32 [8192, 128], P(('row', 'col')), may hold values from -6 to 6
- coupling: float32 [128, 128], replicated, may hold values from -0.875 to 0.875
- tiles: bfloat16 [8, 4, 16, 128, 128], P('row', 'col'), may hold values from -0.1875 to 0.1875
- tile_rows: int32 [8, 4, 16], P('row', 'col'), may hold values from 0 to 15
- tile_cols: int32 [8, 4, 16], P('row', 'col'), may hold values from 0 to 7
- tile_counts: int32 [8, 4], P('row', 'col'), may hold values from 4 to 16, as said below
Outputs:
- basis: float32 [8192, 128], P(('row', 'col'))
- projection: float32 [128, 128], replicated
- rfactor: float32 [128, 128], replicated
Inputs may be any that keep to these rules, and one draw needn't show every extreme that they name: Each device uses the first tile_counts of its 16 tile slots; some device uses all of them.
All inputs are finite; a program needn't handle non-finite values.
Results may differ from a plain program's by a relative error of at most 0.0033.
Values may be sent and summed in bfloat16 or wider, within the bound.
No kernel may reach another device: no remote copies, remote signals or barrier semaphores. Data moves between devices by JAX's collectives and lax.ppermute only.
A program may use at most 64 MiB of HBM per device.

v0:
```python
import jax
import jax.numpy as jnp
from jax import lax
from jax.sharding import PartitionSpec as P

HIGHEST = lax.Precision.HIGHEST


def inner_product(left, right):
    return jnp.dot(left.T, right, precision=HIGHEST)


def upper_cholesky(gram):
    return jnp.linalg.cholesky(gram).T


def lower_inverse(lower_part):
    identity = jnp.eye(lower_part.shape[0], dtype=lower_part.dtype)
    return jax.scipy.linalg.solve_triangular(lower_part, identity, lower=True)


def on_device(basis_now, basis_prev, coupling, tiles, tile_rows, tile_cols, tile_counts):
    rows_dev, block_width = basis_now.shape
    tile_block = tiles[0, 0]
    row_ids = tile_rows[0, 0]
    col_ids = tile_cols[0, 0]
    tile_total = tile_counts[0, 0]
    tile_size = tile_block.shape[-1]
    slot_count = tile_block.shape[0]
    half_basis = basis_now.astype(jnp.bfloat16)
    gathered = lax.all_gather(half_basis, "col", axis=0, tiled=True)
    stacked = gathered.reshape(-1, tile_size, block_width)
    chosen = jnp.take(stacked, col_ids, axis=0)
    products = jnp.einsum("tij,tjb->tib", tile_block, chosen, preferred_element_type=jnp.float32)
    usable = jnp.arange(slot_count) < tile_total
    row_tiles = lax.axis_size("row") * rows_dev // tile_size
    selector = (row_ids[None, :] == jnp.arange(row_tiles)[:, None]) & usable[None, :]
    combined = jnp.einsum("rt,tib->rib", selector.astype(jnp.float32), products, precision=HIGHEST)
    product = lax.psum_scatter(
        combined.reshape(row_tiles * tile_size, block_width), "row", scatter_dimension=0, tiled=True
    )
    device_count = lax.axis_size("row") * lax.axis_size("col")
    total_rows = float(rows_dev * device_count)
    norm_scale = total_rows ** (-0.5)
    upper_part = jnp.triu(coupling)
    pieces = (
        inner_product(basis_now, product),
        inner_product(product, product),
        inner_product(basis_prev, product),
        inner_product(basis_now, basis_now),
        inner_product(basis_prev, basis_now),
        inner_product(basis_prev, basis_prev),
    )
    totals = lax.psum(
        (pieces[0], pieces[1], pieces[2], pieces[3], pieces[4], pieces[5]), ("row", "col")
    )
    projection = totals[0] * norm_scale
    residual = product - jnp.dot(basis_now, projection, precision=HIGHEST) * norm_scale
    residual = residual - jnp.dot(basis_prev, upper_part.T, precision=HIGHEST)
    (
        basis_product,
        product_square,
        previous_product,
        basis_square,
        previous_basis,
        previous_square,
    ) = totals
    scaled_proj = projection * norm_scale
    first_cross = jnp.dot(basis_product.T, scaled_proj, precision=HIGHEST)
    second_cross = jnp.dot(previous_product.T, upper_part.T, precision=HIGHEST)
    mixed_term = jnp.dot(
        jnp.dot(scaled_proj.T, previous_basis.T, precision=HIGHEST), upper_part.T, precision=HIGHEST
    )
    gram = product_square - first_cross - first_cross.T - second_cross - second_cross.T
    gram = gram + jnp.dot(
        jnp.dot(scaled_proj.T, basis_square, precision=HIGHEST), scaled_proj, precision=HIGHEST
    )
    gram = gram + mixed_term + mixed_term.T
    gram = gram + jnp.dot(
        jnp.dot(upper_part, previous_square, precision=HIGHEST), upper_part.T, precision=HIGHEST
    )
    gram = 0.5 * (gram + gram.T)
    rfactor = upper_cholesky(gram / total_rows)
    inverse = lower_inverse(rfactor.T)
    basis = jnp.dot(residual, inverse.T, precision=HIGHEST)
    return (basis, projection, rfactor)


def solution(mesh):
    placed = (
        P(("row", "col"), None),
        P(("row", "col"), None),
        P(),
        P("row", "col", None, None, None),
        P("row", "col", None),
        P("row", "col", None),
        P("row", "col"),
    )
    return jax.shard_map(
        on_device,
        mesh=mesh,
        in_specs=placed,
        out_specs=(P(("row", "col"), None), P(), P()),
        check_vma=False,
    )
```

profile of v0, /device:TPU:1, one launch (start us, length us, event | category | flops | bytes accessed | tf_op | source)
XLA Modules:
  0.0 262.5 jit_solution(10091509824565772220)
XLA Ops:
  7.2 0.0 copy-start
  7.2 0.0 copy-start.12
  7.2 0.0 reduce-scatter.2.cloned.1.call-start
  7.2 0.7 fusion.53
  7.9 0.0 copy-done.12
  8.0 0.9 convert_element_type.2
  8.9 7.1 %all_gather.3 = bf16[1024,128]{1,0:T(8,128)(2,1)S(1)} all-gather(bf16[256,128]{1,0:T(8,128)(2,1)S(1)} %convert_element_type.2), channel_id=1, replica_groups=mesh['row'=8,'col'=4] {'col'}, dimensions={0}, use_global_device_ids=true | all-gather | bytes 327680 | tf_op jit(solution)/shard_map/all_gather | solution.py:31
  16.0 0.6 gather_fusion
  16.6 0.0 copy-done
  16.6 0.7 fusion.7
  17.3 0.5 copy.25
  18.5 0.0 copy-start.11
  18.5 0.6 copy-done.11
  19.2 0.6 fusion.5
  19.8 1.3 copy.17
  21.1 0.0 copy-start.1
  21.1 0.0 reduce-scatter.2.cloned.1.call-update
  21.1 0.0 copy-start.2
  21.1 0.2 all-reduce.3.cloned.1.call-start
  21.3 0.6 copy-done.1
  22.0 1.0 fusion.65
  23.0 0.0 copy-done.2
  23.0 1.0 fusion.66
  24.0 1.0 fusion.67
  25.0 58.8 %reduce-scatter.2.cloned.1.call-done = f32[256,128]{1,0:T(8,128)} async-done(((f32[2048,128]{1,0:T(8,128)}), f32[256,128]{1,0:T(8,128)}) %reduce-scatter.2.cloned.1.call-update) | async-done | bytes 131088 | tf_op jit(solution)/shard_map/reduce_scatter | solution.py:39
  83.8 0.0 copy-start.3
  83.8 2.0 convolution_bitcast_fusion.1
  85.8 0.0 copy-done.3
  85.8 1.0 convolution_bitcast_fusion.2
  86.9 1.0 fusion.64
  87.9 0.0 all-reduce.3.cloned.1.call-update
  87.9 133.6 %all-reduce.3.cloned.1.call-done = (f32[128,128]{0,1:T(8,128)}, f32[128,128]{1,0:T(8,128)}, f32[128,128]{1,0:T(8,128)}, f32[128,128]{0,1:T(8,128)}, f32[128,128]{1,0:T(8,128)}, /*index=5*/f32[128,128]{1,0:T(8,128)}) async-done(((f32[128,128]{0,1:T(8,128)}, f32[128,128]{1,0:T(8,128)}, f32[128,128]{1,0:T(8,128)}, f32[128,128]{0,1:T(8,128)}, f32[128,128]{1,0:T(8,128)}, /*index=5*/f32[128,128]{1,0:T(8,128)}), ...) | async-done | bytes 393232 | tf_op jit(solution)/shard_map/psum | solution.py:54
  221.5 1.2 fusion.17
  222.8 0.0 copy-done.4
  222.8 0.0 copy-start.10
  222.8 0.8 copy-done.10
  223.6 0.3 fusion.12
  223.9 0.6 copy-done.5
  224.4 0.3 fusion.29
  224.8 0.1 copy.20
  224.9 0.7 copy-done.9
  225.6 0.2 fusion.15
  225.8 0.0 copy-start.8
  225.8 0.1 copy.18
  225.9 0.7 copy-done.8
  226.7 0.3 fusion.31
  227.0 0.1 copy.19
  227.1 0.7 copy-done.7
  227.9 0.3 fusion.27
  228.1 0.6 copy-done.6
  228.7 0.3 fusion.4
  229.0 0.3 convolution_add_fusion
  229.3 0.1 copy.21
  229.4 0.1 copy.22
  229.5 11.7 %cholesky.16 = f32[128,128]{1,0:T(8,128)S(1)} custom-call(f32[128,128]{1,0:T(8,128)S(1)} %fusion.21), custom_call_target="Cholesky" | custom-call | tf_op jit(solution)/shard_map/jit(cholesky)/cholesky | solution.py:14
  241.3 0.6 compare_reduce_fusion
  241.9 0.7 fusion.25
  242.6 9.8 %custom-call.7 = f32[1,128,128]{1,2,0:T(8,128)S(1)} custom-call(f32[1,128,128]{2,1,0:T(8,128)S(1)} %get-tuple-element.16), custom_call_target="InvertDiagBlocksLowerTriangular" | custom-call | tf_op jit(solution)/shard_map/jit(_solve_triangular)/triangular_solve | solution.py:19
  252.4 0.2 fusion.19
  252.7 0.3 fusion.2
  253.0 0.4 fusion
  253.3 0.7 copy.24
  254.0 0.7 copy.23
  254.8 0.9 fusion.68
  (13 shorter events, 0.1 us)
Async XLA Ops:
  7.2 9.5 %copy-start = (bf16[1,1,16,128,128]{4,3,2,1,0:T(8,128)(2,1)S(1)}, bf16[1,1,16,128,128]{4,3,2,1,0:T(8,128)(2,1)}, u32[]{:S(2)}) copy-start(bf16[1,1,16,128,128]{4,3,2,1,0:T(8,128)(2,1)} %param.10) | copy-start | bytes 1572868
  7.2 0.8 copy-start.12
  7.2 76.7 %reduce-scatter.2.cloned.1.call-start = ((), (), s32[]{:S(2)}) async-start(), calls=%async_computation.1 | async-start | bytes 1179648 | tf_op jit(solution)/shard_map/reduce_scatter | solution.py:39
  18.5 0.7 copy-start.11
  21.1 0.9 copy-start.1
  21.1 1.9 copy-start.2
  21.1 200.4 %all-reduce.3.cloned.1.call-start = ((), (), s32[]{:S(2)}) async-start(), calls=%async_computation.2 | async-start | bytes 786432 | tf_op jit(solution)/shard_map/psum | solution.py:54
  83.8 2.0 copy-start.3
  221.5 1.2 copy-start.4
  222.8 0.8 copy-start.10
  223.6 0.8 copy-start.5
  224.8 0.8 copy-start.9
  225.8 0.8 copy-start.8
  227.0 0.8 copy-start.7
  227.9 0.8 copy-start.6
Sparse Core Ops, SparseCore 0:
  21.2 62.5 reduce-scatter.1
  91.8 129.7 all-reduce.2
where the time goes:
time: 265 us; the launch traced here: 263 us
  waiting for transfers between devices  192 us (72%)
  other arithmetic  24.5 us (9%)
  between operations  14.9 us (6%)
  matrix products  13.4 us (5%)
  local copies, waits for them, and re-layouts  9.87 us (4%)
  blocking collectives  7.1 us (3%)
    psum x1, waiting for transfers between devices, on_device(): lax.psum((pieces[0], pieces[1], pieces[2], pieces[3], pieces[4], pieces[5...  134 us
    reduce_scatter x1, waiting for transfers between devices, on_device(): lax.psum_scatter(combined.reshape(row_tiles * tile_size, block_width), 'r...  58.8 us
    another operation x3, other arithmetic, upper_cholesky(): return jnp.linalg.cholesky(gram).T  12.4 us
    another operation x1, other arithmetic, lower_inverse(): return jax.scipy.linalg.solve_triangular(lower_part, identity, lower=True)  9.81 us
    all_gather x1, blocking collectives, on_device(): gathered = lax.all_gather(half_basis, 'col', axis=0, tiled=True)  7.1 us
    dot_general x6, matrix products, inner_product(): return jnp.dot(left.T, right, precision=HIGHEST)  7.07 us
    unnamed x28, local copies, waits for them, and re-layouts  6.97 us
  transfers between devices with their start and end apart: 2, of which 2 were waited for; matrix products, arithmetic and copies ran while one was open for 1% of the time, Pallas kernels for 0%

commit v1 on v0

v1 whole, which is shorter than its diff:
```python
import functools

import jax
import jax.numpy as jnp
from jax import lax
from jax.experimental import pallas as pl
from jax.experimental.pallas import tpu as pltpu
from jax.sharding import PartitionSpec as P

HIGHEST = lax.Precision.HIGHEST
F32 = jnp.float32
BF16 = jnp.bfloat16


def dot(a, b):
    return jnp.dot(a, b, precision=HIGHEST, preferred_element_type=F32)


def dot_tn(a, b):
    return lax.dot_general(a, b, (((0,), (0,)), ((), ())), precision=HIGHEST, preferred_element_type=F32)


def dot_nt(a, b):
    return lax.dot_general(a, b, (((1,), (1,)), ((), ())), precision=HIGHEST, preferred_element_type=F32)


def upper_of(x):
    rows = lax.broadcasted_iota(jnp.int32, x.shape, 0)
    cols = lax.broadcasted_iota(jnp.int32, x.shape, 1)
    return jnp.where(rows <= cols, x, 0.0)


def tiles_kernel(rows_ref, cols_ref, count_ref, tiles_ref, basis_ref, out_ref, total_ref):
    slots, size, _ = tiles_ref.shape
    total_ref[...] = jnp.zeros_like(total_ref)
    used = count_ref[0]
    for slot in range(slots):
        start = pl.multiple_of(cols_ref[slot] * size, size)
        value = jnp.dot(tiles_ref[slot], basis_ref[pl.ds(start, size), :], preferred_element_type=F32)
        value = jnp.where(slot < used, value, 0.0)
        place = pl.ds(pl.multiple_of(rows_ref[slot] * size, size), size)
        total_ref[place, :] += value
    out_ref[...] = total_ref[...].astype(BF16)


def early_kernel(now_ref, prev_ref, coupling_ref, grams_ref, shift_ref):
    width = now_ref.shape[1]
    now, prev = now_ref[...], prev_ref[...]
    grams_ref[:width, :] = dot_tn(now, now)
    grams_ref[width:, :] = dot_tn(now, prev)
    shift_ref[...] = dot_nt(prev, upper_of(coupling_ref[...]))


def late_kernel(parts_ref, now_ref, shift_ref, shifted_ref, grams_ref):
    width = now_ref.shape[1]
    shifted = -shift_ref[...]
    for part in range(parts_ref.shape[0]):
        shifted = shifted + parts_ref[part].astype(F32)
    shifted_ref[...] = shifted
    grams_ref[:width, :] = dot_tn(now_ref[...], shifted)
    grams_ref[width:, :] = dot_tn(shifted, shifted)


def sum_kernel(parts_ref, out_ref):
    total = parts_ref[0]
    for part in range(1, parts_ref.shape[0]):
        total = total + parts_ref[part]
    out_ref[...] = total


def eliminate(gram):
    width = gram.shape[0]
    lanes = lax.broadcasted_iota(jnp.int32, (1, width), 1)
    block = 8
    strips = [gram[r : r + block, :] for r in range(0, width, block)]
    subs = lax.broadcasted_iota(jnp.int32, (block, 1), 0)
    for k in range(width):
        at, inside = divmod(k, block)
        row = strips[at][inside : inside + 1, :]
        pivot = row[:, k : k + 1]
        scaled = jnp.where(lanes == k, 1.0, row) * (1.0 / pivot)
        for s in range(at, len(strips)):
            factor = strips[s][:, k : k + 1]
            if s == at:
                factor = jnp.where(subs > inside, factor, 0.0)
                kept = jnp.where((lanes == k) & (subs > inside), 0.0, strips[s])
            else:
                kept = jnp.where(lanes == k, 0.0, strips[s])
            strips[s] = kept - factor * scaled
    return jnp.concatenate(strips, axis=0)


def final_kernel(total_rows, parts_ref, early_ref, coupling_ref, now_ref, shifted_ref, basis_ref, projection_ref, rfactor_ref):
    width = now_ref.shape[1]
    late = parts_ref[0]
    for part in range(1, parts_ref.shape[0]):
        late = late + parts_ref[part]
    cross, square = late[:width], late[width:]
    now_square, now_prev = early_ref[:width, :], early_ref[width:, :]
    norm_scale = total_rows**-0.5
    projection = (cross + dot_nt(now_prev, upper_of(coupling_ref[...]))) * norm_scale
    projection_ref[...] = projection
    scaled = projection * norm_scale
    mixed = dot_tn(scaled, cross - 0.5 * dot(now_square, scaled))
    gram = square - mixed - mixed.T
    reduced = eliminate(gram * (1.0 / total_rows))
    rows = lax.broadcasted_iota(jnp.int32, reduced.shape, 0)
    cols = lax.broadcasted_iota(jnp.int32, reduced.shape, 1)
    diagonal = jnp.sum(jnp.where(rows == cols, reduced, 0.0), axis=1, keepdims=True)
    root = lax.rsqrt(diagonal)
    rfactor_ref[...] = jnp.where(rows <= cols, reduced, 0.0) * root
    inverse = jnp.where(rows > cols, reduced, jnp.where(rows == cols, 1.0, 0.0)) * root
    residual = shifted_ref[...] - dot(now_ref[...], scaled)
    basis_ref[...] = dot_nt(residual, inverse)


def on_device(basis_now, basis_prev, coupling, tiles, tile_rows, tile_cols, tile_counts):
    rows_dev, width = basis_now.shape
    n_row, n_col = lax.axis_size("row"), lax.axis_size("col")
    tile_block = tiles[0, 0]
    total_rows = float(rows_dev * n_row * n_col)
    smem = pl.BlockSpec(memory_space=pltpu.SMEM)
    vmem = pl.BlockSpec(memory_space=pltpu.VMEM)
    params = pltpu.CompilerParams(vmem_limit_bytes=48 * 1024 * 1024)

    gathered = lax.all_gather(basis_now.astype(BF16), "col", axis=0, tiled=True)
    partial = pl.pallas_call(
        tiles_kernel,
        out_shape=jax.ShapeDtypeStruct((n_row * rows_dev, width), BF16),
        in_specs=[smem, smem, smem, vmem, vmem],
        out_specs=vmem,
        scratch_shapes=[pltpu.VMEM((n_row * rows_dev, width), F32)],
        compiler_params=params,
        name="tile_products",
    )(tile_rows.reshape(-1), tile_cols.reshape(-1), tile_counts.reshape(-1), tile_block, gathered)
    parts = lax.all_to_all(partial.reshape(n_row, rows_dev, width), "row", split_axis=0, concat_axis=0, tiled=True)

    early, shift = pl.pallas_call(
        early_kernel,
        out_shape=(
            jax.ShapeDtypeStruct((2 * width, width), F32),
            jax.ShapeDtypeStruct((rows_dev, width), F32),
        ),
        in_specs=[vmem] * 3,
        out_specs=(vmem, vmem),
        compiler_params=params,
        name="early_grams",
    )(basis_now, basis_prev, coupling)
    early = lax.psum(early, ("row", "col"))

    shifted, late = pl.pallas_call(
        late_kernel,
        out_shape=(
            jax.ShapeDtypeStruct((rows_dev, width), F32),
            jax.ShapeDtypeStruct((2 * width, width), F32),
        ),
        in_specs=[vmem] * 3,
        out_specs=(vmem, vmem),
        compiler_params=params,
        name="late_grams",
    )(parts, basis_now, shift)
    late = lax.all_gather(late, "col", axis=0)
    late = pl.pallas_call(
        sum_kernel,
        out_shape=jax.ShapeDtypeStruct((2 * width, width), F32),
        in_specs=[vmem],
        out_specs=vmem,
        compiler_params=params,
        name="column_sum",
    )(late)
    late = lax.all_gather(late, "row", axis=0)
    return pl.pallas_call(
        functools.partial(final_kernel, total_rows),
        out_shape=(
            jax.ShapeDtypeStruct((rows_dev, width), F32),
            jax.ShapeDtypeStruct((width, width), F32),
            jax.ShapeDtypeStruct((width, width), F32),
        ),
        in_specs=[vmem] * 5,
        out_specs=(vmem, vmem, vmem),
        compiler_params=params,
        name="factor_and_basis",
    )(late, early, coupling, basis_now, shifted)


def solution(mesh):
    placed = (
        P(("row", "col"), None),
        P(("row", "col"), None),
        P(),
        P("row", "col", None, None, None),
        P("row", "col", None),
        P("row", "col", None),
        P("row", "col"),
    )
    return jax.shard_map(
        on_device,
        mesh=mesh,
        in_specs=placed,
        out_specs=(P(("row", "col"), None), P(), P()),
        check_vma=False,
    )
```

time: 265 us -> 181 us (0.68)
  waiting for transfers between devices: 192 us -> 121 us
  other arithmetic: 24.5 us -> 0.91 us
  Pallas kernels: 0 us -> 16.6 us
  matrix products: 13.4 us -> 0 us
  blocking collectives: 7.1 us -> 15.8 us
  local copies, waits for them, and re-layouts: 9.87 us -> 2.81 us
  starting transfers between devices: 0.26 us -> 5.74 us
    reduce_scatter x1 -> x0, waiting for transfers between devices: 58.8 us -> none  [on_device(): lax.psum_scatter(combined.reshape(row_tiles * tile_size, block_width), 'r...]
    psum x1, waiting for transfers between devices: 134 us -> 108 us  [on_device(): early = lax.psum(early, ('row', 'col'))]
    another operation x4 -> x0, other arithmetic: 22.2 us -> none  [the longest x3 12.4 us: upper_cholesky(): return jnp.linalg.cholesky(gram).T]
    pallas_call x0 -> x5, Pallas kernels: none -> 16.6 us  [the longest x1 12.6 us: on_device(): pl.pallas_call(functools.partial(final_kernel, total_rows), out_shape=(ja...]
    dot_general x19 -> x0, matrix products: 13.1 us -> none  [the longest x6 7.07 us: inner_product(): return jnp.dot(left.T, right, precision=HIGHEST)]
    all_to_all x0 -> x1, waiting for transfers between devices: none -> 12.5 us  [on_device(): lax.all_to_all(partial.reshape(n_row, rows_dev, width), 'row', split_axis...]
    all_gather x1 -> x2, blocking collectives: 7.1 us -> 15.8 us  [the longest x1 8.7 us: on_device(): late = lax.all_gather(late, 'col', axis=0)]
    all_to_all x0 -> x1, starting transfers between devices: none -> 5.66 us  [on_device(): lax.all_to_all(partial.reshape(n_row, rows_dev, width), 'row', split_axis...]
  transfers between devices with their start and end apart: 2 -> 3, of which waited for: 2 -> 2; matrix products, arithmetic and copies ran while one was open for 1% -> 0% of each run, Pallas kernels for 0% -> 1%
where the time goes in v1:
time: 181 us; the launch traced here: 179 us
  waiting for transfers between devices  121 us (67%)
  Pallas kernels  16.6 us (9%)
  between operations  16.2 us (9%)
  blocking collectives  15.8 us (9%)
  starting transfers between devices  5.74 us (3%)
  local copies, waits for them, and re-layouts  2.81 us (2%)
    psum x1, waiting for transfers between devices, on_device(): early = lax.psum(early, ('row', 'col'))  108 us
    pallas_call x1, Pallas kernels, on_device(): pl.pallas_call(functools.partial(final_kernel, total_rows), out_shape=(ja...  12.6 us
    all_to_all x1, waiting for transfers between devices, on_device(): lax.all_to_all(partial.reshape(n_row, rows_dev, width), 'row', split_axis...  12.5 us
    all_gather x1, blocking collectives, on_device(): late = lax.all_gather(late, 'col', axis=0)  8.7 us
    all_gather x1, blocking collectives, on_device(): gathered = lax.all_gather(basis_now.astype(BF16), 'col', axis=0, tiled=True)  7.1 us
    all_to_all x1, starting transfers between devices, on_device(): lax.all_to_all(partial.reshape(n_row, rows_dev, width), 'row', split_axis...  5.66 us
  transfers between devices with their start and end apart: 3, of which 2 were waited for; matrix products, arithmetic and copies ran while one was open for 0% of the time, Pallas kernels for 1%

profile of v1, /device:TPU:1, one launch (start us, length us, event | category | flops | bytes accessed | tf_op | source)
XLA Modules:
  0.0 179.2 jit_solution(11895551040288223121)
XLA Ops:
  8.0 0.0 copy-start.2
  8.7 0.9 convert_element_type.3
  9.6 7.1 %all_gather.15.basis_ref = bf16[1024,128]{1,0:T(8,128)(2,1)S(1)} all-gather(bf16[256,128]{1,0:T(8,128)(2,1)S(1)} %convert_element_type.3), channel_id=1, replica_groups=mesh['row'=8,'col'=4] {'col'}, dimensions={0}, use_global_device_ids=true | all-gather | bytes 327680 | tf_op jit(solution)/shard_map/all_gather | solution.py:126
  16.7 0.0 copy-start.6
  16.7 0.0 copy-start.7
  16.7 0.0 copy-done.2
  16.7 0.6 copy-done.6
  17.4 0.0 copy-done.7
  17.4 1.7 tile_products.1
  19.1 0.0 copy-start
  19.1 0.0 copy-start.3
  19.1 0.0 copy-start.5
  19.1 5.7 %all-to-all-start = ((bf16[8,256,128]{2,1,0:T(8,128)(2,1)}), bf16[8,256,128]{2,1,0:T(8,128)(2,1)S(1)}, u32[]{:S(2)}, u32[]{:S(2)}) async-start(bf16[8,256,128]{2,1,0:T(8,128)(2,1)} %bitcast.4), calls=%async_computation | async-start | bytes 1048576 | tf_op jit(solution)/shard_map/all_to_all | solution.py:136
  24.8 0.0 all-reduce.2.cloned.1.call-start
  24.8 0.0 copy-done
  24.8 0.0 copy-done.3
  24.8 0.0 copy-done.5
  24.8 1.2 early_grams.1
  26.0 0.0 all-reduce.2.cloned.1.call-update
  26.0 0.0 all-gather.4.cloned.1.call-start
  26.1 12.5 %all-to-all-done.parts_ref = bf16[8,256,128]{2,1,0:T(8,128)(2,1)S(1)} async-done(((bf16[8,256,128]{2,1,0:T(8,128)(2,1)}), bf16[8,256,128]{2,1,0:T(8,128)(2,1)S(1)}, u32[]{:S(2)}, u32[]{:S(2)}) %all-to-all-start) | async-done | bytes 524320 | tf_op jit(solution)/shard_map/all_to_all | solution.py:136
  38.6 0.5 late_grams.1
  39.1 8.7 %all-gather = f32[1024,128]{1,0:T(8,128)S(1)} all-gather(f32[256,128]{1,0:T(8,128)S(1)} %get-tuple-element.8), channel_id=2, replica_groups=mesh['row'=8,'col'=4] {'col'}, dimensions={0}, use_global_device_ids=true | all-gather | bytes 655360 | tf_op jit(solution)/shard_map/all_gather | solution.py:162
  47.8 0.7 column_sum.1
  48.5 0.0 all-gather.4.cloned.1.call-update
  48.5 108.5 %all-reduce.2.cloned.1.call-done.early_ref = f32[256,128]{1,0:T(8,128)} async-done(((f32[256,128]{1,0:T(8,128)}), f32[256,128]{1,0:T(8,128)}) %all-reduce.2.cloned.1.call-update) | async-done | bytes 131088 | tf_op jit(solution)/shard_map/psum | solution.py:149
  157.0 0.0 all-gather.4.cloned.1.call-done
  157.0 0.0 copy-start.1
  157.0 1.2 copy-done.1
  158.2 0.0 copy-start.4
  158.2 0.9 copy-done.4
  159.1 12.6 %factor_and_basis.1 = (f32[256,128]{1,0:T(8,128)}, f32[128,128]{1,0:T(8,128)}, f32[128,128]{1,0:T(8,128)}) custom-call(f32[8,256,128]{2,1,0:T(8,128)S(1)} %bitcast.9, f32[256,128]{1,0:T(8,128)S(1)} %copy-done.4, f32[128,128]{1,0:T(8,128)S(1)} %copy-done.3, f32[256,128]{1,0:T(8,128)S(1)} %copy-done, f32[256,128]{1,0:T(8,128)S(1)} %get-tuple-element.10.shifted_ref), custom_call_target="tpu_custom_call" | custom-call | tf_op jit(solution)/shard_map/factor_and_basis/pallas_call | solution.py:172
Async XLA Ops:
  8.0 8.7 %copy-start.2 = (bf16[1,1,16,128,128]{4,3,2,1,0:T(8,128)(2,1)S(1)}, bf16[1,1,16,128,128]{4,3,2,1,0:T(8,128)(2,1)}, u32[]{:S(2)}) copy-start(bf16[1,1,16,128,128]{4,3,2,1,0:T(8,128)(2,1)} %param.10) | copy-start | bytes 1572868
  16.7 0.7 copy-start.6
  16.7 0.7 copy-start.7
  19.1 5.7 %copy-start = (f32[256,128]{1,0:T(8,128)S(1)}, f32[256,128]{1,0:T(8,128)}, u32[]{:S(2)}) copy-start(f32[256,128]{1,0:T(8,128)} %now_ref.5) | copy-start | bytes 393220
  19.1 5.7 %copy-start.3 = (f32[128,128]{1,0:T(8,128)S(1)}, f32[128,128]{1,0:T(8,128)}, u32[]{:S(2)}) copy-start(f32[128,128]{1,0:T(8,128)} %coupling_ref.3) | copy-start | bytes 196612
  19.1 5.7 %copy-start.5 = (f32[256,128]{1,0:T(8,128)S(1)}, f32[256,128]{1,0:T(8,128)}, u32[]{:S(2)}) copy-start(f32[256,128]{1,0:T(8,128)} %prev_ref.1) | copy-start | bytes 393220
  19.1 19.5 %all-to-all-start = ((bf16[8,256,128]{2,1,0:T(8,128)(2,1)}), bf16[8,256,128]{2,1,0:T(8,128)(2,1)S(1)}, u32[]{:S(2)}, u32[]{:S(2)}) async-start(bf16[8,256,128]{2,1,0:T(8,128)(2,1)} %bitcast.4), calls=%async_computation | async-start | bytes 1048576 | tf_op jit(solution)/shard_map/all_to_all | solution.py:136
  24.8 132.2 %all-reduce.2.cloned.1.call-start = ((), (), s32[]{:S(2)}) async-start(), calls=%async_computation.1 | async-start | bytes 262144 | tf_op jit(solution)/shard_map/psum | solution.py:149
  26.0 130.9 %all-gather.4.cloned.1.call-start = ((), (), s32[]{:S(2)}) async-start(), calls=%async_computation.2 | async-start | bytes 1179648 | tf_op jit(solution)/shard_map/all_gather | solution.py:171
  157.0 1.2 copy-start.1
  158.2 0.9 copy-start.4
Sparse Core Ops, SparseCore 0:
  31.7 125.2 all-reduce.1
Sparse Core Ops, SparseCore 1:
  48.6 36.9 all-gather.3

commit v2 on v1

--- a/solution.py
+++ b/solution.py
@@ -43,22 +43,17 @@
     out_ref[...] = total_ref[...].astype(BF16)
 
 
-def early_kernel(now_ref, prev_ref, coupling_ref, grams_ref, shift_ref):
+def grams_kernel(parts_ref, now_ref, prev_ref, coupling_ref, shifted_ref, grams_ref):
     width = now_ref.shape[1]
     now, prev = now_ref[...], prev_ref[...]
-    grams_ref[:width, :] = dot_tn(now, now)
-    grams_ref[width:, :] = dot_tn(now, prev)
-    shift_ref[...] = dot_nt(prev, upper_of(coupling_ref[...]))
-
-
-def late_kernel(parts_ref, now_ref, shift_ref, shifted_ref, grams_ref):
-    width = now_ref.shape[1]
-    shifted = -shift_ref[...]
+    shifted = -dot_nt(prev, upper_of(coupling_ref[...]))
     for part in range(parts_ref.shape[0]):
         shifted = shifted + parts_ref[part].astype(F32)
     shifted_ref[...] = shifted
-    grams_ref[:width, :] = dot_tn(now_ref[...], shifted)
-    grams_ref[width:, :] = dot_tn(shifted, shifted)
+    grams_ref[:width, :] = dot_tn(now, shifted)
+    grams_ref[width : 2 * width, :] = dot_tn(shifted, shifted)
+    grams_ref[2 * width : 3 * width, :] = dot_tn(now, now)
+    grams_ref[3 * width :, :] = dot_tn(now, prev)
 
 
 def sum_kernel(parts_ref, out_ref):
@@ -90,13 +85,9 @@
     return jnp.concatenate(strips, axis=0)
 
 
-def final_kernel(total_rows, parts_ref, early_ref, coupling_ref, now_ref, shifted_ref, basis_ref, projection_ref, rfactor_ref):
+def final_kernel(total_rows, grams_ref, coupling_ref, now_ref, shifted_ref, basis_ref, projection_ref, rfactor_ref):
     width = now_ref.shape[1]
-    late = parts_ref[0]
-    for part in range(1, parts_ref.shape[0]):
-        late = late + parts_ref[part]
-    cross, square = late[:width], late[width:]
-    now_square, now_prev = early_ref[:width, :], early_ref[width:, :]
+    cross, square, now_square, now_prev = [grams_ref[k * width : (k + 1) * width, :] for k in range(4)]
     norm_scale = total_rows**-0.5
     projection = (cross + dot_nt(now_prev, upper_of(coupling_ref[...]))) * norm_scale
     projection_ref[...] = projection
@@ -135,40 +126,28 @@
     )(tile_rows.reshape(-1), tile_cols.reshape(-1), tile_counts.reshape(-1), tile_block, gathered)
     parts = lax.all_to_all(partial.reshape(n_row, rows_dev, width), "row", split_axis=0, concat_axis=0, tiled=True)
 
-    early, shift = pl.pallas_call(
-        early_kernel,
+    shifted, grams = pl.pallas_call(
+        grams_kernel,
         out_shape=(
-            jax.ShapeDtypeStruct((2 * width, width), F32),
             jax.ShapeDtypeStruct((rows_dev, width), F32),
+            jax.ShapeDtypeStruct((4 * width, width), F32),
         ),
-        in_specs=[vmem] * 3,
+        in_specs=[vmem] * 4,
         out_specs=(vmem, vmem),
         compiler_params=params,
-        name="early_grams",
-    )(basis_now, basis_prev, coupling)
-    early = lax.psum(early, ("row", "col"))
-
-    shifted, late = pl.pallas_call(
-        late_kernel,
-        out_shape=(
-            jax.ShapeDtypeStruct((rows_dev, width), F32),
-            jax.ShapeDtypeStruct((2 * width, width), F32),
-        ),
-        in_specs=[vmem] * 3,
-        out_specs=(vmem, vmem),
-        compiler_params=params,
-        name="late_grams",
-    )(parts, basis_now, shift)
-    late = lax.all_gather(late, "col", axis=0)
-    late = pl.pallas_call(
+        name="local_grams",
+    )(parts, basis_now, basis_prev, coupling)
+    everyone = ("row", "col")
+    pieces = lax.all_to_all(grams.reshape(n_row * n_col, -1, width), everyone, split_axis=0, concat_axis=0, tiled=True)
+    piece = pl.pallas_call(
         sum_kernel,
-        out_shape=jax.ShapeDtypeStruct((2 * width, width), F32),
+        out_shape=jax.ShapeDtypeStruct(pieces.shape[1:], F32),
         in_specs=[vmem],
         out_specs=vmem,
         compiler_params=params,
-        name="column_sum",
-    )(late)
-    late = lax.all_gather(late, "row", axis=0)
+        name="sum_of_pieces",
+    )(pieces)
+    grams = lax.all_gather(piece, everyone, axis=0, tiled=True)
     return pl.pallas_call(
         functools.partial(final_kernel, total_rows),
         out_shape=(
@@ -176,11 +155,11 @@
             jax.ShapeDtypeStruct((width, width), F32),
             jax.ShapeDtypeStruct((width, width), F32),
         ),
-        in_specs=[vmem] * 5,
+        in_specs=[vmem] * 4,
         out_specs=(vmem, vmem, vmem),
         compiler_params=params,
         name="factor_and_basis",
-    )(late, early, coupling, basis_now, shifted)
+    )(grams, coupling, basis_now, shifted)
 
 
 def solution(mesh):

time: 181 us -> 98.9 us (0.55)
  waiting for transfers between devices: 121 us -> 0 us
  blocking collectives: 15.8 us -> 81 us
  between operations: 16.2 us -> 1.39 us
  starting transfers between devices: 5.74 us -> 0 us
  local copies, waits for them, and re-layouts: 2.81 us -> 0.69 us
  Pallas kernels: 16.6 us -> 14.6 us
    psum x1 -> x0, waiting for transfers between devices: 108 us -> none  [on_device(): early = lax.psum(early, ('row', 'col'))]
    all_to_all x0 -> x2, blocking collectives: none -> 34.4 us  [the longest x1 19.6 us: on_device(): lax.all_to_all(partial.reshape(n_row, rows_dev, width), 'row', split_axis...]
    all_gather x1, blocking collectives: 8.7 us -> 39.5 us  [on_device(): grams = lax.all_gather(piece, everyone, axis=0, tiled=True)]
    all_to_all x1 -> x0, waiting for transfers between devices: 12.5 us -> none  [on_device(): lax.all_to_all(partial.reshape(n_row, rows_dev, width), 'row', split_axis...]
    all_to_all x1 -> x0, starting transfers between devices: 5.66 us -> none  [on_device(): lax.all_to_all(partial.reshape(n_row, rows_dev, width), 'row', split_axis...]
    unnamed x16 -> x12, local copies, waits for them, and re-layouts: 2.81 us -> 0.69 us
  transfers between devices with their start and end apart: 3 -> 0, of which waited for: 2 -> 0; matrix products, arithmetic and copies ran while one was open for 0% -> 0% of each run, Pallas kernels for 1% -> 0%
where the time goes in v2:
time: 98.9 us; the launch traced here: 98.6 us
  blocking collectives  81 us (82%)
  Pallas kernels  14.6 us (15%)
  between operations  1.39 us (1%)
    all_gather x1, blocking collectives, on_device(): grams = lax.all_gather(piece, everyone, axis=0, tiled=True)  39.5 us
    all_to_all x1, blocking collectives, on_device(): lax.all_to_all(partial.reshape(n_row, rows_dev, width), 'row', split_axis...  19.6 us
    all_to_all x1, blocking collectives, on_device(): lax.all_to_all(grams.reshape(n_row * n_col, -1, width), everyone, split_a...  14.8 us
    pallas_call x1, Pallas kernels, on_device(): pl.pallas_call(functools.partial(final_kernel, total_rows), out_shape=(ja...  12.6 us
    all_gather x1, blocking collectives, on_device(): gathered = lax.all_gather(basis_now.astype(BF16), 'col', axis=0, tiled=True)  7.1 us

profile of v2, /device:TPU:1, one launch (start us, length us, event | category | flops | bytes accessed | tf_op | source)
XLA Modules:
  0.0 98.6 jit_solution(2808594175114692193)
XLA Ops:
  0.6 0.0 copy-start.1
  1.3 0.9 convert_element_type.3
  2.3 7.1 %all_gather.6.basis_ref = bf16[1024,128]{1,0:T(8,128)(2,1)S(1)} all-gather(bf16[256,128]{1,0:T(8,128)(2,1)S(1)} %convert_element_type.3), channel_id=1, replica_groups=mesh['row'=8,'col'=4] {'col'}, dimensions={0}, use_global_device_ids=true | all-gather | bytes 327680 | tf_op jit(solution)/shard_map/all_gather | solution.py:117
  9.4 0.0 copy-start.4
  9.4 0.0 copy-start.5
  9.4 0.0 copy-done.1
  9.4 0.6 copy-done.4
  10.0 0.0 copy-done.5
  10.0 0.9 tile_products.1
  10.9 0.0 copy-start
  11.0 0.0 copy-start.2
  11.0 0.0 copy-start.3
  11.0 19.6 %all_to_all.10.parts_ref = bf16[8,256,128]{2,1,0:T(8,128)(2,1)S(1)} all-to-all(bf16[8,256,128]{2,1,0:T(8,128)(2,1)S(1)} %bitcast.7), channel_id=1, replica_groups=mesh['row'=8,'col'=4] {'row'}, dimensions={0} | all-to-all | bytes 1048576 | tf_op jit(solution)/shard_map/all_to_all | solution.py:127
  30.6 0.0 copy-done
  30.6 0.0 copy-done.2
  30.6 0.0 copy-done.3
  30.6 1.1 %local_grams.1 = (f32[256,128]{1,0:T(8,128)S(1)}, f32[512,128]{1,0:T(8,128)S(1)}) custom-call(bf16[8,256,128]{2,1,0:T(8,128)(2,1)S(1)} %all_to_all.10.parts_ref, f32[256,128]{1,0:T(8,128)S(1)} %copy-done, f32[256,128]{1,0:T(8,128)S(1)} %copy-done.3, f32[128,128]{1,0:T(8,128)S(1)} %copy-done.2), custom_call_target="tpu_custom_call" | custom-call | tf_op jit(solution)/shard_map/local_grams/pallas_call | solution.py:129
  31.7 14.8 %all_to_all.11.parts_ref = f32[32,16,128]{2,1,0:T(8,128)S(1)} all-to-all(f32[32,16,128]{2,1,0:T(8,128)S(1)} %bitcast.9), channel_id=1, replica_groups=mesh['row'=8,'col'=4] {'row','col'}, dimensions={0} | all-to-all | bytes 524288 | tf_op jit(solution)/shard_map/all_to_all | solution.py:141
  46.5 39.5 %all_gather.7.grams_ref = f32[512,128]{1,0:T(8,128)S(1)} all-gather(f32[16,128]{1,0:T(8,128)S(1)} %sum_of_pieces.1), channel_id=1, replica_groups=mesh['row'=8,'col'=4] {'row','col'}, dimensions={0}, use_global_device_ids=true | all-gather | bytes 270336 | tf_op jit(solution)/shard_map/all_gather | solution.py:150
  86.0 12.6 %factor_and_basis.1 = (f32[256,128]{1,0:T(8,128)}, f32[128,128]{1,0:T(8,128)}, f32[128,128]{1,0:T(8,128)}) custom-call(f32[512,128]{1,0:T(8,128)S(1)} %all_gather.7.grams_ref, f32[128,128]{1,0:T(8,128)S(1)} %copy-done.2, f32[256,128]{1,0:T(8,128)S(1)} %copy-done, f32[256,128]{1,0:T(8,128)S(1)} %get-tuple-element.6.shifted_ref), custom_call_target="tpu_custom_call" | custom-call | tf_op jit(solution)/shard_map/factor_and_basis/pallas_call | solution.py:151
  (1 shorter events, 0.0 us)
Async XLA Ops:
  0.6 8.7 %copy-start.1 = (bf16[1,1,16,128,128]{4,3,2,1,0:T(8,128)(2,1)S(1)}, bf16[1,1,16,128,128]{4,3,2,1,0:T(8,128)(2,1)}, u32[]{:S(2)}) copy-start(bf16[1,1,16,128,128]{4,3,2,1,0:T(8,128)(2,1)} %param.10) | copy-start | bytes 1572868
  9.4 0.7 copy-start.4
  9.4 0.7 copy-start.5
  10.9 19.7 %copy-start = (f32[256,128]{1,0:T(8,128)S(1)}, f32[256,128]{1,0:T(8,128)}, u32[]{:S(2)}) copy-start(f32[256,128]{1,0:T(8,128)} %now_ref.3) | copy-start | bytes 393220
  11.0 19.6 %copy-start.2 = (f32[128,128]{1,0:T(8,128)S(1)}, f32[128,128]{1,0:T(8,128)}, u32[]{:S(2)}) copy-start(f32[128,128]{1,0:T(8,128)} %coupling_ref.3) | copy-start | bytes 196612
  11.0 19.6 %copy-start.3 = (f32[256,128]{1,0:T(8,128)S(1)}, f32[256,128]{1,0:T(8,128)}, u32[]{:S(2)}) copy-start(f32[256,128]{1,0:T(8,128)} %prev_ref.1) | copy-start | bytes 393220

commit v3 on v2

v3 whole, which is shorter than its diff:
```python
import functools

import jax
import jax.numpy as jnp
from jax import lax
from jax.experimental import pallas as pl
from jax.experimental.pallas import tpu as pltpu
from jax.sharding import PartitionSpec as P

HIGHEST = lax.Precision.HIGHEST
F32 = jnp.float32
BF16 = jnp.bfloat16


def dot(a, b):
    return jnp.dot(a, b, precision=HIGHEST, preferred_element_type=F32)


def dot_tn(a, b, precision=HIGHEST):
    return lax.dot_general(a, b, (((0,), (0,)), ((), ())), precision=precision, preferred_element_type=F32)


def dot_nt(a, b):
    return lax.dot_general(a, b, (((1,), (1,)), ((), ())), precision=HIGHEST, preferred_element_type=F32)


def upper_of(x):
    rows = lax.broadcasted_iota(jnp.int32, x.shape, 0)
    cols = lax.broadcasted_iota(jnp.int32, x.shape, 1)
    return jnp.where(rows <= cols, x, 0.0)


def tiles_kernel(n_col, rows_ref, cols_ref, count_ref, me_ref, tiles_ref, basis_ref, out_ref, total_ref, early_ref):
    slots, size, _ = tiles_ref.shape
    n_row, depth, width = out_ref.shape
    rows_dev = total_ref.shape[0] // n_row
    piece = early_ref.shape[0] // (n_row * n_col)
    total_ref[...] = jnp.zeros_like(total_ref)
    used = count_ref[0]
    for slot in range(slots):
        col = cols_ref[slot]
        per_slab = rows_dev // size
        start = pl.multiple_of((2 * per_slab * (col // per_slab) + lax.rem(col, per_slab)) * size, size)
        value = jnp.dot(tiles_ref[slot], basis_ref[pl.ds(start, size), :], preferred_element_type=F32)
        value = jnp.where(slot < used, value, 0.0)
        place = pl.ds(pl.multiple_of(rows_ref[slot] * size, size), size)
        total_ref[place, :] += value
    square = jnp.zeros((width, width), F32)
    cross = jnp.zeros((width, width), F32)
    for slab in range(n_col):
        now = basis_ref[2 * slab * rows_dev : (2 * slab + 1) * rows_dev, :]
        prev = basis_ref[(2 * slab + 1) * rows_dev : (2 * slab + 2) * rows_dev, :]
        square += dot_tn(now, now, None)
        cross += dot_tn(now, prev, None)
    if early_ref.shape[0] > 2 * width:
        early_ref[...] = jnp.zeros_like(early_ref)
    early_ref[:width, :] = square
    early_ref[width : 2 * width, :] = cross
    me = me_ref[0]
    for row in range(n_row):
        out_ref[row, :rows_dev, :] = total_ref[row * rows_dev : (row + 1) * rows_dev, :].astype(BF16)
        value = early_ref[pl.ds(pl.multiple_of((row * n_col + me) * piece, piece), piece), :]
        high = value.astype(BF16)
        low = (value - high.astype(F32)).astype(BF16)
        out_ref[row, rows_dev:, :] = jnp.concatenate([high, low], axis=0)


def grams_kernel(parts_ref, now_ref, prev_ref, coupling_ref, shifted_ref, grams_ref, early_ref):
    rows_dev, width = now_ref.shape
    piece = early_ref.shape[0]
    product = jnp.zeros((rows_dev, width), F32)
    early = jnp.zeros((piece, width), F32)
    for part in range(parts_ref.shape[0]):
        product = product + parts_ref[part, :rows_dev, :].astype(F32)
        both = parts_ref[part, rows_dev:, :].astype(F32)
        early = early + (both[:piece] + both[piece:])
    early_ref[...] = early
    shifted = product - dot_nt(prev_ref[...], upper_of(coupling_ref[...]))
    shifted_ref[...] = shifted
    if grams_ref.shape[0] > 2 * width:
        grams_ref[...] = jnp.zeros_like(grams_ref)
    grams_ref[:width, :] = dot_tn(now_ref[...], product)
    grams_ref[width : 2 * width, :] = dot_tn(shifted, shifted)


def spread_kernel(parts_ref, early_ref, out_ref):
    piece = early_ref.shape[0]
    total = parts_ref[0]
    for part in range(1, parts_ref.shape[0]):
        total = total + parts_ref[part]
    early = early_ref[...]
    for part in range(out_ref.shape[0]):
        out_ref[part, :piece, :] = total
        out_ref[part, piece:, :] = early


def eliminate(gram):
    width = gram.shape[0]
    lanes = lax.broadcasted_iota(jnp.int32, (1, width), 1)
    block = 8
    strips = [gram[r : r + block, :] for r in range(0, width, block)]
    subs = lax.broadcasted_iota(jnp.int32, (block, 1), 0)
    for k in range(width):
        at, inside = divmod(k, block)
        row = strips[at][inside : inside + 1, :]
        pivot = row[:, k : k + 1]
        scaled = jnp.where(lanes == k, 1.0, row) * (1.0 / pivot)
        for s in range(at, len(strips)):
            factor = strips[s][:, k : k + 1]
            if s == at:
                factor = jnp.where(subs > inside, factor, 0.0)
                kept = jnp.where((lanes == k) & (subs > inside), 0.0, strips[s])
            else:
                kept = jnp.where(lanes == k, 0.0, strips[s])
            strips[s] = kept - factor * scaled
    return jnp.concatenate(strips, axis=0)


def final_kernel(total_rows, pieces_ref, coupling_ref, now_ref, shifted_ref, basis_ref, projection_ref, rfactor_ref):
    width = now_ref.shape[1]
    piece = pieces_ref.shape[1] // 2
    late = pieces_ref[:, :piece, :].reshape(-1, width)
    early = pieces_ref[:, piece:, :].reshape(-1, width)
    now_product, square = late[:width], late[width : 2 * width]
    now_square, now_prev = early[:width], early[width : 2 * width]
    norm_scale = total_rows**-0.5
    projection = now_product * norm_scale
    projection_ref[...] = projection
    scaled = projection * norm_scale
    cross = now_product - dot_nt(now_prev, upper_of(coupling_ref[...]))
    mixed = dot_tn(scaled, cross - 0.5 * dot(now_square, scaled))
    gram = square - mixed - mixed.T
    reduced = eliminate(gram * (1.0 / total_rows))
    rows = lax.broadcasted_iota(jnp.int32, reduced.shape, 0)
    cols = lax.broadcasted_iota(jnp.int32, reduced.shape, 1)
    diagonal = jnp.sum(jnp.where(rows == cols, reduced, 0.0), axis=1, keepdims=True)
    root = lax.rsqrt(diagonal)
    rfactor_ref[...] = jnp.where(rows <= cols, reduced, 0.0) * root
    inverse = jnp.where(rows > cols, reduced, jnp.where(rows == cols, 1.0, 0.0)) * root
    residual = shifted_ref[...] - dot(now_ref[...], scaled)
    basis_ref[...] = dot_nt(residual, inverse)


def on_device(basis_now, basis_prev, coupling, tiles, tile_rows, tile_cols, tile_counts):
    rows_dev, width = basis_now.shape
    n_row, n_col = lax.axis_size("row"), lax.axis_size("col")
    devices = n_row * n_col
    tile_block = tiles[0, 0]
    total_rows = float(rows_dev * devices)
    piece = -(-2 * width // (8 * devices)) * 8
    smem = pl.BlockSpec(memory_space=pltpu.SMEM)
    vmem = pl.BlockSpec(memory_space=pltpu.VMEM)
    params = pltpu.CompilerParams(vmem_limit_bytes=48 * 1024 * 1024)

    both = jnp.concatenate([basis_now, basis_prev], axis=0).astype(BF16)
    gathered = lax.all_gather(both, "col", axis=0, tiled=True)
    partial = pl.pallas_call(
        functools.partial(tiles_kernel, n_col),
        out_shape=jax.ShapeDtypeStruct((n_row, rows_dev + 2 * piece, width), BF16),
        in_specs=[smem, smem, smem, smem, vmem, vmem],
        out_specs=vmem,
        scratch_shapes=[
            pltpu.VMEM((n_row * rows_dev, width), F32),
            pltpu.VMEM((devices * piece, width), F32),
        ],
        compiler_params=params,
        name="tile_products",
    )(
        tile_rows.reshape(-1),
        tile_cols.reshape(-1),
        tile_counts.reshape(-1),
        lax.axis_index("col").reshape(1),
        tile_block,
        gathered,
    )
    parts = lax.all_to_all(partial, "row", split_axis=0, concat_axis=0, tiled=True)

    shifted, grams, early = pl.pallas_call(
        grams_kernel,
        out_shape=(
            jax.ShapeDtypeStruct((rows_dev, width), F32),
            jax.ShapeDtypeStruct((devices * piece, width), F32),
            jax.ShapeDtypeStruct((piece, width), F32),
        ),
        in_specs=[vmem] * 4,
        out_specs=(vmem, vmem, vmem),
        compiler_params=params,
        name="local_grams",
    )(parts, basis_now, basis_prev, coupling)
    everyone = ("row", "col")
    pieces = lax.all_to_all(grams.reshape(devices, piece, width), everyone, split_axis=0, concat_axis=0, tiled=True)
    copies = pl.pallas_call(
        spread_kernel,
        out_shape=jax.ShapeDtypeStruct((devices, 2 * piece, width), F32),
        in_specs=[vmem, vmem],
        out_specs=vmem,
        compiler_params=params,
        name="sum_and_spread",
    )(pieces, early)
    sums = lax.all_to_all(copies, everyone, split_axis=0, concat_axis=0, tiled=True)
    return pl.pallas_call(
        functools.partial(final_kernel, total_rows),
        out_shape=(
            jax.ShapeDtypeStruct((rows_dev, width), F32),
            jax.ShapeDtypeStruct((width, width), F32),
            jax.ShapeDtypeStruct((width, width), F32),
        ),
        in_specs=[vmem] * 4,
        out_specs=(vmem, vmem, vmem),
        compiler_params=params,
        name="factor_and_basis",
    )(sums, coupling, basis_now, shifted)


def solution(mesh):
    placed = (
        P(("row", "col"), None),
        P(("row", "col"), None),
        P(),
        P("row", "col", None, None, None),
        P("row", "col", None),
        P("row", "col", None),
        P("row", "col"),
    )
    return jax.shard_map(
        on_device,
        mesh=mesh,
        in_specs=placed,
        out_specs=(P(("row", "col"), None), P(), P()),
        check_vma=False,
    )
```

time: 98.9 us -> 71.4 us (0.72)
  blocking collectives: 81 us -> 53.3 us
    all_gather x2 -> x1, blocking collectives: 46.6 us -> 8.67 us  [on_device(): gathered = lax.all_gather(both, 'col', axis=0, tiled=True)]
    all_to_all x2 -> x3, blocking collectives: 34.4 us -> 44.7 us  [the longest x1 20.7 us: on_device(): lax.all_to_all(partial, 'row', split_axis=0, concat_axis=0, tiled=True)]
where the time goes in v3:
time: 71.4 us; the launch traced here: 70.6 us
  blocking collectives  53.3 us (75%)
  Pallas kernels  14.2 us (20%)
  between operations  1.39 us (2%)
  other arithmetic  0.94 us (1%)
    all_to_all x1, blocking collectives, on_device(): lax.all_to_all(partial, 'row', split_axis=0, concat_axis=0, tiled=True)  20.7 us
    pallas_call x1, Pallas kernels, on_device(): pl.pallas_call(functools.partial(final_kernel, total_rows), out_shape=(ja...  12.4 us
    all_to_all x1, blocking collectives, on_device(): lax.all_to_all(copies, everyone, split_axis=0, concat_axis=0, tiled=True)  12.1 us
    all_to_all x1, blocking collectives, on_device(): lax.all_to_all(grams.reshape(devices, piece, width), everyone, split_axis...  11.9 us
    all_gather x1, blocking collectives, on_device(): gathered = lax.all_gather(both, 'col', axis=0, tiled=True)  8.67 us

profile of v3, /device:TPU:1, one launch (start us, length us, event | category | flops | bytes accessed | tf_op | source)
XLA Modules:
  0.0 70.6 jit_solution(5893824541171631400)
XLA Ops:
  0.6 0.0 copy-start
  1.3 0.9 %convert.7 = bf16[256,128]{1,0:T(8,128)(2,1)S(1)} convert(f32[256,128]{1,0:T(8,128)} %prev_ref.1) | non-fusion elementwise | flops 32768 | bytes 196608 | tf_op jit(solution)/shard_map/convert.1
  2.2 0.0 copy-done
  2.2 0.0 copy-start.2
  2.3 8.7 %all_gather.3.basis_ref = bf16[2048,128]{1,0:T(8,128)(2,1)S(1)} all-gather(bf16[512,128]{1,0:T(8,128)(2,1)S(1)} %pad_maximum_fusion), channel_id=1, replica_groups=mesh['row'=8,'col'=4] {'col'}, dimensions={0}, use_global_device_ids=true | all-gather | bytes 655360 | tf_op jit(solution)/shard_map/all_gather | solution.py:156
  11.0 0.0 copy-start.4
  11.0 0.0 copy-start.5
  11.0 0.0 copy-done.2
  11.0 0.6 copy-done.4
  11.6 0.0 copy-done.5
  11.6 1.0 %tile_products.1 = bf16[8,272,128]{2,1,0:T(8,128)(2,1)S(1)} custom-call(s32[16]{0:T(128)S(1)} %bitcast.9, s32[16]{0:T(128)S(1)} %bitcast.10, s32[1]{0:T(128)} %bitcast.6.count_ref, s32[1]{0:T(128)} %bitcast.3.me_ref, bf16[16,128,128]{2,1,0:T(8,128)(2,1)S(1)} %bitcast.7, bf16[2048,128]{1,0:T(8,128)(2,1)S(1)} %all_gather.3.basis_ref), custom_call_target="tpu_custom_call" | custom-call | tf_op jit(solution)/shard_map/tile_products/pallas_call | solution.py:157
  12.7 0.0 copy-start.1
  12.7 0.0 copy-start.3
  12.7 20.7 %all_to_all.15.parts_ref = bf16[8,272,128]{2,1,0:T(8,128)(2,1)S(1)} all-to-all(bf16[8,272,128]{2,1,0:T(8,128)(2,1)S(1)} %tile_products.1), channel_id=1, replica_groups=mesh['row'=8,'col'=4] {'row'}, dimensions={0} | all-to-all | bytes 1114112 | tf_op jit(solution)/shard_map/all_to_all | solution.py:176
  33.4 0.0 copy-done.1
  33.4 0.0 copy-done.3
  33.4 0.7 %local_grams.1 = (f32[256,128]{1,0:T(8,128)S(1)}, f32[256,128]{1,0:T(8,128)S(1)}, f32[8,128]{1,0:T(8,128)S(1)}) custom-call(bf16[8,272,128]{2,1,0:T(8,128)(2,1)S(1)} %all_to_all.15.parts_ref, f32[256,128]{1,0:T(8,128)S(1)} %copy-done, f32[256,128]{1,0:T(8,128)S(1)} %copy-done.1, f32[128,128]{1,0:T(8,128)S(1)} %copy-done.3), custom_call_target="tpu_custom_call" | custom-call | tf_op jit(solution)/shard_map/local_grams/pallas_call | solution.py:178
  34.1 11.9 %all_to_all.16.parts_ref = f32[32,8,128]{2,1,0:T(8,128)S(1)} all-to-all(f32[32,8,128]{2,1,0:T(8,128)S(1)} %bitcast.8), channel_id=1, replica_groups=mesh['row'=8,'col'=4] {'row','col'}, dimensions={0} | all-to-all | bytes 262144 | tf_op jit(solution)/shard_map/all_to_all | solution.py:191
  46.1 12.1 %all_to_all.17.pieces_ref = f32[32,16,128]{2,1,0:T(8,128)S(1)} all-to-all(f32[32,16,128]{2,1,0:T(8,128)S(1)} %sum_and_spread.1), channel_id=1, replica_groups=mesh['row'=8,'col'=4] {'row','col'}, dimensions={0} | all-to-all | bytes 524288 | tf_op jit(solution)/shard_map/all_to_all | solution.py:200
  58.2 12.4 %factor_and_basis.1 = (f32[256,128]{1,0:T(8,128)}, f32[128,128]{1,0:T(8,128)}, f32[128,128]{1,0:T(8,128)}) custom-call(f32[32,16,128]{2,1,0:T(8,128)S(1)} %all_to_all.17.pieces_ref, f32[128,128]{1,0:T(8,128)S(1)} %copy-done.3, f32[256,128]{1,0:T(8,128)S(1)} %copy-done, f32[256,128]{1,0:T(8,128)S(1)} %get-tuple-element.8.shifted_ref), custom_call_target="tpu_custom_call" | custom-call | tf_op jit(solution)/shard_map/factor_and_basis/pallas_call | solution.py:201
  (3 shorter events, 0.1 us)
Async XLA Ops:
  0.6 1.6 %copy-start = (f32[256,128]{1,0:T(8,128)S(1)}, f32[256,128]{1,0:T(8,128)}, u32[]{:S(2)}) copy-start(f32[256,128]{1,0:T(8,128)} %now_ref.3) | copy-start | bytes 393220
  2.2 8.7 %copy-start.2 = (bf16[1,1,16,128,128]{4,3,2,1,0:T(8,128)(2,1)S(1)}, bf16[1,1,16,128,128]{4,3,2,1,0:T(8,128)(2,1)}, u32[]{:S(2)}) copy-start(bf16[1,1,16,128,128]{4,3,2,1,0:T(8,128)(2,1)} %param.10) | copy-start | bytes 1572868
  11.0 0.7 copy-start.4
  11.0 0.7 copy-start.5
  12.7 20.7 %copy-start.1 = (f32[256,128]{1,0:T(8,128)S(1)}, f32[256,128]{1,0:T(8,128)}, u32[]{:S(2)}) copy-start(f32[256,128]{1,0:T(8,128)} %prev_ref.1) | copy-start | bytes 393220
  12.7 20.7 %copy-start.3 = (f32[128,128]{1,0:T(8,128)S(1)}, f32[128,128]{1,0:T(8,128)}, u32[]{:S(2)}) copy-start(f32[128,128]{1,0:T(8,128)} %coupling_ref.3) | copy-start | bytes 196612

commit v4 on v3

--- a/solution.py
+++ b/solution.py
@@ -30,49 +30,53 @@
     return jnp.where(rows <= cols, x, 0.0)
 
 
-def tiles_kernel(n_col, rows_ref, cols_ref, count_ref, me_ref, tiles_ref, basis_ref, out_ref, total_ref, early_ref):
+def tiles_kernel(n_row, n_col, rows_ref, cols_ref, count_ref, me_ref, tiles_ref, *refs):
+    basis_refs, out_refs = refs[:n_col], refs[n_col : n_col + n_row]
+    total_ref, early_ref, basis_ref = refs[n_col + n_row :]
     slots, size, _ = tiles_ref.shape
-    n_row, depth, width = out_ref.shape
+    depth, width = out_refs[0].shape
     rows_dev = total_ref.shape[0] // n_row
     piece = early_ref.shape[0] // (n_row * n_col)
+    my_row, my_col = me_ref[0], me_ref[1]
+    square = jnp.zeros((width, width), F32)
+    cross = jnp.zeros((width, width), F32)
+    for step in range(n_col):
+        now, prev = basis_refs[step][:rows_dev, :], basis_refs[step][rows_dev:, :]
+        owner = lax.rem(my_col + n_col - step, n_col)
+        basis_ref[pl.ds(pl.multiple_of(owner * rows_dev, rows_dev), rows_dev), :] = now
+        square += dot_tn(now, now, None)
+        cross += dot_tn(now, prev, None)
     total_ref[...] = jnp.zeros_like(total_ref)
     used = count_ref[0]
     for slot in range(slots):
-        col = cols_ref[slot]
-        per_slab = rows_dev // size
-        start = pl.multiple_of((2 * per_slab * (col // per_slab) + lax.rem(col, per_slab)) * size, size)
+        start = pl.multiple_of(cols_ref[slot] * size, size)
         value = jnp.dot(tiles_ref[slot], basis_ref[pl.ds(start, size), :], preferred_element_type=F32)
         value = jnp.where(slot < used, value, 0.0)
         place = pl.ds(pl.multiple_of(rows_ref[slot] * size, size), size)
         total_ref[place, :] += value
-    square = jnp.zeros((width, width), F32)
-    cross = jnp.zeros((width, width), F32)
-    for slab in range(n_col):
-        now = basis_ref[2 * slab * rows_dev : (2 * slab + 1) * rows_dev, :]
-        prev = basis_ref[(2 * slab + 1) * rows_dev : (2 * slab + 2) * rows_dev, :]
-        square += dot_tn(now, now, None)
-        cross += dot_tn(now, prev, None)
     if early_ref.shape[0] > 2 * width:
         early_ref[...] = jnp.zeros_like(early_ref)
     early_ref[:width, :] = square
     early_ref[width : 2 * width, :] = cross
-    me = me_ref[0]
-    for row in range(n_row):
-        out_ref[row, :rows_dev, :] = total_ref[row * rows_dev : (row + 1) * rows_dev, :].astype(BF16)
-        value = early_ref[pl.ds(pl.multiple_of((row * n_col + me) * piece, piece), piece), :]
+    for step in range(n_row):
+        row = lax.rem(my_row + step, n_row)
+        out_ref = out_refs[step]
+        out_ref[:rows_dev, :] = total_ref[pl.ds(pl.multiple_of(row * rows_dev, rows_dev), rows_dev), :].astype(BF16)
+        value = early_ref[pl.ds(pl.multiple_of((row * n_col + my_col) * piece, piece), piece), :]
         high = value.astype(BF16)
         low = (value - high.astype(F32)).astype(BF16)
-        out_ref[row, rows_dev:, :] = jnp.concatenate([high, low], axis=0)
-
-
-def grams_kernel(parts_ref, now_ref, prev_ref, coupling_ref, shifted_ref, grams_ref, early_ref):
+        out_ref[rows_dev:, :] = jnp.concatenate([high, low], axis=0)
+
+
+def grams_kernel(now_ref, prev_ref, coupling_ref, *refs):
+    part_refs, (shifted_ref, grams_ref, early_ref) = refs[:-3], refs[-3:]
     rows_dev, width = now_ref.shape
     piece = early_ref.shape[0]
     product = jnp.zeros((rows_dev, width), F32)
     early = jnp.zeros((piece, width), F32)
-    for part in range(parts_ref.shape[0]):
-        product = product + parts_ref[part, :rows_dev, :].astype(F32)
-        both = parts_ref[part, rows_dev:, :].astype(F32)
+    for part_ref in part_refs:
+        product = product + part_ref[:rows_dev, :].astype(F32)
+        both = part_ref[rows_dev:, :].astype(F32)
         early = early + (both[:piece] + both[piece:])
     early_ref[...] = early
     shifted = product - dot_nt(prev_ref[...], upper_of(coupling_ref[...]))
@@ -141,6 +145,13 @@
     basis_ref[...] = dot_nt(residual, inverse)
 
 
+def shifted_copies(blocks, axis):
+    n = lax.axis_size(axis)
+    return [blocks[0]] + [
+        lax.ppermute(blocks[step], axis, [(source, (source + step) % n) for source in range(n)]) for step in range(1, n)
+    ]
+
+
 def on_device(basis_now, basis_prev, coupling, tiles, tile_rows, tile_cols, tile_counts):
     rows_dev, width = basis_now.shape
     n_row, n_col = lax.axis_size("row"), lax.axis_size("col")
@@ -153,15 +164,16 @@
     params = pltpu.CompilerParams(vmem_limit_bytes=48 * 1024 * 1024)
 
     both = jnp.concatenate([basis_now, basis_prev], axis=0).astype(BF16)
-    gathered = lax.all_gather(both, "col", axis=0, tiled=True)
-    partial = pl.pallas_call(
-        functools.partial(tiles_kernel, n_col),
-        out_shape=jax.ShapeDtypeStruct((n_row, rows_dev + 2 * piece, width), BF16),
-        in_specs=[smem, smem, smem, smem, vmem, vmem],
-        out_specs=vmem,
+    slabs = shifted_copies([both] * n_col, "col")
+    blocks = pl.pallas_call(
+        functools.partial(tiles_kernel, n_row, n_col),
+        out_shape=[jax.ShapeDtypeStruct((rows_dev + 2 * piece, width), BF16)] * n_row,
+        in_specs=[smem] * 4 + [vmem] * (1 + n_col),
+        out_specs=[vmem] * n_row,
         scratch_shapes=[
             pltpu.VMEM((n_row * rows_dev, width), F32),
             pltpu.VMEM((devices * piece, width), F32),
+            pltpu.VMEM((n_col * rows_dev, width), BF16),
         ],
         compiler_params=params,
         name="tile_products",
@@ -169,11 +181,11 @@
         tile_rows.reshape(-1),
         tile_cols.reshape(-1),
         tile_counts.reshape(-1),
-        lax.axis_index("col").reshape(1),
+        jnp.stack([lax.axis_index("row"), lax.axis_index("col")]),
         tile_block,
-        gathered,
+        *slabs,
     )
-    parts = lax.all_to_all(partial, "row", split_axis=0, concat_axis=0, tiled=True)
+    parts = shifted_copies(blocks, "row")
 
     shifted, grams, early = pl.pallas_call(
         grams_kernel,
@@ -182,11 +194,11 @@
             jax.ShapeDtypeStruct((devices * piece, width), F32),
             jax.ShapeDtypeStruct((piece, width), F32),
         ),
-        in_specs=[vmem] * 4,
+        in_specs=[vmem] * (3 + n_row),
         out_specs=(vmem, vmem, vmem),
         compiler_params=params,
         name="local_grams",
-    )(parts, basis_now, basis_prev, coupling)
+    )(basis_now, basis_prev, coupling, *parts)
     everyone = ("row", "col")
     pieces = lax.all_to_all(grams.reshape(devices, piece, width), everyone, split_axis=0, concat_axis=0, tiled=True)
     copies = pl.pallas_call(

time: 71.4 us -> 68.8 us (0.964)
  blocking collectives: 53.3 us -> 28.4 us
  starting transfers between devices: 0 us -> 14.5 us
  waiting for transfers between devices: 0 us -> 7.68 us
    all_to_all x1 -> x0, blocking collectives: 20.7 us -> none  [on_device(): lax.all_to_all(partial, 'row', split_axis=0, concat_axis=0, tiled=True)]
    ppermute x0 -> x10, starting transfers between devices: none -> 14.5 us  [shifted_copies(): lax.ppermute(blocks[step], axis, [(source, (source + step) % n) for sourc...]
    all_gather x1 -> x0, blocking collectives: 8.67 us -> none  [on_device(): gathered = lax.all_gather(both, 'col', axis=0, tiled=True)]
    ppermute x0 -> x10, waiting for transfers between devices: none -> 7.68 us  [shifted_copies(): lax.ppermute(blocks[step], axis, [(source, (source + step) % n) for sourc...]
    all_to_all x1, blocking collectives: 11.9 us -> 16.3 us  [on_device(): lax.all_to_all(grams.reshape(devices, piece, width), everyone, split_axis...]
  transfers between devices with their start and end apart: 0 -> 10, of which waited for: 0 -> 5; matrix products, arithmetic and copies ran while one was open for 0% -> 0% of each run, Pallas kernels for 0% -> 0%
where the time goes in v4:
time: 68.8 us; the launch traced here: 68 us
  blocking collectives  28.4 us (41%)
  starting transfers between devices  14.5 us (21%)
  Pallas kernels  14.3 us (21%)
  waiting for transfers between devices  7.68 us (11%)
  between operations  1.35 us (2%)
  other arithmetic  1.07 us (2%)
    all_to_all x1, blocking collectives, on_device(): lax.all_to_all(grams.reshape(devices, piece, width), everyone, split_axis...  16.3 us
    ppermute x10, starting transfers between devices, shifted_copies(): lax.ppermute(blocks[step], axis, [(source, (source + step) % n) for sourc...  14.5 us
    pallas_call x1, Pallas kernels, on_device(): pl.pallas_call(functools.partial(final_kernel, total_rows), out_shape=(ja...  12.4 us
    all_to_all x1, blocking collectives, on_device(): lax.all_to_all(copies, everyone, split_axis=0, concat_axis=0, tiled=True)  12.1 us
    ppermute x10, waiting for transfers between devices, shifted_copies(): lax.ppermute(blocks[step], axis, [(source, (source + step) % n) for sourc...  7.68 us
  transfers between devices with their start and end apart: 10, of which 5 were waited for; matrix products, arithmetic and copies ran while one was open for 0% of the time, Pallas kernels for 0%

profile of v4, /device:TPU:1, one launch (start us, length us, event | category | flops | bytes accessed | tf_op | source)
XLA Modules:
  0.0 68.0 jit_solution(13069480107677397838)
XLA Ops:
  0.6 0.0 copy-start
  0.6 0.0 copy-start.2
  0.6 1.0 %convert.7 = bf16[256,128]{1,0:T(8,128)(2,1)S(1)} convert(f32[256,128]{1,0:T(8,128)} %prev_ref.1) | non-fusion elementwise | flops 32768 | bytes 196608 | tf_op jit(solution)/shard_map/convert.1
  1.6 0.0 copy-done
  1.7 0.1 collective-permute-start.2
  1.8 2.7 %collective-permute-start.1 = (bf16[512,128]{1,0:T(8,128)(2,1)S(1)}, bf16[512,128]{1,0:T(8,128)(2,1)S(1)}, u32[]{:S(2)}, u32[]{:S(2)}) collective-permute-start(bf16[512,128]{1,0:T(8,128)(2,1)S(1)} %pad_maximum_fusion.refs_0_), channel_id=1, source_target_pairs={{0,2},{1,3},{2,0},{3,1},{4,6},{5,7},{6,4},{7,5},{8,10},{9,11},{10,... | collective-permute-start | bytes 393224 | tf_op jit(solution)/shard_map/ppermute | solution.py:151
  4.5 1.3 %collective-permute-start = (bf16[512,128]{1,0:T(8,128)(2,1)S(1)}, bf16[512,128]{1,0:T(8,128)(2,1)S(1)}, u32[]{:S(2)}, u32[]{:S(2)}) collective-permute-start(bf16[512,128]{1,0:T(8,128)(2,1)S(1)} %pad_maximum_fusion.refs_0_), channel_id=1, source_target_pairs={{0,1},{1,2},{2,3},{3,0},{4,5},{5,6},{6,7},{7,4},{8,9},{9,10},{10,1... | collective-permute-start | bytes 393224 | tf_op jit(solution)/shard_map/ppermute | solution.py:151
  6.5 0.1 pad_add_fusion.me_ref
  6.5 2.2 %collective-permute-done.2.refs_3_ = bf16[512,128]{1,0:T(8,128)(2,1)S(1)} collective-permute-done((bf16[512,128]{1,0:T(8,128)(2,1)S(1)}, bf16[512,128]{1,0:T(8,128)(2,1)S(1)}, u32[]{:S(2)}, u32[]{:S(2)}) %collective-permute-start.2) | collective-permute-done | bytes 131104 | tf_op jit(solution)/shard_map/ppermute | solution.py:151
  8.7 0.0 collective-permute-done.1.refs_2_
  8.7 1.9 %collective-permute-done.refs_1_ = bf16[512,128]{1,0:T(8,128)(2,1)S(1)} collective-permute-done((bf16[512,128]{1,0:T(8,128)(2,1)S(1)}, bf16[512,128]{1,0:T(8,128)(2,1)S(1)}, u32[]{:S(2)}, u32[]{:S(2)}) %collective-permute-start) | collective-permute-done | bytes 131104 | tf_op jit(solution)/shard_map/ppermute | solution.py:151
  10.6 0.0 copy-start.4
  10.6 0.0 copy-start.5
  10.6 0.0 copy-done.2
  10.6 0.6 copy-done.4
  11.2 0.0 copy-done.5
  11.2 0.0 copy-start.1
  11.2 0.0 copy-start.3
  11.3 1.2 %tile_products.1 = (bf16[272,128]{1,0:T(8,128)(2,1)S(1)}, bf16[272,128]{1,0:T(8,128)(2,1)S(1)}, bf16[272,128]{1,0:T(8,128)(2,1)S(1)}, bf16[272,128]{1,0:T(8,128)...) custom-call(s32[16]{0:T(128)S(1)} %bitcast.10, ...), custom_call_target="tpu_custom_call" | custom-call | tf_op jit(solution)/shard_map/tile_products/pallas_call | solution.py:168
  12.4 1.3 %collective-permute-start.3 = (bf16[272,128]{1,0:T(8,128)(2,1)S(1)}, bf16[272,128]{1,0:T(8,128)(2,1)S(1)}, u32[]{:S(2)}, u32[]{:S(2)}) collective-permute-start(bf16[272,128]{1,0:T(8,128)(2,1)S(1)} %get-tuple-element.15), channel_id=1, source_target_pairs={{0,4},{4,8},{8,12},{12,16},{16,20},{20,24},{24,28},{28,0},{1,5},{5... | collective-permute-start | bytes 208904 | tf_op jit(solution)/shard_map/ppermute | solution.py:151
  13.7 1.3 %collective-permute-start.4 = (bf16[272,128]{1,0:T(8,128)(2,1)S(1)}, bf16[272,128]{1,0:T(8,128)(2,1)S(1)}, u32[]{:S(2)}, u32[]{:S(2)}) collective-permute-start(bf16[272,128]{1,0:T(8,128)(2,1)S(1)} %get-tuple-element.16), channel_id=1, source_target_pairs={{0,8},{4,12},{8,16},{12,20},{16,24},{20,28},{24,0},{28,4},{1,9},{5... | collective-permute-start | bytes 208904 | tf_op jit(solution)/shard_map/ppermute | solution.py:151
  15.0 2.3 %collective-permute-start.5 = (bf16[272,128]{1,0:T(8,128)(2,1)S(1)}, bf16[272,128]{1,0:T(8,128)(2,1)S(1)}, u32[]{:S(2)}, u32[]{:S(2)}) collective-permute-start(bf16[272,128]{1,0:T(8,128)(2,1)S(1)} %get-tuple-element.17), channel_id=1, source_target_pairs={{0,12},{4,16},{8,20},{12,24},{16,28},{20,0},{24,4},{28,8},{1,13},{... | collective-permute-start | bytes 208904 | tf_op jit(solution)/shard_map/ppermute | solution.py:151
  17.3 0.9 %collective-permute-start.6 = (bf16[272,128]{1,0:T(8,128)(2,1)S(1)}, bf16[272,128]{1,0:T(8,128)(2,1)S(1)}, u32[]{:S(2)}, u32[]{:S(2)}) collective-permute-start(bf16[272,128]{1,0:T(8,128)(2,1)S(1)} %get-tuple-element.18), channel_id=1, source_target_pairs={{0,16},{4,20},{8,24},{12,28},{16,0},{20,4},{24,8},{28,12},{1,17},{... | collective-permute-start | bytes 208904 | tf_op jit(solution)/shard_map/ppermute | solution.py:151
  18.2 2.3 %collective-permute-start.7 = (bf16[272,128]{1,0:T(8,128)(2,1)S(1)}, bf16[272,128]{1,0:T(8,128)(2,1)S(1)}, u32[]{:S(2)}, u32[]{:S(2)}) collective-permute-start(bf16[272,128]{1,0:T(8,128)(2,1)S(1)} %get-tuple-element.19), channel_id=1, source_target_pairs={{0,20},{4,24},{8,28},{12,0},{16,4},{20,8},{24,12},{28,16},{1,21},{... | collective-permute-start | bytes 208904 | tf_op jit(solution)/shard_map/ppermute | solution.py:151
  20.6 0.0 collective-permute-done.3.refs_1_
  20.6 1.1 %collective-permute-start.8 = (bf16[272,128]{1,0:T(8,128)(2,1)S(1)}, bf16[272,128]{1,0:T(8,128)(2,1)S(1)}, u32[]{:S(2)}, u32[]{:S(2)}) collective-permute-start(bf16[272,128]{1,0:T(8,128)(2,1)S(1)} %get-tuple-element.20), channel_id=1, source_target_pairs={{0,24},{4,28},{8,0},{12,4},{16,8},{20,12},{24,16},{28,20},{1,25},{... | collective-permute-start | bytes 208904 | tf_op jit(solution)/shard_map/ppermute | solution.py:151
  21.6 0.0 collective-permute-done.4.refs_2_
  21.6 1.2 %collective-permute-start.9 = (bf16[272,128]{1,0:T(8,128)(2,1)S(1)}, bf16[272,128]{1,0:T(8,128)(2,1)S(1)}, u32[]{:S(2)}, u32[]{:S(2)}) collective-permute-start(bf16[272,128]{1,0:T(8,128)(2,1)S(1)} %get-tuple-element.21), channel_id=1, source_target_pairs={{0,28},{4,0},{8,4},{12,8},{16,12},{20,16},{24,20},{28,24},{1,29},{... | collective-permute-start | bytes 208904 | tf_op jit(solution)/shard_map/ppermute | solution.py:151
  22.8 2.9 %collective-permute-done.5.refs_3_ = bf16[272,128]{1,0:T(8,128)(2,1)S(1)} collective-permute-done((bf16[272,128]{1,0:T(8,128)(2,1)S(1)}, bf16[272,128]{1,0:T(8,128)(2,1)S(1)}, u32[]{:S(2)}, u32[]{:S(2)}) %collective-permute-start.5) | collective-permute-done | bytes 69664 | tf_op jit(solution)/shard_map/ppermute | solution.py:151
  25.7 0.4 collective-permute-done.6.refs_4_
  26.0 0.0 collective-permute-done.7.refs_5_
  26.0 0.0 collective-permute-done.8.refs_6_
  26.0 0.4 collective-permute-done.9.refs_7_
  26.4 0.0 copy-done.1
  26.4 0.0 copy-done.3
  26.4 0.7 %local_grams.1 = (f32[256,128]{1,0:T(8,128)S(1)}, f32[256,128]{1,0:T(8,128)S(1)}, f32[8,128]{1,0:T(8,128)S(1)}) custom-call(f32[256,128]{1,0:T(8,128)S(1)} %copy-done, f32[256,128]{1,0:T(8,128)S(1)} %copy-done.1, f32[128,128]{1,0:T(8,128)S(1)} %copy-done.3, bf16[272,128]{1,0:T(8,128)(2,1)S(1)} %get-tuple-element.14.refs_0_, ...), custom_call_target="tpu_custom_call" | custom-call | tf_op jit(solution)/shard_map/local_grams/pallas_call | solution.py:190
  27.2 16.3 %all_to_all.10.parts_ref = f32[32,8,128]{2,1,0:T(8,128)S(1)} all-to-all(f32[32,8,128]{2,1,0:T(8,128)S(1)} %bitcast.9), channel_id=1, replica_groups=mesh['row'=8,'col'=4] {'row','col'}, dimensions={0} | all-to-all | bytes 262144 | tf_op jit(solution)/shard_map/all_to_all | solution.py:203
  43.6 12.1 %all_to_all.11.pieces_ref = f32[32,16,128]{2,1,0:T(8,128)S(1)} all-to-all(f32[32,16,128]{2,1,0:T(8,128)S(1)} %sum_and_spread.1), channel_id=1, replica_groups=mesh['row'=8,'col'=4] {'row','col'}, dimensions={0} | all-to-all | bytes 524288 | tf_op jit(solution)/shard_map/all_to_all | solution.py:212
  55.6 12.4 %factor_and_basis.1 = (f32[256,128]{1,0:T(8,128)}, f32[128,128]{1,0:T(8,128)}, f32[128,128]{1,0:T(8,128)}) custom-call(f32[32,16,128]{2,1,0:T(8,128)S(1)} %all_to_all.11.pieces_ref, f32[128,128]{1,0:T(8,128)S(1)} %copy-done.3, f32[256,128]{1,0:T(8,128)S(1)} %copy-done, f32[256,128]{1,0:T(8,128)S(1)} %get-tuple-element.24.shifted_ref), custom_call_target="tpu_custom_call" | custom-call | tf_op jit(solution)/shard_map/factor_and_basis/pallas_call | solution.py:213
  (3 shorter events, 0.1 us)
Async XLA Ops:
  0.6 1.0 %copy-start = (f32[256,128]{1,0:T(8,128)S(1)}, f32[256,128]{1,0:T(8,128)}, u32[]{:S(2)}) copy-start(f32[256,128]{1,0:T(8,128)} %now_ref.3) | copy-start | bytes 393220
  0.6 9.9 %copy-start.2 = (bf16[1,1,16,128,128]{4,3,2,1,0:T(8,128)(2,1)S(1)}, bf16[1,1,16,128,128]{4,3,2,1,0:T(8,128)(2,1)}, u32[]{:S(2)}) copy-start(bf16[1,1,16,128,128]{4,3,2,1,0:T(8,128)(2,1)} %param.10) | copy-start | bytes 1572868
  1.7 7.0 %collective-permute-start.2 = (bf16[512,128]{1,0:T(8,128)(2,1)S(1)}, bf16[512,128]{1,0:T(8,128)(2,1)S(1)}, u32[]{:S(2)}, u32[]{:S(2)}) collective-permute-start(bf16[512,128]{1,0:T(8,128)(2,1)S(1)} %pad_maximum_fusion.refs_0_), channel_id=1, source_target_pairs={{0,3},{1,0},{2,1},{3,2},{4,7},{5,4},{6,5},{7,6},{8,11},{9,8},{10,9... | collective-permute-start | bytes 393224 | tf_op jit(solution)/shard_map/ppermute | solution.py:151
  1.8 6.9 %collective-permute-start.1 = (bf16[512,128]{1,0:T(8,128)(2,1)S(1)}, bf16[512,128]{1,0:T(8,128)(2,1)S(1)}, u32[]{:S(2)}, u32[]{:S(2)}) collective-permute-start(bf16[512,128]{1,0:T(8,128)(2,1)S(1)} %pad_maximum_fusion.refs_0_), channel_id=1, source_target_pairs={{0,2},{1,3},{2,0},{3,1},{4,6},{5,7},{6,4},{7,5},{8,10},{9,11},{10,... | collective-permute-start | bytes 393224 | tf_op jit(solution)/shard_map/ppermute | solution.py:151
  4.5 6.1 %collective-permute-start = (bf16[512,128]{1,0:T(8,128)(2,1)S(1)}, bf16[512,128]{1,0:T(8,128)(2,1)S(1)}, u32[]{:S(2)}, u32[]{:S(2)}) collective-permute-start(bf16[512,128]{1,0:T(8,128)(2,1)S(1)} %pad_maximum_fusion.refs_0_), channel_id=1, source_target_pairs={{0,1},{1,2},{2,3},{3,0},{4,5},{5,6},{6,7},{7,4},{8,9},{9,10},{10,1... | collective-permute-start | bytes 393224 | tf_op jit(solution)/shard_map/ppermute | solution.py:151
  10.6 0.7 copy-start.4
  10.6 0.7 copy-start.5
  11.2 15.2 %copy-start.1 = (f32[256,128]{1,0:T(8,128)S(1)}, f32[256,128]{1,0:T(8,128)}, u32[]{:S(2)}) copy-start(f32[256,128]{1,0:T(8,128)} %prev_ref.1) | copy-start | bytes 393220
  11.2 15.2 %copy-start.3 = (f32[128,128]{1,0:T(8,128)S(1)}, f32[128,128]{1,0:T(8,128)}, u32[]{:S(2)}) copy-start(f32[128,128]{1,0:T(8,128)} %coupling_ref.3) | copy-start | bytes 196612
  12.4 8.1 %collective-permute-start.3 = (bf16[272,128]{1,0:T(8,128)(2,1)S(1)}, bf16[272,128]{1,0:T(8,128)(2,1)S(1)}, u32[]{:S(2)}, u32[]{:S(2)}) collective-permute-start(bf16[272,128]{1,0:T(8,128)(2,1)S(1)} %get-tuple-element.15), channel_id=1, source_target_pairs={{0,4},{4,8},{8,12},{12,16},{16,20},{20,24},{24,28},{28,0},{1,5},{5... | collective-permute-start | bytes 208904 | tf_op jit(solution)/shard_map/ppermute | solution.py:151
  13.7 7.9 %collective-permute-start.4 = (bf16[272,128]{1,0:T(8,128)(2,1)S(1)}, bf16[272,128]{1,0:T(8,128)(2,1)S(1)}, u32[]{:S(2)}, u32[]{:S(2)}) collective-permute-start(bf16[272,128]{1,0:T(8,128)(2,1)S(1)} %get-tuple-element.16), channel_id=1, source_target_pairs={{0,8},{4,12},{8,16},{12,20},{16,24},{20,28},{24,0},{28,4},{1,9},{5... | collective-permute-start | bytes 208904 | tf_op jit(solution)/shard_map/ppermute | solution.py:151
  15.0 10.7 %collective-permute-start.5 = (bf16[272,128]{1,0:T(8,128)(2,1)S(1)}, bf16[272,128]{1,0:T(8,128)(2,1)S(1)}, u32[]{:S(2)}, u32[]{:S(2)}) collective-permute-start(bf16[272,128]{1,0:T(8,128)(2,1)S(1)} %get-tuple-element.17), channel_id=1, source_target_pairs={{0,12},{4,16},{8,20},{12,24},{16,28},{20,0},{24,4},{28,8},{1,13},{... | collective-permute-start | bytes 208904 | tf_op jit(solution)/shard_map/ppermute | solution.py:151
  17.3 8.8 %collective-permute-start.6 = (bf16[272,128]{1,0:T(8,128)(2,1)S(1)}, bf16[272,128]{1,0:T(8,128)(2,1)S(1)}, u32[]{:S(2)}, u32[]{:S(2)}) collective-permute-start(bf16[272,128]{1,0:T(8,128)(2,1)S(1)} %get-tuple-element.18), channel_id=1, source_target_pairs={{0,16},{4,20},{8,24},{12,28},{16,0},{20,4},{24,8},{28,12},{1,17},{... | collective-permute-start | bytes 208904 | tf_op jit(solution)/shard_map/ppermute | solution.py:151
  18.2 7.8 %collective-permute-start.7 = (bf16[272,128]{1,0:T(8,128)(2,1)S(1)}, bf16[272,128]{1,0:T(8,128)(2,1)S(1)}, u32[]{:S(2)}, u32[]{:S(2)}) collective-permute-start(bf16[272,128]{1,0:T(8,128)(2,1)S(1)} %get-tuple-element.19), channel_id=1, source_target_pairs={{0,20},{4,24},{8,28},{12,0},{16,4},{20,8},{24,12},{28,16},{1,21},{... | collective-permute-start | bytes 208904 | tf_op jit(solution)/shard_map/ppermute | solution.py:151
  20.6 5.5 %collective-permute-start.8 = (bf16[272,128]{1,0:T(8,128)(2,1)S(1)}, bf16[272,128]{1,0:T(8,128)(2,1)S(1)}, u32[]{:S(2)}, u32[]{:S(2)}) collective-permute-start(bf16[272,128]{1,0:T(8,128)(2,1)S(1)} %get-tuple-element.20), channel_id=1, source_target_pairs={{0,24},{4,28},{8,0},{12,4},{16,8},{20,12},{24,16},{28,20},{1,25},{... | collective-permute-start | bytes 208904 | tf_op jit(solution)/shard_map/ppermute | solution.py:151
  21.6 4.8 %collective-permute-start.9 = (bf16[272,128]{1,0:T(8,128)(2,1)S(1)}, bf16[272,128]{1,0:T(8,128)(2,1)S(1)}, u32[]{:S(2)}, u32[]{:S(2)}) collective-permute-start(bf16[272,128]{1,0:T(8,128)(2,1)S(1)} %get-tuple-element.21), channel_id=1, source_target_pairs={{0,28},{4,0},{8,4},{12,8},{16,12},{20,16},{24,20},{28,24},{1,29},{... | collective-permute-start | bytes 208904 | tf_op jit(solution)/shard_map/ppermute | solution.py:151

commit v5 on v4

--- a/solution.py
+++ b/solution.py
@@ -100,24 +100,43 @@
 
 def eliminate(gram):
     width = gram.shape[0]
-    lanes = lax.broadcasted_iota(jnp.int32, (1, width), 1)
     block = 8
+    lanes = lax.broadcasted_iota(jnp.int32, (block, width), 1)
+    subs = lax.broadcasted_iota(jnp.int32, (block, width), 0)
+
+    def column(strip, k):
+        return jnp.broadcast_to(strip[:, k : k + 1], (block, width))
+
+    def row(strip, k):
+        return jnp.broadcast_to(strip[k : k + 1, :], (block, width))
+
     strips = [gram[r : r + block, :] for r in range(0, width, block)]
-    subs = lax.broadcasted_iota(jnp.int32, (block, 1), 0)
-    for k in range(width):
-        at, inside = divmod(k, block)
-        row = strips[at][inside : inside + 1, :]
-        pivot = row[:, k : k + 1]
-        scaled = jnp.where(lanes == k, 1.0, row) * (1.0 / pivot)
-        for s in range(at, len(strips)):
-            factor = strips[s][:, k : k + 1]
-            if s == at:
-                factor = jnp.where(subs > inside, factor, 0.0)
-                kept = jnp.where((lanes == k) & (subs > inside), 0.0, strips[s])
-            else:
-                kept = jnp.where(lanes == k, 0.0, strips[s])
-            strips[s] = kept - factor * scaled
-    return jnp.concatenate(strips, axis=0)
+    finished = []
+    for at in range(len(strips)):
+        first = at * block
+        panel = strips[at]
+        columns = [column(panel, first + j) for j in range(block)]
+        kept = panel
+        for j in range(block):
+            here, pivot_lane = subs == j, lanes == first + j
+            inverse = 1.0 / row(columns[j], j)
+            pivot_row = row(panel, j)
+            kept = jnp.where(here, pivot_row, kept)
+            unit = jnp.where(pivot_lane, 1.0, pivot_row) * inverse
+            factor = columns[j]
+            panel = jnp.where(here, unit, jnp.where(pivot_lane, 0.0, panel) - factor * unit)
+            for m in range(j + 1, block):
+                scaled = row(columns[m], j) * inverse
+                columns[m] = jnp.where(here, scaled, columns[m] - factor * scaled)
+        finished.append(kept)
+        rows = [row(panel, m) for m in range(block)]
+        inside = (lanes >= first) & (lanes < first + block)
+        for s in range(at + 1, len(strips)):
+            terms = [column(strips[s], first + m) * rows[m] for m in range(block)]
+            while len(terms) > 1:
+                terms = [x + y for x, y in zip(terms[::2], terms[1::2])]
+            strips[s] = jnp.where(inside, 0.0, strips[s]) - terms[0]
+    return jnp.concatenate(finished, axis=0)
 
 
 def final_kernel(total_rows, pieces_ref, coupling_ref, now_ref, shifted_ref, basis_ref, projection_ref, rfactor_ref):

time: 68.8 us -> 62.8 us (0.913)
  Pallas kernels: 14.3 us -> 8.37 us
    pallas_call x1, Pallas kernels: 12.4 us -> 6.45 us  [on_device(): pl.pallas_call(functools.partial(final_kernel, total_rows), out_shape=(ja...]
where the time goes in v5:
time: 62.8 us; the launch traced here: 62.1 us
  blocking collectives  28.4 us (45%)
  starting transfers between devices  14.5 us (23%)
  Pallas kernels  8.37 us (13%)
  waiting for transfers between devices  7.68 us (12%)
  between operations  1.35 us (2%)
  other arithmetic  1.07 us (2%)
  local copies, waits for them, and re-layouts  0.68 us (1%)
    all_to_all x1, blocking collectives, on_device(): lax.all_to_all(grams.reshape(devices, piece, width), everyone, split_axis...  16.4 us
    ppermute x10, starting transfers between devices, shifted_copies(): lax.ppermute(blocks[step], axis, [(source, (source + step) % n) for sourc...  14.5 us
    all_to_all x1, blocking collectives, on_device(): lax.all_to_all(copies, everyone, split_axis=0, concat_axis=0, tiled=True)  12.1 us
    ppermute x10, waiting for transfers between devices, shifted_copies(): lax.ppermute(blocks[step], axis, [(source, (source + step) % n) for sourc...  7.68 us
    pallas_call x1, Pallas kernels, on_device(): pl.pallas_call(functools.partial(final_kernel, total_rows), out_shape=(ja...  6.45 us
  transfers between devices with their start and end apart: 10, of which 5 were waited for; matrix products, arithmetic and copies ran while one was open for 0% of the time, Pallas kernels for 0%

profile of v5, /device:TPU:1, one launch (start us, length us, event | category | flops | bytes accessed | tf_op | source)
XLA Modules:
  0.0 62.1 jit_solution(5836179789277787046)
XLA Ops:
  0.6 0.0 copy-start
  0.6 0.0 copy-start.2
  0.6 1.0 %convert.7 = bf16[256,128]{1,0:T(8,128)(2,1)S(1)} convert(f32[256,128]{1,0:T(8,128)} %prev_ref.1) | non-fusion elementwise | flops 32768 | bytes 196608 | tf_op jit(solution)/shard_map/convert.1
  1.6 0.0 copy-done
  1.7 0.1 collective-permute-start.2
  1.8 2.7 %collective-permute-start.1 = (bf16[512,128]{1,0:T(8,128)(2,1)S(1)}, bf16[512,128]{1,0:T(8,128)(2,1)S(1)}, u32[]{:S(2)}, u32[]{:S(2)}) collective-permute-start(bf16[512,128]{1,0:T(8,128)(2,1)S(1)} %pad_maximum_fusion.refs_0_), channel_id=1, source_target_pairs={{0,2},{1,3},{2,0},{3,1},{4,6},{5,7},{6,4},{7,5},{8,10},{9,11},{10,... | collective-permute-start | bytes 393224 | tf_op jit(solution)/shard_map/ppermute | solution.py:170
  4.5 1.3 %collective-permute-start = (bf16[512,128]{1,0:T(8,128)(2,1)S(1)}, bf16[512,128]{1,0:T(8,128)(2,1)S(1)}, u32[]{:S(2)}, u32[]{:S(2)}) collective-permute-start(bf16[512,128]{1,0:T(8,128)(2,1)S(1)} %pad_maximum_fusion.refs_0_), channel_id=1, source_target_pairs={{0,1},{1,2},{2,3},{3,0},{4,5},{5,6},{6,7},{7,4},{8,9},{9,10},{10,1... | collective-permute-start | bytes 393224 | tf_op jit(solution)/shard_map/ppermute | solution.py:170
  6.5 0.1 pad_add_fusion.me_ref
  6.5 2.2 %collective-permute-done.2.refs_3_ = bf16[512,128]{1,0:T(8,128)(2,1)S(1)} collective-permute-done((bf16[512,128]{1,0:T(8,128)(2,1)S(1)}, bf16[512,128]{1,0:T(8,128)(2,1)S(1)}, u32[]{:S(2)}, u32[]{:S(2)}) %collective-permute-start.2) | collective-permute-done | bytes 131104 | tf_op jit(solution)/shard_map/ppermute | solution.py:170
  8.7 0.0 collective-permute-done.1.refs_2_
  8.7 1.9 %collective-permute-done.refs_1_ = bf16[512,128]{1,0:T(8,128)(2,1)S(1)} collective-permute-done((bf16[512,128]{1,0:T(8,128)(2,1)S(1)}, bf16[512,128]{1,0:T(8,128)(2,1)S(1)}, u32[]{:S(2)}, u32[]{:S(2)}) %collective-permute-start) | collective-permute-done | bytes 131104 | tf_op jit(solution)/shard_map/ppermute | solution.py:170
  10.6 0.0 copy-start.4
  10.6 0.0 copy-start.5
  10.6 0.0 copy-done.2
  10.6 0.6 %copy-done.4 = s32[1,1,16]{2,1,0:T(1,128)S(1)} copy-done((s32[1,1,16]{2,1,0:T(1,128)S(1)}, s32[1,1,16]{2,1,0:T(1,128)}, u32[]{:S(2)}) %copy-start.4) | copy-done | bytes 88
  11.2 0.0 copy-done.5
  11.2 0.0 copy-start.1
  11.2 0.0 copy-start.3
  11.3 1.2 %tile_products.1 = (bf16[272,128]{1,0:T(8,128)(2,1)S(1)}, bf16[272,128]{1,0:T(8,128)(2,1)S(1)}, bf16[272,128]{1,0:T(8,128)(2,1)S(1)}, bf16[272,128]{1,0:T(8,128)...) custom-call(s32[16]{0:T(128)S(1)} %bitcast.10, ...), custom_call_target="tpu_custom_call" | custom-call | tf_op jit(solution)/shard_map/tile_products/pallas_call | solution.py:187
  12.4 1.3 %collective-permute-start.3 = (bf16[272,128]{1,0:T(8,128)(2,1)S(1)}, bf16[272,128]{1,0:T(8,128)(2,1)S(1)}, u32[]{:S(2)}, u32[]{:S(2)}) collective-permute-start(bf16[272,128]{1,0:T(8,128)(2,1)S(1)} %get-tuple-element.15), channel_id=1, source_target_pairs={{0,4},{4,8},{8,12},{12,16},{16,20},{20,24},{24,28},{28,0},{1,5},{5... | collective-permute-start | bytes 208904 | tf_op jit(solution)/shard_map/ppermute | solution.py:170
  13.7 1.3 %collective-permute-start.4 = (bf16[272,128]{1,0:T(8,128)(2,1)S(1)}, bf16[272,128]{1,0:T(8,128)(2,1)S(1)}, u32[]{:S(2)}, u32[]{:S(2)}) collective-permute-start(bf16[272,128]{1,0:T(8,128)(2,1)S(1)} %get-tuple-element.16), channel_id=1, source_target_pairs={{0,8},{4,12},{8,16},{12,20},{16,24},{20,28},{24,0},{28,4},{1,9},{5... | collective-permute-start | bytes 208904 | tf_op jit(solution)/shard_map/ppermute | solution.py:170
  15.0 2.3 %collective-permute-start.5 = (bf16[272,128]{1,0:T(8,128)(2,1)S(1)}, bf16[272,128]{1,0:T(8,128)(2,1)S(1)}, u32[]{:S(2)}, u32[]{:S(2)}) collective-permute-start(bf16[272,128]{1,0:T(8,128)(2,1)S(1)} %get-tuple-element.17), channel_id=1, source_target_pairs={{0,12},{4,16},{8,20},{12,24},{16,28},{20,0},{24,4},{28,8},{1,13},{... | collective-permute-start | bytes 208904 | tf_op jit(solution)/shard_map/ppermute | solution.py:170
  17.3 0.9 %collective-permute-start.6 = (bf16[272,128]{1,0:T(8,128)(2,1)S(1)}, bf16[272,128]{1,0:T(8,128)(2,1)S(1)}, u32[]{:S(2)}, u32[]{:S(2)}) collective-permute-start(bf16[272,128]{1,0:T(8,128)(2,1)S(1)} %get-tuple-element.18), channel_id=1, source_target_pairs={{0,16},{4,20},{8,24},{12,28},{16,0},{20,4},{24,8},{28,12},{1,17},{... | collective-permute-start | bytes 208904 | tf_op jit(solution)/shard_map/ppermute | solution.py:170
  18.2 2.3 %collective-permute-start.7 = (bf16[272,128]{1,0:T(8,128)(2,1)S(1)}, bf16[272,128]{1,0:T(8,128)(2,1)S(1)}, u32[]{:S(2)}, u32[]{:S(2)}) collective-permute-start(bf16[272,128]{1,0:T(8,128)(2,1)S(1)} %get-tuple-element.19), channel_id=1, source_target_pairs={{0,20},{4,24},{8,28},{12,0},{16,4},{20,8},{24,12},{28,16},{1,21},{... | collective-permute-start | bytes 208904 | tf_op jit(solution)/shard_map/ppermute | solution.py:170
  20.6 0.0 collective-permute-done.3.refs_1_
  20.6 1.1 %collective-permute-start.8 = (bf16[272,128]{1,0:T(8,128)(2,1)S(1)}, bf16[272,128]{1,0:T(8,128)(2,1)S(1)}, u32[]{:S(2)}, u32[]{:S(2)}) collective-permute-start(bf16[272,128]{1,0:T(8,128)(2,1)S(1)} %get-tuple-element.20), channel_id=1, source_target_pairs={{0,24},{4,28},{8,0},{12,4},{16,8},{20,12},{24,16},{28,20},{1,25},{... | collective-permute-start | bytes 208904 | tf_op jit(solution)/shard_map/ppermute | solution.py:170
  21.6 0.0 collective-permute-done.4.refs_2_
  21.6 1.2 %collective-permute-start.9 = (bf16[272,128]{1,0:T(8,128)(2,1)S(1)}, bf16[272,128]{1,0:T(8,128)(2,1)S(1)}, u32[]{:S(2)}, u32[]{:S(2)}) collective-permute-start(bf16[272,128]{1,0:T(8,128)(2,1)S(1)} %get-tuple-element.21), channel_id=1, source_target_pairs={{0,28},{4,0},{8,4},{12,8},{16,12},{20,16},{24,20},{28,24},{1,29},{... | collective-permute-start | bytes 208904 | tf_op jit(solution)/shard_map/ppermute | solution.py:170
  22.8 2.9 %collective-permute-done.5.refs_3_ = bf16[272,128]{1,0:T(8,128)(2,1)S(1)} collective-permute-done((bf16[272,128]{1,0:T(8,128)(2,1)S(1)}, bf16[272,128]{1,0:T(8,128)(2,1)S(1)}, u32[]{:S(2)}, u32[]{:S(2)}) %collective-permute-start.5) | collective-permute-done | bytes 69664 | tf_op jit(solution)/shard_map/ppermute | solution.py:170
  25.7 0.3 collective-permute-done.6.refs_4_
  26.0 0.0 collective-permute-done.7.refs_5_
  26.0 0.0 collective-permute-done.8.refs_6_
  26.0 0.4 collective-permute-done.9.refs_7_
  26.4 0.0 copy-done.1
  26.4 0.0 copy-done.3
  26.4 0.7 %local_grams.1 = (f32[256,128]{1,0:T(8,128)S(1)}, f32[256,128]{1,0:T(8,128)S(1)}, f32[8,128]{1,0:T(8,128)S(1)}) custom-call(f32[256,128]{1,0:T(8,128)S(1)} %copy-done, f32[256,128]{1,0:T(8,128)S(1)} %copy-done.1, f32[128,128]{1,0:T(8,128)S(1)} %copy-done.3, bf16[272,128]{1,0:T(8,128)(2,1)S(1)} %get-tuple-element.14.refs_0_, ...), custom_call_target="tpu_custom_call" | custom-call | tf_op jit(solution)/shard_map/local_grams/pallas_call | solution.py:209
  27.2 16.4 %all_to_all.10.parts_ref = f32[32,8,128]{2,1,0:T(8,128)S(1)} all-to-all(f32[32,8,128]{2,1,0:T(8,128)S(1)} %bitcast.9), channel_id=1, replica_groups=mesh['row'=8,'col'=4] {'row','col'}, dimensions={0} | all-to-all | bytes 262144 | tf_op jit(solution)/shard_map/all_to_all | solution.py:222
  43.6 12.1 %all_to_all.11.pieces_ref = f32[32,16,128]{2,1,0:T(8,128)S(1)} all-to-all(f32[32,16,128]{2,1,0:T(8,128)S(1)} %sum_and_spread.1), channel_id=1, replica_groups=mesh['row'=8,'col'=4] {'row','col'}, dimensions={0} | all-to-all | bytes 524288 | tf_op jit(solution)/shard_map/all_to_all | solution.py:231
  55.6 6.4 %factor_and_basis.1 = (f32[256,128]{1,0:T(8,128)}, f32[128,128]{1,0:T(8,128)}, f32[128,128]{1,0:T(8,128)}) custom-call(f32[32,16,128]{2,1,0:T(8,128)S(1)} %all_to_all.11.pieces_ref, f32[128,128]{1,0:T(8,128)S(1)} %copy-done.3, f32[256,128]{1,0:T(8,128)S(1)} %copy-done, f32[256,128]{1,0:T(8,128)S(1)} %get-tuple-element.24.shifted_ref), custom_call_target="tpu_custom_call" | custom-call | tf_op jit(solution)/shard_map/factor_and_basis/pallas_call | solution.py:232
  (3 shorter events, 0.1 us)
Async XLA Ops:
  0.6 1.0 %copy-start = (f32[256,128]{1,0:T(8,128)S(1)}, f32[256,128]{1,0:T(8,128)}, u32[]{:S(2)}) copy-start(f32[256,128]{1,0:T(8,128)} %now_ref.3) | copy-start | bytes 393220
  0.6 9.9 %copy-start.2 = (bf16[1,1,16,128,128]{4,3,2,1,0:T(8,128)(2,1)S(1)}, bf16[1,1,16,128,128]{4,3,2,1,0:T(8,128)(2,1)}, u32[]{:S(2)}) copy-start(bf16[1,1,16,128,128]{4,3,2,1,0:T(8,128)(2,1)} %param.10) | copy-start | bytes 1572868
  1.7 7.0 %collective-permute-start.2 = (bf16[512,128]{1,0:T(8,128)(2,1)S(1)}, bf16[512,128]{1,0:T(8,128)(2,1)S(1)}, u32[]{:S(2)}, u32[]{:S(2)}) collective-permute-start(bf16[512,128]{1,0:T(8,128)(2,1)S(1)} %pad_maximum_fusion.refs_0_), channel_id=1, source_target_pairs={{0,3},{1,0},{2,1},{3,2},{4,7},{5,4},{6,5},{7,6},{8,11},{9,8},{10,9... | collective-permute-start | bytes 393224 | tf_op jit(solution)/shard_map/ppermute | solution.py:170
  1.8 6.9 %collective-permute-start.1 = (bf16[512,128]{1,0:T(8,128)(2,1)S(1)}, bf16[512,128]{1,0:T(8,128)(2,1)S(1)}, u32[]{:S(2)}, u32[]{:S(2)}) collective-permute-start(bf16[512,128]{1,0:T(8,128)(2,1)S(1)} %pad_maximum_fusion.refs_0_), channel_id=1, source_target_pairs={{0,2},{1,3},{2,0},{3,1},{4,6},{5,7},{6,4},{7,5},{8,10},{9,11},{10,... | collective-permute-start | bytes 393224 | tf_op jit(solution)/shard_map/ppermute | solution.py:170
  4.5 6.1 %collective-permute-start = (bf16[512,128]{1,0:T(8,128)(2,1)S(1)}, bf16[512,128]{1,0:T(8,128)(2,1)S(1)}, u32[]{:S(2)}, u32[]{:S(2)}) collective-permute-start(bf16[512,128]{1,0:T(8,128)(2,1)S(1)} %pad_maximum_fusion.refs_0_), channel_id=1, source_target_pairs={{0,1},{1,2},{2,3},{3,0},{4,5},{5,6},{6,7},{7,4},{8,9},{9,10},{10,1... | collective-permute-start | bytes 393224 | tf_op jit(solution)/shard_map/ppermute | solution.py:170
  10.6 0.7 %copy-start.4 = (s32[1,1,16]{2,1,0:T(1,128)S(1)}, s32[1,1,16]{2,1,0:T(1,128)}, u32[]{:S(2)}) copy-start(s32[1,1,16]{2,1,0:T(1,128)} %param.11) | copy-start | bytes 196
  10.6 0.7 %copy-start.5 = (s32[1,1,16]{2,1,0:T(1,128)S(1)}, s32[1,1,16]{2,1,0:T(1,128)}, u32[]{:S(2)}) copy-start(s32[1,1,16]{2,1,0:T(1,128)} %param.12) | copy-start | bytes 196
  11.2 15.2 %copy-start.1 = (f32[256,128]{1,0:T(8,128)S(1)}, f32[256,128]{1,0:T(8,128)}, u32[]{:S(2)}) copy-start(f32[256,128]{1,0:T(8,128)} %prev_ref.1) | copy-start | bytes 393220
  11.2 15.2 %copy-start.3 = (f32[128,128]{1,0:T(8,128)S(1)}, f32[128,128]{1,0:T(8,128)}, u32[]{:S(2)}) copy-start(f32[128,128]{1,0:T(8,128)} %coupling_ref.3) | copy-start | bytes 196612
  12.4 8.1 %collective-permute-start.3 = (bf16[272,128]{1,0:T(8,128)(2,1)S(1)}, bf16[272,128]{1,0:T(8,128)(2,1)S(1)}, u32[]{:S(2)}, u32[]{:S(2)}) collective-permute-start(bf16[272,128]{1,0:T(8,128)(2,1)S(1)} %get-tuple-element.15), channel_id=1, source_target_pairs={{0,4},{4,8},{8,12},{12,16},{16,20},{20,24},{24,28},{28,0},{1,5},{5... | collective-permute-start | bytes 208904 | tf_op jit(solution)/shard_map/ppermute | solution.py:170
  13.7 7.9 %collective-permute-start.4 = (bf16[272,128]{1,0:T(8,128)(2,1)S(1)}, bf16[272,128]{1,0:T(8,128)(2,1)S(1)}, u32[]{:S(2)}, u32[]{:S(2)}) collective-permute-start(bf16[272,128]{1,0:T(8,128)(2,1)S(1)} %get-tuple-element.16), channel_id=1, source_target_pairs={{0,8},{4,12},{8,16},{12,20},{16,24},{20,28},{24,0},{28,4},{1,9},{5... | collective-permute-start | bytes 208904 | tf_op jit(solution)/shard_map/ppermute | solution.py:170
  15.0 10.7 %collective-permute-start.5 = (bf16[272,128]{1,0:T(8,128)(2,1)S(1)}, bf16[272,128]{1,0:T(8,128)(2,1)S(1)}, u32[]{:S(2)}, u32[]{:S(2)}) collective-permute-start(bf16[272,128]{1,0:T(8,128)(2,1)S(1)} %get-tuple-element.17), channel_id=1, source_target_pairs={{0,12},{4,16},{8,20},{12,24},{16,28},{20,0},{24,4},{28,8},{1,13},{... | collective-permute-start | bytes 208904 | tf_op jit(solution)/shard_map/ppermute | solution.py:170
  17.3 8.7 %collective-permute-start.6 = (bf16[272,128]{1,0:T(8,128)(2,1)S(1)}, bf16[272,128]{1,0:T(8,128)(2,1)S(1)}, u32[]{:S(2)}, u32[]{:S(2)}) collective-permute-start(bf16[272,128]{1,0:T(8,128)(2,1)S(1)} %get-tuple-element.18), channel_id=1, source_target_pairs={{0,16},{4,20},{8,24},{12,28},{16,0},{20,4},{24,8},{28,12},{1,17},{... | collective-permute-start | bytes 208904 | tf_op jit(solution)/shard_map/ppermute | solution.py:170
  18.2 7.8 %collective-permute-start.7 = (bf16[272,128]{1,0:T(8,128)(2,1)S(1)}, bf16[272,128]{1,0:T(8,128)(2,1)S(1)}, u32[]{:S(2)}, u32[]{:S(2)}) collective-permute-start(bf16[272,128]{1,0:T(8,128)(2,1)S(1)} %get-tuple-element.19), channel_id=1, source_target_pairs={{0,20},{4,24},{8,28},{12,0},{16,4},{20,8},{24,12},{28,16},{1,21},{... | collective-permute-start | bytes 208904 | tf_op jit(solution)/shard_map/ppermute | solution.py:170
  20.6 5.4 %collective-permute-start.8 = (bf16[272,128]{1,0:T(8,128)(2,1)S(1)}, bf16[272,128]{1,0:T(8,128)(2,1)S(1)}, u32[]{:S(2)}, u32[]{:S(2)}) collective-permute-start(bf16[272,128]{1,0:T(8,128)(2,1)S(1)} %get-tuple-element.20), channel_id=1, source_target_pairs={{0,24},{4,28},{8,0},{12,4},{16,8},{20,12},{24,16},{28,20},{1,25},{... | collective-permute-start | bytes 208904 | tf_op jit(solution)/shard_map/ppermute | solution.py:170
  21.6 4.8 %collective-permute-start.9 = (bf16[272,128]{1,0:T(8,128)(2,1)S(1)}, bf16[272,128]{1,0:T(8,128)(2,1)S(1)}, u32[]{:S(2)}, u32[]{:S(2)}) collective-permute-start(bf16[272,128]{1,0:T(8,128)(2,1)S(1)} %get-tuple-element.21), channel_id=1, source_target_pairs={{0,28},{4,0},{8,4},{12,8},{16,12},{20,16},{24,20},{28,24},{1,29},{... | collective-permute-start | bytes 208904 | tf_op jit(solution)/shard_map/ppermute | solution.py:170

commit v6 on v5

--- a/solution.py
+++ b/solution.py
@@ -30,22 +30,56 @@
     return jnp.where(rows <= cols, x, 0.0)
 
 
-def tiles_kernel(n_row, n_col, rows_ref, cols_ref, count_ref, me_ref, tiles_ref, *refs):
-    basis_refs, out_refs = refs[:n_col], refs[n_col : n_col + n_row]
+def distances(n):
+    return range(n - 1, -1, -1)
+
+
+def high_and_low(value):
+    high = value.astype(BF16)
+    low = (value - high.astype(F32)).astype(BF16)
+    return jnp.concatenate([high, low], axis=0)
+
+
+def sum_high_and_low(value):
+    half = value.shape[0] // 2
+    value = value.astype(F32)
+    return value[:half] + value[half:]
+
+
+def start_kernel(n_row, n_col, me_ref, rows_ref, cols_ref, count_ref, now_ref, prev_ref, *refs):
+    slab_refs, (rows_out_ref, cols_out_ref, count_out_ref, early_ref) = refs[:n_col], refs[n_col:]
+    rows_out_ref[...] = rows_ref[...]
+    cols_out_ref[...] = cols_ref[...]
+    count_out_ref[...] = count_ref[...]
+    rows_dev, width = now_ref.shape
+    piece = early_ref.shape[0] // (n_row * n_col)
+    now, prev = now_ref[...], prev_ref[...]
+    if early_ref.shape[0] > 2 * width:
+        early_ref[...] = jnp.zeros_like(early_ref)
+    early_ref[:width, :] = dot_tn(now, now)
+    early_ref[width : 2 * width, :] = dot_tn(now, prev)
+    half = now.astype(BF16)
+    for step, slab_ref in zip(distances(n_col), slab_refs):
+        col = me_ref[1] ^ step
+        places = [pl.multiple_of((row * n_col + col) * piece, piece) for row in range(n_row)]
+        early = jnp.concatenate([early_ref[pl.ds(place, piece), :] for place in places], axis=0)
+        slab_ref[:rows_dev, :] = half
+        slab_ref[rows_dev:, :] = high_and_low(early)
+
+
+def tiles_kernel(n_row, n_col, me_ref, rows_ref, cols_ref, count_ref, tiles_ref, *refs):
+    slab_refs, out_refs = refs[:n_col], refs[n_col : n_col + n_row]
     total_ref, early_ref, basis_ref = refs[n_col + n_row :]
     slots, size, _ = tiles_ref.shape
-    depth, width = out_refs[0].shape
+    width = total_ref.shape[1]
     rows_dev = total_ref.shape[0] // n_row
-    piece = early_ref.shape[0] // (n_row * n_col)
-    my_row, my_col = me_ref[0], me_ref[1]
-    square = jnp.zeros((width, width), F32)
-    cross = jnp.zeros((width, width), F32)
-    for step in range(n_col):
-        now, prev = basis_refs[step][:rows_dev, :], basis_refs[step][rows_dev:, :]
-        owner = lax.rem(my_col + n_col - step, n_col)
-        basis_ref[pl.ds(pl.multiple_of(owner * rows_dev, rows_dev), rows_dev), :] = now
-        square += dot_tn(now, now, None)
-        cross += dot_tn(now, prev, None)
+    piece = early_ref.shape[0] // n_row
+    early = jnp.zeros(early_ref.shape, F32)
+    for step, slab_ref in zip(distances(n_col), slab_refs):
+        place = pl.multiple_of((me_ref[1] ^ step) * rows_dev, rows_dev)
+        basis_ref[pl.ds(place, rows_dev), :] = slab_ref[:rows_dev, :]
+        early += sum_high_and_low(slab_ref[rows_dev:, :])
+    early_ref[...] = early
     total_ref[...] = jnp.zeros_like(total_ref)
     used = count_ref[0]
     for slot in range(slots):
@@ -54,18 +88,10 @@
         value = jnp.where(slot < used, value, 0.0)
         place = pl.ds(pl.multiple_of(rows_ref[slot] * size, size), size)
         total_ref[place, :] += value
-    if early_ref.shape[0] > 2 * width:
-        early_ref[...] = jnp.zeros_like(early_ref)
-    early_ref[:width, :] = square
-    early_ref[width : 2 * width, :] = cross
-    for step in range(n_row):
-        row = lax.rem(my_row + step, n_row)
-        out_ref = out_refs[step]
+    for step, out_ref in zip(distances(n_row), out_refs):
+        row = me_ref[0] ^ step
         out_ref[:rows_dev, :] = total_ref[pl.ds(pl.multiple_of(row * rows_dev, rows_dev), rows_dev), :].astype(BF16)
-        value = early_ref[pl.ds(pl.multiple_of((row * n_col + my_col) * piece, piece), piece), :]
-        high = value.astype(BF16)
-        low = (value - high.astype(F32)).astype(BF16)
-        out_ref[rows_dev:, :] = jnp.concatenate([high, low], axis=0)
+        out_ref[rows_dev:, :] = high_and_low(early_ref[pl.ds(pl.multiple_of(row * piece, piece), piece), :])
 
 
 def grams_kernel(now_ref, prev_ref, coupling_ref, *refs):
@@ -76,8 +102,7 @@
     early = jnp.zeros((piece, width), F32)
     for part_ref in part_refs:
         product = product + part_ref[:rows_dev, :].astype(F32)
-        both = part_ref[rows_dev:, :].astype(F32)
-        early = early + (both[:piece] + both[piece:])
+        early = early + sum_high_and_low(part_ref[rows_dev:, :])
     early_ref[...] = early
     shifted = product - dot_nt(prev_ref[...], upper_of(coupling_ref[...]))
     shifted_ref[...] = shifted
@@ -164,11 +189,11 @@
     basis_ref[...] = dot_nt(residual, inverse)
 
 
-def shifted_copies(blocks, axis):
+def exchange(blocks, axis):
     n = lax.axis_size(axis)
-    return [blocks[0]] + [
-        lax.ppermute(blocks[step], axis, [(source, (source + step) % n) for source in range(n)]) for step in range(1, n)
-    ]
+    assert n & (n - 1) == 0
+    steps = distances(n)[:-1]
+    return [lax.ppermute(block, axis, [(i, i ^ step) for i in range(n)]) for step, block in zip(steps, blocks)] + [blocks[-1]]
 
 
 def on_device(basis_now, basis_prev, coupling, tiles, tile_rows, tile_cols, tile_counts):
@@ -182,8 +207,19 @@
     vmem = pl.BlockSpec(memory_space=pltpu.VMEM)
     params = pltpu.CompilerParams(vmem_limit_bytes=48 * 1024 * 1024)
 
-    both = jnp.concatenate([basis_now, basis_prev], axis=0).astype(BF16)
-    slabs = shifted_copies([both] * n_col, "col")
+    me = jnp.stack([lax.axis_index("row"), lax.axis_index("col")])
+    index_arrays = (tile_rows.reshape(-1), tile_cols.reshape(-1), tile_counts.reshape(-1))
+    *slabs, rows, cols, count = pl.pallas_call(
+        functools.partial(start_kernel, n_row, n_col),
+        out_shape=[jax.ShapeDtypeStruct((rows_dev + 2 * n_row * piece, width), BF16)] * n_col
+        + [jax.ShapeDtypeStruct(array.shape, array.dtype) for array in index_arrays],
+        in_specs=[smem] + [vmem] * 5,
+        out_specs=[vmem] * (n_col + 3),
+        scratch_shapes=[pltpu.VMEM((devices * piece, width), F32)],
+        compiler_params=params,
+        name="slab_and_early_grams",
+    )(me, *index_arrays, basis_now, basis_prev)
+    slabs = exchange(slabs, "col")
     blocks = pl.pallas_call(
         functools.partial(tiles_kernel, n_row, n_col),
         out_shape=[jax.ShapeDtypeStruct((rows_dev + 2 * piece, width), BF16)] * n_row,
@@ -191,20 +227,13 @@
         out_specs=[vmem] * n_row,
         scratch_shapes=[
             pltpu.VMEM((n_row * rows_dev, width), F32),
-            pltpu.VMEM((devices * piece, width), F32),
+            pltpu.VMEM((n_row * piece, width), F32),
             pltpu.VMEM((n_col * rows_dev, width), BF16),
         ],
         compiler_params=params,
         name="tile_products",
-    )(
-        tile_rows.reshape(-1),
-        tile_cols.reshape(-1),
-        tile_counts.reshape(-1),
-        jnp.stack([lax.axis_index("row"), lax.axis_index("col")]),
-        tile_block,
-        *slabs,
-    )
-    parts = shifted_copies(blocks, "row")
+    )(me, rows, cols, count, tile_block, *slabs)
+    parts = exchange(blocks, "row")
 
     shifted, grams, early = pl.pallas_call(
         grams_kernel,

time: 62.8 us -> 66.7 us (1.062)
  waiting for transfers between devices: 7.68 us -> 10.9 us
  local copies, waits for them, and re-layouts: 0.68 us -> 3.53 us
  Pallas kernels: 8.37 us -> 10.3 us
  blocking collectives: 28.4 us -> 26.5 us
  starting transfers between devices: 14.5 us -> 13.3 us
  other arithmetic: 1.07 us -> 0.08 us
    ppermute x10, waiting for transfers between devices: 7.68 us -> 10.9 us  [exchange(): lax.ppermute(block, axis, [(i, i ^ step) for i in range(n)])]
    unnamed x12 -> x16, local copies, waits for them, and re-layouts: 0.68 us -> 3.53 us
    all_to_all x1, blocking collectives: 16.4 us -> 14.4 us  [on_device(): lax.all_to_all(grams.reshape(devices, piece, width), everyone, split_axis...]
    pallas_call x0 -> x1, Pallas kernels: none -> 1.42 us  [on_device(): pl.pallas_call(functools.partial(start_kernel, n_row, n_col), out_shape=[...]
    ppermute x10, starting transfers between devices: 14.5 us -> 13.3 us  [exchange(): lax.ppermute(block, axis, [(i, i ^ step) for i in range(n)])]
    another operation x3 -> x1, other arithmetic: 1.06 us -> 0.08 us  [on_device(): me = jnp.stack([lax.axis_index('row'), lax.axis_index('col')])]
where the time goes in v6:
time: 66.7 us; the launch traced here: 65.9 us
  blocking collectives  26.5 us (40%)
  starting transfers between devices  13.3 us (20%)
  waiting for transfers between devices  10.9 us (16%)
  Pallas kernels  10.3 us (15%)
  local copies, waits for them, and re-layouts  3.53 us (5%)
  between operations  1.34 us (2%)
    all_to_all x1, blocking collectives, on_device(): lax.all_to_all(grams.reshape(devices, piece, width), everyone, split_axis...  14.4 us
    ppermute x10, starting transfers between devices, exchange(): lax.ppermute(block, axis, [(i, i ^ step) for i in range(n)])  13.3 us
    all_to_all x1, blocking collectives, on_device(): lax.all_to_all(copies, everyone, split_axis=0, concat_axis=0, tiled=True)  12.1 us
    ppermute x10, waiting for transfers between devices, exchange(): lax.ppermute(block, axis, [(i, i ^ step) for i in range(n)])  10.9 us
    pallas_call x1, Pallas kernels, on_device(): pl.pallas_call(functools.partial(final_kernel, total_rows), out_shape=(ja...  6.45 us
    unnamed x16, local copies, waits for them, and re-layouts  3.53 us
    pallas_call x1, Pallas kernels, on_device(): pl.pallas_call(functools.partial(tiles_kernel, n_row, n_col), out_shape=[...  1.62 us
    pallas_call x1, Pallas kernels, on_device(): pl.pallas_call(functools.partial(start_kernel, n_row, n_col), out_shape=[...  1.42 us
  transfers between devices with their start and end apart: 10, of which 5 were waited for; matrix products, arithmetic and copies ran while one was open for 0% of the time, Pallas kernels for 0%

profile of v6, /device:TPU:1, one launch (start us, length us, event | category | flops | bytes accessed | tf_op | source)
XLA Modules:
  0.0 65.9 jit_solution(8565116998393447639)
XLA Ops:
  1.3 0.1 pad_add_fusion.me_ref
  1.4 0.0 copy-start.6
  1.4 0.0 copy-start.7
  1.4 0.7 copy-done.6
  2.0 0.0 copy-done.7
  2.0 0.0 copy-start
  2.0 0.9 %copy-done = f32[256,128]{1,0:T(8,128)S(1)} copy-done((f32[256,128]{1,0:T(8,128)S(1)}, f32[256,128]{1,0:T(8,128)}, u32[]{:S(2)}) %copy-start) | copy-done | bytes 131096
  2.9 0.0 copy-start.3
  2.9 0.9 %copy-done.3 = f32[256,128]{1,0:T(8,128)S(1)} copy-done((f32[256,128]{1,0:T(8,128)S(1)}, f32[256,128]{1,0:T(8,128)}, u32[]{:S(2)}) %copy-start.3) | copy-done | bytes 131096
  3.8 1.4 %slab_and_early_grams.1 = (bf16[384,128]{1,0:T(8,128)(2,1)S(1)}, bf16[384,128]{1,0:T(8,128)(2,1)S(1)}, bf16[384,128]{1,0:T(8,128)(2,1)S(1)}, bf16[384,128]{1,0:T...) custom-call(s32[2]{0:T(128)S(1)} %pad_add_fusion.me_ref, s32[16]{0:T(128)S(1)} %bitcast.10, ...), custom_call_target="tpu_custom_call" | custom-call | tf_op jit(solution)/shard_map/slab_and_early_grams/pallas_call | solution.py:212
  5.3 2.6 %collective-permute-start = (bf16[384,128]{1,0:T(8,128)(2,1)S(1)}, bf16[384,128]{1,0:T(8,128)(2,1)S(1)}, u32[]{:S(2)}, u32[]{:S(2)}) collective-permute-start(bf16[384,128]{1,0:T(8,128)(2,1)S(1)} %get-tuple-element.24), channel_id=1, source_target_pairs={{0,3},{1,2},{2,1},{3,0},{4,7},{5,6},{6,5},{7,4},{8,11},{9,10},{10,... | collective-permute-start | bytes 294920 | tf_op jit(solution)/shard_map/ppermute | solution.py:196
  7.9 0.0 collective-permute-start.1
  7.9 0.4 collective-permute-start.2
  8.3 2.2 %collective-permute-done.refs_0_ = bf16[384,128]{1,0:T(8,128)(2,1)S(1)} collective-permute-done((bf16[384,128]{1,0:T(8,128)(2,1)S(1)}, bf16[384,128]{1,0:T(8,128)(2,1)S(1)}, u32[]{:S(2)}, u32[]{:S(2)}) %collective-permute-start) | collective-permute-done | bytes 98336 | tf_op jit(solution)/shard_map/ppermute | solution.py:196
  10.5 2.1 %collective-permute-done.1.refs_1_ = bf16[384,128]{1,0:T(8,128)(2,1)S(1)} collective-permute-done((bf16[384,128]{1,0:T(8,128)(2,1)S(1)}, bf16[384,128]{1,0:T(8,128)(2,1)S(1)}, u32[]{:S(2)}, u32[]{:S(2)}) %collective-permute-start.1) | collective-permute-done | bytes 98336 | tf_op jit(solution)/shard_map/ppermute | solution.py:196
  12.6 0.0 collective-permute-done.2.refs_2_
  12.6 0.0 copy-start.2
  12.6 1.0 %copy-done.2 = bf16[1,1,16,128,128]{4,3,2,1,0:T(8,128)(2,1)S(1)} copy-done((bf16[1,1,16,128,128]{4,3,2,1,0:T(8,128)(2,1)S(1)}, bf16[1,1,16,128,128]{4,3,2,1,0:T(8,128)(2,1)}, u32[]{:S(2)}) %copy-start.2) | copy-done | bytes 524312
  13.6 0.0 copy-start.1
  13.6 0.0 copy-start.4
  13.6 0.0 copy-start.5
  13.6 1.6 %tile_products.1 = (bf16[272,128]{1,0:T(8,128)(2,1)S(1)}, bf16[272,128]{1,0:T(8,128)(2,1)S(1)}, bf16[272,128]{1,0:T(8,128)(2,1)S(1)}, bf16[272,128]{1,0:T(8,128)...) custom-call(s32[2]{0:T(128)S(1)} %pad_add_fusion.me_ref, ...), custom_call_target="tpu_custom_call" | custom-call | tf_op jit(solution)/shard_map/tile_products/pallas_call | solution.py:223
  15.3 5.2 %collective-permute-start.3 = (bf16[272,128]{1,0:T(8,128)(2,1)S(1)}, bf16[272,128]{1,0:T(8,128)(2,1)S(1)}, u32[]{:S(2)}, u32[]{:S(2)}) collective-permute-start(bf16[272,128]{1,0:T(8,128)(2,1)S(1)} %get-tuple-element.28), channel_id=1, source_target_pairs={{0,28},{4,24},{8,20},{12,16},{16,12},{20,8},{24,4},{28,0},{1,29},{... | collective-permute-start | bytes 208904 | tf_op jit(solution)/shard_map/ppermute | solution.py:196
  20.5 0.0 collective-permute-start.4
  20.5 0.4 collective-permute-start.5
  20.9 2.0 %collective-permute-start.6 = (bf16[272,128]{1,0:T(8,128)(2,1)S(1)}, bf16[272,128]{1,0:T(8,128)(2,1)S(1)}, u32[]{:S(2)}, u32[]{:S(2)}) collective-permute-start(bf16[272,128]{1,0:T(8,128)(2,1)S(1)} %get-tuple-element.31), channel_id=1, source_target_pairs={{0,16},{4,20},{8,24},{12,28},{16,0},{20,4},{24,8},{28,12},{1,17},{... | collective-permute-start | bytes 208904 | tf_op jit(solution)/shard_map/ppermute | solution.py:196
  23.0 2.0 %collective-permute-start.7 = (bf16[272,128]{1,0:T(8,128)(2,1)S(1)}, bf16[272,128]{1,0:T(8,128)(2,1)S(1)}, u32[]{:S(2)}, u32[]{:S(2)}) collective-permute-start(bf16[272,128]{1,0:T(8,128)(2,1)S(1)} %get-tuple-element.32), channel_id=1, source_target_pairs={{0,12},{4,8},{8,4},{12,0},{16,28},{20,24},{24,20},{28,16},{1,13},{... | collective-permute-start | bytes 208904 | tf_op jit(solution)/shard_map/ppermute | solution.py:196
  25.0 0.0 collective-permute-done.3.refs_0_
  25.0 0.3 collective-permute-start.8
  25.2 0.3 collective-permute-done.4.refs_1_
  25.6 0.3 collective-permute-start.9
  25.8 4.7 %collective-permute-done.5.refs_2_ = bf16[272,128]{1,0:T(8,128)(2,1)S(1)} collective-permute-done((bf16[272,128]{1,0:T(8,128)(2,1)S(1)}, bf16[272,128]{1,0:T(8,128)(2,1)S(1)}, u32[]{:S(2)}, u32[]{:S(2)}) %collective-permute-start.5) | collective-permute-done | bytes 69664 | tf_op jit(solution)/shard_map/ppermute | solution.py:196
  30.5 1.7 %collective-permute-done.6.refs_3_ = bf16[272,128]{1,0:T(8,128)(2,1)S(1)} collective-permute-done((bf16[272,128]{1,0:T(8,128)(2,1)S(1)}, bf16[272,128]{1,0:T(8,128)(2,1)S(1)}, u32[]{:S(2)}, u32[]{:S(2)}) %collective-permute-start.6) | collective-permute-done | bytes 69664 | tf_op jit(solution)/shard_map/ppermute | solution.py:196
  32.2 0.0 collective-permute-done.7.refs_4_
  32.2 0.0 collective-permute-done.8.refs_5_
  32.2 0.0 collective-permute-done.9.refs_6_
  32.2 0.0 copy-done.1
  32.2 0.0 copy-done.4
  32.2 0.0 copy-done.5
  32.2 0.7 %local_grams.1 = (f32[256,128]{1,0:T(8,128)S(1)}, f32[256,128]{1,0:T(8,128)S(1)}, f32[8,128]{1,0:T(8,128)S(1)}) custom-call(f32[256,128]{1,0:T(8,128)S(1)} %copy-done.1, f32[256,128]{1,0:T(8,128)S(1)} %copy-done.4, f32[128,128]{1,0:T(8,128)S(1)} %copy-done.5, bf16[272,128]{1,0:T(8,128)(2,1)S(1)} %collective-permute-done.3.refs_0_, ...), custom_call_target="tpu_custom_call" | custom-call | tf_op jit(solution)/shard_map/local_grams/pallas_call | solution.py:238
  32.9 14.4 %all_to_all.10.parts_ref = f32[32,8,128]{2,1,0:T(8,128)S(1)} all-to-all(f32[32,8,128]{2,1,0:T(8,128)S(1)} %bitcast.9), channel_id=1, replica_groups=mesh['row'=8,'col'=4] {'row','col'}, dimensions={0} | all-to-all | bytes 262144 | tf_op jit(solution)/shard_map/all_to_all | solution.py:251
  47.4 12.1 %all_to_all.11.pieces_ref = f32[32,16,128]{2,1,0:T(8,128)S(1)} all-to-all(f32[32,16,128]{2,1,0:T(8,128)S(1)} %sum_and_spread.1), channel_id=1, replica_groups=mesh['row'=8,'col'=4] {'row','col'}, dimensions={0} | all-to-all | bytes 524288 | tf_op jit(solution)/shard_map/all_to_all | solution.py:260
  59.5 6.4 %factor_and_basis.1 = (f32[256,128]{1,0:T(8,128)}, f32[128,128]{1,0:T(8,128)}, f32[128,128]{1,0:T(8,128)}) custom-call(f32[32,16,128]{2,1,0:T(8,128)S(1)} %all_to_all.11.pieces_ref, f32[128,128]{1,0:T(8,128)S(1)} %copy-done.5, f32[256,128]{1,0:T(8,128)S(1)} %copy-done.1, f32[256,128]{1,0:T(8,128)S(1)} %get-tuple-element.38.shifted_ref), custom_call_target="tpu_custom_call" | custom-call | tf_op jit(solution)/shard_map/factor_and_basis/pallas_call | solution.py:261
  (1 shorter events, 0.0 us)
Async XLA Ops:
  1.4 0.7 copy-start.6
  1.4 0.7 %copy-start.7 = (s32[1,1,16]{2,1,0:T(1,128)S(1)}, s32[1,1,16]{2,1,0:T(1,128)}, u32[]{:S(2)}) copy-start(s32[1,1,16]{2,1,0:T(1,128)} %param.12) | copy-start | bytes 196
  2.0 0.9 %copy-start = (f32[256,128]{1,0:T(8,128)S(1)}, f32[256,128]{1,0:T(8,128)}, u32[]{:S(2)}) copy-start(f32[256,128]{1,0:T(8,128)} %now_ref.5) | copy-start | bytes 393220
  2.9 0.9 %copy-start.3 = (f32[256,128]{1,0:T(8,128)S(1)}, f32[256,128]{1,0:T(8,128)}, u32[]{:S(2)}) copy-start(f32[256,128]{1,0:T(8,128)} %prev_ref.3) | copy-start | bytes 393220
  5.3 5.2 %collective-permute-start = (bf16[384,128]{1,0:T(8,128)(2,1)S(1)}, bf16[384,128]{1,0:T(8,128)(2,1)S(1)}, u32[]{:S(2)}, u32[]{:S(2)}) collective-permute-start(bf16[384,128]{1,0:T(8,128)(2,1)S(1)} %get-tuple-element.24), channel_id=1, source_target_pairs={{0,3},{1,2},{2,1},{3,0},{4,7},{5,6},{6,5},{7,4},{8,11},{9,10},{10,... | collective-permute-start | bytes 294920 | tf_op jit(solution)/shard_map/ppermute | solution.py:196
  7.9 4.7 %collective-permute-start.1 = (bf16[384,128]{1,0:T(8,128)(2,1)S(1)}, bf16[384,128]{1,0:T(8,128)(2,1)S(1)}, u32[]{:S(2)}, u32[]{:S(2)}) collective-permute-start(bf16[384,128]{1,0:T(8,128)(2,1)S(1)} %get-tuple-element.25), channel_id=1, source_target_pairs={{0,2},{1,3},{2,0},{3,1},{4,6},{5,7},{6,4},{7,5},{8,10},{9,11},{10,... | collective-permute-start | bytes 294920 | tf_op jit(solution)/shard_map/ppermute | solution.py:196
  7.9 4.7 %collective-permute-start.2 = (bf16[384,128]{1,0:T(8,128)(2,1)S(1)}, bf16[384,128]{1,0:T(8,128)(2,1)S(1)}, u32[]{:S(2)}, u32[]{:S(2)}) collective-permute-start(bf16[384,128]{1,0:T(8,128)(2,1)S(1)} %get-tuple-element.26), channel_id=1, source_target_pairs={{0,1},{1,0},{2,3},{3,2},{4,5},{5,4},{6,7},{7,6},{8,9},{9,8},{10,11... | collective-permute-start | bytes 294920 | tf_op jit(solution)/shard_map/ppermute | solution.py:196
  12.6 1.0 %copy-start.2 = (bf16[1,1,16,128,128]{4,3,2,1,0:T(8,128)(2,1)S(1)}, bf16[1,1,16,128,128]{4,3,2,1,0:T(8,128)(2,1)}, u32[]{:S(2)}) copy-start(bf16[1,1,16,128,128]{4,3,2,1,0:T(8,128)(2,1)} %param.10) | copy-start | bytes 1572868
  13.6 18.5 %copy-start.1 = (f32[256,128]{1,0:T(8,128)S(1)}, f32[256,128]{1,0:T(8,128)}, u32[]{:S(2)}) copy-start(f32[256,128]{1,0:T(8,128)} %now_ref.5) | copy-start | bytes 393220
  13.6 18.5 %copy-start.4 = (f32[256,128]{1,0:T(8,128)S(1)}, f32[256,128]{1,0:T(8,128)}, u32[]{:S(2)}) copy-start(f32[256,128]{1,0:T(8,128)} %prev_ref.3) | copy-start | bytes 393220
  13.6 18.5 %copy-start.5 = (f32[128,128]{1,0:T(8,128)S(1)}, f32[128,128]{1,0:T(8,128)}, u32[]{:S(2)}) copy-start(f32[128,128]{1,0:T(8,128)} %coupling_ref.3) | copy-start | bytes 196612
  15.3 9.7 %collective-permute-start.3 = (bf16[272,128]{1,0:T(8,128)(2,1)S(1)}, bf16[272,128]{1,0:T(8,128)(2,1)S(1)}, u32[]{:S(2)}, u32[]{:S(2)}) collective-permute-start(bf16[272,128]{1,0:T(8,128)(2,1)S(1)} %get-tuple-element.28), channel_id=1, source_target_pairs={{0,28},{4,24},{8,20},{12,16},{16,12},{20,8},{24,4},{28,0},{1,29},{... | collective-permute-start | bytes 208904 | tf_op jit(solution)/shard_map/ppermute | solution.py:196
  20.5 5.1 %collective-permute-start.4 = (bf16[272,128]{1,0:T(8,128)(2,1)S(1)}, bf16[272,128]{1,0:T(8,128)(2,1)S(1)}, u32[]{:S(2)}, u32[]{:S(2)}) collective-permute-start(bf16[272,128]{1,0:T(8,128)(2,1)S(1)} %get-tuple-element.29), channel_id=1, source_target_pairs={{0,24},{4,28},{8,16},{12,20},{16,8},{20,12},{24,0},{28,4},{1,25},{... | collective-permute-start | bytes 208904 | tf_op jit(solution)/shard_map/ppermute | solution.py:196
  20.5 10.0 %collective-permute-start.5 = (bf16[272,128]{1,0:T(8,128)(2,1)S(1)}, bf16[272,128]{1,0:T(8,128)(2,1)S(1)}, u32[]{:S(2)}, u32[]{:S(2)}) collective-permute-start(bf16[272,128]{1,0:T(8,128)(2,1)S(1)} %get-tuple-element.30), channel_id=1, source_target_pairs={{0,20},{4,16},{8,28},{12,24},{16,4},{20,0},{24,12},{28,8},{1,21},{... | collective-permute-start | bytes 208904 | tf_op jit(solution)/shard_map/ppermute | solution.py:196
  20.9 11.2 %collective-permute-start.6 = (bf16[272,128]{1,0:T(8,128)(2,1)S(1)}, bf16[272,128]{1,0:T(8,128)(2,1)S(1)}, u32[]{:S(2)}, u32[]{:S(2)}) collective-permute-start(bf16[272,128]{1,0:T(8,128)(2,1)S(1)} %get-tuple-element.31), channel_id=1, source_target_pairs={{0,16},{4,20},{8,24},{12,28},{16,0},{20,4},{24,8},{28,12},{1,17},{... | collective-permute-start | bytes 208904 | tf_op jit(solution)/shard_map/ppermute | solution.py:196
  23.0 9.2 %collective-permute-start.7 = (bf16[272,128]{1,0:T(8,128)(2,1)S(1)}, bf16[272,128]{1,0:T(8,128)(2,1)S(1)}, u32[]{:S(2)}, u32[]{:S(2)}) collective-permute-start(bf16[272,128]{1,0:T(8,128)(2,1)S(1)} %get-tuple-element.32), channel_id=1, source_target_pairs={{0,12},{4,8},{8,4},{12,0},{16,28},{20,24},{24,20},{28,16},{1,13},{... | collective-permute-start | bytes 208904 | tf_op jit(solution)/shard_map/ppermute | solution.py:196
  25.0 7.2 %collective-permute-start.8 = (bf16[272,128]{1,0:T(8,128)(2,1)S(1)}, bf16[272,128]{1,0:T(8,128)(2,1)S(1)}, u32[]{:S(2)}, u32[]{:S(2)}) collective-permute-start(bf16[272,128]{1,0:T(8,128)(2,1)S(1)} %get-tuple-element.33), channel_id=1, source_target_pairs={{0,8},{4,12},{8,0},{12,4},{16,24},{20,28},{24,16},{28,20},{1,9},{5... | collective-permute-start | bytes 208904 | tf_op jit(solution)/shard_map/ppermute | solution.py:196
  25.6 6.6 %collective-permute-start.9 = (bf16[272,128]{1,0:T(8,128)(2,1)S(1)}, bf16[272,128]{1,0:T(8,128)(2,1)S(1)}, u32[]{:S(2)}, u32[]{:S(2)}) collective-permute-start(bf16[272,128]{1,0:T(8,128)(2,1)S(1)} %get-tuple-element.34), channel_id=1, source_target_pairs={{0,4},{4,0},{8,12},{12,8},{16,20},{20,16},{24,28},{28,24},{1,5},{5... | collective-permute-start | bytes 208904 | tf_op jit(solution)/shard_map/ppermute | solution.py:196

commit v7 on v5

v7 whole, which is shorter than its diff:
```python
import functools

import jax
import jax.numpy as jnp
from jax import lax
from jax.experimental import pallas as pl
from jax.experimental.pallas import tpu as pltpu
from jax.sharding import PartitionSpec as P

HIGHEST = lax.Precision.HIGHEST
F32 = jnp.float32
BF16 = jnp.bfloat16


def dot(a, b):
    return jnp.dot(a, b, precision=HIGHEST, preferred_element_type=F32)


def dot_tn(a, b, precision=HIGHEST):
    return lax.dot_general(a, b, (((0,), (0,)), ((), ())), precision=precision, preferred_element_type=F32)


def dot_nt(a, b):
    return lax.dot_general(a, b, (((1,), (1,)), ((), ())), precision=HIGHEST, preferred_element_type=F32)


def upper_of(x):
    rows = lax.broadcasted_iota(jnp.int32, x.shape, 0)
    cols = lax.broadcasted_iota(jnp.int32, x.shape, 1)
    return jnp.where(rows <= cols, x, 0.0)


def distances(n):
    return range(n - 1, -1, -1)


def high_and_low(value):
    high = value.astype(BF16)
    low = (value - high.astype(F32)).astype(BF16)
    return jnp.concatenate([high, low], axis=0)


def sum_high_and_low(value):
    half = value.shape[-2] // 2
    value = value.astype(F32)
    return value[..., :half, :] + value[..., half:, :]


def tiles_kernel(n_row, n_col, index_ref, tiles_ref, *refs):
    slab_refs, out_refs = refs[:n_col], refs[n_col : n_col + n_row]
    total_ref, early_ref, basis_ref = refs[n_col + n_row :]
    slots, size, _ = tiles_ref.shape
    width = total_ref.shape[1]
    rows_dev = total_ref.shape[0] // n_row
    piece = early_ref.shape[0] // (n_row * n_col)
    used, my_row, my_col = [index_ref[2 * slots + k] for k in range(3)]
    square = jnp.zeros((width, width), F32)
    cross = jnp.zeros((width, width), F32)
    for step in range(n_col):
        now, prev = slab_refs[step][:rows_dev, :], slab_refs[step][rows_dev:, :]
        owner = lax.rem(my_col + n_col - step, n_col)
        basis_ref[pl.ds(pl.multiple_of(owner * rows_dev, rows_dev), rows_dev), :] = now
        square += dot_tn(now, now, None)
        cross += dot_tn(now, prev, None)
    total_ref[...] = jnp.zeros_like(total_ref)
    for slot in range(slots):
        start = pl.multiple_of(index_ref[slots + slot] * size, size)
        value = jnp.dot(tiles_ref[slot], basis_ref[pl.ds(start, size), :], preferred_element_type=F32)
        value = jnp.where(slot < used, value, 0.0)
        place = pl.ds(pl.multiple_of(index_ref[slot] * size, size), size)
        total_ref[place, :] += value
    if early_ref.shape[0] > 2 * width:
        early_ref[...] = jnp.zeros_like(early_ref)
    early_ref[:width, :] = square
    early_ref[width : 2 * width, :] = cross
    for step, out_ref in zip(distances(n_row), out_refs):
        row = my_row ^ step
        out_ref[:rows_dev, :] = total_ref[pl.ds(pl.multiple_of(row * rows_dev, rows_dev), rows_dev), :].astype(BF16)
        value = early_ref[pl.ds(pl.multiple_of((row * n_col + my_col) * piece, piece), piece), :]
        out_ref[rows_dev:, :] = high_and_low(value)


def grams_kernel(total_rows, n_col, index_ref, now_ref, prev_ref, coupling_ref, *refs):
    part_refs, (shifted_ref, grams_ref, early_ref) = refs[:-3], refs[-3:]
    rows_dev, width = now_ref.shape
    piece = early_ref.shape[0]
    product = jnp.zeros((rows_dev, width), F32)
    early = jnp.zeros((piece, width), F32)
    for part_ref in part_refs:
        product = product + part_ref[:rows_dev, :].astype(F32)
        early = early + sum_high_and_low(part_ref[rows_dev:, :])
    upper = upper_of(coupling_ref[...])
    shifted = product - dot_nt(prev_ref[...], upper)
    shifted_ref[...] = shifted
    if grams_ref.shape[0] > 2 * width:
        grams_ref[...] = jnp.zeros_like(grams_ref)
    grams_ref[:width, :] = dot_tn(now_ref[...], product)
    grams_ref[width : 2 * width, :] = dot_tn(shifted, shifted)
    last = index_ref.shape[0] - 1
    first = (index_ref[last - 1] * n_col + index_ref[last]) * piece
    places = first + lax.broadcasted_iota(jnp.int32, early.shape, 0)
    lanes = lax.broadcasted_iota(jnp.int32, early.shape, 1)
    square = early - jnp.where(places == lanes, total_rows, 0.0)
    early_ref[...] = jnp.where(places < width, square, dot_nt(early, upper))


def spread_kernel(parts_ref, early_ref, out_ref):
    total = parts_ref[0]
    for part in range(1, parts_ref.shape[0]):
        total = total + parts_ref[part]
    value = jnp.concatenate([high_and_low(total), early_ref[...].astype(BF16)], axis=0)
    for part in range(out_ref.shape[0]):
        out_ref[part] = value


def reciprocal(x):
    estimate = pl.reciprocal(x, approx=True)
    estimate = estimate * (2.0 - x * estimate)
    return estimate * (2.0 - x * estimate)


def eliminate(gram):
    width = gram.shape[0]
    block = 8
    lanes = lax.broadcasted_iota(jnp.int32, (block, width), 1)
    subs = lax.broadcasted_iota(jnp.int32, (block, width), 0)

    def column(strip, k):
        return jnp.broadcast_to(strip[:, k : k + 1], (block, width))

    def row(strip, k):
        return jnp.broadcast_to(strip[k : k + 1, :], (block, width))

    strips = [gram[r : r + block, :] for r in range(0, width, block)]
    finished = []
    for at in range(len(strips)):
        first = at * block
        panel = strips[at]
        columns = [column(panel, first + j) for j in range(block)]
        kept = panel
        for j in range(0, block, 2):
            here, there = subs == j, subs == j + 1
            lane, next_lane = lanes == first + j, lanes == first + j + 1
            left, right = columns[j], columns[j + 1]
            a, b, c = row(left, j), row(right, j), row(right, j + 1)
            scale = reciprocal(a * c - b * b)
            top, bottom = row(panel, j), row(panel, j + 1)
            ratio = b * reciprocal(a)
            kept = jnp.where(here, top, jnp.where(there, bottom - ratio * jnp.where(lane, 1.0, top), kept))
            kept = jnp.where(there & lane, -ratio, kept)
            top = jnp.where(lane, 1.0, jnp.where(next_lane, 0.0, top))
            bottom = jnp.where(lane, 0.0, jnp.where(next_lane, 1.0, bottom))
            unit_top = (c * top - b * bottom) * scale
            unit_bottom = (a * bottom - b * top) * scale
            others = jnp.where(lane | next_lane, 0.0, panel) - (left * unit_top + right * unit_bottom)
            panel = jnp.where(here, unit_top, jnp.where(there, unit_bottom, others))
            for m in range(j + 2, block):
                up, down = row(columns[m], j), row(columns[m], j + 1)
                up, down = (c * up - b * down) * scale, (a * down - b * up) * scale
                others = columns[m] - (left * up + right * down)
                columns[m] = jnp.where(here, up, jnp.where(there, down, others))
        finished.append(kept)
        rows = [row(panel, m) for m in range(block)]
        inside = (lanes >= first) & (lanes < first + block)
        for s in range(at + 1, len(strips)):
            terms = [column(strips[s], first + m) * rows[m] for m in range(block)]
            while len(terms) > 1:
                terms = [x + y for x, y in zip(terms[::2], terms[1::2])]
            strips[s] = jnp.where(inside, 0.0, strips[s]) - terms[0]
    return jnp.concatenate(finished, axis=0)


def final_kernel(total_rows, pieces_ref, now_ref, shifted_ref, basis_ref, projection_ref, rfactor_ref):
    width = now_ref.shape[1]
    piece = pieces_ref.shape[1] // 3
    pieces = pieces_ref[...]
    late = sum_high_and_low(pieces[:, : 2 * piece, :]).reshape(-1, width)
    early = pieces[:, 2 * piece :, :].astype(F32).reshape(-1, width)
    now_product, square = late[:width], late[width : 2 * width]
    now_square, shift = early[:width], early[width : 2 * width]
    projection = now_product * total_rows**-0.5
    projection_ref[...] = projection
    scaled = now_product * (1.0 / total_rows)
    half = shift - 0.5 * now_product + 0.5 * dot(now_square, scaled)
    mixed = dot_tn(scaled, half)
    gram = square + mixed + mixed.T
    reduced = eliminate(gram * (1.0 / total_rows))
    rows = lax.broadcasted_iota(jnp.int32, reduced.shape, 0)
    cols = lax.broadcasted_iota(jnp.int32, reduced.shape, 1)
    diagonal = jnp.sum(jnp.where(rows == cols, reduced, 0.0), axis=1, keepdims=True)
    root = lax.rsqrt(diagonal)
    rfactor_ref[...] = jnp.where(rows <= cols, reduced, 0.0) * root
    inverse = jnp.where(rows > cols, reduced, jnp.where(rows == cols, 1.0, 0.0)) * root
    residual = shifted_ref[...] - dot(now_ref[...], scaled)
    basis_ref[...] = dot_nt(residual, inverse)


def gather(block, axis):
    n = lax.axis_size(axis)
    return [block] + [lax.ppermute(block, axis, [(i, (i + step) % n) for i in range(n)]) for step in range(1, n)]


def exchange(blocks, axis):
    n = lax.axis_size(axis)
    assert n & (n - 1) == 0
    steps = distances(n)[:-1]
    return [lax.ppermute(block, axis, [(i, i ^ step) for i in range(n)]) for step, block in zip(steps, blocks)] + [blocks[-1]]


def on_device(basis_now, basis_prev, coupling, tiles, tile_rows, tile_cols, tile_counts):
    rows_dev, width = basis_now.shape
    n_row, n_col = lax.axis_size("row"), lax.axis_size("col")
    devices = n_row * n_col
    tile_block = tiles[0, 0]
    total_rows = float(rows_dev * devices)
    piece = -(-2 * width // (8 * devices)) * 8
    smem = pl.BlockSpec(memory_space=pltpu.SMEM)
    vmem = pl.BlockSpec(memory_space=pltpu.VMEM)
    params = pltpu.CompilerParams(vmem_limit_bytes=48 * 1024 * 1024)

    both = jnp.concatenate([basis_now, basis_prev], axis=0).astype(BF16)
    slabs = gather(both, "col")
    index = jnp.concatenate(
        [tile_rows.reshape(-1), tile_cols.reshape(-1), tile_counts.reshape(-1)]
        + [lax.axis_index(axis).reshape(1) for axis in ("row", "col")]
    )
    blocks = pl.pallas_call(
        functools.partial(tiles_kernel, n_row, n_col),
        out_shape=[jax.ShapeDtypeStruct((rows_dev + 2 * piece, width), BF16)] * n_row,
        in_specs=[smem] + [vmem] * (1 + n_col),
        out_specs=[vmem] * n_row,
        scratch_shapes=[
            pltpu.VMEM((n_row * rows_dev, width), F32),
            pltpu.VMEM((devices * piece, width), F32),
            pltpu.VMEM((n_col * rows_dev, width), BF16),
        ],
        compiler_params=params,
        name="tile_products",
    )(index, tile_block, *slabs)
    parts = exchange(blocks, "row")

    shifted, grams, early = pl.pallas_call(
        functools.partial(grams_kernel, total_rows, n_col),
        out_shape=(
            jax.ShapeDtypeStruct((rows_dev, width), F32),
            jax.ShapeDtypeStruct((devices * piece, width), F32),
            jax.ShapeDtypeStruct((piece, width), F32),
        ),
        in_specs=[smem] + [vmem] * (3 + n_row),
        out_specs=(vmem, vmem, vmem),
        compiler_params=params,
        name="local_grams",
    )(index, basis_now, basis_prev, coupling, *parts)
    everyone = ("row", "col")
    pieces = lax.all_to_all(grams.reshape(devices, piece, width), everyone, split_axis=0, concat_axis=0, tiled=True)
    copies = pl.pallas_call(
        spread_kernel,
        out_shape=jax.ShapeDtypeStruct((devices, 3 * piece, width), BF16),
        in_specs=[vmem, vmem],
        out_specs=vmem,
        compiler_params=params,
        name="sum_and_spread",
    )(pieces, early)
    sums = lax.all_to_all(copies, everyone, split_axis=0, concat_axis=0, tiled=True)
    return pl.pallas_call(
        functools.partial(final_kernel, total_rows),
        out_shape=(
            jax.ShapeDtypeStruct((rows_dev, width), F32),
            jax.ShapeDtypeStruct((width, width), F32),
            jax.ShapeDtypeStruct((width, width), F32),
        ),
        in_specs=[vmem] * 3,
        out_specs=(vmem, vmem, vmem),
        compiler_params=params,
        name="factor_and_basis",
    )(sums, basis_now, shifted)


def solution(mesh):
    placed = (
        P(("row", "col"), None),
        P(("row", "col"), None),
        P(),
        P("row", "col", None, None, None),
        P("row", "col", None),
        P("row", "col", None),
        P("row", "col"),
    )
    return jax.shard_map(
        on_device,
        mesh=mesh,
        in_specs=placed,
        out_specs=(P(("row", "col"), None), P(), P()),
        check_vma=False,
    )
```

time: 62.8 us -> 61 us (0.971)
  blocking collectives: 28.4 us -> 25.6 us
  waiting for transfers between devices: 7.68 us -> 9.76 us
  starting transfers between devices: 14.5 us -> 13.4 us
    ppermute x10, waiting for transfers between devices: 7.68 us -> 9.76 us  [the longest x7 6.41 us: exchange(): lax.ppermute(block, axis, [(i, i ^ step) for i in range(n)])]
    all_to_all x1, blocking collectives: 16.4 us -> 14.5 us  [on_device(): lax.all_to_all(grams.reshape(devices, piece, width), everyone, split_axis...]
    ppermute x10, starting transfers between devices: 14.5 us -> 13.4 us  [the longest x7 9.3 us: exchange(): lax.ppermute(block, axis, [(i, i ^ step) for i in range(n)])]
    all_to_all x1, blocking collectives: 12.1 us -> 11 us  [on_device(): lax.all_to_all(copies, everyone, split_axis=0, concat_axis=0, tiled=True)]
where the time goes in v7:
time: 61 us; the launch traced here: 60.8 us
  blocking collectives  25.6 us (42%)
  starting transfers between devices  13.4 us (22%)
  waiting for transfers between devices  9.76 us (16%)
  Pallas kernels  8.89 us (15%)
  between operations  1.38 us (2%)
  other arithmetic  1 us (2%)
  local copies, waits for them, and re-layouts  0.76 us (1%)
    all_to_all x1, blocking collectives, on_device(): lax.all_to_all(grams.reshape(devices, piece, width), everyone, split_axis...  14.5 us
    all_to_all x1, blocking collectives, on_device(): lax.all_to_all(copies, everyone, split_axis=0, concat_axis=0, tiled=True)  11 us
    ppermute x7, starting transfers between devices, exchange(): lax.ppermute(block, axis, [(i, i ^ step) for i in range(n)])  9.3 us
    ppermute x7, waiting for transfers between devices, exchange(): lax.ppermute(block, axis, [(i, i ^ step) for i in range(n)])  6.41 us
    pallas_call x1, Pallas kernels, on_device(): pl.pallas_call(functools.partial(final_kernel, total_rows), out_shape=(ja...  6.34 us
    ppermute x3, starting transfers between devices, gather(): lax.ppermute(block, axis, [(i, (i + step) % n) for i in range(n)])  4.15 us
    ppermute x3, waiting for transfers between devices, gather(): lax.ppermute(block, axis, [(i, (i + step) % n) for i in range(n)])  3.35 us
    pallas_call x1, Pallas kernels, on_device(): pl.pallas_call(functools.partial(grams_kernel, total_rows, n_col), out_sh...  1.34 us
  transfers between devices with their start and end apart: 10, of which 5 were waited for; matrix products, arithmetic and copies ran while one was open for 0% of the time, Pallas kernels for 0%

profile of v7, /device:TPU:1, one launch (start us, length us, event | category | flops | bytes accessed | tf_op | source)
XLA Modules:
  0.0 60.8 jit_solution(2895245425796561827)
XLA Ops:
  0.6 0.0 copy-start
  0.6 0.0 copy-start.1
  0.6 1.0 %convert.7 = bf16[256,128]{1,0:T(8,128)(2,1)S(1)} convert(f32[256,128]{1,0:T(8,128)} %prev_ref.1) | non-fusion elementwise | flops 32768 | bytes 196608 | tf_op jit(solution)/shard_map/convert.1
  1.6 0.0 copy-done
  1.7 0.1 collective-permute-start.2
  1.8 2.7 %collective-permute-start.1 = (bf16[512,128]{1,0:T(8,128)(2,1)S(1)}, bf16[512,128]{1,0:T(8,128)(2,1)S(1)}, u32[]{:S(2)}, u32[]{:S(2)}) collective-permute-start(bf16[512,128]{1,0:T(8,128)(2,1)S(1)} %pad_maximum_fusion.refs_0_), channel_id=1, source_target_pairs={{0,2},{1,3},{2,0},{3,1},{4,6},{5,7},{6,4},{7,5},{8,10},{9,11},{10,... | collective-permute-start | bytes 393224 | tf_op jit(solution)/shard_map/ppermute | solution.py:200
  4.5 1.3 %collective-permute-start = (bf16[512,128]{1,0:T(8,128)(2,1)S(1)}, bf16[512,128]{1,0:T(8,128)(2,1)S(1)}, u32[]{:S(2)}, u32[]{:S(2)}) collective-permute-start(bf16[512,128]{1,0:T(8,128)(2,1)S(1)} %pad_maximum_fusion.refs_0_), channel_id=1, source_target_pairs={{0,1},{1,2},{2,3},{3,0},{4,5},{5,6},{6,7},{7,4},{8,9},{9,10},{10,1... | collective-permute-start | bytes 393224 | tf_op jit(solution)/shard_map/ppermute | solution.py:200
  6.5 0.0 copy-start.4
  6.5 0.0 copy-start.5
  6.5 0.6 %copy-done.4 = s32[1,1,16]{2,1,0:T(1,128)S(1)} copy-done((s32[1,1,16]{2,1,0:T(1,128)S(1)}, s32[1,1,16]{2,1,0:T(1,128)}, u32[]{:S(2)}) %copy-start.4) | copy-done | bytes 88
  7.1 0.0 copy-done.5
  7.1 0.1 concatenate.7.index_ref
  7.2 1.5 %collective-permute-done.2.refs_3_ = bf16[512,128]{1,0:T(8,128)(2,1)S(1)} collective-permute-done((bf16[512,128]{1,0:T(8,128)(2,1)S(1)}, bf16[512,128]{1,0:T(8,128)(2,1)S(1)}, u32[]{:S(2)}, u32[]{:S(2)}) %collective-permute-start.2) | collective-permute-done | bytes 131104 | tf_op jit(solution)/shard_map/ppermute | solution.py:200
  8.7 0.0 collective-permute-done.1.refs_2_
  8.7 1.9 %collective-permute-done.refs_1_ = bf16[512,128]{1,0:T(8,128)(2,1)S(1)} collective-permute-done((bf16[512,128]{1,0:T(8,128)(2,1)S(1)}, bf16[512,128]{1,0:T(8,128)(2,1)S(1)}, u32[]{:S(2)}, u32[]{:S(2)}) %collective-permute-start) | collective-permute-done | bytes 131104 | tf_op jit(solution)/shard_map/ppermute | solution.py:200
  10.6 0.0 copy-done.1
  10.6 0.0 copy-start.2
  10.6 0.0 copy-start.3
  10.6 1.2 %tile_products.1 = (bf16[272,128]{1,0:T(8,128)(2,1)S(1)}, bf16[272,128]{1,0:T(8,128)(2,1)S(1)}, bf16[272,128]{1,0:T(8,128)(2,1)S(1)}, bf16[272,128]{1,0:T(8,128)...) custom-call(s32[35]{0:T(128)S(1)} %concatenate.7.index_ref, ...), custom_call_target="tpu_custom_call" | custom-call | tf_op jit(solution)/shard_map/tile_products/pallas_call | solution.py:227
  11.7 4.3 %collective-permute-start.3 = (bf16[272,128]{1,0:T(8,128)(2,1)S(1)}, bf16[272,128]{1,0:T(8,128)(2,1)S(1)}, u32[]{:S(2)}, u32[]{:S(2)}) collective-permute-start(bf16[272,128]{1,0:T(8,128)(2,1)S(1)} %get-tuple-element.14), channel_id=1, source_target_pairs={{0,28},{4,24},{8,20},{12,16},{16,12},{20,8},{24,4},{28,0},{1,29},{... | collective-permute-start | bytes 208904 | tf_op jit(solution)/shard_map/ppermute | solution.py:207
  16.1 0.0 collective-permute-start.4
  16.1 0.4 collective-permute-start.5
  16.5 2.0 %collective-permute-start.6 = (bf16[272,128]{1,0:T(8,128)(2,1)S(1)}, bf16[272,128]{1,0:T(8,128)(2,1)S(1)}, u32[]{:S(2)}, u32[]{:S(2)}) collective-permute-start(bf16[272,128]{1,0:T(8,128)(2,1)S(1)} %get-tuple-element.17), channel_id=1, source_target_pairs={{0,16},{4,20},{8,24},{12,28},{16,0},{20,4},{24,8},{28,12},{1,17},{... | collective-permute-start | bytes 208904 | tf_op jit(solution)/shard_map/ppermute | solution.py:207
  18.5 2.0 %collective-permute-start.7 = (bf16[272,128]{1,0:T(8,128)(2,1)S(1)}, bf16[272,128]{1,0:T(8,128)(2,1)S(1)}, u32[]{:S(2)}, u32[]{:S(2)}) collective-permute-start(bf16[272,128]{1,0:T(8,128)(2,1)S(1)} %get-tuple-element.18), channel_id=1, source_target_pairs={{0,12},{4,8},{8,4},{12,0},{16,28},{20,24},{24,20},{28,16},{1,13},{... | collective-permute-start | bytes 208904 | tf_op jit(solution)/shard_map/ppermute | solution.py:207
  20.5 0.0 collective-permute-done.3.refs_0_
  20.5 0.3 collective-permute-start.8
  20.8 0.3 collective-permute-done.4.refs_1_
  21.1 0.2 collective-permute-start.9
  21.4 4.5 %collective-permute-done.5.refs_2_ = bf16[272,128]{1,0:T(8,128)(2,1)S(1)} collective-permute-done((bf16[272,128]{1,0:T(8,128)(2,1)S(1)}, bf16[272,128]{1,0:T(8,128)(2,1)S(1)}, u32[]{:S(2)}, u32[]{:S(2)}) %collective-permute-start.5) | collective-permute-done | bytes 69664 | tf_op jit(solution)/shard_map/ppermute | solution.py:207
  25.8 1.6 %collective-permute-done.6.refs_3_ = bf16[272,128]{1,0:T(8,128)(2,1)S(1)} collective-permute-done((bf16[272,128]{1,0:T(8,128)(2,1)S(1)}, bf16[272,128]{1,0:T(8,128)(2,1)S(1)}, u32[]{:S(2)}, u32[]{:S(2)}) %collective-permute-start.6) | collective-permute-done | bytes 69664 | tf_op jit(solution)/shard_map/ppermute | solution.py:207
  27.4 0.0 collective-permute-done.7.refs_4_
  27.5 0.0 collective-permute-done.8.refs_5_
  27.5 0.0 collective-permute-done.9.refs_6_
  27.5 0.0 copy-done.2
  27.5 0.0 copy-done.3
  27.5 1.3 %local_grams.1 = (f32[256,128]{1,0:T(8,128)S(1)}, f32[256,128]{1,0:T(8,128)S(1)}, f32[8,128]{1,0:T(8,128)S(1)}) custom-call(s32[35]{0:T(128)S(1)} %concatenate.7.index_ref, f32[256,128]{1,0:T(8,128)S(1)} %copy-done, f32[256,128]{1,0:T(8,128)S(1)} %copy-done.2, f32[128,128]{1,0:T(8,128)S(1)} %copy-done.3, ...), custom_call_target="tpu_custom_call" | custom-call | tf_op jit(solution)/shard_map/local_grams/pallas_call | solution.py:242
  28.8 14.5 %all_to_all.10.parts_ref = f32[32,8,128]{2,1,0:T(8,128)S(1)} all-to-all(f32[32,8,128]{2,1,0:T(8,128)S(1)} %bitcast.9), channel_id=1, replica_groups=mesh['row'=8,'col'=4] {'row','col'}, dimensions={0} | all-to-all | bytes 262144 | tf_op jit(solution)/shard_map/all_to_all | solution.py:255
  43.4 0.1 sum_and_spread.1
  43.4 11.0 %all_to_all.11.pieces_ref = bf16[32,24,128]{2,1,0:T(8,128)(2,1)S(1)} all-to-all(bf16[32,24,128]{2,1,0:T(8,128)(2,1)S(1)} %sum_and_spread.1), channel_id=1, replica_groups=mesh['row'=8,'col'=4] {'row','col'}, dimensions={0} | all-to-all | bytes 393216 | tf_op jit(solution)/shard_map/all_to_all | solution.py:264
  54.5 6.3 %factor_and_basis.1 = (f32[256,128]{1,0:T(8,128)}, f32[128,128]{1,0:T(8,128)}, f32[128,128]{1,0:T(8,128)}) custom-call(bf16[32,24,128]{2,1,0:T(8,128)(2,1)S(1)} %all_to_all.11.pieces_ref, f32[256,128]{1,0:T(8,128)S(1)} %copy-done, f32[256,128]{1,0:T(8,128)S(1)} %get-tuple-element.24.shifted_ref), custom_call_target="tpu_custom_call" | custom-call | tf_op jit(solution)/shard_map/factor_and_basis/pallas_call | solution.py:265
  (2 shorter events, 0.0 us)
Async XLA Ops:
  0.6 1.0 %copy-start = (f32[256,128]{1,0:T(8,128)S(1)}, f32[256,128]{1,0:T(8,128)}, u32[]{:S(2)}) copy-start(f32[256,128]{1,0:T(8,128)} %now_ref.3) | copy-start | bytes 393220
  0.6 9.9 %copy-start.1 = (bf16[1,1,16,128,128]{4,3,2,1,0:T(8,128)(2,1)S(1)}, bf16[1,1,16,128,128]{4,3,2,1,0:T(8,128)(2,1)}, u32[]{:S(2)}) copy-start(bf16[1,1,16,128,128]{4,3,2,1,0:T(8,128)(2,1)} %param.10) | copy-start | bytes 1572868
  1.7 7.0 %collective-permute-start.2 = (bf16[512,128]{1,0:T(8,128)(2,1)S(1)}, bf16[512,128]{1,0:T(8,128)(2,1)S(1)}, u32[]{:S(2)}, u32[]{:S(2)}) collective-permute-start(bf16[512,128]{1,0:T(8,128)(2,1)S(1)} %pad_maximum_fusion.refs_0_), channel_id=1, source_target_pairs={{0,3},{1,0},{2,1},{3,2},{4,7},{5,4},{6,5},{7,6},{8,11},{9,8},{10,9... | collective-permute-start | bytes 393224 | tf_op jit(solution)/shard_map/ppermute | solution.py:200
  1.8 6.9 %collective-permute-start.1 = (bf16[512,128]{1,0:T(8,128)(2,1)S(1)}, bf16[512,128]{1,0:T(8,128)(2,1)S(1)}, u32[]{:S(2)}, u32[]{:S(2)}) collective-permute-start(bf16[512,128]{1,0:T(8,128)(2,1)S(1)} %pad_maximum_fusion.refs_0_), channel_id=1, source_target_pairs={{0,2},{1,3},{2,0},{3,1},{4,6},{5,7},{6,4},{7,5},{8,10},{9,11},{10,... | collective-permute-start | bytes 393224 | tf_op jit(solution)/shard_map/ppermute | solution.py:200
  4.5 6.1 %collective-permute-start = (bf16[512,128]{1,0:T(8,128)(2,1)S(1)}, bf16[512,128]{1,0:T(8,128)(2,1)S(1)}, u32[]{:S(2)}, u32[]{:S(2)}) collective-permute-start(bf16[512,128]{1,0:T(8,128)(2,1)S(1)} %pad_maximum_fusion.refs_0_), channel_id=1, source_target_pairs={{0,1},{1,2},{2,3},{3,0},{4,5},{5,6},{6,7},{7,4},{8,9},{9,10},{10,1... | collective-permute-start | bytes 393224 | tf_op jit(solution)/shard_map/ppermute | solution.py:200
  6.5 0.7 %copy-start.4 = (s32[1,1,16]{2,1,0:T(1,128)S(1)}, s32[1,1,16]{2,1,0:T(1,128)}, u32[]{:S(2)}) copy-start(s32[1,1,16]{2,1,0:T(1,128)} %param.11) | copy-start | bytes 196
  6.5 0.7 %copy-start.5 = (s32[1,1,16]{2,1,0:T(1,128)S(1)}, s32[1,1,16]{2,1,0:T(1,128)}, u32[]{:S(2)}) copy-start(s32[1,1,16]{2,1,0:T(1,128)} %param.12) | copy-start | bytes 196
  10.6 16.9 %copy-start.2 = (f32[256,128]{1,0:T(8,128)S(1)}, f32[256,128]{1,0:T(8,128)}, u32[]{:S(2)}) copy-start(f32[256,128]{1,0:T(8,128)} %prev_ref.1) | copy-start | bytes 393220
  10.6 16.9 %copy-start.3 = (f32[128,128]{1,0:T(8,128)S(1)}, f32[128,128]{1,0:T(8,128)}, u32[]{:S(2)}) copy-start(f32[128,128]{1,0:T(8,128)} %coupling_ref.1) | copy-start | bytes 196612
  11.7 8.8 %collective-permute-start.3 = (bf16[272,128]{1,0:T(8,128)(2,1)S(1)}, bf16[272,128]{1,0:T(8,128)(2,1)S(1)}, u32[]{:S(2)}, u32[]{:S(2)}) collective-permute-start(bf16[272,128]{1,0:T(8,128)(2,1)S(1)} %get-tuple-element.14), channel_id=1, source_target_pairs={{0,28},{4,24},{8,20},{12,16},{16,12},{20,8},{24,4},{28,0},{1,29},{... | collective-permute-start | bytes 208904 | tf_op jit(solution)/shard_map/ppermute | solution.py:207
  16.1 5.1 %collective-permute-start.4 = (bf16[272,128]{1,0:T(8,128)(2,1)S(1)}, bf16[272,128]{1,0:T(8,128)(2,1)S(1)}, u32[]{:S(2)}, u32[]{:S(2)}) collective-permute-start(bf16[272,128]{1,0:T(8,128)(2,1)S(1)} %get-tuple-element.15), channel_id=1, source_target_pairs={{0,24},{4,28},{8,16},{12,20},{16,8},{20,12},{24,0},{28,4},{1,25},{... | collective-permute-start | bytes 208904 | tf_op jit(solution)/shard_map/ppermute | solution.py:207
  16.1 9.8 %collective-permute-start.5 = (bf16[272,128]{1,0:T(8,128)(2,1)S(1)}, bf16[272,128]{1,0:T(8,128)(2,1)S(1)}, u32[]{:S(2)}, u32[]{:S(2)}) collective-permute-start(bf16[272,128]{1,0:T(8,128)(2,1)S(1)} %get-tuple-element.16), channel_id=1, source_target_pairs={{0,20},{4,16},{8,28},{12,24},{16,4},{20,0},{24,12},{28,8},{1,21},{... | collective-permute-start | bytes 208904 | tf_op jit(solution)/shard_map/ppermute | solution.py:207
  16.5 11.0 %collective-permute-start.6 = (bf16[272,128]{1,0:T(8,128)(2,1)S(1)}, bf16[272,128]{1,0:T(8,128)(2,1)S(1)}, u32[]{:S(2)}, u32[]{:S(2)}) collective-permute-start(bf16[272,128]{1,0:T(8,128)(2,1)S(1)} %get-tuple-element.17), channel_id=1, source_target_pairs={{0,16},{4,20},{8,24},{12,28},{16,0},{20,4},{24,8},{28,12},{1,17},{... | collective-permute-start | bytes 208904 | tf_op jit(solution)/shard_map/ppermute | solution.py:207
  18.5 8.9 %collective-permute-start.7 = (bf16[272,128]{1,0:T(8,128)(2,1)S(1)}, bf16[272,128]{1,0:T(8,128)(2,1)S(1)}, u32[]{:S(2)}, u32[]{:S(2)}) collective-permute-start(bf16[272,128]{1,0:T(8,128)(2,1)S(1)} %get-tuple-element.18), channel_id=1, source_target_pairs={{0,12},{4,8},{8,4},{12,0},{16,28},{20,24},{24,20},{28,16},{1,13},{... | collective-permute-start | bytes 208904 | tf_op jit(solution)/shard_map/ppermute | solution.py:207
  20.5 6.9 %collective-permute-start.8 = (bf16[272,128]{1,0:T(8,128)(2,1)S(1)}, bf16[272,128]{1,0:T(8,128)(2,1)S(1)}, u32[]{:S(2)}, u32[]{:S(2)}) collective-permute-start(bf16[272,128]{1,0:T(8,128)(2,1)S(1)} %get-tuple-element.19), channel_id=1, source_target_pairs={{0,8},{4,12},{8,0},{12,4},{16,24},{20,28},{24,16},{28,20},{1,9},{5... | collective-permute-start | bytes 208904 | tf_op jit(solution)/shard_map/ppermute | solution.py:207
  21.1 6.3 %collective-permute-start.9 = (bf16[272,128]{1,0:T(8,128)(2,1)S(1)}, bf16[272,128]{1,0:T(8,128)(2,1)S(1)}, u32[]{:S(2)}, u32[]{:S(2)}) collective-permute-start(bf16[272,128]{1,0:T(8,128)(2,1)S(1)} %get-tuple-element.20), channel_id=1, source_target_pairs={{0,4},{4,0},{8,12},{12,8},{16,20},{20,16},{24,28},{28,24},{1,5},{5... | collective-permute-start | bytes 208904 | tf_op jit(solution)/shard_map/ppermute | solution.py:207

commit v8 on v7

v8 whole, which is shorter than its diff:
```python
import functools

import jax
import jax.numpy as jnp
from jax import lax
from jax.experimental import pallas as pl
from jax.experimental.pallas import tpu as pltpu
from jax.sharding import PartitionSpec as P

HIGHEST = lax.Precision.HIGHEST
F32 = jnp.float32
BF16 = jnp.bfloat16


def dot(a, b):
    return jnp.dot(a, b, precision=HIGHEST, preferred_element_type=F32)


def dot_tn(a, b, precision=HIGHEST):
    return lax.dot_general(a, b, (((0,), (0,)), ((), ())), precision=precision, preferred_element_type=F32)


def dot_nt(a, b):
    return lax.dot_general(a, b, (((1,), (1,)), ((), ())), precision=HIGHEST, preferred_element_type=F32)


def upper_of(x):
    rows = lax.broadcasted_iota(jnp.int32, x.shape, 0)
    cols = lax.broadcasted_iota(jnp.int32, x.shape, 1)
    return jnp.where(rows <= cols, x, 0.0)


def distances(n):
    return range(n - 1, -1, -1)


def high_and_low(value):
    high = value.astype(BF16)
    low = (value - high.astype(F32)).astype(BF16)
    return jnp.concatenate([high, low], axis=0)


def sum_high_and_low(value):
    half = value.shape[-2] // 2
    value = value.astype(F32)
    return value[..., :half, :] + value[..., half:, :]


def tiles_kernel(n_row, n_col, total_rows, index_ref, tiles_ref, basis_ref, coupling_ref, *refs):
    half = n_row // 2
    mirror_refs, near_refs, (far_ref, own_ref, total_ref, early_ref) = refs[: half - 1], refs[half - 1 : -4], refs[-4:]
    slots, size, _ = tiles_ref.shape
    width = total_ref.shape[1]
    rows_dev = total_ref.shape[0] // n_row
    piece = early_ref.shape[0] // (n_row * n_col)
    used, my_row, my_col = [index_ref[2 * slots + k] for k in range(3)]
    total_ref[...] = jnp.zeros_like(total_ref)
    per_slab = rows_dev // size
    for slot in range(slots):
        col = index_ref[slots + slot]
        start = pl.multiple_of((2 * per_slab * (col // per_slab) + lax.rem(col, per_slab)) * size, size)
        value = jnp.dot(tiles_ref[slot], basis_ref[pl.ds(start, size), :], preferred_element_type=F32)
        value = jnp.where(slot < used, value, 0.0)
        place = pl.ds(pl.multiple_of(index_ref[slot] * size, size), size)
        total_ref[place, :] += value
    square = jnp.zeros((width, width), F32)
    cross = jnp.zeros((width, width), F32)
    for slab in range(n_col):
        now = basis_ref[2 * slab * rows_dev : (2 * slab + 1) * rows_dev, :]
        prev = basis_ref[(2 * slab + 1) * rows_dev : (2 * slab + 2) * rows_dev, :]
        square += dot_tn(now, now, None)
        cross += dot_tn(now, prev, None)
    rows = lax.broadcasted_iota(jnp.int32, square.shape, 0)
    cols = lax.broadcasted_iota(jnp.int32, square.shape, 1)
    if early_ref.shape[0] > 2 * width:
        early_ref[...] = jnp.zeros_like(early_ref)
    early_ref[:width, :] = square - jnp.where(rows == cols, total_rows / n_row, 0.0)
    early_ref[width : 2 * width, :] = dot_nt(cross, upper_of(coupling_ref[...]))

    def parts_of(row):
        slab = total_ref[pl.ds(pl.multiple_of(row * rows_dev, rows_dev), rows_dev), :]
        return slab, early_ref[pl.ds(pl.multiple_of((row * n_col + my_col) * piece, piece), piece), :]

    for step, mirror_ref, near_ref in zip(distances(half), mirror_refs, near_refs):
        write_block(mirror_ref, *parts_of(my_row ^ (step + half)))
        write_block(near_ref, *parts_of(my_row ^ step))
    for row, ref in ((my_row ^ half, far_ref), (my_row, own_ref)):
        ref[:rows_dev, :], ref[rows_dev:, :] = parts_of(row)


def write_block(ref, slab, early):
    rows_dev = slab.shape[0]
    ref[:rows_dev, :] = slab.astype(BF16)
    ref[rows_dev:, :] = high_and_low(early)


def add_blocks(own_ref, block_refs, rows_dev):
    slab, early = own_ref[:rows_dev, :], own_ref[rows_dev:, :]
    for ref in block_refs:
        slab = slab + ref[:rows_dev, :].astype(F32)
        early = early + sum_high_and_low(ref[rows_dev:, :])
    return slab, early


def mirror_kernel(rows_dev, own_ref, *refs):
    block_refs, out_ref = refs[:-1], refs[-1]
    write_block(out_ref, *add_blocks(own_ref, block_refs, rows_dev))


def grams_kernel(now_ref, prev_ref, coupling_ref, own_ref, *refs):
    block_refs, (shifted_ref, grams_ref, early_ref) = refs[:-3], refs[-3:]
    rows_dev, width = now_ref.shape
    product, early_ref[...] = add_blocks(own_ref, block_refs, rows_dev)
    shifted = product - dot_nt(prev_ref[...], upper_of(coupling_ref[...]))
    shifted_ref[...] = shifted
    if grams_ref.shape[0] > 2 * width:
        grams_ref[...] = jnp.zeros_like(grams_ref)
    grams_ref[:width, :] = dot_tn(now_ref[...], product)
    grams_ref[width : 2 * width, :] = dot_tn(shifted, shifted)


def spread_kernel(parts_ref, early_ref, out_ref):
    total = parts_ref[0]
    for part in range(1, parts_ref.shape[0]):
        total = total + parts_ref[part]
    value = jnp.concatenate([high_and_low(total), early_ref[...].astype(BF16)], axis=0)
    for part in range(out_ref.shape[0]):
        out_ref[part] = value


def reciprocal(x):
    estimate = pl.reciprocal(x, approx=True)
    estimate = estimate * (2.0 - x * estimate)
    return estimate * (2.0 - x * estimate)


def eliminate(gram):
    width = gram.shape[0]
    block = 8
    lanes = lax.broadcasted_iota(jnp.int32, (block, width), 1)
    subs = lax.broadcasted_iota(jnp.int32, (block, width), 0)

    def column(strip, k):
        return jnp.broadcast_to(strip[:, k : k + 1], (block, width))

    def row(strip, k):
        return jnp.broadcast_to(strip[k : k + 1, :], (block, width))

    strips = [gram[r : r + block, :] for r in range(0, width, block)]
    finished = []
    per_group = 4
    for begin in range(0, len(strips), per_group):
        group = strips[:per_group]
        for at in range(per_group):
            first = (begin + at) * block
            panel = group[at]
            columns = [column(panel, first + j) for j in range(block)]
            kept = panel
            for j in range(0, block, 2):
                here, there = subs == j, subs == j + 1
                lane, next_lane = lanes == first + j, lanes == first + j + 1
                left, right = columns[j], columns[j + 1]
                a, b, c = row(left, j), row(right, j), row(right, j + 1)
                scale = reciprocal(a * c - b * b)
                top, bottom = row(panel, j), row(panel, j + 1)
                ratio = b * reciprocal(a)
                kept = jnp.where(here, top, jnp.where(there, bottom - ratio * jnp.where(lane, 1.0, top), kept))
                kept = jnp.where(there & lane, -ratio, kept)
                top = jnp.where(lane, 1.0, jnp.where(next_lane, 0.0, top))
                bottom = jnp.where(lane, 0.0, jnp.where(next_lane, 1.0, bottom))
                unit_top = (c * top - b * bottom) * scale
                unit_bottom = (a * bottom - b * top) * scale
                others = jnp.where(lane | next_lane, 0.0, panel) - (left * unit_top + right * unit_bottom)
                panel = jnp.where(here, unit_top, jnp.where(there, unit_bottom, others))
                for m in range(j + 2, block):
                    up, down = row(columns[m], j), row(columns[m], j + 1)
                    up, down = (c * up - b * down) * scale, (a * down - b * up) * scale
                    others = columns[m] - (left * up + right * down)
                    columns[m] = jnp.where(here, up, jnp.where(there, down, others))
            finished.append(kept)
            group[at] = panel
            rows = [row(panel, m) for m in range(block)]
            inside = (lanes >= first) & (lanes < first + block)
            for s in range(per_group):
                if s != at:
                    terms = [column(group[s], first + m) * rows[m] for m in range(block)]
                    while len(terms) > 1:
                        terms = [x + y for x, y in zip(terms[::2], terms[1::2])]
                    group[s] = jnp.where(inside, 0.0, group[s]) - terms[0]
        strips = strips[per_group:]
        if strips:
            first, last = begin * block, (begin + per_group) * block
            below = jnp.concatenate(strips, axis=0)
            solved = [jnp.zeros((first, width), F32)] if first else []
            solved = jnp.concatenate(solved + group + [jnp.zeros((width - last, width), F32)], axis=0)
            cols = lax.broadcasted_iota(jnp.int32, below.shape, 1)
            below = jnp.where((cols >= first) & (cols < last), 0.0, below) - dot(below, solved)
            strips = [below[r : r + block, :] for r in range(0, below.shape[0], block)]
    return jnp.concatenate(finished, axis=0)


def final_kernel(total_rows, pieces_ref, now_ref, shifted_ref, basis_ref, projection_ref, rfactor_ref):
    width = now_ref.shape[1]
    piece = pieces_ref.shape[1] // 3
    pieces = pieces_ref[...]
    late = sum_high_and_low(pieces[:, : 2 * piece, :]).reshape(-1, width)
    early = pieces[:, 2 * piece :, :].astype(F32).reshape(-1, width)
    now_product, square = late[:width], late[width : 2 * width]
    now_square, shift = early[:width], early[width : 2 * width]
    projection = now_product * total_rows**-0.5
    projection_ref[...] = projection
    scaled = now_product * (1.0 / total_rows)
    half = shift - 0.5 * now_product + 0.5 * dot(now_square, scaled)
    mixed = dot_tn(scaled, half)
    gram = square + mixed + mixed.T
    reduced = eliminate(gram * (1.0 / total_rows))
    rows = lax.broadcasted_iota(jnp.int32, reduced.shape, 0)
    cols = lax.broadcasted_iota(jnp.int32, reduced.shape, 1)
    diagonal = jnp.sum(jnp.where(rows == cols, reduced, 0.0), axis=1, keepdims=True)
    root = lax.rsqrt(diagonal)
    rfactor_ref[...] = jnp.where(rows <= cols, reduced, 0.0) * root
    inverse = jnp.where(rows > cols, reduced, jnp.where(rows == cols, 1.0, 0.0)) * root
    residual = shifted_ref[...] - dot(now_ref[...], scaled)
    basis_ref[...] = dot_nt(residual, inverse)


def exchange(blocks, axis, steps):
    n = lax.axis_size(axis)
    assert n & (n - 1) == 0
    return [lax.ppermute(block, axis, [(i, i ^ step) for i in range(n)]) for step, block in zip(steps, blocks)]


def on_device(basis_now, basis_prev, coupling, tiles, tile_rows, tile_cols, tile_counts):
    rows_dev, width = basis_now.shape
    n_row, n_col = lax.axis_size("row"), lax.axis_size("col")
    devices = n_row * n_col
    tile_block = tiles[0, 0]
    total_rows = float(rows_dev * devices)
    piece = -(-2 * width // (8 * devices)) * 8
    smem = pl.BlockSpec(memory_space=pltpu.SMEM)
    vmem = pl.BlockSpec(memory_space=pltpu.VMEM)
    params = pltpu.CompilerParams(vmem_limit_bytes=48 * 1024 * 1024)

    both = jnp.concatenate([basis_now, basis_prev], axis=0).astype(BF16)
    gathered = lax.all_gather(both, "col", axis=0, tiled=True)
    index = jnp.concatenate(
        [tile_rows.reshape(-1), tile_cols.reshape(-1), tile_counts.reshape(-1)]
        + [lax.axis_index(axis).reshape(1) for axis in ("row", "col")]
    )
    half = n_row // 2
    block = jax.ShapeDtypeStruct((rows_dev + 2 * piece, width), BF16)
    sums = jax.ShapeDtypeStruct((rows_dev + piece, width), F32)
    *blocks, far, own = pl.pallas_call(
        functools.partial(tiles_kernel, n_row, n_col, total_rows),
        out_shape=[block] * (2 * half - 2) + [sums] * 2,
        in_specs=[smem] + [vmem] * 3,
        out_specs=[vmem] * (2 * half),
        scratch_shapes=[
            pltpu.VMEM((n_row * rows_dev, width), F32),
            pltpu.VMEM((devices * piece, width), F32),
        ],
        compiler_params=params,
        name="tile_products",
    )(index, tile_block, gathered, coupling)
    steps = distances(half)[:-1]
    mirrors = exchange(blocks[: half - 1], "row", steps)
    near = exchange(blocks[half - 1 :], "row", steps)
    mirror = pl.pallas_call(
        functools.partial(mirror_kernel, rows_dev),
        out_shape=block,
        in_specs=[vmem] * half,
        out_specs=vmem,
        compiler_params=params,
        name="mirror_sum",
    )(far, *mirrors)
    across = exchange([mirror], "row", [half])

    shifted, grams, early = pl.pallas_call(
        grams_kernel,
        out_shape=(
            jax.ShapeDtypeStruct((rows_dev, width), F32),
            jax.ShapeDtypeStruct((devices * piece, width), F32),
            jax.ShapeDtypeStruct((piece, width), F32),
        ),
        in_specs=[vmem] * (4 + half),
        out_specs=(vmem, vmem, vmem),
        compiler_params=params,
        name="local_grams",
    )(basis_now, basis_prev, coupling, own, *near, *across)
    everyone = ("row", "col")
    pieces = lax.all_to_all(grams.reshape(devices, piece, width), everyone, split_axis=0, concat_axis=0, tiled=True)
    copies = pl.pallas_call(
        spread_kernel,
        out_shape=jax.ShapeDtypeStruct((devices, 3 * piece, width), BF16),
        in_specs=[vmem, vmem],
        out_specs=vmem,
        compiler_params=params,
        name="sum_and_spread",
    )(pieces, early)
    gathered_sums = lax.all_to_all(copies, everyone, split_axis=0, concat_axis=0, tiled=True)
    return pl.pallas_call(
        functools.partial(final_kernel, total_rows),
        out_shape=(
            jax.ShapeDtypeStruct((rows_dev, width), F32),
            jax.ShapeDtypeStruct((width, width), F32),
            jax.ShapeDtypeStruct((width, width), F32),
        ),
        in_specs=[vmem] * 3,
        out_specs=(vmem, vmem, vmem),
        compiler_params=params,
        name="factor_and_basis",
    )(gathered_sums, basis_now, shifted)


def solution(mesh):
    placed = (
        P(("row", "col"), None),
        P(("row", "col"), None),
        P(),
        P("row", "col", None, None, None),
        P("row", "col", None),
        P("row", "col", None),
        P("row", "col"),
    )
    return jax.shard_map(
        on_device,
        mesh=mesh,
        in_specs=placed,
        out_specs=(P(("row", "col"), None), P(), P()),
        check_vma=False,
    )
```

time: 61 us -> 57.7 us (0.946)
  blocking collectives: 25.6 us -> 36 us
  waiting for transfers between devices: 9.76 us -> 2.09 us
  starting transfers between devices: 13.4 us -> 8.17 us
  Pallas kernels: 8.89 us -> 8.12 us
    all_gather x0 -> x1, blocking collectives: none -> 8.67 us  [on_device(): gathered = lax.all_gather(both, 'col', axis=0, tiled=True)]
    ppermute x7, waiting for transfers between devices: 6.41 us -> 2.09 us  [exchange(): lax.ppermute(block, axis, [(i, i ^ step) for i in range(n)])]
    ppermute x3 -> x0, starting transfers between devices: 4.15 us -> none  [gather(): lax.ppermute(block, axis, [(i, (i + step) % n) for i in range(n)])]
    ppermute x3 -> x0, waiting for transfers between devices: 3.35 us -> none  [gather(): lax.ppermute(block, axis, [(i, (i + step) % n) for i in range(n)])]
    all_to_all x1, blocking collectives: 14.5 us -> 16.3 us  [on_device(): lax.all_to_all(grams.reshape(devices, piece, width), everyone, split_axis...]
    ppermute x7, starting transfers between devices: 9.3 us -> 8.17 us  [exchange(): lax.ppermute(block, axis, [(i, i ^ step) for i in range(n)])]
    pallas_call x2 -> x3, Pallas kernels: 2.49 us -> 2.11 us  [the longest x1 1.36 us: on_device(): pl.pallas_call(functools.partial(tiles_kernel, n_row, n_col, total_rows),...]
  transfers between devices with their start and end apart: 10 -> 7, of which waited for: 5 -> 4; matrix products, arithmetic and copies ran while one was open for 0% -> 0% of each run, Pallas kernels for 0% -> 0%
where the time goes in v8:
time: 57.7 us; the launch traced here: 57.4 us
  blocking collectives  36 us (62%)
  starting transfers between devices  8.17 us (14%)
  Pallas kernels  8.12 us (14%)
  waiting for transfers between devices  2.09 us (4%)
  between operations  1.39 us (2%)
  other arithmetic  0.94 us (2%)
  local copies, waits for them, and re-layouts  0.77 us (1%)
    all_to_all x1, blocking collectives, on_device(): lax.all_to_all(grams.reshape(devices, piece, width), everyone, split_axis...  16.3 us
    all_to_all x1, blocking collectives, on_device(): lax.all_to_all(copies, everyone, split_axis=0, concat_axis=0, tiled=True)  11 us
    all_gather x1, blocking collectives, on_device(): gathered = lax.all_gather(both, 'col', axis=0, tiled=True)  8.67 us
    ppermute x7, starting transfers between devices, exchange(): lax.ppermute(block, axis, [(i, i ^ step) for i in range(n)])  8.17 us
    pallas_call x1, Pallas kernels, on_device(): pl.pallas_call(functools.partial(final_kernel, total_rows), out_shape=(ja...  5.96 us
    ppermute x7, waiting for transfers between devices, exchange(): lax.ppermute(block, axis, [(i, i ^ step) for i in range(n)])  2.09 us
    pallas_call x1, Pallas kernels, on_device(): pl.pallas_call(functools.partial(tiles_kernel, n_row, n_col, total_rows),...  1.36 us
  transfers between devices with their start and end apart: 7, of which 4 were waited for; matrix products, arithmetic and copies ran while one was open for 0% of the time, Pallas kernels for 0%

profile of v8, /device:TPU:1, one launch (start us, length us, event | category | flops | bytes accessed | tf_op | source)
XLA Modules:
  0.0 57.4 jit_solution(14705966593947461269)
XLA Ops:
  0.6 0.0 copy-start
  1.3 0.9 %convert.7 = bf16[256,128]{1,0:T(8,128)(2,1)S(1)} convert(f32[256,128]{1,0:T(8,128)} %prev_ref.1) | non-fusion elementwise | flops 32768 | bytes 196608 | tf_op jit(solution)/shard_map/convert.1
  2.2 0.0 copy-done
  2.2 0.0 copy-start.1
  2.3 0.0 copy-start.3
  2.3 8.7 %all_gather.3.basis_ref = bf16[2048,128]{1,0:T(8,128)(2,1)S(1)} all-gather(bf16[512,128]{1,0:T(8,128)(2,1)S(1)} %pad_maximum_fusion), channel_id=1, replica_groups=mesh['row'=8,'col'=4] {'col'}, dimensions={0}, use_global_device_ids=true | all-gather | bytes 655360 | tf_op jit(solution)/shard_map/all_gather | solution.py:245
  11.0 0.0 copy-start.4
  11.0 0.0 copy-start.5
  11.0 0.7 %copy-done.4 = s32[1,1,16]{2,1,0:T(1,128)S(1)} copy-done((s32[1,1,16]{2,1,0:T(1,128)S(1)}, s32[1,1,16]{2,1,0:T(1,128)}, u32[]{:S(2)}) %copy-start.4) | copy-done | bytes 88
  11.6 0.0 copy-done.5
  11.7 0.1 concatenate.7.index_ref
  11.7 0.0 copy-done.1
  11.7 0.0 copy-done.3
  11.7 1.4 %tile_products.1 = (bf16[272,128]{1,0:T(8,128)(2,1)S(1)}, bf16[272,128]{1,0:T(8,128)(2,1)S(1)}, bf16[272,128]{1,0:T(8,128)(2,1)S(1)}, bf16[272,128]{1,0:T(8,128)...) custom-call(s32[35]{0:T(128)S(1)} %concatenate.7.index_ref, ...), custom_call_target="tpu_custom_call" | custom-call | tf_op jit(solution)/shard_map/tile_products/pallas_call | solution.py:253
  13.1 2.3 %collective-permute-start.3 = (bf16[272,128]{1,0:T(8,128)(2,1)S(1)}, bf16[272,128]{1,0:T(8,128)(2,1)S(1)}, u32[]{:S(2)}, u32[]{:S(2)}) collective-permute-start(bf16[272,128]{1,0:T(8,128)(2,1)S(1)} %get-tuple-element.19), channel_id=1, source_target_pairs={{0,12},{4,8},{8,4},{12,0},{16,28},{20,24},{24,20},{28,16},{1,13},{... | collective-permute-start | bytes 208904 | tf_op jit(solution)/shard_map/ppermute | solution.py:230
  15.4 0.2 collective-permute-start.4
  15.6 0.3 collective-permute-start.5
  15.8 2.2 %collective-permute-start = (bf16[272,128]{1,0:T(8,128)(2,1)S(1)}, bf16[272,128]{1,0:T(8,128)(2,1)S(1)}, u32[]{:S(2)}, u32[]{:S(2)}) collective-permute-start(bf16[272,128]{1,0:T(8,128)(2,1)S(1)} %get-tuple-element.15), channel_id=1, source_target_pairs={{0,12},{4,8},{8,4},{12,0},{16,28},{20,24},{24,20},{28,16},{1,13},{... | collective-permute-start | bytes 208904 | tf_op jit(solution)/shard_map/ppermute | solution.py:230
  18.0 0.2 collective-permute-start.1
  18.2 0.0 collective-permute-done.3.refs_0_
  18.2 0.7 %collective-permute-start.2 = (bf16[272,128]{1,0:T(8,128)(2,1)S(1)}, bf16[272,128]{1,0:T(8,128)(2,1)S(1)}, u32[]{:S(2)}, u32[]{:S(2)}) collective-permute-start(bf16[272,128]{1,0:T(8,128)(2,1)S(1)} %get-tuple-element.17), channel_id=1, source_target_pairs={{0,4},{4,0},{8,12},{12,8},{16,20},{20,16},{24,28},{28,24},{1,5},{5... | collective-permute-start | bytes 208904 | tf_op jit(solution)/shard_map/ppermute | solution.py:230
  18.9 0.2 collective-permute-done.4.refs_1_
  19.1 0.0 collective-permute-done.5.refs_2_
  19.1 0.0 copy-start.2
  19.2 2.4 %collective-permute-start.6 = (bf16[272,128]{1,0:T(8,128)(2,1)S(1)}, bf16[272,128]{1,0:T(8,128)(2,1)S(1)}, u32[]{:S(2)}, u32[]{:S(2)}) collective-permute-start(bf16[272,128]{1,0:T(8,128)(2,1)S(1)} %mirror_sum.1), channel_id=1, source_target_pairs={{0,16},{4,20},{8,24},{12,28},{16,0},{20,4},{24,8},{28,12},{1,17},{... | collective-permute-start | bytes 208904 | tf_op jit(solution)/shard_map/ppermute | solution.py:230
  21.6 0.0 collective-permute-done.refs_0_
  21.6 0.5 collective-permute-done.1.refs_1_
  22.1 0.2 collective-permute-done.2.refs_2_
  22.2 1.2 %collective-permute-done.6.refs_3_ = bf16[272,128]{1,0:T(8,128)(2,1)S(1)} collective-permute-done((bf16[272,128]{1,0:T(8,128)(2,1)S(1)}, bf16[272,128]{1,0:T(8,128)(2,1)S(1)}, u32[]{:S(2)}, u32[]{:S(2)}) %collective-permute-start.6) | collective-permute-done | bytes 69664 | tf_op jit(solution)/shard_map/ppermute | solution.py:230
  23.4 0.0 copy-done.2
  23.4 0.7 %local_grams.1 = (f32[256,128]{1,0:T(8,128)S(1)}, f32[256,128]{1,0:T(8,128)S(1)}, f32[8,128]{1,0:T(8,128)S(1)}) custom-call(f32[256,128]{1,0:T(8,128)S(1)} %copy-done, f32[256,128]{1,0:T(8,128)S(1)} %copy-done.2, f32[128,128]{1,0:T(8,128)S(1)} %copy-done.3, f32[264,128]{1,0:T(8,128)S(1)} %get-tuple-element.14.own_ref, ...), custom_call_target="tpu_custom_call" | custom-call | tf_op jit(solution)/shard_map/local_grams/pallas_call | solution.py:278
  24.1 16.3 %all_to_all.10.parts_ref = f32[32,8,128]{2,1,0:T(8,128)S(1)} all-to-all(f32[32,8,128]{2,1,0:T(8,128)S(1)} %bitcast.9), channel_id=1, replica_groups=mesh['row'=8,'col'=4] {'row','col'}, dimensions={0} | all-to-all | bytes 262144 | tf_op jit(solution)/shard_map/all_to_all | solution.py:291
  40.4 0.1 sum_and_spread.1
  40.5 11.0 %all_to_all.11.pieces_ref = bf16[32,24,128]{2,1,0:T(8,128)(2,1)S(1)} all-to-all(bf16[32,24,128]{2,1,0:T(8,128)(2,1)S(1)} %sum_and_spread.1), channel_id=1, replica_groups=mesh['row'=8,'col'=4] {'row','col'}, dimensions={0} | all-to-all | bytes 393216 | tf_op jit(solution)/shard_map/all_to_all | solution.py:300
  51.5 6.0 %factor_and_basis.1 = (f32[256,128]{1,0:T(8,128)}, f32[128,128]{1,0:T(8,128)}, f32[128,128]{1,0:T(8,128)}) custom-call(bf16[32,24,128]{2,1,0:T(8,128)(2,1)S(1)} %all_to_all.11.pieces_ref, f32[256,128]{1,0:T(8,128)S(1)} %copy-done, f32[256,128]{1,0:T(8,128)S(1)} %get-tuple-element.24.shifted_ref), custom_call_target="tpu_custom_call" | custom-call | tf_op jit(solution)/shard_map/factor_and_basis/pallas_call | solution.py:301
  (3 shorter events, 0.1 us)
Async XLA Ops:
  0.6 1.6 %copy-start = (f32[256,128]{1,0:T(8,128)S(1)}, f32[256,128]{1,0:T(8,128)}, u32[]{:S(2)}) copy-start(f32[256,128]{1,0:T(8,128)} %now_ref.3) | copy-start | bytes 393220
  2.2 9.5 %copy-start.1 = (bf16[1,1,16,128,128]{4,3,2,1,0:T(8,128)(2,1)S(1)}, bf16[1,1,16,128,128]{4,3,2,1,0:T(8,128)(2,1)}, u32[]{:S(2)}) copy-start(bf16[1,1,16,128,128]{4,3,2,1,0:T(8,128)(2,1)} %param.10) | copy-start | bytes 1572868
  2.3 9.4 %copy-start.3 = (f32[128,128]{1,0:T(8,128)S(1)}, f32[128,128]{1,0:T(8,128)}, u32[]{:S(2)}) copy-start(f32[128,128]{1,0:T(8,128)} %coupling_ref.3) | copy-start | bytes 196612
  11.0 0.7 %copy-start.4 = (s32[1,1,16]{2,1,0:T(1,128)S(1)}, s32[1,1,16]{2,1,0:T(1,128)}, u32[]{:S(2)}) copy-start(s32[1,1,16]{2,1,0:T(1,128)} %param.11) | copy-start | bytes 196
  11.0 0.7 %copy-start.5 = (s32[1,1,16]{2,1,0:T(1,128)S(1)}, s32[1,1,16]{2,1,0:T(1,128)}, u32[]{:S(2)}) copy-start(s32[1,1,16]{2,1,0:T(1,128)} %param.12) | copy-start | bytes 196
  13.1 5.1 %collective-permute-start.3 = (bf16[272,128]{1,0:T(8,128)(2,1)S(1)}, bf16[272,128]{1,0:T(8,128)(2,1)S(1)}, u32[]{:S(2)}, u32[]{:S(2)}) collective-permute-start(bf16[272,128]{1,0:T(8,128)(2,1)S(1)} %get-tuple-element.19), channel_id=1, source_target_pairs={{0,12},{4,8},{8,4},{12,0},{16,28},{20,24},{24,20},{28,16},{1,13},{... | collective-permute-start | bytes 208904 | tf_op jit(solution)/shard_map/ppermute | solution.py:230
  15.4 3.7 %collective-permute-start.4 = (bf16[272,128]{1,0:T(8,128)(2,1)S(1)}, bf16[272,128]{1,0:T(8,128)(2,1)S(1)}, u32[]{:S(2)}, u32[]{:S(2)}) collective-permute-start(bf16[272,128]{1,0:T(8,128)(2,1)S(1)} %get-tuple-element.20), channel_id=1, source_target_pairs={{0,8},{4,12},{8,0},{12,4},{16,24},{20,28},{24,16},{28,20},{1,9},{5... | collective-permute-start | bytes 208904 | tf_op jit(solution)/shard_map/ppermute | solution.py:230
  15.6 3.6 %collective-permute-start.5 = (bf16[272,128]{1,0:T(8,128)(2,1)S(1)}, bf16[272,128]{1,0:T(8,128)(2,1)S(1)}, u32[]{:S(2)}, u32[]{:S(2)}) collective-permute-start(bf16[272,128]{1,0:T(8,128)(2,1)S(1)} %get-tuple-element.21), channel_id=1, source_target_pairs={{0,4},{4,0},{8,12},{12,8},{16,20},{20,16},{24,28},{28,24},{1,5},{5... | collective-permute-start | bytes 208904 | tf_op jit(solution)/shard_map/ppermute | solution.py:230
  15.8 5.7 %collective-permute-start = (bf16[272,128]{1,0:T(8,128)(2,1)S(1)}, bf16[272,128]{1,0:T(8,128)(2,1)S(1)}, u32[]{:S(2)}, u32[]{:S(2)}) collective-permute-start(bf16[272,128]{1,0:T(8,128)(2,1)S(1)} %get-tuple-element.15), channel_id=1, source_target_pairs={{0,12},{4,8},{8,4},{12,0},{16,28},{20,24},{24,20},{28,16},{1,13},{... | collective-permute-start | bytes 208904 | tf_op jit(solution)/shard_map/ppermute | solution.py:230
  18.0 4.0 %collective-permute-start.1 = (bf16[272,128]{1,0:T(8,128)(2,1)S(1)}, bf16[272,128]{1,0:T(8,128)(2,1)S(1)}, u32[]{:S(2)}, u32[]{:S(2)}) collective-permute-start(bf16[272,128]{1,0:T(8,128)(2,1)S(1)} %get-tuple-element.16), channel_id=1, source_target_pairs={{0,8},{4,12},{8,0},{12,4},{16,24},{20,28},{24,16},{28,20},{1,9},{5... | collective-permute-start | bytes 208904 | tf_op jit(solution)/shard_map/ppermute | solution.py:230
  18.2 4.0 %collective-permute-start.2 = (bf16[272,128]{1,0:T(8,128)(2,1)S(1)}, bf16[272,128]{1,0:T(8,128)(2,1)S(1)}, u32[]{:S(2)}, u32[]{:S(2)}) collective-permute-start(bf16[272,128]{1,0:T(8,128)(2,1)S(1)} %get-tuple-element.17), channel_id=1, source_target_pairs={{0,4},{4,0},{8,12},{12,8},{16,20},{20,16},{24,28},{28,24},{1,5},{5... | collective-permute-start | bytes 208904 | tf_op jit(solution)/shard_map/ppermute | solution.py:230
  19.1 4.3 %copy-start.2 = (f32[256,128]{1,0:T(8,128)S(1)}, f32[256,128]{1,0:T(8,128)}, u32[]{:S(2)}) copy-start(f32[256,128]{1,0:T(8,128)} %prev_ref.1) | copy-start | bytes 393220
  19.2 4.2 %collective-permute-start.6 = (bf16[272,128]{1,0:T(8,128)(2,1)S(1)}, bf16[272,128]{1,0:T(8,128)(2,1)S(1)}, u32[]{:S(2)}, u32[]{:S(2)}) collective-permute-start(bf16[272,128]{1,0:T(8,128)(2,1)S(1)} %mirror_sum.1), channel_id=1, source_target_pairs={{0,16},{4,20},{8,24},{12,28},{16,0},{20,4},{24,8},{28,12},{1,17},{... | collective-permute-start | bytes 208904 | tf_op jit(solution)/shard_map/ppermute | solution.py:230

commit v9 on v8

--- a/solution.py
+++ b/solution.py
@@ -46,36 +46,36 @@
     return value[..., :half, :] + value[..., half:, :]
 
 
-def tiles_kernel(n_row, n_col, total_rows, index_ref, tiles_ref, basis_ref, coupling_ref, *refs):
+def tiles_kernel(n_row, n_col, total_rows, me_ref, rows_ref, cols_ref, count_ref, tiles_ref, basis_ref, coupling_ref, *refs):
     half = n_row // 2
     mirror_refs, near_refs, (far_ref, own_ref, total_ref, early_ref) = refs[: half - 1], refs[half - 1 : -4], refs[-4:]
     slots, size, _ = tiles_ref.shape
     width = total_ref.shape[1]
     rows_dev = total_ref.shape[0] // n_row
     piece = early_ref.shape[0] // (n_row * n_col)
-    used, my_row, my_col = [index_ref[2 * slots + k] for k in range(3)]
+    my_row, my_col = me_ref[0], me_ref[1]
     total_ref[...] = jnp.zeros_like(total_ref)
-    per_slab = rows_dev // size
-    for slot in range(slots):
-        col = index_ref[slots + slot]
-        start = pl.multiple_of((2 * per_slab * (col // per_slab) + lax.rem(col, per_slab)) * size, size)
-        value = jnp.dot(tiles_ref[slot], basis_ref[pl.ds(start, size), :], preferred_element_type=F32)
-        value = jnp.where(slot < used, value, 0.0)
-        place = pl.ds(pl.multiple_of(index_ref[slot] * size, size), size)
-        total_ref[place, :] += value
-    square = jnp.zeros((width, width), F32)
-    cross = jnp.zeros((width, width), F32)
+    grams = jnp.zeros((width, 2 * width), F32)
     for slab in range(n_col):
         now = basis_ref[2 * slab * rows_dev : (2 * slab + 1) * rows_dev, :]
         prev = basis_ref[(2 * slab + 1) * rows_dev : (2 * slab + 2) * rows_dev, :]
-        square += dot_tn(now, now, None)
-        cross += dot_tn(now, prev, None)
+        grams += dot_tn(now, jnp.concatenate([now, prev], axis=1), None)
+    square, cross = grams[:, :width], grams[:, width:]
     rows = lax.broadcasted_iota(jnp.int32, square.shape, 0)
     cols = lax.broadcasted_iota(jnp.int32, square.shape, 1)
     if early_ref.shape[0] > 2 * width:
         early_ref[...] = jnp.zeros_like(early_ref)
     early_ref[:width, :] = square - jnp.where(rows == cols, total_rows / n_row, 0.0)
     early_ref[width : 2 * width, :] = dot_nt(cross, upper_of(coupling_ref[...]))
+    used = count_ref[...]
+    per_slab = rows_dev // size
+    for slot in range(slots):
+        col = cols_ref[0, 0, slot]
+        start = pl.multiple_of((2 * per_slab * (col // per_slab) + lax.rem(col, per_slab)) * size, size)
+        value = jnp.dot(tiles_ref[slot], basis_ref[pl.ds(start, size), :], preferred_element_type=F32)
+        value = value * (slot < used).astype(F32)
+        place = pl.ds(pl.multiple_of(rows_ref[0, 0, slot] * size, size), size)
+        total_ref[place, :] += value
 
     def parts_of(row):
         slab = total_ref[pl.ds(pl.multiple_of(row * rows_dev, rows_dev), rows_dev), :]
@@ -107,11 +107,15 @@
     write_block(out_ref, *add_blocks(own_ref, block_refs, rows_dev))
 
 
-def grams_kernel(now_ref, prev_ref, coupling_ref, own_ref, *refs):
+def shift_kernel(prev_ref, coupling_ref, shift_ref):
+    shift_ref[...] = dot_nt(prev_ref[...], upper_of(coupling_ref[...]))
+
+
+def grams_kernel(now_ref, shift_ref, own_ref, *refs):
     block_refs, (shifted_ref, grams_ref, early_ref) = refs[:-3], refs[-3:]
     rows_dev, width = now_ref.shape
     product, early_ref[...] = add_blocks(own_ref, block_refs, rows_dev)
-    shifted = product - dot_nt(prev_ref[...], upper_of(coupling_ref[...]))
+    shifted = product - shift_ref[...]
     shifted_ref[...] = shifted
     if grams_ref.shape[0] > 2 * width:
         grams_ref[...] = jnp.zeros_like(grams_ref)
@@ -128,15 +132,23 @@
         out_ref[part] = value
 
 
-def reciprocal(x):
-    estimate = pl.reciprocal(x, approx=True)
-    estimate = estimate * (2.0 - x * estimate)
-    return estimate * (2.0 - x * estimate)
+def split(x):
+    high = x.astype(BF16)
+    return high, (x - high.astype(F32)).astype(BF16)
+
+
+def dot3(a, b, dims=((1,), (0,))):
+    (a_high, a_low), (b_high, b_low) = split(a), split(b)
+
+    def one(x, y):
+        return lax.dot_general(x, y, (dims, ((), ())), preferred_element_type=F32)
+
+    return one(a_high, b_low) + one(a_low, b_high) + one(a_high, b_high)
 
 
 def eliminate(gram):
     width = gram.shape[0]
-    block = 8
+    block, per_group = 16, 2
     lanes = lax.broadcasted_iota(jnp.int32, (block, width), 1)
     subs = lax.broadcasted_iota(jnp.int32, (block, width), 0)
 
@@ -148,7 +160,6 @@
 
     strips = [gram[r : r + block, :] for r in range(0, width, block)]
     finished = []
-    per_group = 4
     for begin in range(0, len(strips), per_group):
         group = strips[:per_group]
         for at in range(per_group):
@@ -161,9 +172,9 @@
                 lane, next_lane = lanes == first + j, lanes == first + j + 1
                 left, right = columns[j], columns[j + 1]
                 a, b, c = row(left, j), row(right, j), row(right, j + 1)
-                scale = reciprocal(a * c - b * b)
+                scale = 1.0 / (a * c - b * b)
                 top, bottom = row(panel, j), row(panel, j + 1)
-                ratio = b * reciprocal(a)
+                ratio = b / a
                 kept = jnp.where(here, top, jnp.where(there, bottom - ratio * jnp.where(lane, 1.0, top), kept))
                 kept = jnp.where(there & lane, -ratio, kept)
                 top = jnp.where(lane, 1.0, jnp.where(next_lane, 0.0, top))
@@ -194,7 +205,7 @@
             solved = [jnp.zeros((first, width), F32)] if first else []
             solved = jnp.concatenate(solved + group + [jnp.zeros((width - last, width), F32)], axis=0)
             cols = lax.broadcasted_iota(jnp.int32, below.shape, 1)
-            below = jnp.where((cols >= first) & (cols < last), 0.0, below) - dot(below, solved)
+            below = jnp.where((cols >= first) & (cols < last), 0.0, below) - dot3(below, solved)
             strips = [below[r : r + block, :] for r in range(0, below.shape[0], block)]
     return jnp.concatenate(finished, axis=0)
 
@@ -210,8 +221,8 @@
     projection = now_product * total_rows**-0.5
     projection_ref[...] = projection
     scaled = now_product * (1.0 / total_rows)
-    half = shift - 0.5 * now_product + 0.5 * dot(now_square, scaled)
-    mixed = dot_tn(scaled, half)
+    half = shift - 0.5 * now_product + 0.5 * dot3(now_square, scaled)
+    mixed = dot3(scaled, half, ((0,), (0,)))
     gram = square + mixed + mixed.T
     reduced = eliminate(gram * (1.0 / total_rows))
     rows = lax.broadcasted_iota(jnp.int32, reduced.shape, 0)
@@ -220,8 +231,8 @@
     root = lax.rsqrt(diagonal)
     rfactor_ref[...] = jnp.where(rows <= cols, reduced, 0.0) * root
     inverse = jnp.where(rows > cols, reduced, jnp.where(rows == cols, 1.0, 0.0)) * root
-    residual = shifted_ref[...] - dot(now_ref[...], scaled)
-    basis_ref[...] = dot_nt(residual, inverse)
+    residual = shifted_ref[...] - dot3(now_ref[...], scaled)
+    basis_ref[...] = dot3(residual, inverse, ((1,), (1,)))
 
 
 def exchange(blocks, axis, steps):
@@ -243,17 +254,14 @@
 
     both = jnp.concatenate([basis_now, basis_prev], axis=0).astype(BF16)
     gathered = lax.all_gather(both, "col", axis=0, tiled=True)
-    index = jnp.concatenate(
-        [tile_rows.reshape(-1), tile_cols.reshape(-1), tile_counts.reshape(-1)]
-        + [lax.axis_index(axis).reshape(1) for axis in ("row", "col")]
-    )
+    me = jnp.stack([lax.axis_index("row"), lax.axis_index("col")])
     half = n_row // 2
     block = jax.ShapeDtypeStruct((rows_dev + 2 * piece, width), BF16)
     sums = jax.ShapeDtypeStruct((rows_dev + piece, width), F32)
     *blocks, far, own = pl.pallas_call(
         functools.partial(tiles_kernel, n_row, n_col, total_rows),
         out_shape=[block] * (2 * half - 2) + [sums] * 2,
-        in_specs=[smem] + [vmem] * 3,
+        in_specs=[smem] * 3 + [vmem] * 4,
         out_specs=[vmem] * (2 * half),
         scratch_shapes=[
             pltpu.VMEM((n_row * rows_dev, width), F32),
@@ -261,7 +269,7 @@
         ],
         compiler_params=params,
         name="tile_products",
-    )(index, tile_block, gathered, coupling)
+    )(me, tile_rows, tile_cols, tile_counts, tile_block, gathered, coupling)
     steps = distances(half)[:-1]
     mirrors = exchange(blocks[: half - 1], "row", steps)
     near = exchange(blocks[half - 1 :], "row", steps)
@@ -275,6 +283,15 @@
     )(far, *mirrors)
     across = exchange([mirror], "row", [half])
 
+    shift = pl.pallas_call(
+        shift_kernel,
+        out_shape=jax.ShapeDtypeStruct((rows_dev, width), F32),
+        in_specs=[vmem] * 2,
+        out_specs=vmem,
+        compiler_params=params,
+        cost_estimate=pl.CostEstimate(flops=12 * rows_dev * width * width, bytes_accessed=12 * rows_dev * width, transcendentals=0),
+        name="shift_by_previous",
+    )(basis_prev, coupling)
     shifted, grams, early = pl.pallas_call(
         grams_kernel,
         out_shape=(
@@ -282,11 +299,11 @@
             jax.ShapeDtypeStruct((devices * piece, width), F32),
             jax.ShapeDtypeStruct((piece, width), F32),
         ),
-        in_specs=[vmem] * (4 + half),
+        in_specs=[vmem] * (3 + half),
         out_specs=(vmem, vmem, vmem),
         compiler_params=params,
         name="local_grams",
-    )(basis_now, basis_prev, coupling, own, *near, *across)
+    )(basis_now, shift, own, *near, *across)
     everyone = ("row", "col")
     pieces = lax.all_to_all(grams.reshape(devices, piece, width), everyone, split_axis=0, concat_axis=0, tiled=True)
     copies = pl.pallas_call(

time: 57.7 us -> 56 us (0.971)
  Pallas kernels: 8.12 us -> 6.76 us
    pallas_call x1, Pallas kernels: 5.96 us -> 4.65 us  [on_device(): pl.pallas_call(functools.partial(final_kernel, total_rows), out_shape=(ja...]
  transfers between devices with their start and end apart: 7 -> 7, of which waited for: 4 -> 4; matrix products, arithmetic and copies ran while one was open for 0% -> 0% of each run, Pallas kernels for 0% -> 1%
where the time goes in v9:
time: 56 us; the launch traced here: 55.8 us
  blocking collectives  36 us (64%)
  starting transfers between devices  8.17 us (15%)
  Pallas kernels  6.76 us (12%)
  waiting for transfers between devices  1.8 us (3%)
  between operations  1.39 us (2%)
  other arithmetic  1.05 us (2%)
  local copies, waits for them, and re-layouts  0.69 us (1%)
    all_to_all x1, blocking collectives, on_device(): lax.all_to_all(grams.reshape(devices, piece, width), everyone, split_axis...  16.2 us
    all_to_all x1, blocking collectives, on_device(): lax.all_to_all(copies, everyone, split_axis=0, concat_axis=0, tiled=True)  11 us
    all_gather x1, blocking collectives, on_device(): gathered = lax.all_gather(both, 'col', axis=0, tiled=True)  8.67 us
    ppermute x7, starting transfers between devices, exchange(): lax.ppermute(block, axis, [(i, i ^ step) for i in range(n)])  8.17 us
    pallas_call x1, Pallas kernels, on_device(): pl.pallas_call(functools.partial(final_kernel, total_rows), out_shape=(ja...  4.65 us
    ppermute x7, waiting for transfers between devices, exchange(): lax.ppermute(block, axis, [(i, i ^ step) for i in range(n)])  1.8 us
    pallas_call x1, Pallas kernels, on_device(): pl.pallas_call(functools.partial(tiles_kernel, n_row, n_col, total_rows),...  1.32 us
  transfers between devices with their start and end apart: 7, of which 4 were waited for; matrix products, arithmetic and copies ran while one was open for 0% of the time, Pallas kernels for 1%

profile of v9, /device:TPU:1, one launch (start us, length us, event | category | flops | bytes accessed | tf_op | source)
XLA Modules:
  0.0 55.8 jit_solution(17573939108137632761)
XLA Ops:
  0.6 0.0 copy-start.2
  0.6 0.9 %convert.6 = bf16[256,128]{1,0:T(8,128)(2,1)S(1)} convert(f32[256,128]{1,0:T(8,128)} %now_ref.3) | non-fusion elementwise | flops 32768 | bytes 196608 | tf_op jit(solution)/shard_map/convert
  1.6 0.0 copy-done.2
  1.6 0.0 copy-start.1
  1.6 0.0 copy-start.3
  1.7 8.7 %all_gather.3.basis_ref = bf16[2048,128]{1,0:T(8,128)(2,1)S(1)} all-gather(bf16[512,128]{1,0:T(8,128)(2,1)S(1)} %pad_maximum_fusion), channel_id=1, replica_groups=mesh['row'=8,'col'=4] {'col'}, dimensions={0}, use_global_device_ids=true | all-gather | bytes 655360 | tf_op jit(solution)/shard_map/all_gather | solution.py:256
  11.0 0.1 pad_add_fusion.me_ref
  11.1 0.0 copy-start.4
  11.1 0.0 copy-start.5
  11.1 0.0 copy-done.1
  11.1 0.0 copy-done.3
  11.1 0.6 %copy-done.4 = s32[1,1,16]{2,1,0:T(1,128)S(1)} copy-done((s32[1,1,16]{2,1,0:T(1,128)S(1)}, s32[1,1,16]{2,1,0:T(1,128)}, u32[]{:S(2)}) %copy-start.4) | copy-done | bytes 88
  11.7 0.0 copy-done.5
  11.7 1.3 %tile_products.1 = (bf16[272,128]{1,0:T(8,128)(2,1)S(1)}, bf16[272,128]{1,0:T(8,128)(2,1)S(1)}, bf16[272,128]{1,0:T(8,128)(2,1)S(1)}, bf16[272,128]{1,0:T(8,128)...) custom-call(s32[2]{0:T(128)S(1)} %pad_add_fusion.me_ref, ...), custom_call_target="tpu_custom_call" | custom-call | tf_op jit(solution)/shard_map/tile_products/pallas_call | solution.py:261
  13.1 2.3 %collective-permute-start.3 = (bf16[272,128]{1,0:T(8,128)(2,1)S(1)}, bf16[272,128]{1,0:T(8,128)(2,1)S(1)}, u32[]{:S(2)}, u32[]{:S(2)}) collective-permute-start(bf16[272,128]{1,0:T(8,128)(2,1)S(1)} %get-tuple-element.19), channel_id=1, source_target_pairs={{0,12},{4,8},{8,4},{12,0},{16,28},{20,24},{24,20},{28,16},{1,13},{... | collective-permute-start | bytes 208904 | tf_op jit(solution)/shard_map/ppermute | solution.py:241
  15.4 0.2 collective-permute-start.4
  15.5 0.3 collective-permute-start.5
  15.8 2.2 %collective-permute-start = (bf16[272,128]{1,0:T(8,128)(2,1)S(1)}, bf16[272,128]{1,0:T(8,128)(2,1)S(1)}, u32[]{:S(2)}, u32[]{:S(2)}) collective-permute-start(bf16[272,128]{1,0:T(8,128)(2,1)S(1)} %get-tuple-element.15), channel_id=1, source_target_pairs={{0,12},{4,8},{8,4},{12,0},{16,28},{20,24},{24,20},{28,16},{1,13},{... | collective-permute-start | bytes 208904 | tf_op jit(solution)/shard_map/ppermute | solution.py:241
  18.0 0.2 collective-permute-start.1
  18.2 0.0 collective-permute-done.3.refs_0_
  18.2 0.7 %collective-permute-start.2 = (bf16[272,128]{1,0:T(8,128)(2,1)S(1)}, bf16[272,128]{1,0:T(8,128)(2,1)S(1)}, u32[]{:S(2)}, u32[]{:S(2)}) collective-permute-start(bf16[272,128]{1,0:T(8,128)(2,1)S(1)} %get-tuple-element.17), channel_id=1, source_target_pairs={{0,4},{4,0},{8,12},{12,8},{16,20},{20,16},{24,28},{28,24},{1,5},{5... | collective-permute-start | bytes 208904 | tf_op jit(solution)/shard_map/ppermute | solution.py:241
  18.9 0.2 collective-permute-done.4.refs_1_
  19.1 0.0 collective-permute-done.5.refs_2_
  19.1 0.0 copy-start
  19.2 2.4 %collective-permute-start.6 = (bf16[272,128]{1,0:T(8,128)(2,1)S(1)}, bf16[272,128]{1,0:T(8,128)(2,1)S(1)}, u32[]{:S(2)}, u32[]{:S(2)}) collective-permute-start(bf16[272,128]{1,0:T(8,128)(2,1)S(1)} %mirror_sum.1), channel_id=1, source_target_pairs={{0,16},{4,20},{8,24},{12,28},{16,0},{20,4},{24,8},{28,12},{1,17},{... | collective-permute-start | bytes 208904 | tf_op jit(solution)/shard_map/ppermute | solution.py:241
  21.5 0.3 shift_by_previous.1.shift_ref
  21.8 0.0 collective-permute-done.refs_0_
  21.8 0.2 collective-permute-done.1.refs_1_
  22.0 0.1 collective-permute-done.2.refs_2_
  22.2 1.2 %collective-permute-done.6.refs_3_ = bf16[272,128]{1,0:T(8,128)(2,1)S(1)} collective-permute-done((bf16[272,128]{1,0:T(8,128)(2,1)S(1)}, bf16[272,128]{1,0:T(8,128)(2,1)S(1)}, u32[]{:S(2)}, u32[]{:S(2)}) %collective-permute-start.6) | collective-permute-done | bytes 69664 | tf_op jit(solution)/shard_map/ppermute | solution.py:241
  23.4 0.0 copy-done
  23.4 0.4 local_grams.1
  23.8 16.2 %all_to_all.10.parts_ref = f32[32,8,128]{2,1,0:T(8,128)S(1)} all-to-all(f32[32,8,128]{2,1,0:T(8,128)S(1)} %bitcast.5), channel_id=1, replica_groups=mesh['row'=8,'col'=4] {'row','col'}, dimensions={0} | all-to-all | bytes 262144 | tf_op jit(solution)/shard_map/all_to_all | solution.py:308
  40.1 0.1 sum_and_spread.1
  40.1 11.0 %all_to_all.11.pieces_ref = bf16[32,24,128]{2,1,0:T(8,128)(2,1)S(1)} all-to-all(bf16[32,24,128]{2,1,0:T(8,128)(2,1)S(1)} %sum_and_spread.1), channel_id=1, replica_groups=mesh['row'=8,'col'=4] {'row','col'}, dimensions={0} | all-to-all | bytes 393216 | tf_op jit(solution)/shard_map/all_to_all | solution.py:317
  51.2 4.7 %factor_and_basis.1 = (f32[256,128]{1,0:T(8,128)}, f32[128,128]{1,0:T(8,128)}, f32[128,128]{1,0:T(8,128)}) custom-call(bf16[32,24,128]{2,1,0:T(8,128)(2,1)S(1)} %all_to_all.11.pieces_ref, f32[256,128]{1,0:T(8,128)S(1)} %copy-done, f32[256,128]{1,0:T(8,128)S(1)} %get-tuple-element.24.shifted_ref), custom_call_target="tpu_custom_call" | custom-call | tf_op jit(solution)/shard_map/factor_and_basis/pallas_call | solution.py:318
  (3 shorter events, 0.1 us)
Async XLA Ops:
  0.6 1.0 %copy-start.2 = (f32[256,128]{1,0:T(8,128)S(1)}, f32[256,128]{1,0:T(8,128)}, u32[]{:S(2)}) copy-start(f32[256,128]{1,0:T(8,128)} %prev_ref.1) | copy-start | bytes 393220
  1.6 9.5 %copy-start.1 = (bf16[1,1,16,128,128]{4,3,2,1,0:T(8,128)(2,1)S(1)}, bf16[1,1,16,128,128]{4,3,2,1,0:T(8,128)(2,1)}, u32[]{:S(2)}) copy-start(bf16[1,1,16,128,128]{4,3,2,1,0:T(8,128)(2,1)} %param.10) | copy-start | bytes 1572868
  1.6 9.4 %copy-start.3 = (f32[128,128]{1,0:T(8,128)S(1)}, f32[128,128]{1,0:T(8,128)}, u32[]{:S(2)}) copy-start(f32[128,128]{1,0:T(8,128)} %coupling_ref.3) | copy-start | bytes 196612
  11.1 0.7 %copy-start.4 = (s32[1,1,16]{2,1,0:T(1,128)S(1)}, s32[1,1,16]{2,1,0:T(1,128)}, u32[]{:S(2)}) copy-start(s32[1,1,16]{2,1,0:T(1,128)} %rows_ref.1) | copy-start | bytes 196
  11.1 0.7 %copy-start.5 = (s32[1,1,16]{2,1,0:T(1,128)S(1)}, s32[1,1,16]{2,1,0:T(1,128)}, u32[]{:S(2)}) copy-start(s32[1,1,16]{2,1,0:T(1,128)} %cols_ref.1) | copy-start | bytes 196
  13.1 5.1 %collective-permute-start.3 = (bf16[272,128]{1,0:T(8,128)(2,1)S(1)}, bf16[272,128]{1,0:T(8,128)(2,1)S(1)}, u32[]{:S(2)}, u32[]{:S(2)}) collective-permute-start(bf16[272,128]{1,0:T(8,128)(2,1)S(1)} %get-tuple-element.19), channel_id=1, source_target_pairs={{0,12},{4,8},{8,4},{12,0},{16,28},{20,24},{24,20},{28,16},{1,13},{... | collective-permute-start | bytes 208904 | tf_op jit(solution)/shard_map/ppermute | solution.py:241
  15.4 3.7 %collective-permute-start.4 = (bf16[272,128]{1,0:T(8,128)(2,1)S(1)}, bf16[272,128]{1,0:T(8,128)(2,1)S(1)}, u32[]{:S(2)}, u32[]{:S(2)}) collective-permute-start(bf16[272,128]{1,0:T(8,128)(2,1)S(1)} %get-tuple-element.20), channel_id=1, source_target_pairs={{0,8},{4,12},{8,0},{12,4},{16,24},{20,28},{24,16},{28,20},{1,9},{5... | collective-permute-start | bytes 208904 | tf_op jit(solution)/shard_map/ppermute | solution.py:241
  15.5 3.6 %collective-permute-start.5 = (bf16[272,128]{1,0:T(8,128)(2,1)S(1)}, bf16[272,128]{1,0:T(8,128)(2,1)S(1)}, u32[]{:S(2)}, u32[]{:S(2)}) collective-permute-start(bf16[272,128]{1,0:T(8,128)(2,1)S(1)} %get-tuple-element.21), channel_id=1, source_target_pairs={{0,4},{4,0},{8,12},{12,8},{16,20},{20,16},{24,28},{28,24},{1,5},{5... | collective-permute-start | bytes 208904 | tf_op jit(solution)/shard_map/ppermute | solution.py:241
  15.8 6.0 %collective-permute-start = (bf16[272,128]{1,0:T(8,128)(2,1)S(1)}, bf16[272,128]{1,0:T(8,128)(2,1)S(1)}, u32[]{:S(2)}, u32[]{:S(2)}) collective-permute-start(bf16[272,128]{1,0:T(8,128)(2,1)S(1)} %get-tuple-element.15), channel_id=1, source_target_pairs={{0,12},{4,8},{8,4},{12,0},{16,28},{20,24},{24,20},{28,16},{1,13},{... | collective-permute-start | bytes 208904 | tf_op jit(solution)/shard_map/ppermute | solution.py:241
  18.0 4.0 %collective-permute-start.1 = (bf16[272,128]{1,0:T(8,128)(2,1)S(1)}, bf16[272,128]{1,0:T(8,128)(2,1)S(1)}, u32[]{:S(2)}, u32[]{:S(2)}) collective-permute-start(bf16[272,128]{1,0:T(8,128)(2,1)S(1)} %get-tuple-element.16), channel_id=1, source_target_pairs={{0,8},{4,12},{8,0},{12,4},{16,24},{20,28},{24,16},{28,20},{1,9},{5... | collective-permute-start | bytes 208904 | tf_op jit(solution)/shard_map/ppermute | solution.py:241
  18.2 4.0 %collective-permute-start.2 = (bf16[272,128]{1,0:T(8,128)(2,1)S(1)}, bf16[272,128]{1,0:T(8,128)(2,1)S(1)}, u32[]{:S(2)}, u32[]{:S(2)}) collective-permute-start(bf16[272,128]{1,0:T(8,128)(2,1)S(1)} %get-tuple-element.17), channel_id=1, source_target_pairs={{0,4},{4,0},{8,12},{12,8},{16,20},{20,16},{24,28},{28,24},{1,5},{5... | collective-permute-start | bytes 208904 | tf_op jit(solution)/shard_map/ppermute | solution.py:241
  19.1 4.2 %copy-start = (f32[256,128]{1,0:T(8,128)S(1)}, f32[256,128]{1,0:T(8,128)}, u32[]{:S(2)}) copy-start(f32[256,128]{1,0:T(8,128)} %now_ref.3) | copy-start | bytes 393220
  19.2 4.2 %collective-permute-start.6 = (bf16[272,128]{1,0:T(8,128)(2,1)S(1)}, bf16[272,128]{1,0:T(8,128)(2,1)S(1)}, u32[]{:S(2)}, u32[]{:S(2)}) collective-permute-start(bf16[272,128]{1,0:T(8,128)(2,1)S(1)} %mirror_sum.1), channel_id=1, source_target_pairs={{0,16},{4,20},{8,24},{12,28},{16,0},{20,4},{24,8},{28,12},{1,17},{... | collective-permute-start | bytes 208904 | tf_op jit(solution)/shard_map/ppermute | solution.py:241

commit v10 on v9

--- a/solution.py
+++ b/solution.py
@@ -46,9 +46,16 @@
     return value[..., :half, :] + value[..., half:, :]
 
 
-def tiles_kernel(n_row, n_col, total_rows, me_ref, rows_ref, cols_ref, count_ref, tiles_ref, basis_ref, coupling_ref, *refs):
+def tiles_kernel(n_row, n_col, total_rows, me_ref, rows_hbm, cols_hbm, used_ref, tiles_ref, basis_ref, coupling_ref, *refs):
     half = n_row // 2
-    mirror_refs, near_refs, (far_ref, own_ref, total_ref, early_ref) = refs[: half - 1], refs[half - 1 : -4], refs[-4:]
+    refs, (far_ref, own_ref, total_ref, early_ref, rows_ref, cols_ref, sems) = refs[:-7], refs[-7:]
+    mirror_refs, near_refs = refs[: half - 1], refs[half - 1 :]
+    copies = [
+        pltpu.make_async_copy(source, target, sems.at[k])
+        for k, (source, target) in enumerate(((rows_hbm, rows_ref), (cols_hbm, cols_ref)))
+    ]
+    for copy in copies:
+        copy.start()
     slots, size, _ = tiles_ref.shape
     width = total_ref.shape[1]
     rows_dev = total_ref.shape[0] // n_row
@@ -67,13 +74,14 @@
         early_ref[...] = jnp.zeros_like(early_ref)
     early_ref[:width, :] = square - jnp.where(rows == cols, total_rows / n_row, 0.0)
     early_ref[width : 2 * width, :] = dot_nt(cross, upper_of(coupling_ref[...]))
-    used = count_ref[...]
+    for copy in copies:
+        copy.wait()
     per_slab = rows_dev // size
     for slot in range(slots):
         col = cols_ref[0, 0, slot]
         start = pl.multiple_of((2 * per_slab * (col // per_slab) + lax.rem(col, per_slab)) * size, size)
         value = jnp.dot(tiles_ref[slot], basis_ref[pl.ds(start, size), :], preferred_element_type=F32)
-        value = value * (slot < used).astype(F32)
+        value = value * used_ref[slot : slot + 1, :]
         place = pl.ds(pl.multiple_of(rows_ref[0, 0, slot] * size, size), size)
         total_ref[place, :] += value
 
@@ -250,10 +258,14 @@
     piece = -(-2 * width // (8 * devices)) * 8
     smem = pl.BlockSpec(memory_space=pltpu.SMEM)
     vmem = pl.BlockSpec(memory_space=pltpu.VMEM)
+    hbm = pl.BlockSpec(memory_space=pltpu.HBM)
     params = pltpu.CompilerParams(vmem_limit_bytes=48 * 1024 * 1024)
 
     both = jnp.concatenate([basis_now, basis_prev], axis=0).astype(BF16)
     gathered = lax.all_gather(both, "col", axis=0, tiled=True)
+    index_arrays = [pltpu.with_memory_space_constraint(x, pltpu.HBM) for x in (tile_rows, tile_cols)]
+    slots = lax.broadcasted_iota(jnp.int32, (tile_rows.shape[-1], width), 0)
+    used = (slots < tile_counts).astype(F32)
     me = jnp.stack([lax.axis_index("row"), lax.axis_index("col")])
     half = n_row // 2
     block = jax.ShapeDtypeStruct((rows_dev + 2 * piece, width), BF16)
@@ -261,18 +273,22 @@
     *blocks, far, own = pl.pallas_call(
         functools.partial(tiles_kernel, n_row, n_col, total_rows),
         out_shape=[block] * (2 * half - 2) + [sums] * 2,
-        in_specs=[smem] * 3 + [vmem] * 4,
+        in_specs=[smem] + [hbm] * 2 + [vmem] * 4,
         out_specs=[vmem] * (2 * half),
         scratch_shapes=[
             pltpu.VMEM((n_row * rows_dev, width), F32),
             pltpu.VMEM((devices * piece, width), F32),
+            pltpu.SMEM(tile_rows.shape, tile_rows.dtype),
+            pltpu.SMEM(tile_cols.shape, tile_cols.dtype),
+            pltpu.SemaphoreType.DMA((2,)),
         ],
         compiler_params=params,
         name="tile_products",
-    )(me, tile_rows, tile_cols, tile_counts, tile_block, gathered, coupling)
+    )(me, *index_arrays, used, tile_block, gathered, coupling)
     steps = distances(half)[:-1]
     mirrors = exchange(blocks[: half - 1], "row", steps)
-    near = exchange(blocks[half - 1 :], "row", steps)
+    near = blocks[half - 1 :]
+    nearest = exchange(near[-1:], "row", steps[-1:])
     mirror = pl.pallas_call(
         functools.partial(mirror_kernel, rows_dev),
         out_shape=block,
@@ -281,7 +297,9 @@
         compiler_params=params,
         name="mirror_sum",
     )(far, *mirrors)
+    mirror, *near = lax.optimization_barrier((mirror, *near[:-1]))
     across = exchange([mirror], "row", [half])
+    near = exchange(near, "row", steps[:-1])
 
     shift = pl.pallas_call(
         shift_kernel,
@@ -303,7 +321,7 @@
         out_specs=(vmem, vmem, vmem),
         compiler_params=params,
         name="local_grams",
-    )(basis_now, shift, own, *near, *across)
+    )(basis_now, shift, own, *nearest, *across, *near)
     everyone = ("row", "col")
     pieces = lax.all_to_all(grams.reshape(devices, piece, width), everyone, split_axis=0, concat_axis=0, tiled=True)
     copies = pl.pallas_call(

time: 56 us -> 56.8 us (1.014)
  blocking collectives: 36 us -> 32.9 us
  waiting for transfers between devices: 1.8 us -> 4.82 us
  starting transfers between devices: 8.17 us -> 9.07 us
  local copies, waits for them, and re-layouts: 0.69 us -> 0.09 us
    all_to_all x1, blocking collectives: 16.2 us -> 13.2 us  [on_device(): lax.all_to_all(grams.reshape(devices, piece, width), everyone, split_axis...]
    ppermute x7, waiting for transfers between devices: 1.8 us -> 4.82 us  [exchange(): lax.ppermute(block, axis, [(i, i ^ step) for i in range(n)])]
    ppermute x7, starting transfers between devices: 8.17 us -> 9.07 us  [exchange(): lax.ppermute(block, axis, [(i, i ^ step) for i in range(n)])]
    unnamed x12 -> x8, local copies, waits for them, and re-layouts: 0.69 us -> 0.02 us
where the time goes in v10:
time: 56.8 us; the launch traced here: 56.6 us
  blocking collectives  32.9 us (58%)
  starting transfers between devices  9.07 us (16%)
  Pallas kernels  7.24 us (13%)
  waiting for transfers between devices  4.82 us (8%)
  between operations  1.4 us (2%)
  other arithmetic  1.05 us (2%)
    all_to_all x1, blocking collectives, on_device(): lax.all_to_all(grams.reshape(devices, piece, width), everyone, split_axis...  13.2 us
    all_to_all x1, blocking collectives, on_device(): lax.all_to_all(copies, everyone, split_axis=0, concat_axis=0, tiled=True)  11 us
    ppermute x7, starting transfers between devices, exchange(): lax.ppermute(block, axis, [(i, i ^ step) for i in range(n)])  9.07 us
    all_gather x1, blocking collectives, on_device(): gathered = lax.all_gather(both, 'col', axis=0, tiled=True)  8.67 us
    ppermute x7, waiting for transfers between devices, exchange(): lax.ppermute(block, axis, [(i, i ^ step) for i in range(n)])  4.82 us
    pallas_call x1, Pallas kernels, on_device(): pl.pallas_call(functools.partial(final_kernel, total_rows), out_shape=(ja...  4.65 us
    pallas_call x1, Pallas kernels, on_device(): pl.pallas_call(functools.partial(tiles_kernel, n_row, n_col, total_rows),...  1.79 us
  transfers between devices with their start and end apart: 7, of which 4 were waited for; matrix products, arithmetic and copies ran while one was open for 0% of the time, Pallas kernels for 1%

profile of v10, /device:TPU:1, one launch (start us, length us, event | category | flops | bytes accessed | tf_op | source)
XLA Modules:
  0.0 56.6 jit_solution(9076259694876596328)
XLA Ops:
  0.6 0.0 copy-start.2
  0.6 0.9 %convert.6 = bf16[256,128]{1,0:T(8,128)(2,1)S(1)} convert(f32[256,128]{1,0:T(8,128)} %now_ref.3) | non-fusion elementwise | flops 32768 | bytes 196608 | tf_op jit(solution)/shard_map/convert
  1.6 0.0 copy-done.2
  1.6 0.0 copy-start.1
  1.6 0.0 copy-start.3
  1.7 8.7 %all_gather.3.basis_ref = bf16[2048,128]{1,0:T(8,128)(2,1)S(1)} all-gather(bf16[512,128]{1,0:T(8,128)(2,1)S(1)} %pad_maximum_fusion), channel_id=1, replica_groups=mesh['row'=8,'col'=4] {'col'}, dimensions={0}, use_global_device_ids=true | all-gather | bytes 655360 | tf_op jit(solution)/shard_map/all_gather | solution.py:265
  11.0 0.1 pad_add_fusion.me_ref
  11.1 0.1 iota.7.used_ref
  11.1 0.0 copy-done.1
  11.1 0.0 copy-done.3
  11.2 1.8 %tile_products.1 = (bf16[272,128]{1,0:T(8,128)(2,1)S(1)}, bf16[272,128]{1,0:T(8,128)(2,1)S(1)}, bf16[272,128]{1,0:T(8,128)(2,1)S(1)}, bf16[272,128]{1,0:T(8,128)...) custom-call(s32[2]{0:T(128)S(1)} %pad_add_fusion.me_ref, ...), custom_call_target="tpu_custom_call" | custom-call | tf_op jit(solution)/shard_map/tile_products/pallas_call | solution.py:273
  13.0 2.3 %collective-permute-start.1 = (bf16[272,128]{1,0:T(8,128)(2,1)S(1)}, bf16[272,128]{1,0:T(8,128)(2,1)S(1)}, u32[]{:S(2)}, u32[]{:S(2)}) collective-permute-start(bf16[272,128]{1,0:T(8,128)(2,1)S(1)} %get-tuple-element.20), channel_id=1, source_target_pairs={{0,12},{4,8},{8,4},{12,0},{16,28},{20,24},{24,20},{28,16},{1,13},{... | collective-permute-start | bytes 208904 | tf_op jit(solution)/shard_map/ppermute | solution.py:249
  15.2 0.2 collective-permute-start.2
  15.4 0.3 collective-permute-start.3
  15.7 1.2 %collective-permute-start = (bf16[272,128]{1,0:T(8,128)(2,1)S(1)}, bf16[272,128]{1,0:T(8,128)(2,1)S(1)}, u32[]{:S(2)}, u32[]{:S(2)}) collective-permute-start(bf16[272,128]{1,0:T(8,128)(2,1)S(1)} %get-tuple-element.18), channel_id=1, source_target_pairs={{0,4},{4,0},{8,12},{12,8},{16,20},{20,16},{24,28},{28,24},{1,5},{5... | collective-permute-start | bytes 208904 | tf_op jit(solution)/shard_map/ppermute | solution.py:249
  16.9 0.7 %collective-permute-done.1.refs_0_ = bf16[272,128]{1,0:T(8,128)(2,1)S(1)} collective-permute-done((bf16[272,128]{1,0:T(8,128)(2,1)S(1)}, bf16[272,128]{1,0:T(8,128)(2,1)S(1)}, u32[]{:S(2)}, u32[]{:S(2)}) %collective-permute-start.1) | collective-permute-done | bytes 69664 | tf_op jit(solution)/shard_map/ppermute | solution.py:249
  17.5 1.4 %collective-permute-done.2.refs_1_ = bf16[272,128]{1,0:T(8,128)(2,1)S(1)} collective-permute-done((bf16[272,128]{1,0:T(8,128)(2,1)S(1)}, bf16[272,128]{1,0:T(8,128)(2,1)S(1)}, u32[]{:S(2)}, u32[]{:S(2)}) %collective-permute-start.2) | collective-permute-done | bytes 69664 | tf_op jit(solution)/shard_map/ppermute | solution.py:249
  18.9 0.0 collective-permute-done.3.refs_2_
  19.0 0.0 copy-start
  19.0 2.4 %collective-permute-start.4 = (bf16[272,128]{1,0:T(8,128)(2,1)S(1)}, bf16[272,128]{1,0:T(8,128)(2,1)S(1)}, u32[]{:S(2)}, u32[]{:S(2)}) collective-permute-start(bf16[272,128]{1,0:T(8,128)(2,1)S(1)} %mirror_sum.1), channel_id=1, source_target_pairs={{0,16},{4,20},{8,24},{12,28},{16,0},{20,4},{24,8},{28,12},{1,17},{... | collective-permute-start | bytes 208904 | tf_op jit(solution)/shard_map/ppermute | solution.py:249
  21.4 2.4 %collective-permute-start.5 = (bf16[272,128]{1,0:T(8,128)(2,1)S(1)}, bf16[272,128]{1,0:T(8,128)(2,1)S(1)}, u32[]{:S(2)}, u32[]{:S(2)}) collective-permute-start(bf16[272,128]{1,0:T(8,128)(2,1)S(1)} %get-tuple-element.26), channel_id=1, source_target_pairs={{0,12},{4,8},{8,4},{12,0},{16,28},{20,24},{24,20},{28,16},{1,13},{... | collective-permute-start | bytes 208904 | tf_op jit(solution)/shard_map/ppermute | solution.py:249
  23.8 0.4 collective-permute-start.6
  24.2 0.3 shift_by_previous.1.shift_ref
  24.5 0.0 collective-permute-done.refs_0_
  24.5 0.0 collective-permute-done.4.refs_1_
  24.5 1.8 %collective-permute-done.5.refs_2_ = bf16[272,128]{1,0:T(8,128)(2,1)S(1)} collective-permute-done((bf16[272,128]{1,0:T(8,128)(2,1)S(1)}, bf16[272,128]{1,0:T(8,128)(2,1)S(1)}, u32[]{:S(2)}, u32[]{:S(2)}) %collective-permute-start.5) | collective-permute-done | bytes 69664 | tf_op jit(solution)/shard_map/ppermute | solution.py:249
  26.3 0.9 %collective-permute-done.6.refs_3_ = bf16[272,128]{1,0:T(8,128)(2,1)S(1)} collective-permute-done((bf16[272,128]{1,0:T(8,128)(2,1)S(1)}, bf16[272,128]{1,0:T(8,128)(2,1)S(1)}, u32[]{:S(2)}, u32[]{:S(2)}) %collective-permute-start.6) | collective-permute-done | bytes 69664 | tf_op jit(solution)/shard_map/ppermute | solution.py:249
  27.2 0.0 copy-done
  27.2 0.4 local_grams.1
  27.6 13.2 %all_to_all.10.parts_ref = f32[32,8,128]{2,1,0:T(8,128)S(1)} all-to-all(f32[32,8,128]{2,1,0:T(8,128)S(1)} %bitcast.7), channel_id=1, replica_groups=mesh['row'=8,'col'=4] {'row','col'}, dimensions={0} | all-to-all | bytes 262144 | tf_op jit(solution)/shard_map/all_to_all | solution.py:326
  40.9 0.1 sum_and_spread.1
  40.9 11.0 %all_to_all.11.pieces_ref = bf16[32,24,128]{2,1,0:T(8,128)(2,1)S(1)} all-to-all(bf16[32,24,128]{2,1,0:T(8,128)(2,1)S(1)} %sum_and_spread.1), channel_id=1, replica_groups=mesh['row'=8,'col'=4] {'row','col'}, dimensions={0} | all-to-all | bytes 393216 | tf_op jit(solution)/shard_map/all_to_all | solution.py:335
  52.0 4.7 %factor_and_basis.1 = (f32[256,128]{1,0:T(8,128)}, f32[128,128]{1,0:T(8,128)}, f32[128,128]{1,0:T(8,128)}) custom-call(bf16[32,24,128]{2,1,0:T(8,128)(2,1)S(1)} %all_to_all.11.pieces_ref, f32[256,128]{1,0:T(8,128)S(1)} %copy-done, f32[256,128]{1,0:T(8,128)S(1)} %get-tuple-element.30.shifted_ref), custom_call_target="tpu_custom_call" | custom-call | tf_op jit(solution)/shard_map/factor_and_basis/pallas_call | solution.py:336
  (4 shorter events, 0.1 us)
Async XLA Ops:
  0.6 1.0 %copy-start.2 = (f32[256,128]{1,0:T(8,128)S(1)}, f32[256,128]{1,0:T(8,128)}, u32[]{:S(2)}) copy-start(f32[256,128]{1,0:T(8,128)} %prev_ref.1) | copy-start | bytes 393220
  1.6 9.5 %copy-start.1 = (bf16[1,1,16,128,128]{4,3,2,1,0:T(8,128)(2,1)S(1)}, bf16[1,1,16,128,128]{4,3,2,1,0:T(8,128)(2,1)}, u32[]{:S(2)}) copy-start(bf16[1,1,16,128,128]{4,3,2,1,0:T(8,128)(2,1)} %param.10) | copy-start | bytes 1572868
  1.6 9.5 %copy-start.3 = (f32[128,128]{1,0:T(8,128)S(1)}, f32[128,128]{1,0:T(8,128)}, u32[]{:S(2)}) copy-start(f32[128,128]{1,0:T(8,128)} %coupling_ref.3) | copy-start | bytes 196612
  13.0 4.6 %collective-permute-start.1 = (bf16[272,128]{1,0:T(8,128)(2,1)S(1)}, bf16[272,128]{1,0:T(8,128)(2,1)S(1)}, u32[]{:S(2)}, u32[]{:S(2)}) collective-permute-start(bf16[272,128]{1,0:T(8,128)(2,1)S(1)} %get-tuple-element.20), channel_id=1, source_target_pairs={{0,12},{4,8},{8,4},{12,0},{16,28},{20,24},{24,20},{28,16},{1,13},{... | collective-permute-start | bytes 208904 | tf_op jit(solution)/shard_map/ppermute | solution.py:249
  15.2 3.7 %collective-permute-start.2 = (bf16[272,128]{1,0:T(8,128)(2,1)S(1)}, bf16[272,128]{1,0:T(8,128)(2,1)S(1)}, u32[]{:S(2)}, u32[]{:S(2)}) collective-permute-start(bf16[272,128]{1,0:T(8,128)(2,1)S(1)} %get-tuple-element.21), channel_id=1, source_target_pairs={{0,8},{4,12},{8,0},{12,4},{16,24},{20,28},{24,16},{28,20},{1,9},{5... | collective-permute-start | bytes 208904 | tf_op jit(solution)/shard_map/ppermute | solution.py:249
  15.4 3.6 %collective-permute-start.3 = (bf16[272,128]{1,0:T(8,128)(2,1)S(1)}, bf16[272,128]{1,0:T(8,128)(2,1)S(1)}, u32[]{:S(2)}, u32[]{:S(2)}) collective-permute-start(bf16[272,128]{1,0:T(8,128)(2,1)S(1)} %get-tuple-element.22), channel_id=1, source_target_pairs={{0,4},{4,0},{8,12},{12,8},{16,20},{20,16},{24,28},{28,24},{1,5},{5... | collective-permute-start | bytes 208904 | tf_op jit(solution)/shard_map/ppermute | solution.py:249
  15.7 8.8 %collective-permute-start = (bf16[272,128]{1,0:T(8,128)(2,1)S(1)}, bf16[272,128]{1,0:T(8,128)(2,1)S(1)}, u32[]{:S(2)}, u32[]{:S(2)}) collective-permute-start(bf16[272,128]{1,0:T(8,128)(2,1)S(1)} %get-tuple-element.18), channel_id=1, source_target_pairs={{0,4},{4,0},{8,12},{12,8},{16,20},{20,16},{24,28},{28,24},{1,5},{5... | collective-permute-start | bytes 208904 | tf_op jit(solution)/shard_map/ppermute | solution.py:249
  19.0 8.2 %copy-start = (f32[256,128]{1,0:T(8,128)S(1)}, f32[256,128]{1,0:T(8,128)}, u32[]{:S(2)}) copy-start(f32[256,128]{1,0:T(8,128)} %now_ref.3) | copy-start | bytes 393220
  19.0 5.5 %collective-permute-start.4 = (bf16[272,128]{1,0:T(8,128)(2,1)S(1)}, bf16[272,128]{1,0:T(8,128)(2,1)S(1)}, u32[]{:S(2)}, u32[]{:S(2)}) collective-permute-start(bf16[272,128]{1,0:T(8,128)(2,1)S(1)} %mirror_sum.1), channel_id=1, source_target_pairs={{0,16},{4,20},{8,24},{12,28},{16,0},{20,4},{24,8},{28,12},{1,17},{... | collective-permute-start | bytes 208904 | tf_op jit(solution)/shard_map/ppermute | solution.py:249
  21.4 4.9 %collective-permute-start.5 = (bf16[272,128]{1,0:T(8,128)(2,1)S(1)}, bf16[272,128]{1,0:T(8,128)(2,1)S(1)}, u32[]{:S(2)}, u32[]{:S(2)}) collective-permute-start(bf16[272,128]{1,0:T(8,128)(2,1)S(1)} %get-tuple-element.26), channel_id=1, source_target_pairs={{0,12},{4,8},{8,4},{12,0},{16,28},{20,24},{24,20},{28,16},{1,13},{... | collective-permute-start | bytes 208904 | tf_op jit(solution)/shard_map/ppermute | solution.py:249
  23.8 3.4 %collective-permute-start.6 = (bf16[272,128]{1,0:T(8,128)(2,1)S(1)}, bf16[272,128]{1,0:T(8,128)(2,1)S(1)}, u32[]{:S(2)}, u32[]{:S(2)}) collective-permute-start(bf16[272,128]{1,0:T(8,128)(2,1)S(1)} %get-tuple-element.27), channel_id=1, source_target_pairs={{0,8},{4,12},{8,0},{12,4},{16,24},{20,28},{24,16},{28,20},{1,9},{5... | collective-permute-start | bytes 208904 | tf_op jit(solution)/shard_map/ppermute | solution.py:249

commit v11 on v9

--- a/solution.py
+++ b/solution.py
@@ -7,21 +7,23 @@
 from jax.experimental.pallas import tpu as pltpu
 from jax.sharding import PartitionSpec as P
 
-HIGHEST = lax.Precision.HIGHEST
 F32 = jnp.float32
 BF16 = jnp.bfloat16
-
-
-def dot(a, b):
-    return jnp.dot(a, b, precision=HIGHEST, preferred_element_type=F32)
-
-
-def dot_tn(a, b, precision=HIGHEST):
-    return lax.dot_general(a, b, (((0,), (0,)), ((), ())), precision=precision, preferred_element_type=F32)
-
-
-def dot_nt(a, b):
-    return lax.dot_general(a, b, (((1,), (1,)), ((), ())), precision=HIGHEST, preferred_element_type=F32)
+NN, TN, NT = [(((x,), (y,)), ((), ())) for x, y in ((1, 0), (0, 0), (1, 1))]
+
+
+def split(x):
+    high = x.astype(BF16)
+    return high, (x - high.astype(F32)).astype(BF16)
+
+
+def dot3(a, b, dims=NN):
+    (a_high, a_low), (b_high, b_low) = split(a), split(b)
+
+    def one(x, y):
+        return lax.dot_general(x, y, dims, preferred_element_type=F32)
+
+    return one(a_high, b_low) + one(a_low, b_high) + one(a_high, b_high)
 
 
 def upper_of(x):
@@ -59,14 +61,14 @@
     for slab in range(n_col):
         now = basis_ref[2 * slab * rows_dev : (2 * slab + 1) * rows_dev, :]
         prev = basis_ref[(2 * slab + 1) * rows_dev : (2 * slab + 2) * rows_dev, :]
-        grams += dot_tn(now, jnp.concatenate([now, prev], axis=1), None)
+        grams += lax.dot_general(now, jnp.concatenate([now, prev], axis=1), TN, preferred_element_type=F32)
     square, cross = grams[:, :width], grams[:, width:]
     rows = lax.broadcasted_iota(jnp.int32, square.shape, 0)
     cols = lax.broadcasted_iota(jnp.int32, square.shape, 1)
     if early_ref.shape[0] > 2 * width:
         early_ref[...] = jnp.zeros_like(early_ref)
     early_ref[:width, :] = square - jnp.where(rows == cols, total_rows / n_row, 0.0)
-    early_ref[width : 2 * width, :] = dot_nt(cross, upper_of(coupling_ref[...]))
+    early_ref[width : 2 * width, :] = dot3(cross, upper_of(coupling_ref[...]), NT)
     used = count_ref[...]
     per_slab = rows_dev // size
     for slot in range(slots):
@@ -108,7 +110,7 @@
 
 
 def shift_kernel(prev_ref, coupling_ref, shift_ref):
-    shift_ref[...] = dot_nt(prev_ref[...], upper_of(coupling_ref[...]))
+    shift_ref[...] = dot3(prev_ref[...], upper_of(coupling_ref[...]), NT)
 
 
 def grams_kernel(now_ref, shift_ref, own_ref, *refs):
@@ -119,8 +121,8 @@
     shifted_ref[...] = shifted
     if grams_ref.shape[0] > 2 * width:
         grams_ref[...] = jnp.zeros_like(grams_ref)
-    grams_ref[:width, :] = dot_tn(now_ref[...], product)
-    grams_ref[width : 2 * width, :] = dot_tn(shifted, shifted)
+    grams_ref[:width, :] = dot3(now_ref[...], product, TN)
+    grams_ref[width : 2 * width, :] = dot3(shifted, shifted, TN)
 
 
 def spread_kernel(parts_ref, early_ref, out_ref):
@@ -130,20 +132,6 @@
     value = jnp.concatenate([high_and_low(total), early_ref[...].astype(BF16)], axis=0)
     for part in range(out_ref.shape[0]):
         out_ref[part] = value
-
-
-def split(x):
-    high = x.astype(BF16)
-    return high, (x - high.astype(F32)).astype(BF16)
-
-
-def dot3(a, b, dims=((1,), (0,))):
-    (a_high, a_low), (b_high, b_low) = split(a), split(b)
-
-    def one(x, y):
-        return lax.dot_general(x, y, (dims, ((), ())), preferred_element_type=F32)
-
-    return one(a_high, b_low) + one(a_low, b_high) + one(a_high, b_high)
 
 
 def eliminate(gram):
@@ -169,25 +157,23 @@
             kept = panel
             for j in range(0, block, 2):
                 here, there = subs == j, subs == j + 1
+                both = here | there
                 lane, next_lane = lanes == first + j, lanes == first + j + 1
                 left, right = columns[j], columns[j + 1]
                 a, b, c = row(left, j), row(right, j), row(right, j + 1)
                 scale = 1.0 / (a * c - b * b)
+                by_top = jnp.where(here, -c, jnp.where(there, b, left * c - right * b))
+                by_bottom = jnp.where(here, b, jnp.where(there, -a, right * a - left * b))
                 top, bottom = row(panel, j), row(panel, j + 1)
                 ratio = b / a
                 kept = jnp.where(here, top, jnp.where(there, bottom - ratio * jnp.where(lane, 1.0, top), kept))
                 kept = jnp.where(there & lane, -ratio, kept)
                 top = jnp.where(lane, 1.0, jnp.where(next_lane, 0.0, top))
                 bottom = jnp.where(lane, 0.0, jnp.where(next_lane, 1.0, bottom))
-                unit_top = (c * top - b * bottom) * scale
-                unit_bottom = (a * bottom - b * top) * scale
-                others = jnp.where(lane | next_lane, 0.0, panel) - (left * unit_top + right * unit_bottom)
-                panel = jnp.where(here, unit_top, jnp.where(there, unit_bottom, others))
+                panel = jnp.where(both | lane | next_lane, 0.0, panel) - (by_top * top + by_bottom * bottom) * scale
                 for m in range(j + 2, block):
                     up, down = row(columns[m], j), row(columns[m], j + 1)
-                    up, down = (c * up - b * down) * scale, (a * down - b * up) * scale
-                    others = columns[m] - (left * up + right * down)
-                    columns[m] = jnp.where(here, up, jnp.where(there, down, others))
+                    columns[m] = jnp.where(both, 0.0, columns[m]) - (by_top * up + by_bottom * down) * scale
             finished.append(kept)
             group[at] = panel
             rows = [row(panel, m) for m in range(block)]
@@ -222,7 +208,7 @@
     projection_ref[...] = projection
     scaled = now_product * (1.0 / total_rows)
     half = shift - 0.5 * now_product + 0.5 * dot3(now_square, scaled)
-    mixed = dot3(scaled, half, ((0,), (0,)))
+    mixed = dot3(scaled, half, TN)
     gram = square + mixed + mixed.T
     reduced = eliminate(gram * (1.0 / total_rows))
     rows = lax.broadcasted_iota(jnp.int32, reduced.shape, 0)
@@ -232,7 +218,7 @@
     rfactor_ref[...] = jnp.where(rows <= cols, reduced, 0.0) * root
     inverse = jnp.where(rows > cols, reduced, jnp.where(rows == cols, 1.0, 0.0)) * root
     residual = shifted_ref[...] - dot3(now_ref[...], scaled)
-    basis_ref[...] = dot3(residual, inverse, ((1,), (1,)))
+    basis_ref[...] = dot3(residual, inverse, NT)
 
 
 def exchange(blocks, axis, steps):

time: 56 us -> 55.5 us (level)
  Pallas kernels: 6.76 us -> 6.16 us
  transfers between devices with their start and end apart: 7 -> 7, of which waited for: 4 -> 4; matrix products, arithmetic and copies ran while one was open for 0% -> 0% of each run, Pallas kernels for 1% -> 0%
where the time goes in v11:
time: 55.5 us; the launch traced here: 55.3 us
  blocking collectives  36 us (65%)
  starting transfers between devices  8.18 us (15%)
  Pallas kernels  6.16 us (11%)
  waiting for transfers between devices  1.86 us (3%)
  between operations  1.39 us (3%)
  other arithmetic  1.05 us (2%)
  local copies, waits for them, and re-layouts  0.69 us (1%)
    all_to_all x1, blocking collectives, on_device(): lax.all_to_all(grams.reshape(devices, piece, width), everyone, split_axis...  16.2 us
    all_to_all x1, blocking collectives, on_device(): lax.all_to_all(copies, everyone, split_axis=0, concat_axis=0, tiled=True)  11 us
    all_gather x1, blocking collectives, on_device(): gathered = lax.all_gather(both, 'col', axis=0, tiled=True)  8.67 us
    ppermute x7, starting transfers between devices, exchange(): lax.ppermute(block, axis, [(i, i ^ step) for i in range(n)])  8.18 us
    pallas_call x1, Pallas kernels, on_device(): pl.pallas_call(functools.partial(final_kernel, total_rows), out_shape=(ja...  4.26 us
    ppermute x7, waiting for transfers between devices, exchange(): lax.ppermute(block, axis, [(i, i ^ step) for i in range(n)])  1.86 us
    pallas_call x1, Pallas kernels, on_device(): pl.pallas_call(functools.partial(tiles_kernel, n_row, n_col, total_rows),...  1.27 us
  transfers between devices with their start and end apart: 7, of which 4 were waited for; matrix products, arithmetic and copies ran while one was open for 0% of the time, Pallas kernels for 0%

profile of v11, /device:TPU:1, one launch (start us, length us, event | category | flops | bytes accessed | tf_op | source)
XLA Modules:
  0.0 55.3 jit_solution(15356074616568895871)
XLA Ops:
  0.6 0.0 copy-start.2
  0.6 0.9 %convert.6 = bf16[256,128]{1,0:T(8,128)(2,1)S(1)} convert(f32[256,128]{1,0:T(8,128)} %now_ref.3) | non-fusion elementwise | flops 32768 | bytes 196608 | tf_op jit(solution)/shard_map/convert
  1.6 0.0 copy-done.2
  1.6 0.0 copy-start.1
  1.6 0.0 copy-start.3
  1.7 8.7 %all_gather.3.basis_ref = bf16[2048,128]{1,0:T(8,128)(2,1)S(1)} all-gather(bf16[512,128]{1,0:T(8,128)(2,1)S(1)} %pad_maximum_fusion), channel_id=1, replica_groups=mesh['row'=8,'col'=4] {'col'}, dimensions={0}, use_global_device_ids=true | all-gather | bytes 655360 | tf_op jit(solution)/shard_map/all_gather | solution.py:242
  11.0 0.1 pad_add_fusion.me_ref
  11.1 0.0 copy-start.4
  11.1 0.0 copy-start.5
  11.1 0.0 copy-done.1
  11.1 0.0 copy-done.3
  11.1 0.6 %copy-done.4 = s32[1,1,16]{2,1,0:T(1,128)S(1)} copy-done((s32[1,1,16]{2,1,0:T(1,128)S(1)}, s32[1,1,16]{2,1,0:T(1,128)}, u32[]{:S(2)}) %copy-start.4) | copy-done | bytes 88
  11.7 0.0 copy-done.5
  11.7 1.3 %tile_products.1 = (bf16[272,128]{1,0:T(8,128)(2,1)S(1)}, bf16[272,128]{1,0:T(8,128)(2,1)S(1)}, bf16[272,128]{1,0:T(8,128)(2,1)S(1)}, bf16[272,128]{1,0:T(8,128)...) custom-call(s32[2]{0:T(128)S(1)} %pad_add_fusion.me_ref, ...), custom_call_target="tpu_custom_call" | custom-call | tf_op jit(solution)/shard_map/tile_products/pallas_call | solution.py:247
  13.0 2.3 %collective-permute-start.3 = (bf16[272,128]{1,0:T(8,128)(2,1)S(1)}, bf16[272,128]{1,0:T(8,128)(2,1)S(1)}, u32[]{:S(2)}, u32[]{:S(2)}) collective-permute-start(bf16[272,128]{1,0:T(8,128)(2,1)S(1)} %get-tuple-element.19), channel_id=1, source_target_pairs={{0,12},{4,8},{8,4},{12,0},{16,28},{20,24},{24,20},{28,16},{1,13},{... | collective-permute-start | bytes 208904 | tf_op jit(solution)/shard_map/ppermute | solution.py:227
  15.3 0.2 collective-permute-start.4
  15.5 0.3 collective-permute-start.5
  15.7 2.2 %collective-permute-start = (bf16[272,128]{1,0:T(8,128)(2,1)S(1)}, bf16[272,128]{1,0:T(8,128)(2,1)S(1)}, u32[]{:S(2)}, u32[]{:S(2)}) collective-permute-start(bf16[272,128]{1,0:T(8,128)(2,1)S(1)} %get-tuple-element.15), channel_id=1, source_target_pairs={{0,12},{4,8},{8,4},{12,0},{16,28},{20,24},{24,20},{28,16},{1,13},{... | collective-permute-start | bytes 208904 | tf_op jit(solution)/shard_map/ppermute | solution.py:227
  18.0 0.2 collective-permute-start.1
  18.1 0.0 collective-permute-done.3.refs_0_
  18.1 0.7 %collective-permute-start.2 = (bf16[272,128]{1,0:T(8,128)(2,1)S(1)}, bf16[272,128]{1,0:T(8,128)(2,1)S(1)}, u32[]{:S(2)}, u32[]{:S(2)}) collective-permute-start(bf16[272,128]{1,0:T(8,128)(2,1)S(1)} %get-tuple-element.17), channel_id=1, source_target_pairs={{0,4},{4,0},{8,12},{12,8},{16,20},{20,16},{24,28},{28,24},{1,5},{5... | collective-permute-start | bytes 208904 | tf_op jit(solution)/shard_map/ppermute | solution.py:227
  18.8 0.2 collective-permute-done.4.refs_1_
  19.0 0.0 collective-permute-done.5.refs_2_
  19.1 0.0 copy-start
  19.1 2.4 %collective-permute-start.6 = (bf16[272,128]{1,0:T(8,128)(2,1)S(1)}, bf16[272,128]{1,0:T(8,128)(2,1)S(1)}, u32[]{:S(2)}, u32[]{:S(2)}) collective-permute-start(bf16[272,128]{1,0:T(8,128)(2,1)S(1)} %mirror_sum.1), channel_id=1, source_target_pairs={{0,16},{4,20},{8,24},{12,28},{16,0},{20,4},{24,8},{28,12},{1,17},{... | collective-permute-start | bytes 208904 | tf_op jit(solution)/shard_map/ppermute | solution.py:227
  21.5 0.2 shift_by_previous.1.shift_ref
  21.7 0.0 collective-permute-done.refs_0_
  21.7 0.3 collective-permute-done.1.refs_1_
  22.0 0.1 collective-permute-done.2.refs_2_
  22.1 1.2 %collective-permute-done.6.refs_3_ = bf16[272,128]{1,0:T(8,128)(2,1)S(1)} collective-permute-done((bf16[272,128]{1,0:T(8,128)(2,1)S(1)}, bf16[272,128]{1,0:T(8,128)(2,1)S(1)}, u32[]{:S(2)}, u32[]{:S(2)}) %collective-permute-start.6) | collective-permute-done | bytes 69664 | tf_op jit(solution)/shard_map/ppermute | solution.py:227
  23.3 0.0 copy-done
  23.3 0.3 local_grams.1
  23.7 16.2 %all_to_all.10.parts_ref = f32[32,8,128]{2,1,0:T(8,128)S(1)} all-to-all(f32[32,8,128]{2,1,0:T(8,128)S(1)} %bitcast.5), channel_id=1, replica_groups=mesh['row'=8,'col'=4] {'row','col'}, dimensions={0} | all-to-all | bytes 262144 | tf_op jit(solution)/shard_map/all_to_all | solution.py:294
  39.9 0.1 sum_and_spread.1
  40.0 11.0 %all_to_all.11.pieces_ref = bf16[32,24,128]{2,1,0:T(8,128)(2,1)S(1)} all-to-all(bf16[32,24,128]{2,1,0:T(8,128)(2,1)S(1)} %sum_and_spread.1), channel_id=1, replica_groups=mesh['row'=8,'col'=4] {'row','col'}, dimensions={0} | all-to-all | bytes 393216 | tf_op jit(solution)/shard_map/all_to_all | solution.py:303
  51.0 4.3 %factor_and_basis.1 = (f32[256,128]{1,0:T(8,128)}, f32[128,128]{1,0:T(8,128)}, f32[128,128]{1,0:T(8,128)}) custom-call(bf16[32,24,128]{2,1,0:T(8,128)(2,1)S(1)} %all_to_all.11.pieces_ref, f32[256,128]{1,0:T(8,128)S(1)} %copy-done, f32[256,128]{1,0:T(8,128)S(1)} %get-tuple-element.24.shifted_ref), custom_call_target="tpu_custom_call" | custom-call | tf_op jit(solution)/shard_map/factor_and_basis/pallas_call | solution.py:304
  (3 shorter events, 0.1 us)
Async XLA Ops:
  0.6 1.0 %copy-start.2 = (f32[256,128]{1,0:T(8,128)S(1)}, f32[256,128]{1,0:T(8,128)}, u32[]{:S(2)}) copy-start(f32[256,128]{1,0:T(8,128)} %prev_ref.1) | copy-start | bytes 393220
  1.6 9.5 %copy-start.1 = (bf16[1,1,16,128,128]{4,3,2,1,0:T(8,128)(2,1)S(1)}, bf16[1,1,16,128,128]{4,3,2,1,0:T(8,128)(2,1)}, u32[]{:S(2)}) copy-start(bf16[1,1,16,128,128]{4,3,2,1,0:T(8,128)(2,1)} %param.10) | copy-start | bytes 1572868
  1.6 9.4 %copy-start.3 = (f32[128,128]{1,0:T(8,128)S(1)}, f32[128,128]{1,0:T(8,128)}, u32[]{:S(2)}) copy-start(f32[128,128]{1,0:T(8,128)} %coupling_ref.3) | copy-start | bytes 196612
  11.1 0.7 %copy-start.4 = (s32[1,1,16]{2,1,0:T(1,128)S(1)}, s32[1,1,16]{2,1,0:T(1,128)}, u32[]{:S(2)}) copy-start(s32[1,1,16]{2,1,0:T(1,128)} %rows_ref.1) | copy-start | bytes 196
  11.1 0.7 %copy-start.5 = (s32[1,1,16]{2,1,0:T(1,128)S(1)}, s32[1,1,16]{2,1,0:T(1,128)}, u32[]{:S(2)}) copy-start(s32[1,1,16]{2,1,0:T(1,128)} %cols_ref.1) | copy-start | bytes 196
  13.0 5.1 %collective-permute-start.3 = (bf16[272,128]{1,0:T(8,128)(2,1)S(1)}, bf16[272,128]{1,0:T(8,128)(2,1)S(1)}, u32[]{:S(2)}, u32[]{:S(2)}) collective-permute-start(bf16[272,128]{1,0:T(8,128)(2,1)S(1)} %get-tuple-element.19), channel_id=1, source_target_pairs={{0,12},{4,8},{8,4},{12,0},{16,28},{20,24},{24,20},{28,16},{1,13},{... | collective-permute-start | bytes 208904 | tf_op jit(solution)/shard_map/ppermute | solution.py:227
  15.3 3.7 %collective-permute-start.4 = (bf16[272,128]{1,0:T(8,128)(2,1)S(1)}, bf16[272,128]{1,0:T(8,128)(2,1)S(1)}, u32[]{:S(2)}, u32[]{:S(2)}) collective-permute-start(bf16[272,128]{1,0:T(8,128)(2,1)S(1)} %get-tuple-element.20), channel_id=1, source_target_pairs={{0,8},{4,12},{8,0},{12,4},{16,24},{20,28},{24,16},{28,20},{1,9},{5... | collective-permute-start | bytes 208904 | tf_op jit(solution)/shard_map/ppermute | solution.py:227
  15.5 3.6 %collective-permute-start.5 = (bf16[272,128]{1,0:T(8,128)(2,1)S(1)}, bf16[272,128]{1,0:T(8,128)(2,1)S(1)}, u32[]{:S(2)}, u32[]{:S(2)}) collective-permute-start(bf16[272,128]{1,0:T(8,128)(2,1)S(1)} %get-tuple-element.21), channel_id=1, source_target_pairs={{0,4},{4,0},{8,12},{12,8},{16,20},{20,16},{24,28},{28,24},{1,5},{5... | collective-permute-start | bytes 208904 | tf_op jit(solution)/shard_map/ppermute | solution.py:227
  15.7 6.0 %collective-permute-start = (bf16[272,128]{1,0:T(8,128)(2,1)S(1)}, bf16[272,128]{1,0:T(8,128)(2,1)S(1)}, u32[]{:S(2)}, u32[]{:S(2)}) collective-permute-start(bf16[272,128]{1,0:T(8,128)(2,1)S(1)} %get-tuple-element.15), channel_id=1, source_target_pairs={{0,12},{4,8},{8,4},{12,0},{16,28},{20,24},{24,20},{28,16},{1,13},{... | collective-permute-start | bytes 208904 | tf_op jit(solution)/shard_map/ppermute | solution.py:227
  18.0 4.0 %collective-permute-start.1 = (bf16[272,128]{1,0:T(8,128)(2,1)S(1)}, bf16[272,128]{1,0:T(8,128)(2,1)S(1)}, u32[]{:S(2)}, u32[]{:S(2)}) collective-permute-start(bf16[272,128]{1,0:T(8,128)(2,1)S(1)} %get-tuple-element.16), channel_id=1, source_target_pairs={{0,8},{4,12},{8,0},{12,4},{16,24},{20,28},{24,16},{28,20},{1,9},{5... | collective-permute-start | bytes 208904 | tf_op jit(solution)/shard_map/ppermute | solution.py:227
  18.1 4.0 %collective-permute-start.2 = (bf16[272,128]{1,0:T(8,128)(2,1)S(1)}, bf16[272,128]{1,0:T(8,128)(2,1)S(1)}, u32[]{:S(2)}, u32[]{:S(2)}) collective-permute-start(bf16[272,128]{1,0:T(8,128)(2,1)S(1)} %get-tuple-element.17), channel_id=1, source_target_pairs={{0,4},{4,0},{8,12},{12,8},{16,20},{20,16},{24,28},{28,24},{1,5},{5... | collective-permute-start | bytes 208904 | tf_op jit(solution)/shard_map/ppermute | solution.py:227
  19.1 4.2 %copy-start = (f32[256,128]{1,0:T(8,128)S(1)}, f32[256,128]{1,0:T(8,128)}, u32[]{:S(2)}) copy-start(f32[256,128]{1,0:T(8,128)} %now_ref.3) | copy-start | bytes 393220
  19.1 4.2 %collective-permute-start.6 = (bf16[272,128]{1,0:T(8,128)(2,1)S(1)}, bf16[272,128]{1,0:T(8,128)(2,1)S(1)}, u32[]{:S(2)}, u32[]{:S(2)}) collective-permute-start(bf16[272,128]{1,0:T(8,128)(2,1)S(1)} %mirror_sum.1), channel_id=1, source_target_pairs={{0,16},{4,20},{8,24},{12,28},{16,0},{20,4},{24,8},{28,12},{1,17},{... | collective-permute-start | bytes 208904 | tf_op jit(solution)/shard_map/ppermute | solution.py:227

commit v12 on v11

--- a/solution.py
+++ b/solution.py
@@ -93,14 +93,14 @@
 def write_block(ref, slab, early):
     rows_dev = slab.shape[0]
     ref[:rows_dev, :] = slab.astype(BF16)
-    ref[rows_dev:, :] = high_and_low(early)
+    ref[rows_dev:, :] = early.astype(BF16)
 
 
 def add_blocks(own_ref, block_refs, rows_dev):
     slab, early = own_ref[:rows_dev, :], own_ref[rows_dev:, :]
     for ref in block_refs:
         slab = slab + ref[:rows_dev, :].astype(F32)
-        early = early + sum_high_and_low(ref[rows_dev:, :])
+        early = early + ref[rows_dev:, :].astype(F32)
     return slab, early
 
 
@@ -155,25 +155,55 @@
             panel = group[at]
             columns = [column(panel, first + j) for j in range(block)]
             kept = panel
-            for j in range(0, block, 2):
-                here, there = subs == j, subs == j + 1
-                both = here | there
-                lane, next_lane = lanes == first + j, lanes == first + j + 1
-                left, right = columns[j], columns[j + 1]
-                a, b, c = row(left, j), row(right, j), row(right, j + 1)
-                scale = 1.0 / (a * c - b * b)
-                by_top = jnp.where(here, -c, jnp.where(there, b, left * c - right * b))
-                by_bottom = jnp.where(here, b, jnp.where(there, -a, right * a - left * b))
-                top, bottom = row(panel, j), row(panel, j + 1)
-                ratio = b / a
-                kept = jnp.where(here, top, jnp.where(there, bottom - ratio * jnp.where(lane, 1.0, top), kept))
-                kept = jnp.where(there & lane, -ratio, kept)
-                top = jnp.where(lane, 1.0, jnp.where(next_lane, 0.0, top))
-                bottom = jnp.where(lane, 0.0, jnp.where(next_lane, 1.0, bottom))
-                panel = jnp.where(both | lane | next_lane, 0.0, panel) - (by_top * top + by_bottom * bottom) * scale
-                for m in range(j + 2, block):
-                    up, down = row(columns[m], j), row(columns[m], j + 1)
-                    columns[m] = jnp.where(both, 0.0, columns[m]) - (by_top * up + by_bottom * down) * scale
+            for j in range(0, block, 4):
+                here = [subs == j + k for k in range(4)]
+                lane = [lanes == first + j + k for k in range(4)]
+                mine = (subs >= j) & (subs < j + 4)
+                old = columns[j : j + 4]
+                g = {(x, y): row(old[y], j + x) for x in range(4) for y in range(x, 4)}
+                scale = 1.0 / (g[0, 0] * g[1, 1] - g[0, 1] * g[0, 1])
+                a00, a01, a11 = g[1, 1] * scale, -g[0, 1] * scale, g[0, 0] * scale
+                t = {(0, y): a00 * g[0, y] + a01 * g[1, y] for y in (2, 3)}
+                t.update({(1, y): a01 * g[0, y] + a11 * g[1, y] for y in (2, 3)})
+                s22, s23, s33 = [
+                    g[x, y] - (g[0, x] * t[0, y] + g[1, x] * t[1, y]) for x, y in ((2, 2), (2, 3), (3, 3))
+                ]
+                scale = 1.0 / (s22 * s33 - s23 * s23)
+                inverse = {(2, 2): s33 * scale, (2, 3): -s23 * scale, (3, 3): s22 * scale}
+                for x in (0, 1):
+                    inverse[x, 2] = -(t[x, 2] * inverse[2, 2] + t[x, 3] * inverse[2, 3])
+                    inverse[x, 3] = -(t[x, 2] * inverse[2, 3] + t[x, 3] * inverse[3, 3])
+                for x, y, start in ((0, 0, a00), (0, 1, a01), (1, 1, a11)):
+                    inverse[x, y] = start - (t[x, 2] * inverse[y, 2] + t[x, 3] * inverse[y, 3])
+                inverse.update({(y, x): value for (x, y), value in list(inverse.items())})
+                by = []
+                for y in range(4):
+                    terms = [old[x] * inverse[x, y] for x in range(4)]
+                    value = (terms[0] + terms[1]) + (terms[2] + terms[3])
+                    for x in range(4):
+                        value = jnp.where(here[x], -inverse[x, y], value)
+                    by.append(value)
+
+                def update(x, rows):
+                    return jnp.where(mine, 0.0, x) - ((by[0] * rows[0] + by[1] * rows[1]) + (by[2] * rows[2] + by[3] * rows[3]))
+
+                plain = [row(panel, j + k) for k in range(4)]
+                in_pivots = (lanes >= first + j) & (lanes < first + j + 4)
+                unit = [jnp.where(lane[k], 1.0, jnp.where(in_pivots, 0.0, plain[k])) for k in range(4)]
+                done_0 = plain[0]
+                done_1 = jnp.where(lane[0], 0.0, plain[1]) - (g[0, 1] / g[0, 0]) * jnp.where(lane[0], 1.0, plain[0])
+                first_two = lane[0] | lane[1]
+                top = jnp.where(lane[0], 1.0, jnp.where(lane[1], 0.0, plain[0]))
+                bottom = jnp.where(lane[0], 0.0, jnp.where(lane[1], 1.0, plain[1]))
+                done_2, done_3 = [
+                    jnp.where(first_two, 0.0, plain[y]) - (t[0, y] * top + t[1, y] * bottom) for y in (2, 3)
+                ]
+                done_3 = jnp.where(lane[2], 0.0, done_3) - (s23 / s22) * jnp.where(lane[2], 1.0, done_2)
+                for k, done in enumerate((done_0, done_1, done_2, done_3)):
+                    kept = jnp.where(here[k], done, kept)
+                panel = update(jnp.where(in_pivots, 0.0, panel), unit)
+                for m in range(j + 4, block):
+                    columns[m] = update(columns[m], [row(columns[m], j + k) for k in range(4)])
             finished.append(kept)
             group[at] = panel
             rows = [row(panel, m) for m in range(block)]
@@ -242,7 +272,7 @@
     gathered = lax.all_gather(both, "col", axis=0, tiled=True)
     me = jnp.stack([lax.axis_index("row"), lax.axis_index("col")])
     half = n_row // 2
-    block = jax.ShapeDtypeStruct((rows_dev + 2 * piece, width), BF16)
+    block = jax.ShapeDtypeStruct((rows_dev + piece, width), BF16)
     sums = jax.ShapeDtypeStruct((rows_dev + piece, width), F32)
     *blocks, far, own = pl.pallas_call(
         functools.partial(tiles_kernel, n_row, n_col, total_rows),

time: 55.5 us -> 55.8 us (level)
  no operation moved by 1% of the time
where the time goes in v12:
time: 55.8 us; the launch traced here: 55.6 us
  blocking collectives  35.8 us (64%)
  starting transfers between devices  8.14 us (15%)
  Pallas kernels  6.69 us (12%)
  waiting for transfers between devices  1.81 us (3%)
  between operations  1.39 us (2%)
  other arithmetic  1.05 us (2%)
  local copies, waits for them, and re-layouts  0.69 us (1%)
    all_to_all x1, blocking collectives, on_device(): lax.all_to_all(grams.reshape(devices, piece, width), everyone, split_axis...  16.1 us
    all_to_all x1, blocking collectives, on_device(): lax.all_to_all(copies, everyone, split_axis=0, concat_axis=0, tiled=True)  11 us
    all_gather x1, blocking collectives, on_device(): gathered = lax.all_gather(both, 'col', axis=0, tiled=True)  8.67 us
    ppermute x7, starting transfers between devices, exchange(): lax.ppermute(block, axis, [(i, i ^ step) for i in range(n)])  8.14 us
    pallas_call x1, Pallas kernels, on_device(): pl.pallas_call(functools.partial(final_kernel, total_rows), out_shape=(ja...  4.81 us
    ppermute x7, waiting for transfers between devices, exchange(): lax.ppermute(block, axis, [(i, i ^ step) for i in range(n)])  1.81 us
    pallas_call x1, Pallas kernels, on_device(): pl.pallas_call(functools.partial(tiles_kernel, n_row, n_col, total_rows),...  1.27 us
  transfers between devices with their start and end apart: 7, of which 4 were waited for; matrix products, arithmetic and copies ran while one was open for 0% of the time, Pallas kernels for 0%

profile of v12, /device:TPU:1, one launch (start us, length us, event | category | flops | bytes accessed | tf_op | source)
XLA Modules:
  0.0 55.6 jit_solution(10310384285824931453)
XLA Ops:
  0.6 0.0 copy-start.2
  0.6 0.9 %convert.6 = bf16[256,128]{1,0:T(8,128)(2,1)S(1)} convert(f32[256,128]{1,0:T(8,128)} %now_ref.3) | non-fusion elementwise | flops 32768 | bytes 196608 | tf_op jit(solution)/shard_map/convert
  1.6 0.0 copy-done.2
  1.6 0.0 copy-start.1
  1.6 0.0 copy-start.3
  1.7 8.7 %all_gather.3.basis_ref = bf16[2048,128]{1,0:T(8,128)(2,1)S(1)} all-gather(bf16[512,128]{1,0:T(8,128)(2,1)S(1)} %pad_maximum_fusion), channel_id=1, replica_groups=mesh['row'=8,'col'=4] {'col'}, dimensions={0}, use_global_device_ids=true | all-gather | bytes 655360 | tf_op jit(solution)/shard_map/all_gather | solution.py:272
  11.0 0.1 pad_add_fusion.me_ref
  11.1 0.0 copy-start.4
  11.1 0.0 copy-start.5
  11.1 0.0 copy-done.1
  11.1 0.0 copy-done.3
  11.1 0.6 %copy-done.4 = s32[1,1,16]{2,1,0:T(1,128)S(1)} copy-done((s32[1,1,16]{2,1,0:T(1,128)S(1)}, s32[1,1,16]{2,1,0:T(1,128)}, u32[]{:S(2)}) %copy-start.4) | copy-done | bytes 88
  11.7 0.0 copy-done.5
  11.7 1.3 %tile_products.1 = (bf16[264,128]{1,0:T(8,128)(2,1)S(1)}, bf16[264,128]{1,0:T(8,128)(2,1)S(1)}, bf16[264,128]{1,0:T(8,128)(2,1)S(1)}, bf16[264,128]{1,0:T(8,128)...) custom-call(s32[2]{0:T(128)S(1)} %pad_add_fusion.me_ref, ...), custom_call_target="tpu_custom_call" | custom-call | tf_op jit(solution)/shard_map/tile_products/pallas_call | solution.py:277
  13.0 2.3 %collective-permute-start.3 = (bf16[264,128]{1,0:T(8,128)(2,1)S(1)}, bf16[264,128]{1,0:T(8,128)(2,1)S(1)}, u32[]{:S(2)}, u32[]{:S(2)}) collective-permute-start(bf16[264,128]{1,0:T(8,128)(2,1)S(1)} %get-tuple-element.19), channel_id=1, source_target_pairs={{0,12},{4,8},{8,4},{12,0},{16,28},{20,24},{24,20},{28,16},{1,13},{... | collective-permute-start | bytes 202760 | tf_op jit(solution)/shard_map/ppermute | solution.py:257
  15.3 0.2 collective-permute-start.4
  15.5 0.3 collective-permute-start.5
  15.7 2.2 %collective-permute-start = (bf16[264,128]{1,0:T(8,128)(2,1)S(1)}, bf16[264,128]{1,0:T(8,128)(2,1)S(1)}, u32[]{:S(2)}, u32[]{:S(2)}) collective-permute-start(bf16[264,128]{1,0:T(8,128)(2,1)S(1)} %get-tuple-element.15), channel_id=1, source_target_pairs={{0,12},{4,8},{8,4},{12,0},{16,28},{20,24},{24,20},{28,16},{1,13},{... | collective-permute-start | bytes 202760 | tf_op jit(solution)/shard_map/ppermute | solution.py:257
  18.0 0.2 collective-permute-start.1
  18.1 0.0 collective-permute-done.3.refs_0_
  18.1 0.7 %collective-permute-start.2 = (bf16[264,128]{1,0:T(8,128)(2,1)S(1)}, bf16[264,128]{1,0:T(8,128)(2,1)S(1)}, u32[]{:S(2)}, u32[]{:S(2)}) collective-permute-start(bf16[264,128]{1,0:T(8,128)(2,1)S(1)} %get-tuple-element.17), channel_id=1, source_target_pairs={{0,4},{4,0},{8,12},{12,8},{16,20},{20,16},{24,28},{28,24},{1,5},{5... | collective-permute-start | bytes 202760 | tf_op jit(solution)/shard_map/ppermute | solution.py:257
  18.8 0.0 collective-permute-done.4.refs_1_
  18.8 0.2 collective-permute-done.5.refs_2_
  19.0 0.0 copy-start
  19.0 2.4 %collective-permute-start.6 = (bf16[264,128]{1,0:T(8,128)(2,1)S(1)}, bf16[264,128]{1,0:T(8,128)(2,1)S(1)}, u32[]{:S(2)}, u32[]{:S(2)}) collective-permute-start(bf16[264,128]{1,0:T(8,128)(2,1)S(1)} %mirror_sum.1), channel_id=1, source_target_pairs={{0,16},{4,20},{8,24},{12,28},{16,0},{20,4},{24,8},{28,12},{1,17},{... | collective-permute-start | bytes 202760 | tf_op jit(solution)/shard_map/ppermute | solution.py:257
  21.4 0.2 shift_by_previous.1.shift_ref
  21.6 0.0 collective-permute-done.refs_0_
  21.6 0.3 collective-permute-done.1.refs_1_
  21.9 0.1 collective-permute-done.2.refs_2_
  22.1 1.2 %collective-permute-done.6.refs_3_ = bf16[264,128]{1,0:T(8,128)(2,1)S(1)} collective-permute-done((bf16[264,128]{1,0:T(8,128)(2,1)S(1)}, bf16[264,128]{1,0:T(8,128)(2,1)S(1)}, u32[]{:S(2)}, u32[]{:S(2)}) %collective-permute-start.6) | collective-permute-done | bytes 67616 | tf_op jit(solution)/shard_map/ppermute | solution.py:257
  23.3 0.0 copy-done
  23.3 0.3 local_grams.1
  23.6 16.1 %all_to_all.10.parts_ref = f32[32,8,128]{2,1,0:T(8,128)S(1)} all-to-all(f32[32,8,128]{2,1,0:T(8,128)S(1)} %bitcast.5), channel_id=1, replica_groups=mesh['row'=8,'col'=4] {'row','col'}, dimensions={0} | all-to-all | bytes 262144 | tf_op jit(solution)/shard_map/all_to_all | solution.py:324
  39.7 0.1 sum_and_spread.1
  39.8 11.0 %all_to_all.11.pieces_ref = bf16[32,24,128]{2,1,0:T(8,128)(2,1)S(1)} all-to-all(bf16[32,24,128]{2,1,0:T(8,128)(2,1)S(1)} %sum_and_spread.1), channel_id=1, replica_groups=mesh['row'=8,'col'=4] {'row','col'}, dimensions={0} | all-to-all | bytes 393216 | tf_op jit(solution)/shard_map/all_to_all | solution.py:333
  50.8 4.8 %factor_and_basis.1 = (f32[256,128]{1,0:T(8,128)}, f32[128,128]{1,0:T(8,128)}, f32[128,128]{1,0:T(8,128)}) custom-call(bf16[32,24,128]{2,1,0:T(8,128)(2,1)S(1)} %all_to_all.11.pieces_ref, f32[256,128]{1,0:T(8,128)S(1)} %copy-done, f32[256,128]{1,0:T(8,128)S(1)} %get-tuple-element.24.shifted_ref), custom_call_target="tpu_custom_call" | custom-call | tf_op jit(solution)/shard_map/factor_and_basis/pallas_call | solution.py:334
  (3 shorter events, 0.1 us)
Async XLA Ops:
  0.6 1.0 %copy-start.2 = (f32[256,128]{1,0:T(8,128)S(1)}, f32[256,128]{1,0:T(8,128)}, u32[]{:S(2)}) copy-start(f32[256,128]{1,0:T(8,128)} %prev_ref.1) | copy-start | bytes 393220
  1.6 9.5 %copy-start.1 = (bf16[1,1,16,128,128]{4,3,2,1,0:T(8,128)(2,1)S(1)}, bf16[1,1,16,128,128]{4,3,2,1,0:T(8,128)(2,1)}, u32[]{:S(2)}) copy-start(bf16[1,1,16,128,128]{4,3,2,1,0:T(8,128)(2,1)} %param.10) | copy-start | bytes 1572868
  1.6 9.4 %copy-start.3 = (f32[128,128]{1,0:T(8,128)S(1)}, f32[128,128]{1,0:T(8,128)}, u32[]{:S(2)}) copy-start(f32[128,128]{1,0:T(8,128)} %coupling_ref.3) | copy-start | bytes 196612
  11.1 0.7 %copy-start.4 = (s32[1,1,16]{2,1,0:T(1,128)S(1)}, s32[1,1,16]{2,1,0:T(1,128)}, u32[]{:S(2)}) copy-start(s32[1,1,16]{2,1,0:T(1,128)} %rows_ref.1) | copy-start | bytes 196
  11.1 0.7 %copy-start.5 = (s32[1,1,16]{2,1,0:T(1,128)S(1)}, s32[1,1,16]{2,1,0:T(1,128)}, u32[]{:S(2)}) copy-start(s32[1,1,16]{2,1,0:T(1,128)} %cols_ref.1) | copy-start | bytes 196
  13.0 5.1 %collective-permute-start.3 = (bf16[264,128]{1,0:T(8,128)(2,1)S(1)}, bf16[264,128]{1,0:T(8,128)(2,1)S(1)}, u32[]{:S(2)}, u32[]{:S(2)}) collective-permute-start(bf16[264,128]{1,0:T(8,128)(2,1)S(1)} %get-tuple-element.19), channel_id=1, source_target_pairs={{0,12},{4,8},{8,4},{12,0},{16,28},{20,24},{24,20},{28,16},{1,13},{... | collective-permute-start | bytes 202760 | tf_op jit(solution)/shard_map/ppermute | solution.py:257
  15.3 3.5 %collective-permute-start.4 = (bf16[264,128]{1,0:T(8,128)(2,1)S(1)}, bf16[264,128]{1,0:T(8,128)(2,1)S(1)}, u32[]{:S(2)}, u32[]{:S(2)}) collective-permute-start(bf16[264,128]{1,0:T(8,128)(2,1)S(1)} %get-tuple-element.20), channel_id=1, source_target_pairs={{0,8},{4,12},{8,0},{12,4},{16,24},{20,28},{24,16},{28,20},{1,9},{5... | collective-permute-start | bytes 202760 | tf_op jit(solution)/shard_map/ppermute | solution.py:257
  15.5 3.5 %collective-permute-start.5 = (bf16[264,128]{1,0:T(8,128)(2,1)S(1)}, bf16[264,128]{1,0:T(8,128)(2,1)S(1)}, u32[]{:S(2)}, u32[]{:S(2)}) collective-permute-start(bf16[264,128]{1,0:T(8,128)(2,1)S(1)} %get-tuple-element.21), channel_id=1, source_target_pairs={{0,4},{4,0},{8,12},{12,8},{16,20},{20,16},{24,28},{28,24},{1,5},{5... | collective-permute-start | bytes 202760 | tf_op jit(solution)/shard_map/ppermute | solution.py:257
  15.7 5.9 %collective-permute-start = (bf16[264,128]{1,0:T(8,128)(2,1)S(1)}, bf16[264,128]{1,0:T(8,128)(2,1)S(1)}, u32[]{:S(2)}, u32[]{:S(2)}) collective-permute-start(bf16[264,128]{1,0:T(8,128)(2,1)S(1)} %get-tuple-element.15), channel_id=1, source_target_pairs={{0,12},{4,8},{8,4},{12,0},{16,28},{20,24},{24,20},{28,16},{1,13},{... | collective-permute-start | bytes 202760 | tf_op jit(solution)/shard_map/ppermute | solution.py:257
  18.0 4.0 %collective-permute-start.1 = (bf16[264,128]{1,0:T(8,128)(2,1)S(1)}, bf16[264,128]{1,0:T(8,128)(2,1)S(1)}, u32[]{:S(2)}, u32[]{:S(2)}) collective-permute-start(bf16[264,128]{1,0:T(8,128)(2,1)S(1)} %get-tuple-element.16), channel_id=1, source_target_pairs={{0,8},{4,12},{8,0},{12,4},{16,24},{20,28},{24,16},{28,20},{1,9},{5... | collective-permute-start | bytes 202760 | tf_op jit(solution)/shard_map/ppermute | solution.py:257
  18.1 4.0 %collective-permute-start.2 = (bf16[264,128]{1,0:T(8,128)(2,1)S(1)}, bf16[264,128]{1,0:T(8,128)(2,1)S(1)}, u32[]{:S(2)}, u32[]{:S(2)}) collective-permute-start(bf16[264,128]{1,0:T(8,128)(2,1)S(1)} %get-tuple-element.17), channel_id=1, source_target_pairs={{0,4},{4,0},{8,12},{12,8},{16,20},{20,16},{24,28},{28,24},{1,5},{5... | collective-permute-start | bytes 202760 | tf_op jit(solution)/shard_map/ppermute | solution.py:257
  19.0 4.2 %copy-start = (f32[256,128]{1,0:T(8,128)S(1)}, f32[256,128]{1,0:T(8,128)}, u32[]{:S(2)}) copy-start(f32[256,128]{1,0:T(8,128)} %now_ref.3) | copy-start | bytes 393220
  19.0 4.2 %collective-permute-start.6 = (bf16[264,128]{1,0:T(8,128)(2,1)S(1)}, bf16[264,128]{1,0:T(8,128)(2,1)S(1)}, u32[]{:S(2)}, u32[]{:S(2)}) collective-permute-start(bf16[264,128]{1,0:T(8,128)(2,1)S(1)} %mirror_sum.1), channel_id=1, source_target_pairs={{0,16},{4,20},{8,24},{12,28},{16,0},{20,4},{24,8},{28,12},{1,17},{... | collective-permute-start | bytes 202760 | tf_op jit(solution)/shard_map/ppermute | solution.py:257

commit v13 on v11

--- a/solution.py
+++ b/solution.py
@@ -57,11 +57,7 @@
     piece = early_ref.shape[0] // (n_row * n_col)
     my_row, my_col = me_ref[0], me_ref[1]
     total_ref[...] = jnp.zeros_like(total_ref)
-    grams = jnp.zeros((width, 2 * width), F32)
-    for slab in range(n_col):
-        now = basis_ref[2 * slab * rows_dev : (2 * slab + 1) * rows_dev, :]
-        prev = basis_ref[(2 * slab + 1) * rows_dev : (2 * slab + 2) * rows_dev, :]
-        grams += lax.dot_general(now, jnp.concatenate([now, prev], axis=1), TN, preferred_element_type=F32)
+    grams = lax.dot_general(basis_ref[:, :width], basis_ref[...], TN, preferred_element_type=F32)
     square, cross = grams[:, :width], grams[:, width:]
     rows = lax.broadcasted_iota(jnp.int32, square.shape, 0)
     cols = lax.broadcasted_iota(jnp.int32, square.shape, 1)
@@ -70,11 +66,9 @@
     early_ref[:width, :] = square - jnp.where(rows == cols, total_rows / n_row, 0.0)
     early_ref[width : 2 * width, :] = dot3(cross, upper_of(coupling_ref[...]), NT)
     used = count_ref[...]
-    per_slab = rows_dev // size
     for slot in range(slots):
-        col = cols_ref[0, 0, slot]
-        start = pl.multiple_of((2 * per_slab * (col // per_slab) + lax.rem(col, per_slab)) * size, size)
-        value = jnp.dot(tiles_ref[slot], basis_ref[pl.ds(start, size), :], preferred_element_type=F32)
+        start = pl.multiple_of(cols_ref[0, 0, slot] * size, size)
+        value = jnp.dot(tiles_ref[slot], basis_ref[pl.ds(start, size), :width], preferred_element_type=F32)
         value = value * (slot < used).astype(F32)
         place = pl.ds(pl.multiple_of(rows_ref[0, 0, slot] * size, size), size)
         total_ref[place, :] += value
@@ -136,7 +130,7 @@
 
 def eliminate(gram):
     width = gram.shape[0]
-    block, per_group = 16, 2
+    block, per_group = 8, 4
     lanes = lax.broadcasted_iota(jnp.int32, (block, width), 1)
     subs = lax.broadcasted_iota(jnp.int32, (block, width), 0)
 
@@ -238,7 +232,7 @@
     vmem = pl.BlockSpec(memory_space=pltpu.VMEM)
     params = pltpu.CompilerParams(vmem_limit_bytes=48 * 1024 * 1024)
 
-    both = jnp.concatenate([basis_now, basis_prev], axis=0).astype(BF16)
+    both = jnp.concatenate([basis_now, basis_prev], axis=1).astype(BF16)
     gathered = lax.all_gather(both, "col", axis=0, tiled=True)
     me = jnp.stack([lax.axis_index("row"), lax.axis_index("col")])
     half = n_row // 2

time: 55.5 us -> 56.1 us (1.011)
  Pallas kernels: 6.16 us -> 6.77 us
    pallas_call x1, Pallas kernels: 4.26 us -> 4.88 us  [on_device(): pl.pallas_call(functools.partial(final_kernel, total_rows), out_shape=(ja...]
where the time goes in v13:
time: 56.1 us; the launch traced here: 55.9 us
  blocking collectives  36 us (64%)
  starting transfers between devices  8.17 us (15%)
  Pallas kernels  6.77 us (12%)
  waiting for transfers between devices  1.86 us (3%)
  between operations  1.39 us (2%)
  other arithmetic  1.05 us (2%)
  local copies, waits for them, and re-layouts  0.69 us (1%)
    all_to_all x1, blocking collectives, on_device(): lax.all_to_all(grams.reshape(devices, piece, width), everyone, split_axis...  16.2 us
    all_to_all x1, blocking collectives, on_device(): lax.all_to_all(copies, everyone, split_axis=0, concat_axis=0, tiled=True)  11 us
    all_gather x1, blocking collectives, on_device(): gathered = lax.all_gather(both, 'col', axis=0, tiled=True)  8.67 us
    ppermute x7, starting transfers between devices, exchange(): lax.ppermute(block, axis, [(i, i ^ step) for i in range(n)])  8.17 us
    pallas_call x1, Pallas kernels, on_device(): pl.pallas_call(functools.partial(final_kernel, total_rows), out_shape=(ja...  4.88 us
    ppermute x7, waiting for transfers between devices, exchange(): lax.ppermute(block, axis, [(i, i ^ step) for i in range(n)])  1.86 us
    pallas_call x1, Pallas kernels, on_device(): pl.pallas_call(functools.partial(tiles_kernel, n_row, n_col, total_rows),...  1.27 us
  transfers between devices with their start and end apart: 7, of which 4 were waited for; matrix products, arithmetic and copies ran while one was open for 0% of the time, Pallas kernels for 0%

profile of v13, /device:TPU:1, one launch (start us, length us, event | category | flops | bytes accessed | tf_op | source)
XLA Modules:
  0.0 55.9 jit_solution(5488147978879383625)
XLA Ops:
  0.6 0.0 copy-start.2
  0.6 0.9 %convert.6 = bf16[256,128]{1,0:T(8,128)(2,1)S(1)} convert(f32[256,128]{1,0:T(8,128)} %now_ref.3) | non-fusion elementwise | flops 32768 | bytes 196608 | tf_op jit(solution)/shard_map/convert
  1.6 0.0 copy-done.2
  1.6 0.0 copy-start.1
  1.7 0.0 copy-start.3
  1.7 8.7 %all_gather.3.basis_ref = bf16[1024,256]{1,0:T(8,128)(2,1)S(1)} all-gather(bf16[256,256]{1,0:T(8,128)(2,1)S(1)} %pad_maximum_fusion), channel_id=1, replica_groups=mesh['row'=8,'col'=4] {'col'}, dimensions={0}, use_global_device_ids=true | all-gather | bytes 655360 | tf_op jit(solution)/shard_map/all_gather | solution.py:236
  11.0 0.1 pad_add_fusion.me_ref
  11.1 0.0 copy-start.4
  11.1 0.0 copy-start.5
  11.1 0.0 copy-done.1
  11.1 0.0 copy-done.3
  11.1 0.6 %copy-done.4 = s32[1,1,16]{2,1,0:T(1,128)S(1)} copy-done((s32[1,1,16]{2,1,0:T(1,128)S(1)}, s32[1,1,16]{2,1,0:T(1,128)}, u32[]{:S(2)}) %copy-start.4) | copy-done | bytes 88
  11.7 0.0 copy-done.5
  11.7 1.3 %tile_products.1 = (bf16[272,128]{1,0:T(8,128)(2,1)S(1)}, bf16[272,128]{1,0:T(8,128)(2,1)S(1)}, bf16[272,128]{1,0:T(8,128)(2,1)S(1)}, bf16[272,128]{1,0:T(8,128)...) custom-call(s32[2]{0:T(128)S(1)} %pad_add_fusion.me_ref, ...), custom_call_target="tpu_custom_call" | custom-call | tf_op jit(solution)/shard_map/tile_products/pallas_call | solution.py:241
  13.0 2.3 %collective-permute-start.3 = (bf16[272,128]{1,0:T(8,128)(2,1)S(1)}, bf16[272,128]{1,0:T(8,128)(2,1)S(1)}, u32[]{:S(2)}, u32[]{:S(2)}) collective-permute-start(bf16[272,128]{1,0:T(8,128)(2,1)S(1)} %get-tuple-element.19), channel_id=1, source_target_pairs={{0,12},{4,8},{8,4},{12,0},{16,28},{20,24},{24,20},{28,16},{1,13},{... | collective-permute-start | bytes 208904 | tf_op jit(solution)/shard_map/ppermute | solution.py:221
  15.3 0.2 collective-permute-start.4
  15.5 0.3 collective-permute-start.5
  15.7 2.2 %collective-permute-start = (bf16[272,128]{1,0:T(8,128)(2,1)S(1)}, bf16[272,128]{1,0:T(8,128)(2,1)S(1)}, u32[]{:S(2)}, u32[]{:S(2)}) collective-permute-start(bf16[272,128]{1,0:T(8,128)(2,1)S(1)} %get-tuple-element.15), channel_id=1, source_target_pairs={{0,12},{4,8},{8,4},{12,0},{16,28},{20,24},{24,20},{28,16},{1,13},{... | collective-permute-start | bytes 208904 | tf_op jit(solution)/shard_map/ppermute | solution.py:221
  18.0 0.2 collective-permute-start.1
  18.1 0.0 collective-permute-done.3.refs_0_
  18.1 0.7 %collective-permute-start.2 = (bf16[272,128]{1,0:T(8,128)(2,1)S(1)}, bf16[272,128]{1,0:T(8,128)(2,1)S(1)}, u32[]{:S(2)}, u32[]{:S(2)}) collective-permute-start(bf16[272,128]{1,0:T(8,128)(2,1)S(1)} %get-tuple-element.17), channel_id=1, source_target_pairs={{0,4},{4,0},{8,12},{12,8},{16,20},{20,16},{24,28},{28,24},{1,5},{5... | collective-permute-start | bytes 208904 | tf_op jit(solution)/shard_map/ppermute | solution.py:221
  18.8 0.2 collective-permute-done.4.refs_1_
  19.0 0.0 collective-permute-done.5.refs_2_
  19.1 0.0 copy-start
  19.1 2.4 %collective-permute-start.6 = (bf16[272,128]{1,0:T(8,128)(2,1)S(1)}, bf16[272,128]{1,0:T(8,128)(2,1)S(1)}, u32[]{:S(2)}, u32[]{:S(2)}) collective-permute-start(bf16[272,128]{1,0:T(8,128)(2,1)S(1)} %mirror_sum.1), channel_id=1, source_target_pairs={{0,16},{4,20},{8,24},{12,28},{16,0},{20,4},{24,8},{28,12},{1,17},{... | collective-permute-start | bytes 208904 | tf_op jit(solution)/shard_map/ppermute | solution.py:221
  21.5 0.2 shift_by_previous.1.shift_ref
  21.7 0.0 collective-permute-done.refs_0_
  21.7 0.3 collective-permute-done.1.refs_1_
  22.0 0.1 collective-permute-done.2.refs_2_
  22.1 1.2 %collective-permute-done.6.refs_3_ = bf16[272,128]{1,0:T(8,128)(2,1)S(1)} collective-permute-done((bf16[272,128]{1,0:T(8,128)(2,1)S(1)}, bf16[272,128]{1,0:T(8,128)(2,1)S(1)}, u32[]{:S(2)}, u32[]{:S(2)}) %collective-permute-start.6) | collective-permute-done | bytes 69664 | tf_op jit(solution)/shard_map/ppermute | solution.py:221
  23.3 0.0 copy-done
  23.3 0.3 local_grams.1
  23.7 16.2 %all_to_all.10.parts_ref = f32[32,8,128]{2,1,0:T(8,128)S(1)} all-to-all(f32[32,8,128]{2,1,0:T(8,128)S(1)} %bitcast.5), channel_id=1, replica_groups=mesh['row'=8,'col'=4] {'row','col'}, dimensions={0} | all-to-all | bytes 262144 | tf_op jit(solution)/shard_map/all_to_all | solution.py:288
  39.9 0.1 sum_and_spread.1
  40.0 11.0 %all_to_all.11.pieces_ref = bf16[32,24,128]{2,1,0:T(8,128)(2,1)S(1)} all-to-all(bf16[32,24,128]{2,1,0:T(8,128)(2,1)S(1)} %sum_and_spread.1), channel_id=1, replica_groups=mesh['row'=8,'col'=4] {'row','col'}, dimensions={0} | all-to-all | bytes 393216 | tf_op jit(solution)/shard_map/all_to_all | solution.py:297
  51.0 4.9 %factor_and_basis.1 = (f32[256,128]{1,0:T(8,128)}, f32[128,128]{1,0:T(8,128)}, f32[128,128]{1,0:T(8,128)}) custom-call(bf16[32,24,128]{2,1,0:T(8,128)(2,1)S(1)} %all_to_all.11.pieces_ref, f32[256,128]{1,0:T(8,128)S(1)} %copy-done, f32[256,128]{1,0:T(8,128)S(1)} %get-tuple-element.24.shifted_ref), custom_call_target="tpu_custom_call" | custom-call | tf_op jit(solution)/shard_map/factor_and_basis/pallas_call | solution.py:298
  (3 shorter events, 0.1 us)
Async XLA Ops:
  0.6 1.0 %copy-start.2 = (f32[256,128]{1,0:T(8,128)S(1)}, f32[256,128]{1,0:T(8,128)}, u32[]{:S(2)}) copy-start(f32[256,128]{1,0:T(8,128)} %prev_ref.1) | copy-start | bytes 393220
  1.6 9.5 %copy-start.1 = (bf16[1,1,16,128,128]{4,3,2,1,0:T(8,128)(2,1)S(1)}, bf16[1,1,16,128,128]{4,3,2,1,0:T(8,128)(2,1)}, u32[]{:S(2)}) copy-start(bf16[1,1,16,128,128]{4,3,2,1,0:T(8,128)(2,1)} %param.10) | copy-start | bytes 1572868
  1.7 9.4 %copy-start.3 = (f32[128,128]{1,0:T(8,128)S(1)}, f32[128,128]{1,0:T(8,128)}, u32[]{:S(2)}) copy-start(f32[128,128]{1,0:T(8,128)} %coupling_ref.3) | copy-start | bytes 196612
  11.1 0.7 %copy-start.4 = (s32[1,1,16]{2,1,0:T(1,128)S(1)}, s32[1,1,16]{2,1,0:T(1,128)}, u32[]{:S(2)}) copy-start(s32[1,1,16]{2,1,0:T(1,128)} %rows_ref.1) | copy-start | bytes 196
  11.1 0.7 %copy-start.5 = (s32[1,1,16]{2,1,0:T(1,128)S(1)}, s32[1,1,16]{2,1,0:T(1,128)}, u32[]{:S(2)}) copy-start(s32[1,1,16]{2,1,0:T(1,128)} %cols_ref.1) | copy-start | bytes 196
  13.0 5.1 %collective-permute-start.3 = (bf16[272,128]{1,0:T(8,128)(2,1)S(1)}, bf16[272,128]{1,0:T(8,128)(2,1)S(1)}, u32[]{:S(2)}, u32[]{:S(2)}) collective-permute-start(bf16[272,128]{1,0:T(8,128)(2,1)S(1)} %get-tuple-element.19), channel_id=1, source_target_pairs={{0,12},{4,8},{8,4},{12,0},{16,28},{20,24},{24,20},{28,16},{1,13},{... | collective-permute-start | bytes 208904 | tf_op jit(solution)/shard_map/ppermute | solution.py:221
  15.3 3.7 %collective-permute-start.4 = (bf16[272,128]{1,0:T(8,128)(2,1)S(1)}, bf16[272,128]{1,0:T(8,128)(2,1)S(1)}, u32[]{:S(2)}, u32[]{:S(2)}) collective-permute-start(bf16[272,128]{1,0:T(8,128)(2,1)S(1)} %get-tuple-element.20), channel_id=1, source_target_pairs={{0,8},{4,12},{8,0},{12,4},{16,24},{20,28},{24,16},{28,20},{1,9},{5... | collective-permute-start | bytes 208904 | tf_op jit(solution)/shard_map/ppermute | solution.py:221
  15.5 3.6 %collective-permute-start.5 = (bf16[272,128]{1,0:T(8,128)(2,1)S(1)}, bf16[272,128]{1,0:T(8,128)(2,1)S(1)}, u32[]{:S(2)}, u32[]{:S(2)}) collective-permute-start(bf16[272,128]{1,0:T(8,128)(2,1)S(1)} %get-tuple-element.21), channel_id=1, source_target_pairs={{0,4},{4,0},{8,12},{12,8},{16,20},{20,16},{24,28},{28,24},{1,5},{5... | collective-permute-start | bytes 208904 | tf_op jit(solution)/shard_map/ppermute | solution.py:221
  15.7 6.0 %collective-permute-start = (bf16[272,128]{1,0:T(8,128)(2,1)S(1)}, bf16[272,128]{1,0:T(8,128)(2,1)S(1)}, u32[]{:S(2)}, u32[]{:S(2)}) collective-permute-start(bf16[272,128]{1,0:T(8,128)(2,1)S(1)} %get-tuple-element.15), channel_id=1, source_target_pairs={{0,12},{4,8},{8,4},{12,0},{16,28},{20,24},{24,20},{28,16},{1,13},{... | collective-permute-start | bytes 208904 | tf_op jit(solution)/shard_map/ppermute | solution.py:221
  18.0 4.0 %collective-permute-start.1 = (bf16[272,128]{1,0:T(8,128)(2,1)S(1)}, bf16[272,128]{1,0:T(8,128)(2,1)S(1)}, u32[]{:S(2)}, u32[]{:S(2)}) collective-permute-start(bf16[272,128]{1,0:T(8,128)(2,1)S(1)} %get-tuple-element.16), channel_id=1, source_target_pairs={{0,8},{4,12},{8,0},{12,4},{16,24},{20,28},{24,16},{28,20},{1,9},{5... | collective-permute-start | bytes 208904 | tf_op jit(solution)/shard_map/ppermute | solution.py:221
  18.1 4.0 %collective-permute-start.2 = (bf16[272,128]{1,0:T(8,128)(2,1)S(1)}, bf16[272,128]{1,0:T(8,128)(2,1)S(1)}, u32[]{:S(2)}, u32[]{:S(2)}) collective-permute-start(bf16[272,128]{1,0:T(8,128)(2,1)S(1)} %get-tuple-element.17), channel_id=1, source_target_pairs={{0,4},{4,0},{8,12},{12,8},{16,20},{20,16},{24,28},{28,24},{1,5},{5... | collective-permute-start | bytes 208904 | tf_op jit(solution)/shard_map/ppermute | solution.py:221
  19.1 4.2 %copy-start = (f32[256,128]{1,0:T(8,128)S(1)}, f32[256,128]{1,0:T(8,128)}, u32[]{:S(2)}) copy-start(f32[256,128]{1,0:T(8,128)} %now_ref.3) | copy-start | bytes 393220
  19.1 4.2 %collective-permute-start.6 = (bf16[272,128]{1,0:T(8,128)(2,1)S(1)}, bf16[272,128]{1,0:T(8,128)(2,1)S(1)}, u32[]{:S(2)}, u32[]{:S(2)}) collective-permute-start(bf16[272,128]{1,0:T(8,128)(2,1)S(1)} %mirror_sum.1), channel_id=1, source_target_pairs={{0,16},{4,20},{8,24},{12,28},{16,0},{20,4},{24,8},{28,12},{1,17},{... | collective-permute-start | bytes 208904 | tf_op jit(solution)/shard_map/ppermute | solution.py:221

commit v14 on v11

--- a/solution.py
+++ b/solution.py
@@ -46,6 +46,26 @@
     half = value.shape[-2] // 2
     value = value.astype(F32)
     return value[..., :half, :] + value[..., half:, :]
+
+
+def prepare_kernel(now_hbm, prev_hbm, rows_hbm, cols_hbm, tiles_hbm, both_ref, rows_ref, cols_ref, tiles_ref, now_ref, prev_ref, sems):
+    pairs = (
+        (now_hbm, now_ref),
+        (prev_hbm, prev_ref),
+        (rows_hbm, rows_ref),
+        (cols_hbm, cols_ref),
+        (tiles_hbm, tiles_ref),
+    )
+    copies = [pltpu.make_async_copy(source, target, sems.at[k]) for k, (source, target) in enumerate(pairs)]
+    for copy in copies:
+        copy.start()
+    rows_dev = now_ref.shape[0]
+    copies[0].wait()
+    both_ref[:rows_dev, :] = now_ref[...].astype(BF16)
+    copies[1].wait()
+    both_ref[rows_dev:, :] = prev_ref[...].astype(BF16)
+    for copy in copies[2:]:
+        copy.wait()
 
 
 def tiles_kernel(n_row, n_col, total_rows, me_ref, rows_ref, cols_ref, count_ref, tiles_ref, basis_ref, coupling_ref, *refs):
@@ -238,7 +258,25 @@
     vmem = pl.BlockSpec(memory_space=pltpu.VMEM)
     params = pltpu.CompilerParams(vmem_limit_bytes=48 * 1024 * 1024)
 
-    both = jnp.concatenate([basis_now, basis_prev], axis=0).astype(BF16)
+    in_hbm = [pltpu.with_memory_space_constraint(x, pltpu.HBM) for x in (basis_now, basis_prev, tile_rows, tile_cols, tile_block)]
+    both, rows, cols, tile_block = pl.pallas_call(
+        prepare_kernel,
+        out_shape=(
+            jax.ShapeDtypeStruct((2 * rows_dev, width), BF16),
+            jax.ShapeDtypeStruct(tile_rows.shape, tile_rows.dtype),
+            jax.ShapeDtypeStruct(tile_cols.shape, tile_cols.dtype),
+            jax.ShapeDtypeStruct(tile_block.shape, tile_block.dtype),
+        ),
+        in_specs=[pl.BlockSpec(memory_space=pltpu.HBM)] * 5,
+        out_specs=(vmem, vmem, vmem, vmem),
+        scratch_shapes=[
+            pltpu.VMEM(basis_now.shape, F32),
+            pltpu.VMEM(basis_prev.shape, F32),
+            pltpu.SemaphoreType.DMA((5,)),
+        ],
+        compiler_params=params,
+        name="prepare",
+    )(*in_hbm)
     gathered = lax.all_gather(both, "col", axis=0, tiled=True)
     me = jnp.stack([lax.axis_index("row"), lax.axis_index("col")])
     half = n_row // 2
@@ -255,7 +293,7 @@
         ],
         compiler_params=params,
         name="tile_products",
-    )(me, tile_rows, tile_cols, tile_counts, tile_block, gathered, coupling)
+    )(me, rows, cols, tile_counts, tile_block, gathered, coupling)
     steps = distances(half)[:-1]
     mirrors = exchange(blocks[: half - 1], "row", steps)
     near = exchange(blocks[half - 1 :], "row", steps)

time: 55.5 us -> 55.1 us (level)
  Pallas kernels: 6.16 us -> 7.41 us
  other arithmetic: 1.05 us -> 0.08 us
  local copies, waits for them, and re-layouts: 0.69 us -> 0.02 us
    pallas_call x0 -> x1, Pallas kernels: none -> 1.26 us  [on_device(): pl.pallas_call(prepare_kernel, out_shape=(jax.ShapeDtypeStruct((2 * rows_...]
    another operation x2 -> x0, other arithmetic: 0.96 us -> none
    unnamed x12 -> x6, local copies, waits for them, and re-layouts: 0.69 us -> 0.02 us
where the time goes in v14:
time: 55.1 us; the launch traced here: 54.8 us
  blocking collectives  36 us (65%)
  starting transfers between devices  8.17 us (15%)
  Pallas kernels  7.41 us (13%)
  waiting for transfers between devices  1.86 us (3%)
  between operations  1.36 us (2%)
    all_to_all x1, blocking collectives, on_device(): lax.all_to_all(grams.reshape(devices, piece, width), everyone, split_axis...  16.2 us
    all_to_all x1, blocking collectives, on_device(): lax.all_to_all(copies, everyone, split_axis=0, concat_axis=0, tiled=True)  11 us
    all_gather x1, blocking collectives, on_device(): gathered = lax.all_gather(both, 'col', axis=0, tiled=True)  8.67 us
    ppermute x7, starting transfers between devices, exchange(): lax.ppermute(block, axis, [(i, i ^ step) for i in range(n)])  8.17 us
    pallas_call x1, Pallas kernels, on_device(): pl.pallas_call(functools.partial(final_kernel, total_rows), out_shape=(ja...  4.26 us
    ppermute x7, waiting for transfers between devices, exchange(): lax.ppermute(block, axis, [(i, i ^ step) for i in range(n)])  1.86 us
    pallas_call x1, Pallas kernels, on_device(): pl.pallas_call(functools.partial(tiles_kernel, n_row, n_col, total_rows),...  1.27 us
    pallas_call x1, Pallas kernels, on_device(): pl.pallas_call(prepare_kernel, out_shape=(jax.ShapeDtypeStruct((2 * rows_...  1.26 us
  transfers between devices with their start and end apart: 7, of which 4 were waited for; matrix products, arithmetic and copies ran while one was open for 0% of the time, Pallas kernels for 0%

profile of v14, /device:TPU:1, one launch (start us, length us, event | category | flops | bytes accessed | tf_op | source)
XLA Modules:
  0.0 54.8 jit_solution(12995778948342863133)
XLA Ops:
  0.6 1.3 %prepare.1 = (bf16[512,128]{1,0:T(8,128)(2,1)S(1)}, s32[1,1,16]{2,1,0:T(1,128)S(1)}, s32[1,1,16]{2,1,0:T(1,128)S(1)}, bf16[16,128,128]{2,1,0:T(8,128)(2,1)S(1)}) custom-call(f32[256,128]{1,0:T(8,128)} %now_ref.3, f32[256,128]{1,0:T(8,128)} %prev_hbm.1, s32[1,1,16]{2,1,0:T(1,128)} %rows_hbm.1, s32[1,1,16]{2,1,0:T(1,128)} %cols_hbm.1, ...), custom_call_target="tpu_custom_call" | custom-call | tf_op jit(solution)/shard_map/prepare/pallas_call | solution.py:262
  1.9 0.0 copy-start.2
  1.9 8.7 %all_gather.3.basis_ref = bf16[2048,128]{1,0:T(8,128)(2,1)S(1)} all-gather(bf16[512,128]{1,0:T(8,128)(2,1)S(1)} %get-tuple-element.21), channel_id=1, replica_groups=mesh['row'=8,'col'=4] {'col'}, dimensions={0}, use_global_device_ids=true | all-gather | bytes 655360 | tf_op jit(solution)/shard_map/all_gather | solution.py:280
  11.2 0.1 pad_add_fusion.me_ref
  11.3 0.0 copy-done.2
  11.3 1.3 %tile_products.1 = (bf16[272,128]{1,0:T(8,128)(2,1)S(1)}, bf16[272,128]{1,0:T(8,128)(2,1)S(1)}, bf16[272,128]{1,0:T(8,128)(2,1)S(1)}, bf16[272,128]{1,0:T(8,128)...) custom-call(s32[2]{0:T(128)S(1)} %pad_add_fusion.me_ref, ...), custom_call_target="tpu_custom_call" | custom-call | tf_op jit(solution)/shard_map/tile_products/pallas_call | solution.py:285
  12.6 2.3 %collective-permute-start.3 = (bf16[272,128]{1,0:T(8,128)(2,1)S(1)}, bf16[272,128]{1,0:T(8,128)(2,1)S(1)}, u32[]{:S(2)}, u32[]{:S(2)}) collective-permute-start(bf16[272,128]{1,0:T(8,128)(2,1)S(1)} %get-tuple-element.27), channel_id=1, source_target_pairs={{0,12},{4,8},{8,4},{12,0},{16,28},{20,24},{24,20},{28,16},{1,13},{... | collective-permute-start | bytes 208904 | tf_op jit(solution)/shard_map/ppermute | solution.py:247
  14.9 0.2 collective-permute-start.4
  15.1 0.3 collective-permute-start.5
  15.3 2.2 %collective-permute-start = (bf16[272,128]{1,0:T(8,128)(2,1)S(1)}, bf16[272,128]{1,0:T(8,128)(2,1)S(1)}, u32[]{:S(2)}, u32[]{:S(2)}) collective-permute-start(bf16[272,128]{1,0:T(8,128)(2,1)S(1)} %get-tuple-element.23), channel_id=1, source_target_pairs={{0,12},{4,8},{8,4},{12,0},{16,28},{20,24},{24,20},{28,16},{1,13},{... | collective-permute-start | bytes 208904 | tf_op jit(solution)/shard_map/ppermute | solution.py:247
  17.5 0.2 collective-permute-start.1
  17.7 0.0 collective-permute-done.3.refs_0_
  17.7 0.7 %collective-permute-start.2 = (bf16[272,128]{1,0:T(8,128)(2,1)S(1)}, bf16[272,128]{1,0:T(8,128)(2,1)S(1)}, u32[]{:S(2)}, u32[]{:S(2)}) collective-permute-start(bf16[272,128]{1,0:T(8,128)(2,1)S(1)} %get-tuple-element.25), channel_id=1, source_target_pairs={{0,4},{4,0},{8,12},{12,8},{16,20},{20,16},{24,28},{28,24},{1,5},{5... | collective-permute-start | bytes 208904 | tf_op jit(solution)/shard_map/ppermute | solution.py:247
  18.4 0.2 collective-permute-done.4.refs_1_
  18.6 0.0 collective-permute-done.5.refs_2_
  18.6 0.0 copy-start.1
  18.7 0.0 copy-start
  18.7 2.4 %collective-permute-start.6 = (bf16[272,128]{1,0:T(8,128)(2,1)S(1)}, bf16[272,128]{1,0:T(8,128)(2,1)S(1)}, u32[]{:S(2)}, u32[]{:S(2)}) collective-permute-start(bf16[272,128]{1,0:T(8,128)(2,1)S(1)} %mirror_sum.1), channel_id=1, source_target_pairs={{0,16},{4,20},{8,24},{12,28},{16,0},{20,4},{24,8},{28,12},{1,17},{... | collective-permute-start | bytes 208904 | tf_op jit(solution)/shard_map/ppermute | solution.py:247
  21.1 0.0 copy-done.1
  21.1 0.2 shift_by_previous.1.shift_ref
  21.3 0.0 collective-permute-done.refs_0_
  21.3 0.3 collective-permute-done.1.refs_1_
  21.6 0.1 collective-permute-done.2.refs_2_
  21.7 1.2 %collective-permute-done.6.refs_3_ = bf16[272,128]{1,0:T(8,128)(2,1)S(1)} collective-permute-done((bf16[272,128]{1,0:T(8,128)(2,1)S(1)}, bf16[272,128]{1,0:T(8,128)(2,1)S(1)}, u32[]{:S(2)}, u32[]{:S(2)}) %collective-permute-start.6) | collective-permute-done | bytes 69664 | tf_op jit(solution)/shard_map/ppermute | solution.py:247
  22.9 0.0 copy-done
  22.9 0.3 local_grams.1
  23.2 16.2 %all_to_all.10.parts_ref = f32[32,8,128]{2,1,0:T(8,128)S(1)} all-to-all(f32[32,8,128]{2,1,0:T(8,128)S(1)} %bitcast.4), channel_id=1, replica_groups=mesh['row'=8,'col'=4] {'row','col'}, dimensions={0} | all-to-all | bytes 262144 | tf_op jit(solution)/shard_map/all_to_all | solution.py:332
  39.5 0.1 sum_and_spread.1
  39.5 11.0 %all_to_all.11.pieces_ref = bf16[32,24,128]{2,1,0:T(8,128)(2,1)S(1)} all-to-all(bf16[32,24,128]{2,1,0:T(8,128)(2,1)S(1)} %sum_and_spread.1), channel_id=1, replica_groups=mesh['row'=8,'col'=4] {'row','col'}, dimensions={0} | all-to-all | bytes 393216 | tf_op jit(solution)/shard_map/all_to_all | solution.py:341
  50.6 4.3 %factor_and_basis.1 = (f32[256,128]{1,0:T(8,128)}, f32[128,128]{1,0:T(8,128)}, f32[128,128]{1,0:T(8,128)}) custom-call(bf16[32,24,128]{2,1,0:T(8,128)(2,1)S(1)} %all_to_all.11.pieces_ref, f32[256,128]{1,0:T(8,128)S(1)} %copy-done, f32[256,128]{1,0:T(8,128)S(1)} %get-tuple-element.32.shifted_ref), custom_call_target="tpu_custom_call" | custom-call | tf_op jit(solution)/shard_map/factor_and_basis/pallas_call | solution.py:342
  (1 shorter events, 0.0 us)
Async XLA Ops:
  1.9 9.4 %copy-start.2 = (f32[128,128]{1,0:T(8,128)S(1)}, f32[128,128]{1,0:T(8,128)}, u32[]{:S(2)}) copy-start(f32[128,128]{1,0:T(8,128)} %coupling_ref.3) | copy-start | bytes 196612
  12.6 5.1 %collective-permute-start.3 = (bf16[272,128]{1,0:T(8,128)(2,1)S(1)}, bf16[272,128]{1,0:T(8,128)(2,1)S(1)}, u32[]{:S(2)}, u32[]{:S(2)}) collective-permute-start(bf16[272,128]{1,0:T(8,128)(2,1)S(1)} %get-tuple-element.27), channel_id=1, source_target_pairs={{0,12},{4,8},{8,4},{12,0},{16,28},{20,24},{24,20},{28,16},{1,13},{... | collective-permute-start | bytes 208904 | tf_op jit(solution)/shard_map/ppermute | solution.py:247
  14.9 3.7 %collective-permute-start.4 = (bf16[272,128]{1,0:T(8,128)(2,1)S(1)}, bf16[272,128]{1,0:T(8,128)(2,1)S(1)}, u32[]{:S(2)}, u32[]{:S(2)}) collective-permute-start(bf16[272,128]{1,0:T(8,128)(2,1)S(1)} %get-tuple-element.28), channel_id=1, source_target_pairs={{0,8},{4,12},{8,0},{12,4},{16,24},{20,28},{24,16},{28,20},{1,9},{5... | collective-permute-start | bytes 208904 | tf_op jit(solution)/shard_map/ppermute | solution.py:247
  15.1 3.6 %collective-permute-start.5 = (bf16[272,128]{1,0:T(8,128)(2,1)S(1)}, bf16[272,128]{1,0:T(8,128)(2,1)S(1)}, u32[]{:S(2)}, u32[]{:S(2)}) collective-permute-start(bf16[272,128]{1,0:T(8,128)(2,1)S(1)} %get-tuple-element.29), channel_id=1, source_target_pairs={{0,4},{4,0},{8,12},{12,8},{16,20},{20,16},{24,28},{28,24},{1,5},{5... | collective-permute-start | bytes 208904 | tf_op jit(solution)/shard_map/ppermute | solution.py:247
  15.3 6.0 %collective-permute-start = (bf16[272,128]{1,0:T(8,128)(2,1)S(1)}, bf16[272,128]{1,0:T(8,128)(2,1)S(1)}, u32[]{:S(2)}, u32[]{:S(2)}) collective-permute-start(bf16[272,128]{1,0:T(8,128)(2,1)S(1)} %get-tuple-element.23), channel_id=1, source_target_pairs={{0,12},{4,8},{8,4},{12,0},{16,28},{20,24},{24,20},{28,16},{1,13},{... | collective-permute-start | bytes 208904 | tf_op jit(solution)/shard_map/ppermute | solution.py:247
  17.5 4.0 %collective-permute-start.1 = (bf16[272,128]{1,0:T(8,128)(2,1)S(1)}, bf16[272,128]{1,0:T(8,128)(2,1)S(1)}, u32[]{:S(2)}, u32[]{:S(2)}) collective-permute-start(bf16[272,128]{1,0:T(8,128)(2,1)S(1)} %get-tuple-element.24), channel_id=1, source_target_pairs={{0,8},{4,12},{8,0},{12,4},{16,24},{20,28},{24,16},{28,20},{1,9},{5... | collective-permute-start | bytes 208904 | tf_op jit(solution)/shard_map/ppermute | solution.py:247
  17.7 4.0 %collective-permute-start.2 = (bf16[272,128]{1,0:T(8,128)(2,1)S(1)}, bf16[272,128]{1,0:T(8,128)(2,1)S(1)}, u32[]{:S(2)}, u32[]{:S(2)}) collective-permute-start(bf16[272,128]{1,0:T(8,128)(2,1)S(1)} %get-tuple-element.25), channel_id=1, source_target_pairs={{0,4},{4,0},{8,12},{12,8},{16,20},{20,16},{24,28},{28,24},{1,5},{5... | collective-permute-start | bytes 208904 | tf_op jit(solution)/shard_map/ppermute | solution.py:247
  18.6 2.4 %copy-start.1 = (f32[256,128]{1,0:T(8,128)S(1)}, f32[256,128]{1,0:T(8,128)}, u32[]{:S(2)}) copy-start(f32[256,128]{1,0:T(8,128)} %prev_hbm.1) | copy-start | bytes 393220
  18.7 4.2 %copy-start = (f32[256,128]{1,0:T(8,128)S(1)}, f32[256,128]{1,0:T(8,128)}, u32[]{:S(2)}) copy-start(f32[256,128]{1,0:T(8,128)} %now_ref.3) | copy-start | bytes 393220
  18.7 4.2 %collective-permute-start.6 = (bf16[272,128]{1,0:T(8,128)(2,1)S(1)}, bf16[272,128]{1,0:T(8,128)(2,1)S(1)}, u32[]{:S(2)}, u32[]{:S(2)}) collective-permute-start(bf16[272,128]{1,0:T(8,128)(2,1)S(1)} %mirror_sum.1), channel_id=1, source_target_pairs={{0,16},{4,20},{8,24},{12,28},{16,0},{20,4},{24,8},{28,12},{1,17},{... | collective-permute-start | bytes 208904 | tf_op jit(solution)/shard_map/ppermute | solution.py:247

commit v15 on v14

--- a/solution.py
+++ b/solution.py
@@ -33,7 +33,11 @@
 
 
 def distances(n):
-    return range(n - 1, -1, -1)
+    even = list(range(n - 1, 0, -1))
+    odd = list(even)
+    for k in range(1, len(odd) - 1, 2):
+        odd[k], odd[k + 1] = odd[k + 1], odd[k]
+    return list(zip(even, odd))
 
 
 def high_and_low(value):
@@ -103,7 +107,9 @@
         slab = total_ref[pl.ds(pl.multiple_of(row * rows_dev, rows_dev), rows_dev), :]
         return slab, early_ref[pl.ds(pl.multiple_of((row * n_col + my_col) * piece, piece), piece), :]
 
-    for step, mirror_ref, near_ref in zip(distances(half), mirror_refs, near_refs):
+    odd_col = lax.rem(my_col, 2) == 1
+    for (even, odd), mirror_ref, near_ref in zip(distances(half), mirror_refs, near_refs):
+        step = jnp.where(odd_col, odd, even)
         write_block(mirror_ref, *parts_of(my_row ^ (step + half)))
         write_block(near_ref, *parts_of(my_row ^ step))
     for row, ref in ((my_row ^ half, far_ref), (my_row, own_ref)):
@@ -156,7 +162,7 @@
 
 def eliminate(gram):
     width = gram.shape[0]
-    block, per_group = 16, 2
+    block, per_group = 16, 4
     lanes = lax.broadcasted_iota(jnp.int32, (block, width), 1)
     subs = lax.broadcasted_iota(jnp.int32, (block, width), 0)
 
@@ -241,10 +247,14 @@
     basis_ref[...] = dot3(residual, inverse, NT)
 
 
-def exchange(blocks, axis, steps):
-    n = lax.axis_size(axis)
-    assert n & (n - 1) == 0
-    return [lax.ppermute(block, axis, [(i, i ^ step) for i in range(n)]) for step, block in zip(steps, blocks)]
+def exchange(blocks, steps):
+    n_row, n_col = lax.axis_size("row"), lax.axis_size("col")
+    assert n_row & (n_row - 1) == 0
+    received = []
+    for step, block in zip(steps, blocks):
+        pairs = [(i * n_col + j, (i ^ step[j % 2]) * n_col + j) for i in range(n_row) for j in range(n_col)]
+        received.append(lax.ppermute(block, ("row", "col"), pairs))
+    return received
 
 
 def on_device(basis_now, basis_prev, coupling, tiles, tile_rows, tile_cols, tile_counts):
@@ -294,9 +304,9 @@
         compiler_params=params,
         name="tile_products",
     )(me, rows, cols, tile_counts, tile_block, gathered, coupling)
-    steps = distances(half)[:-1]
-    mirrors = exchange(blocks[: half - 1], "row", steps)
-    near = exchange(blocks[half - 1 :], "row", steps)
+    steps = distances(half)
+    mirrors = exchange(blocks[: half - 1], steps)
+    near = exchange(blocks[half - 1 :], steps)
     mirror = pl.pallas_call(
         functools.partial(mirror_kernel, rows_dev),
         out_shape=block,
@@ -305,7 +315,7 @@
         compiler_params=params,
         name="mirror_sum",
     )(far, *mirrors)
-    across = exchange([mirror], "row", [half])
+    across = exchange([mirror], [(half, half)])
 
     shift = pl.pallas_call(
         shift_kernel,

time: 55.1 us -> 56.2 us (1.020)
  Pallas kernels: 7.41 us -> 7.98 us
    pallas_call x1, Pallas kernels: 4.26 us -> 4.83 us  [on_device(): pl.pallas_call(functools.partial(final_kernel, total_rows), out_shape=(ja...]
  transfers between devices with their start and end apart: 7 -> 7, of which waited for: 4 -> 3; matrix products, arithmetic and copies ran while one was open for 0% -> 0% of each run, Pallas kernels for 0% -> 0%
where the time goes in v15:
time: 56.2 us; the launch traced here: 56 us
  blocking collectives  36.4 us (65%)
  starting transfers between devices  8.25 us (15%)
  Pallas kernels  7.98 us (14%)
  waiting for transfers between devices  1.89 us (3%)
  between operations  1.35 us (2%)
    all_to_all x1, blocking collectives, on_device(): lax.all_to_all(grams.reshape(devices, piece, width), everyone, split_axis...  16.7 us
    all_to_all x1, blocking collectives, on_device(): lax.all_to_all(copies, everyone, split_axis=0, concat_axis=0, tiled=True)  11 us
    all_gather x1, blocking collectives, on_device(): gathered = lax.all_gather(both, 'col', axis=0, tiled=True)  8.67 us
    ppermute x7, starting transfers between devices, exchange(): received.append(lax.ppermute(block, ('row', 'col'), pairs))  8.25 us
    pallas_call x1, Pallas kernels, on_device(): pl.pallas_call(functools.partial(final_kernel, total_rows), out_shape=(ja...  4.83 us
    ppermute x7, waiting for transfers between devices, exchange(): received.append(lax.ppermute(block, ('row', 'col'), pairs))  1.89 us
    pallas_call x1, Pallas kernels, on_device(): pl.pallas_call(functools.partial(tiles_kernel, n_row, n_col, total_rows),...  1.27 us
    pallas_call x1, Pallas kernels, on_device(): pl.pallas_call(prepare_kernel, out_shape=(jax.ShapeDtypeStruct((2 * rows_...  1.26 us
  transfers between devices with their start and end apart: 7, of which 3 were waited for; matrix products, arithmetic and copies ran while one was open for 0% of the time, Pallas kernels for 0%

profile of v15, /device:TPU:1, one launch (start us, length us, event | category | flops | bytes accessed | tf_op | source)
XLA Modules:
  0.0 56.0 jit_solution(17289550485108878128)
XLA Ops:
  0.6 1.3 %prepare.1 = (bf16[512,128]{1,0:T(8,128)(2,1)S(1)}, s32[1,1,16]{2,1,0:T(1,128)S(1)}, s32[1,1,16]{2,1,0:T(1,128)S(1)}, bf16[16,128,128]{2,1,0:T(8,128)(2,1)S(1)}) custom-call(f32[256,128]{1,0:T(8,128)} %now_ref.3, f32[256,128]{1,0:T(8,128)} %prev_hbm.1, s32[1,1,16]{2,1,0:T(1,128)} %rows_hbm.1, s32[1,1,16]{2,1,0:T(1,128)} %cols_hbm.1, ...), custom_call_target="tpu_custom_call" | custom-call | tf_op jit(solution)/shard_map/prepare/pallas_call | solution.py:272
  1.9 0.0 copy-start.2
  1.9 8.7 %all_gather.3.basis_ref = bf16[2048,128]{1,0:T(8,128)(2,1)S(1)} all-gather(bf16[512,128]{1,0:T(8,128)(2,1)S(1)} %get-tuple-element.21), channel_id=1, replica_groups=mesh['row'=8,'col'=4] {'col'}, dimensions={0}, use_global_device_ids=true | all-gather | bytes 655360 | tf_op jit(solution)/shard_map/all_gather | solution.py:290
  11.2 0.1 pad_add_fusion.me_ref
  11.3 0.0 copy-done.2
  11.3 1.3 %tile_products.1 = (bf16[272,128]{1,0:T(8,128)(2,1)S(1)}, bf16[272,128]{1,0:T(8,128)(2,1)S(1)}, bf16[272,128]{1,0:T(8,128)(2,1)S(1)}, bf16[272,128]{1,0:T(8,128)...) custom-call(s32[2]{0:T(128)S(1)} %pad_add_fusion.me_ref, ...), custom_call_target="tpu_custom_call" | custom-call | tf_op jit(solution)/shard_map/tile_products/pallas_call | solution.py:295
  12.6 2.3 %collective-permute-start.3 = (bf16[272,128]{1,0:T(8,128)(2,1)S(1)}, bf16[272,128]{1,0:T(8,128)(2,1)S(1)}, u32[]{:S(2)}, u32[]{:S(2)}) collective-permute-start(bf16[272,128]{1,0:T(8,128)(2,1)S(1)} %get-tuple-element.27), channel_id=1, source_target_pairs={{0,12},{1,13},{2,14},{3,15},{4,8},{5,9},{6,10},{7,11},{8,4},{9,5},... | collective-permute-start | bytes 208904 | tf_op jit(solution)/shard_map/ppermute | solution.py:256
  14.9 0.3 collective-permute-start.4
  15.1 0.2 collective-permute-start.5
  15.3 2.2 %collective-permute-start = (bf16[272,128]{1,0:T(8,128)(2,1)S(1)}, bf16[272,128]{1,0:T(8,128)(2,1)S(1)}, u32[]{:S(2)}, u32[]{:S(2)}) collective-permute-start(bf16[272,128]{1,0:T(8,128)(2,1)S(1)} %get-tuple-element.23), channel_id=1, source_target_pairs={{0,12},{1,13},{2,14},{3,15},{4,8},{5,9},{6,10},{7,11},{8,4},{9,5},... | collective-permute-start | bytes 208904 | tf_op jit(solution)/shard_map/ppermute | solution.py:256
  17.5 0.3 collective-permute-start.1
  17.8 0.0 collective-permute-done.3.refs_0_
  17.8 0.7 %collective-permute-start.2 = (bf16[272,128]{1,0:T(8,128)(2,1)S(1)}, bf16[272,128]{1,0:T(8,128)(2,1)S(1)}, u32[]{:S(2)}, u32[]{:S(2)}) collective-permute-start(bf16[272,128]{1,0:T(8,128)(2,1)S(1)} %get-tuple-element.25), channel_id=1, source_target_pairs={{0,4},{1,9},{2,6},{3,11},{4,0},{5,13},{6,2},{7,15},{8,12},{9,1},{1... | collective-permute-start | bytes 208904 | tf_op jit(solution)/shard_map/ppermute | solution.py:256
  18.5 0.0 collective-permute-done.4.refs_1_
  18.5 0.2 collective-permute-done.5.refs_2_
  18.7 0.0 copy-start.1
  18.8 0.0 copy-start
  18.8 2.4 %collective-permute-start.6 = (bf16[272,128]{1,0:T(8,128)(2,1)S(1)}, bf16[272,128]{1,0:T(8,128)(2,1)S(1)}, u32[]{:S(2)}, u32[]{:S(2)}) collective-permute-start(bf16[272,128]{1,0:T(8,128)(2,1)S(1)} %mirror_sum.1), channel_id=1, source_target_pairs={{0,16},{1,17},{2,18},{3,19},{4,20},{5,21},{6,22},{7,23},{8,24},{9,... | collective-permute-start | bytes 208904 | tf_op jit(solution)/shard_map/ppermute | solution.py:256
  21.2 0.0 copy-done.1
  21.2 0.2 shift_by_previous.1.shift_ref
  21.4 0.0 collective-permute-done.refs_0_
  21.4 0.8 %collective-permute-done.1.refs_1_ = bf16[272,128]{1,0:T(8,128)(2,1)S(1)} collective-permute-done((bf16[272,128]{1,0:T(8,128)(2,1)S(1)}, bf16[272,128]{1,0:T(8,128)(2,1)S(1)}, u32[]{:S(2)}, u32[]{:S(2)}) %collective-permute-start.1) | collective-permute-done | bytes 69664 | tf_op jit(solution)/shard_map/ppermute | solution.py:256
  22.2 0.0 collective-permute-done.2.refs_2_
  22.2 0.8 %collective-permute-done.6.refs_3_ = bf16[272,128]{1,0:T(8,128)(2,1)S(1)} collective-permute-done((bf16[272,128]{1,0:T(8,128)(2,1)S(1)}, bf16[272,128]{1,0:T(8,128)(2,1)S(1)}, u32[]{:S(2)}, u32[]{:S(2)}) %collective-permute-start.6) | collective-permute-done | bytes 69664 | tf_op jit(solution)/shard_map/ppermute | solution.py:256
  23.0 0.0 copy-done
  23.0 0.3 local_grams.1
  23.4 16.7 %all_to_all.10.parts_ref = f32[32,8,128]{2,1,0:T(8,128)S(1)} all-to-all(f32[32,8,128]{2,1,0:T(8,128)S(1)} %bitcast.4), channel_id=1, replica_groups=mesh['row'=8,'col'=4] {'row','col'}, dimensions={0} | all-to-all | bytes 262144 | tf_op jit(solution)/shard_map/all_to_all | solution.py:342
  40.1 0.1 sum_and_spread.1
  40.1 11.0 %all_to_all.11.pieces_ref = bf16[32,24,128]{2,1,0:T(8,128)(2,1)S(1)} all-to-all(bf16[32,24,128]{2,1,0:T(8,128)(2,1)S(1)} %sum_and_spread.1), channel_id=1, replica_groups=mesh['row'=8,'col'=4] {'row','col'}, dimensions={0} | all-to-all | bytes 393216 | tf_op jit(solution)/shard_map/all_to_all | solution.py:351
  51.2 4.8 %factor_and_basis.1 = (f32[256,128]{1,0:T(8,128)}, f32[128,128]{1,0:T(8,128)}, f32[128,128]{1,0:T(8,128)}) custom-call(bf16[32,24,128]{2,1,0:T(8,128)(2,1)S(1)} %all_to_all.11.pieces_ref, f32[256,128]{1,0:T(8,128)S(1)} %copy-done, f32[256,128]{1,0:T(8,128)S(1)} %get-tuple-element.32.shifted_ref), custom_call_target="tpu_custom_call" | custom-call | tf_op jit(solution)/shard_map/factor_and_basis/pallas_call | solution.py:352
  (1 shorter events, 0.0 us)
Async XLA Ops:
  1.9 9.4 %copy-start.2 = (f32[128,128]{1,0:T(8,128)S(1)}, f32[128,128]{1,0:T(8,128)}, u32[]{:S(2)}) copy-start(f32[128,128]{1,0:T(8,128)} %coupling_ref.3) | copy-start | bytes 196612
  12.6 5.2 %collective-permute-start.3 = (bf16[272,128]{1,0:T(8,128)(2,1)S(1)}, bf16[272,128]{1,0:T(8,128)(2,1)S(1)}, u32[]{:S(2)}, u32[]{:S(2)}) collective-permute-start(bf16[272,128]{1,0:T(8,128)(2,1)S(1)} %get-tuple-element.27), channel_id=1, source_target_pairs={{0,12},{1,13},{2,14},{3,15},{4,8},{5,9},{6,10},{7,11},{8,4},{9,5},... | collective-permute-start | bytes 208904 | tf_op jit(solution)/shard_map/ppermute | solution.py:256
  14.9 3.6 %collective-permute-start.4 = (bf16[272,128]{1,0:T(8,128)(2,1)S(1)}, bf16[272,128]{1,0:T(8,128)(2,1)S(1)}, u32[]{:S(2)}, u32[]{:S(2)}) collective-permute-start(bf16[272,128]{1,0:T(8,128)(2,1)S(1)} %get-tuple-element.28), channel_id=1, source_target_pairs={{0,8},{1,5},{2,10},{3,7},{4,12},{5,1},{6,14},{7,3},{8,0},{9,13},{1... | collective-permute-start | bytes 208904 | tf_op jit(solution)/shard_map/ppermute | solution.py:256
  15.1 3.6 %collective-permute-start.5 = (bf16[272,128]{1,0:T(8,128)(2,1)S(1)}, bf16[272,128]{1,0:T(8,128)(2,1)S(1)}, u32[]{:S(2)}, u32[]{:S(2)}) collective-permute-start(bf16[272,128]{1,0:T(8,128)(2,1)S(1)} %get-tuple-element.29), channel_id=1, source_target_pairs={{0,4},{1,9},{2,6},{3,11},{4,0},{5,13},{6,2},{7,15},{8,12},{9,1},{1... | collective-permute-start | bytes 208904 | tf_op jit(solution)/shard_map/ppermute | solution.py:256
  15.3 6.1 %collective-permute-start = (bf16[272,128]{1,0:T(8,128)(2,1)S(1)}, bf16[272,128]{1,0:T(8,128)(2,1)S(1)}, u32[]{:S(2)}, u32[]{:S(2)}) collective-permute-start(bf16[272,128]{1,0:T(8,128)(2,1)S(1)} %get-tuple-element.23), channel_id=1, source_target_pairs={{0,12},{1,13},{2,14},{3,15},{4,8},{5,9},{6,10},{7,11},{8,4},{9,5},... | collective-permute-start | bytes 208904 | tf_op jit(solution)/shard_map/ppermute | solution.py:256
  17.5 4.7 %collective-permute-start.1 = (bf16[272,128]{1,0:T(8,128)(2,1)S(1)}, bf16[272,128]{1,0:T(8,128)(2,1)S(1)}, u32[]{:S(2)}, u32[]{:S(2)}) collective-permute-start(bf16[272,128]{1,0:T(8,128)(2,1)S(1)} %get-tuple-element.24), channel_id=1, source_target_pairs={{0,8},{1,5},{2,10},{3,7},{4,12},{5,1},{6,14},{7,3},{8,0},{9,13},{1... | collective-permute-start | bytes 208904 | tf_op jit(solution)/shard_map/ppermute | solution.py:256
  17.8 4.4 %collective-permute-start.2 = (bf16[272,128]{1,0:T(8,128)(2,1)S(1)}, bf16[272,128]{1,0:T(8,128)(2,1)S(1)}, u32[]{:S(2)}, u32[]{:S(2)}) collective-permute-start(bf16[272,128]{1,0:T(8,128)(2,1)S(1)} %get-tuple-element.25), channel_id=1, source_target_pairs={{0,4},{1,9},{2,6},{3,11},{4,0},{5,13},{6,2},{7,15},{8,12},{9,1},{1... | collective-permute-start | bytes 208904 | tf_op jit(solution)/shard_map/ppermute | solution.py:256
  18.7 2.4 %copy-start.1 = (f32[256,128]{1,0:T(8,128)S(1)}, f32[256,128]{1,0:T(8,128)}, u32[]{:S(2)}) copy-start(f32[256,128]{1,0:T(8,128)} %prev_hbm.1) | copy-start | bytes 393220
  18.8 4.2 %copy-start = (f32[256,128]{1,0:T(8,128)S(1)}, f32[256,128]{1,0:T(8,128)}, u32[]{:S(2)}) copy-start(f32[256,128]{1,0:T(8,128)} %now_ref.3) | copy-start | bytes 393220
  18.8 4.2 %collective-permute-start.6 = (bf16[272,128]{1,0:T(8,128)(2,1)S(1)}, bf16[272,128]{1,0:T(8,128)(2,1)S(1)}, u32[]{:S(2)}, u32[]{:S(2)}) collective-permute-start(bf16[272,128]{1,0:T(8,128)(2,1)S(1)} %mirror_sum.1), channel_id=1, source_target_pairs={{0,16},{1,17},{2,18},{3,19},{4,20},{5,21},{6,22},{7,23},{8,24},{9,... | collective-permute-start | bytes 208904 | tf_op jit(solution)/shard_map/ppermute | solution.py:256

commit v16 on v14

--- a/solution.py
+++ b/solution.py
@@ -33,7 +33,7 @@
 
 
 def distances(n):
-    return range(n - 1, -1, -1)
+    return [1, *range(n - 1, 1, -1)]
 
 
 def high_and_low(value):
@@ -113,14 +113,14 @@
 def write_block(ref, slab, early):
     rows_dev = slab.shape[0]
     ref[:rows_dev, :] = slab.astype(BF16)
-    ref[rows_dev:, :] = high_and_low(early)
+    ref[rows_dev:, :] = early.astype(BF16)
 
 
 def add_blocks(own_ref, block_refs, rows_dev):
     slab, early = own_ref[:rows_dev, :], own_ref[rows_dev:, :]
     for ref in block_refs:
         slab = slab + ref[:rows_dev, :].astype(F32)
-        early = early + sum_high_and_low(ref[rows_dev:, :])
+        early = early + ref[rows_dev:, :].astype(F32)
     return slab, early
 
 
@@ -280,7 +280,7 @@
     gathered = lax.all_gather(both, "col", axis=0, tiled=True)
     me = jnp.stack([lax.axis_index("row"), lax.axis_index("col")])
     half = n_row // 2
-    block = jax.ShapeDtypeStruct((rows_dev + 2 * piece, width), BF16)
+    block = jax.ShapeDtypeStruct((rows_dev + piece, width), BF16)
     sums = jax.ShapeDtypeStruct((rows_dev + piece, width), F32)
     *blocks, far, own = pl.pallas_call(
         functools.partial(tiles_kernel, n_row, n_col, total_rows),
@@ -294,7 +294,7 @@
         compiler_params=params,
         name="tile_products",
     )(me, rows, cols, tile_counts, tile_block, gathered, coupling)
-    steps = distances(half)[:-1]
+    steps = distances(half)
     mirrors = exchange(blocks[: half - 1], "row", steps)
     near = exchange(blocks[half - 1 :], "row", steps)
     mirror = pl.pallas_call(

time: 55.1 us -> 55.1 us (level)
  waiting for transfers between devices: 1.86 us -> 2.53 us
    ppermute x7, waiting for transfers between devices: 1.86 us -> 2.53 us  [exchange(): lax.ppermute(block, axis, [(i, i ^ step) for i in range(n)])]
  transfers between devices with their start and end apart: 7 -> 7, of which waited for: 4 -> 2; matrix products, arithmetic and copies ran while one was open for 0% -> 0% of each run, Pallas kernels for 0% -> 0%
where the time goes in v16:
time: 55.1 us; the launch traced here: 54.9 us
  blocking collectives  35.8 us (65%)
  starting transfers between devices  7.74 us (14%)
  Pallas kernels  7.4 us (13%)
  waiting for transfers between devices  2.53 us (5%)
  between operations  1.37 us (2%)
    all_to_all x1, blocking collectives, on_device(): lax.all_to_all(grams.reshape(devices, piece, width), everyone, split_axis...  16.1 us
    all_to_all x1, blocking collectives, on_device(): lax.all_to_all(copies, everyone, split_axis=0, concat_axis=0, tiled=True)  11 us
    all_gather x1, blocking collectives, on_device(): gathered = lax.all_gather(both, 'col', axis=0, tiled=True)  8.67 us
    ppermute x7, starting transfers between devices, exchange(): lax.ppermute(block, axis, [(i, i ^ step) for i in range(n)])  7.74 us
    pallas_call x1, Pallas kernels, on_device(): pl.pallas_call(functools.partial(final_kernel, total_rows), out_shape=(ja...  4.26 us
    ppermute x7, waiting for transfers between devices, exchange(): lax.ppermute(block, axis, [(i, i ^ step) for i in range(n)])  2.53 us
    pallas_call x1, Pallas kernels, on_device(): pl.pallas_call(functools.partial(tiles_kernel, n_row, n_col, total_rows),...  1.27 us
    pallas_call x1, Pallas kernels, on_device(): pl.pallas_call(prepare_kernel, out_shape=(jax.ShapeDtypeStruct((2 * rows_...  1.26 us
  transfers between devices with their start and end apart: 7, of which 2 were waited for; matrix products, arithmetic and copies ran while one was open for 0% of the time, Pallas kernels for 0%

profile of v16, /device:TPU:1, one launch (start us, length us, event | category | flops | bytes accessed | tf_op | source)
XLA Modules:
  0.0 54.9 jit_solution(2869062919540448577)
XLA Ops:
  0.6 1.3 %prepare.1 = (bf16[512,128]{1,0:T(8,128)(2,1)S(1)}, s32[1,1,16]{2,1,0:T(1,128)S(1)}, s32[1,1,16]{2,1,0:T(1,128)S(1)}, bf16[16,128,128]{2,1,0:T(8,128)(2,1)S(1)}) custom-call(f32[256,128]{1,0:T(8,128)} %now_ref.3, f32[256,128]{1,0:T(8,128)} %prev_hbm.1, s32[1,1,16]{2,1,0:T(1,128)} %rows_hbm.1, s32[1,1,16]{2,1,0:T(1,128)} %cols_hbm.1, ...), custom_call_target="tpu_custom_call" | custom-call | tf_op jit(solution)/shard_map/prepare/pallas_call | solution.py:262
  1.9 0.0 copy-start.2
  1.9 8.7 %all_gather.3.basis_ref = bf16[2048,128]{1,0:T(8,128)(2,1)S(1)} all-gather(bf16[512,128]{1,0:T(8,128)(2,1)S(1)} %get-tuple-element.21), channel_id=1, replica_groups=mesh['row'=8,'col'=4] {'col'}, dimensions={0}, use_global_device_ids=true | all-gather | bytes 655360 | tf_op jit(solution)/shard_map/all_gather | solution.py:280
  11.2 0.1 pad_add_fusion.me_ref
  11.3 0.0 copy-done.2
  11.3 1.3 %tile_products.1 = (bf16[264,128]{1,0:T(8,128)(2,1)S(1)}, bf16[264,128]{1,0:T(8,128)(2,1)S(1)}, bf16[264,128]{1,0:T(8,128)(2,1)S(1)}, bf16[264,128]{1,0:T(8,128)...) custom-call(s32[2]{0:T(128)S(1)} %pad_add_fusion.me_ref, ...), custom_call_target="tpu_custom_call" | custom-call | tf_op jit(solution)/shard_map/tile_products/pallas_call | solution.py:285
  12.6 1.3 %collective-permute-start.3 = (bf16[264,128]{1,0:T(8,128)(2,1)S(1)}, bf16[264,128]{1,0:T(8,128)(2,1)S(1)}, u32[]{:S(2)}, u32[]{:S(2)}) collective-permute-start(bf16[264,128]{1,0:T(8,128)(2,1)S(1)} %get-tuple-element.27), channel_id=1, source_target_pairs={{0,4},{4,0},{8,12},{12,8},{16,20},{20,16},{24,28},{28,24},{1,5},{5... | collective-permute-start | bytes 202760 | tf_op jit(solution)/shard_map/ppermute | solution.py:247
  13.9 1.3 %collective-permute-start.4 = (bf16[264,128]{1,0:T(8,128)(2,1)S(1)}, bf16[264,128]{1,0:T(8,128)(2,1)S(1)}, u32[]{:S(2)}, u32[]{:S(2)}) collective-permute-start(bf16[264,128]{1,0:T(8,128)(2,1)S(1)} %get-tuple-element.28), channel_id=1, source_target_pairs={{0,12},{4,8},{8,4},{12,0},{16,28},{20,24},{24,20},{28,16},{1,13},{... | collective-permute-start | bytes 202760 | tf_op jit(solution)/shard_map/ppermute | solution.py:247
  15.1 0.2 collective-permute-start.5
  15.3 1.2 %collective-permute-start = (bf16[264,128]{1,0:T(8,128)(2,1)S(1)}, bf16[264,128]{1,0:T(8,128)(2,1)S(1)}, u32[]{:S(2)}, u32[]{:S(2)}) collective-permute-start(bf16[264,128]{1,0:T(8,128)(2,1)S(1)} %get-tuple-element.23), channel_id=1, source_target_pairs={{0,4},{4,0},{8,12},{12,8},{16,20},{20,16},{24,28},{28,24},{1,5},{5... | collective-permute-start | bytes 202760 | tf_op jit(solution)/shard_map/ppermute | solution.py:247
  16.5 1.3 %collective-permute-start.1 = (bf16[264,128]{1,0:T(8,128)(2,1)S(1)}, bf16[264,128]{1,0:T(8,128)(2,1)S(1)}, u32[]{:S(2)}, u32[]{:S(2)}) collective-permute-start(bf16[264,128]{1,0:T(8,128)(2,1)S(1)} %get-tuple-element.24), channel_id=1, source_target_pairs={{0,12},{4,8},{8,4},{12,0},{16,28},{20,24},{24,20},{28,16},{1,13},{... | collective-permute-start | bytes 202760 | tf_op jit(solution)/shard_map/ppermute | solution.py:247
  17.8 0.0 collective-permute-done.3.refs_0_
  17.8 0.2 collective-permute-start.2
  18.0 0.0 collective-permute-done.4.refs_1_
  18.0 0.9 %collective-permute-done.5.refs_2_ = bf16[264,128]{1,0:T(8,128)(2,1)S(1)} collective-permute-done((bf16[264,128]{1,0:T(8,128)(2,1)S(1)}, bf16[264,128]{1,0:T(8,128)(2,1)S(1)}, u32[]{:S(2)}, u32[]{:S(2)}) %collective-permute-start.5) | collective-permute-done | bytes 67616 | tf_op jit(solution)/shard_map/ppermute | solution.py:247
  18.9 0.0 copy-start.1
  18.9 0.0 copy-start
  19.0 2.4 %collective-permute-start.6 = (bf16[264,128]{1,0:T(8,128)(2,1)S(1)}, bf16[264,128]{1,0:T(8,128)(2,1)S(1)}, u32[]{:S(2)}, u32[]{:S(2)}) collective-permute-start(bf16[264,128]{1,0:T(8,128)(2,1)S(1)} %mirror_sum.1), channel_id=1, source_target_pairs={{0,16},{4,20},{8,24},{12,28},{16,0},{20,4},{24,8},{28,12},{1,17},{... | collective-permute-start | bytes 202760 | tf_op jit(solution)/shard_map/ppermute | solution.py:247
  21.3 0.0 copy-done.1
  21.3 0.2 shift_by_previous.1.shift_ref
  21.6 0.0 collective-permute-done.refs_0_
  21.6 0.0 collective-permute-done.1.refs_1_
  21.6 0.0 collective-permute-done.2.refs_2_
  21.6 1.6 %collective-permute-done.6.refs_3_ = bf16[264,128]{1,0:T(8,128)(2,1)S(1)} collective-permute-done((bf16[264,128]{1,0:T(8,128)(2,1)S(1)}, bf16[264,128]{1,0:T(8,128)(2,1)S(1)}, u32[]{:S(2)}, u32[]{:S(2)}) %collective-permute-start.6) | collective-permute-done | bytes 67616 | tf_op jit(solution)/shard_map/ppermute | solution.py:247
  23.2 0.0 copy-done
  23.2 0.3 local_grams.1
  23.5 16.1 %all_to_all.10.parts_ref = f32[32,8,128]{2,1,0:T(8,128)S(1)} all-to-all(f32[32,8,128]{2,1,0:T(8,128)S(1)} %bitcast.4), channel_id=1, replica_groups=mesh['row'=8,'col'=4] {'row','col'}, dimensions={0} | all-to-all | bytes 262144 | tf_op jit(solution)/shard_map/all_to_all | solution.py:332
  39.5 0.1 sum_and_spread.1
  39.6 11.0 %all_to_all.11.pieces_ref = bf16[32,24,128]{2,1,0:T(8,128)(2,1)S(1)} all-to-all(bf16[32,24,128]{2,1,0:T(8,128)(2,1)S(1)} %sum_and_spread.1), channel_id=1, replica_groups=mesh['row'=8,'col'=4] {'row','col'}, dimensions={0} | all-to-all | bytes 393216 | tf_op jit(solution)/shard_map/all_to_all | solution.py:341
  50.6 4.3 %factor_and_basis.1 = (f32[256,128]{1,0:T(8,128)}, f32[128,128]{1,0:T(8,128)}, f32[128,128]{1,0:T(8,128)}) custom-call(bf16[32,24,128]{2,1,0:T(8,128)(2,1)S(1)} %all_to_all.11.pieces_ref, f32[256,128]{1,0:T(8,128)S(1)} %copy-done, f32[256,128]{1,0:T(8,128)S(1)} %get-tuple-element.32.shifted_ref), custom_call_target="tpu_custom_call" | custom-call | tf_op jit(solution)/shard_map/factor_and_basis/pallas_call | solution.py:342
  (1 shorter events, 0.0 us)
Async XLA Ops:
  1.9 9.4 %copy-start.2 = (f32[128,128]{1,0:T(8,128)S(1)}, f32[128,128]{1,0:T(8,128)}, u32[]{:S(2)}) copy-start(f32[128,128]{1,0:T(8,128)} %coupling_ref.3) | copy-start | bytes 196612
  12.6 5.2 %collective-permute-start.3 = (bf16[264,128]{1,0:T(8,128)(2,1)S(1)}, bf16[264,128]{1,0:T(8,128)(2,1)S(1)}, u32[]{:S(2)}, u32[]{:S(2)}) collective-permute-start(bf16[264,128]{1,0:T(8,128)(2,1)S(1)} %get-tuple-element.27), channel_id=1, source_target_pairs={{0,4},{4,0},{8,12},{12,8},{16,20},{20,16},{24,28},{28,24},{1,5},{5... | collective-permute-start | bytes 202760 | tf_op jit(solution)/shard_map/ppermute | solution.py:247
  13.9 4.1 %collective-permute-start.4 = (bf16[264,128]{1,0:T(8,128)(2,1)S(1)}, bf16[264,128]{1,0:T(8,128)(2,1)S(1)}, u32[]{:S(2)}, u32[]{:S(2)}) collective-permute-start(bf16[264,128]{1,0:T(8,128)(2,1)S(1)} %get-tuple-element.28), channel_id=1, source_target_pairs={{0,12},{4,8},{8,4},{12,0},{16,28},{20,24},{24,20},{28,16},{1,13},{... | collective-permute-start | bytes 202760 | tf_op jit(solution)/shard_map/ppermute | solution.py:247
  15.1 3.8 %collective-permute-start.5 = (bf16[264,128]{1,0:T(8,128)(2,1)S(1)}, bf16[264,128]{1,0:T(8,128)(2,1)S(1)}, u32[]{:S(2)}, u32[]{:S(2)}) collective-permute-start(bf16[264,128]{1,0:T(8,128)(2,1)S(1)} %get-tuple-element.29), channel_id=1, source_target_pairs={{0,8},{4,12},{8,0},{12,4},{16,24},{20,28},{24,16},{28,20},{1,9},{5... | collective-permute-start | bytes 202760 | tf_op jit(solution)/shard_map/ppermute | solution.py:247
  15.3 6.2 %collective-permute-start = (bf16[264,128]{1,0:T(8,128)(2,1)S(1)}, bf16[264,128]{1,0:T(8,128)(2,1)S(1)}, u32[]{:S(2)}, u32[]{:S(2)}) collective-permute-start(bf16[264,128]{1,0:T(8,128)(2,1)S(1)} %get-tuple-element.23), channel_id=1, source_target_pairs={{0,4},{4,0},{8,12},{12,8},{16,20},{20,16},{24,28},{28,24},{1,5},{5... | collective-permute-start | bytes 202760 | tf_op jit(solution)/shard_map/ppermute | solution.py:247
  16.5 5.0 %collective-permute-start.1 = (bf16[264,128]{1,0:T(8,128)(2,1)S(1)}, bf16[264,128]{1,0:T(8,128)(2,1)S(1)}, u32[]{:S(2)}, u32[]{:S(2)}) collective-permute-start(bf16[264,128]{1,0:T(8,128)(2,1)S(1)} %get-tuple-element.24), channel_id=1, source_target_pairs={{0,12},{4,8},{8,4},{12,0},{16,28},{20,24},{24,20},{28,16},{1,13},{... | collective-permute-start | bytes 202760 | tf_op jit(solution)/shard_map/ppermute | solution.py:247
  17.8 3.8 %collective-permute-start.2 = (bf16[264,128]{1,0:T(8,128)(2,1)S(1)}, bf16[264,128]{1,0:T(8,128)(2,1)S(1)}, u32[]{:S(2)}, u32[]{:S(2)}) collective-permute-start(bf16[264,128]{1,0:T(8,128)(2,1)S(1)} %get-tuple-element.25), channel_id=1, source_target_pairs={{0,8},{4,12},{8,0},{12,4},{16,24},{20,28},{24,16},{28,20},{1,9},{5... | collective-permute-start | bytes 202760 | tf_op jit(solution)/shard_map/ppermute | solution.py:247
  18.9 2.4 %copy-start.1 = (f32[256,128]{1,0:T(8,128)S(1)}, f32[256,128]{1,0:T(8,128)}, u32[]{:S(2)}) copy-start(f32[256,128]{1,0:T(8,128)} %prev_hbm.1) | copy-start | bytes 393220
  18.9 4.2 %copy-start = (f32[256,128]{1,0:T(8,128)S(1)}, f32[256,128]{1,0:T(8,128)}, u32[]{:S(2)}) copy-start(f32[256,128]{1,0:T(8,128)} %now_ref.3) | copy-start | bytes 393220
  19.0 4.2 %collective-permute-start.6 = (bf16[264,128]{1,0:T(8,128)(2,1)S(1)}, bf16[264,128]{1,0:T(8,128)(2,1)S(1)}, u32[]{:S(2)}, u32[]{:S(2)}) collective-permute-start(bf16[264,128]{1,0:T(8,128)(2,1)S(1)} %mirror_sum.1), channel_id=1, source_target_pairs={{0,16},{4,20},{8,24},{12,28},{16,0},{20,4},{24,8},{28,12},{1,17},{... | collective-permute-start | bytes 202760 | tf_op jit(solution)/shard_map/ppermute | solution.py:247

commit v17 on v16

--- a/solution.py
+++ b/solution.py
@@ -296,7 +296,7 @@
     )(me, rows, cols, tile_counts, tile_block, gathered, coupling)
     steps = distances(half)
     mirrors = exchange(blocks[: half - 1], "row", steps)
-    near = exchange(blocks[half - 1 :], "row", steps)
+    near = exchange(blocks[half - 1 : -1], "row", steps[:-1])
     mirror = pl.pallas_call(
         functools.partial(mirror_kernel, rows_dev),
         out_shape=block,
@@ -305,7 +305,9 @@
         compiler_params=params,
         name="mirror_sum",
     )(far, *mirrors)
+    mirror, last = lax.optimization_barrier((mirror, blocks[-1]))
     across = exchange([mirror], "row", [half])
+    near += exchange([last], "row", steps[-1:])
 
     shift = pl.pallas_call(
         shift_kernel,
@@ -327,7 +329,7 @@
         out_specs=(vmem, vmem, vmem),
         compiler_params=params,
         name="local_grams",
-    )(basis_now, shift, own, *near, *across)
+    )(basis_now, shift, own, *near[:-1], *across, near[-1])
     everyone = ("row", "col")
     pieces = lax.all_to_all(grams.reshape(devices, piece, width), everyone, split_axis=0, concat_axis=0, tiled=True)
     copies = pl.pallas_call(

time: 55.1 us -> 55.1 us (level)
  blocking collectives: 35.8 us -> 34.5 us
  starting transfers between devices: 7.74 us -> 8.52 us
    all_to_all x1, blocking collectives: 16.1 us -> 14.8 us  [on_device(): lax.all_to_all(grams.reshape(devices, piece, width), everyone, split_axis...]
    ppermute x7, starting transfers between devices: 7.74 us -> 8.52 us  [exchange(): lax.ppermute(block, axis, [(i, i ^ step) for i in range(n)])]
  transfers between devices with their start and end apart: 7 -> 7, of which waited for: 2 -> 4; matrix products, arithmetic and copies ran while one was open for 0% -> 0% of each run, Pallas kernels for 0% -> 0%
where the time goes in v17:
time: 55.1 us; the launch traced here: 54.9 us
  blocking collectives  34.5 us (63%)
  starting transfers between devices  8.52 us (15%)
  Pallas kernels  7.4 us (13%)
  waiting for transfers between devices  3.05 us (6%)
  between operations  1.37 us (2%)
    all_to_all x1, blocking collectives, on_device(): lax.all_to_all(grams.reshape(devices, piece, width), everyone, split_axis...  14.8 us
    all_to_all x1, blocking collectives, on_device(): lax.all_to_all(copies, everyone, split_axis=0, concat_axis=0, tiled=True)  11 us
    all_gather x1, blocking collectives, on_device(): gathered = lax.all_gather(both, 'col', axis=0, tiled=True)  8.67 us
    ppermute x7, starting transfers between devices, exchange(): lax.ppermute(block, axis, [(i, i ^ step) for i in range(n)])  8.52 us
    pallas_call x1, Pallas kernels, on_device(): pl.pallas_call(functools.partial(final_kernel, total_rows), out_shape=(ja...  4.26 us
    ppermute x7, waiting for transfers between devices, exchange(): lax.ppermute(block, axis, [(i, i ^ step) for i in range(n)])  3.05 us
    pallas_call x1, Pallas kernels, on_device(): pl.pallas_call(functools.partial(tiles_kernel, n_row, n_col, total_rows),...  1.27 us
    pallas_call x1, Pallas kernels, on_device(): pl.pallas_call(prepare_kernel, out_shape=(jax.ShapeDtypeStruct((2 * rows_...  1.26 us
  transfers between devices with their start and end apart: 7, of which 4 were waited for; matrix products, arithmetic and copies ran while one was open for 0% of the time, Pallas kernels for 0%

profile of v17, /device:TPU:1, one launch (start us, length us, event | category | flops | bytes accessed | tf_op | source)
XLA Modules:
  0.0 54.9 jit_solution(13108222709352048964)
XLA Ops:
  0.6 1.3 %prepare.1 = (bf16[512,128]{1,0:T(8,128)(2,1)S(1)}, s32[1,1,16]{2,1,0:T(1,128)S(1)}, s32[1,1,16]{2,1,0:T(1,128)S(1)}, bf16[16,128,128]{2,1,0:T(8,128)(2,1)S(1)}) custom-call(f32[256,128]{1,0:T(8,128)} %now_ref.3, f32[256,128]{1,0:T(8,128)} %prev_hbm.1, s32[1,1,16]{2,1,0:T(1,128)} %rows_hbm.1, s32[1,1,16]{2,1,0:T(1,128)} %cols_hbm.1, ...), custom_call_target="tpu_custom_call" | custom-call | tf_op jit(solution)/shard_map/prepare/pallas_call | solution.py:262
  1.9 0.0 copy-start.2
  1.9 8.7 %all_gather.3.basis_ref = bf16[2048,128]{1,0:T(8,128)(2,1)S(1)} all-gather(bf16[512,128]{1,0:T(8,128)(2,1)S(1)} %get-tuple-element.23), channel_id=1, replica_groups=mesh['row'=8,'col'=4] {'col'}, dimensions={0}, use_global_device_ids=true | all-gather | bytes 655360 | tf_op jit(solution)/shard_map/all_gather | solution.py:280
  11.2 0.1 pad_add_fusion.me_ref
  11.3 0.0 copy-done.2
  11.3 1.3 %tile_products.1 = (bf16[264,128]{1,0:T(8,128)(2,1)S(1)}, bf16[264,128]{1,0:T(8,128)(2,1)S(1)}, bf16[264,128]{1,0:T(8,128)(2,1)S(1)}, bf16[264,128]{1,0:T(8,128)...) custom-call(s32[2]{0:T(128)S(1)} %pad_add_fusion.me_ref, ...), custom_call_target="tpu_custom_call" | custom-call | tf_op jit(solution)/shard_map/tile_products/pallas_call | solution.py:285
  12.6 1.3 %collective-permute-start.2 = (bf16[264,128]{1,0:T(8,128)(2,1)S(1)}, bf16[264,128]{1,0:T(8,128)(2,1)S(1)}, u32[]{:S(2)}, u32[]{:S(2)}) collective-permute-start(bf16[264,128]{1,0:T(8,128)(2,1)S(1)} %get-tuple-element.28), channel_id=1, source_target_pairs={{0,4},{4,0},{8,12},{12,8},{16,20},{20,16},{24,28},{28,24},{1,5},{5... | collective-permute-start | bytes 202760 | tf_op jit(solution)/shard_map/ppermute | solution.py:247
  13.9 1.3 %collective-permute-start.3 = (bf16[264,128]{1,0:T(8,128)(2,1)S(1)}, bf16[264,128]{1,0:T(8,128)(2,1)S(1)}, u32[]{:S(2)}, u32[]{:S(2)}) collective-permute-start(bf16[264,128]{1,0:T(8,128)(2,1)S(1)} %get-tuple-element.29), channel_id=1, source_target_pairs={{0,12},{4,8},{8,4},{12,0},{16,28},{20,24},{24,20},{28,16},{1,13},{... | collective-permute-start | bytes 202760 | tf_op jit(solution)/shard_map/ppermute | solution.py:247
  15.1 0.2 collective-permute-start.4
  15.3 1.2 %collective-permute-start = (bf16[264,128]{1,0:T(8,128)(2,1)S(1)}, bf16[264,128]{1,0:T(8,128)(2,1)S(1)}, u32[]{:S(2)}, u32[]{:S(2)}) collective-permute-start(bf16[264,128]{1,0:T(8,128)(2,1)S(1)} %get-tuple-element.25), channel_id=1, source_target_pairs={{0,4},{4,0},{8,12},{12,8},{16,20},{20,16},{24,28},{28,24},{1,5},{5... | collective-permute-start | bytes 202760 | tf_op jit(solution)/shard_map/ppermute | solution.py:247
  16.5 1.3 %collective-permute-start.1 = (bf16[264,128]{1,0:T(8,128)(2,1)S(1)}, bf16[264,128]{1,0:T(8,128)(2,1)S(1)}, u32[]{:S(2)}, u32[]{:S(2)}) collective-permute-start(bf16[264,128]{1,0:T(8,128)(2,1)S(1)} %get-tuple-element.26), channel_id=1, source_target_pairs={{0,12},{4,8},{8,4},{12,0},{16,28},{20,24},{24,20},{28,16},{1,13},{... | collective-permute-start | bytes 202760 | tf_op jit(solution)/shard_map/ppermute | solution.py:247
  17.8 0.0 collective-permute-done.2.refs_0_
  17.8 0.1 collective-permute-done.3.refs_1_
  17.9 1.0 %collective-permute-done.4.refs_2_ = bf16[264,128]{1,0:T(8,128)(2,1)S(1)} collective-permute-done((bf16[264,128]{1,0:T(8,128)(2,1)S(1)}, bf16[264,128]{1,0:T(8,128)(2,1)S(1)}, u32[]{:S(2)}, u32[]{:S(2)}) %collective-permute-start.4) | collective-permute-done | bytes 67616 | tf_op jit(solution)/shard_map/ppermute | solution.py:247
  18.9 0.0 copy-start.1
  18.9 0.0 copy-start
  19.0 2.4 %collective-permute-start.5 = (bf16[264,128]{1,0:T(8,128)(2,1)S(1)}, bf16[264,128]{1,0:T(8,128)(2,1)S(1)}, u32[]{:S(2)}, u32[]{:S(2)}) collective-permute-start(bf16[264,128]{1,0:T(8,128)(2,1)S(1)} %mirror_sum.1), channel_id=1, source_target_pairs={{0,16},{4,20},{8,24},{12,28},{16,0},{20,4},{24,8},{28,12},{1,17},{... | collective-permute-start | bytes 202760 | tf_op jit(solution)/shard_map/ppermute | solution.py:247
  21.3 1.0 %collective-permute-start.6 = (bf16[264,128]{1,0:T(8,128)(2,1)S(1)}, bf16[264,128]{1,0:T(8,128)(2,1)S(1)}, u32[]{:S(2)}, u32[]{:S(2)}) collective-permute-start(bf16[264,128]{1,0:T(8,128)(2,1)S(1)} %get-tuple-element.33), channel_id=1, source_target_pairs={{0,8},{4,12},{8,0},{12,4},{16,24},{20,28},{24,16},{28,20},{1,9},{5... | collective-permute-start | bytes 202760 | tf_op jit(solution)/shard_map/ppermute | solution.py:247
  22.3 0.0 copy-done.1
  22.3 0.2 shift_by_previous.1.shift_ref
  22.5 0.0 collective-permute-done.refs_0_
  22.5 0.0 collective-permute-done.1.refs_1_
  22.5 0.6 %collective-permute-done.5.refs_2_ = bf16[264,128]{1,0:T(8,128)(2,1)S(1)} collective-permute-done((bf16[264,128]{1,0:T(8,128)(2,1)S(1)}, bf16[264,128]{1,0:T(8,128)(2,1)S(1)}, u32[]{:S(2)}, u32[]{:S(2)}) %collective-permute-start.5) | collective-permute-done | bytes 67616 | tf_op jit(solution)/shard_map/ppermute | solution.py:247
  23.1 1.4 %collective-permute-done.6.refs_3_ = bf16[264,128]{1,0:T(8,128)(2,1)S(1)} collective-permute-done((bf16[264,128]{1,0:T(8,128)(2,1)S(1)}, bf16[264,128]{1,0:T(8,128)(2,1)S(1)}, u32[]{:S(2)}, u32[]{:S(2)}) %collective-permute-start.6) | collective-permute-done | bytes 67616 | tf_op jit(solution)/shard_map/ppermute | solution.py:247
  24.5 0.0 copy-done
  24.5 0.3 local_grams.1
  24.8 14.8 %all_to_all.10.parts_ref = f32[32,8,128]{2,1,0:T(8,128)S(1)} all-to-all(f32[32,8,128]{2,1,0:T(8,128)S(1)} %bitcast.4), channel_id=1, replica_groups=mesh['row'=8,'col'=4] {'row','col'}, dimensions={0} | all-to-all | bytes 262144 | tf_op jit(solution)/shard_map/all_to_all | solution.py:334
  39.5 0.1 sum_and_spread.1
  39.6 11.0 %all_to_all.11.pieces_ref = bf16[32,24,128]{2,1,0:T(8,128)(2,1)S(1)} all-to-all(bf16[32,24,128]{2,1,0:T(8,128)(2,1)S(1)} %sum_and_spread.1), channel_id=1, replica_groups=mesh['row'=8,'col'=4] {'row','col'}, dimensions={0} | all-to-all | bytes 393216 | tf_op jit(solution)/shard_map/all_to_all | solution.py:343
  50.6 4.3 %factor_and_basis.1 = (f32[256,128]{1,0:T(8,128)}, f32[128,128]{1,0:T(8,128)}, f32[128,128]{1,0:T(8,128)}) custom-call(bf16[32,24,128]{2,1,0:T(8,128)(2,1)S(1)} %all_to_all.11.pieces_ref, f32[256,128]{1,0:T(8,128)S(1)} %copy-done, f32[256,128]{1,0:T(8,128)S(1)} %get-tuple-element.36.shifted_ref), custom_call_target="tpu_custom_call" | custom-call | tf_op jit(solution)/shard_map/factor_and_basis/pallas_call | solution.py:344
  (1 shorter events, 0.0 us)
Async XLA Ops:
  1.9 9.4 %copy-start.2 = (f32[128,128]{1,0:T(8,128)S(1)}, f32[128,128]{1,0:T(8,128)}, u32[]{:S(2)}) copy-start(f32[128,128]{1,0:T(8,128)} %coupling_ref.3) | copy-start | bytes 196612
  12.6 5.2 %collective-permute-start.2 = (bf16[264,128]{1,0:T(8,128)(2,1)S(1)}, bf16[264,128]{1,0:T(8,128)(2,1)S(1)}, u32[]{:S(2)}, u32[]{:S(2)}) collective-permute-start(bf16[264,128]{1,0:T(8,128)(2,1)S(1)} %get-tuple-element.28), channel_id=1, source_target_pairs={{0,4},{4,0},{8,12},{12,8},{16,20},{20,16},{24,28},{28,24},{1,5},{5... | collective-permute-start | bytes 202760 | tf_op jit(solution)/shard_map/ppermute | solution.py:247
  13.9 4.1 %collective-permute-start.3 = (bf16[264,128]{1,0:T(8,128)(2,1)S(1)}, bf16[264,128]{1,0:T(8,128)(2,1)S(1)}, u32[]{:S(2)}, u32[]{:S(2)}) collective-permute-start(bf16[264,128]{1,0:T(8,128)(2,1)S(1)} %get-tuple-element.29), channel_id=1, source_target_pairs={{0,12},{4,8},{8,4},{12,0},{16,28},{20,24},{24,20},{28,16},{1,13},{... | collective-permute-start | bytes 202760 | tf_op jit(solution)/shard_map/ppermute | solution.py:247
  15.1 3.8 %collective-permute-start.4 = (bf16[264,128]{1,0:T(8,128)(2,1)S(1)}, bf16[264,128]{1,0:T(8,128)(2,1)S(1)}, u32[]{:S(2)}, u32[]{:S(2)}) collective-permute-start(bf16[264,128]{1,0:T(8,128)(2,1)S(1)} %get-tuple-element.30), channel_id=1, source_target_pairs={{0,8},{4,12},{8,0},{12,4},{16,24},{20,28},{24,16},{28,20},{1,9},{5... | collective-permute-start | bytes 202760 | tf_op jit(solution)/shard_map/ppermute | solution.py:247
  15.3 7.2 %collective-permute-start = (bf16[264,128]{1,0:T(8,128)(2,1)S(1)}, bf16[264,128]{1,0:T(8,128)(2,1)S(1)}, u32[]{:S(2)}, u32[]{:S(2)}) collective-permute-start(bf16[264,128]{1,0:T(8,128)(2,1)S(1)} %get-tuple-element.25), channel_id=1, source_target_pairs={{0,4},{4,0},{8,12},{12,8},{16,20},{20,16},{24,28},{28,24},{1,5},{5... | collective-permute-start | bytes 202760 | tf_op jit(solution)/shard_map/ppermute | solution.py:247
  16.5 6.0 %collective-permute-start.1 = (bf16[264,128]{1,0:T(8,128)(2,1)S(1)}, bf16[264,128]{1,0:T(8,128)(2,1)S(1)}, u32[]{:S(2)}, u32[]{:S(2)}) collective-permute-start(bf16[264,128]{1,0:T(8,128)(2,1)S(1)} %get-tuple-element.26), channel_id=1, source_target_pairs={{0,12},{4,8},{8,4},{12,0},{16,28},{20,24},{24,20},{28,16},{1,13},{... | collective-permute-start | bytes 202760 | tf_op jit(solution)/shard_map/ppermute | solution.py:247
  18.9 3.4 %copy-start.1 = (f32[256,128]{1,0:T(8,128)S(1)}, f32[256,128]{1,0:T(8,128)}, u32[]{:S(2)}) copy-start(f32[256,128]{1,0:T(8,128)} %prev_hbm.1) | copy-start | bytes 393220
  18.9 5.5 %copy-start = (f32[256,128]{1,0:T(8,128)S(1)}, f32[256,128]{1,0:T(8,128)}, u32[]{:S(2)}) copy-start(f32[256,128]{1,0:T(8,128)} %now_ref.3) | copy-start | bytes 393220
  19.0 4.1 %collective-permute-start.5 = (bf16[264,128]{1,0:T(8,128)(2,1)S(1)}, bf16[264,128]{1,0:T(8,128)(2,1)S(1)}, u32[]{:S(2)}, u32[]{:S(2)}) collective-permute-start(bf16[264,128]{1,0:T(8,128)(2,1)S(1)} %mirror_sum.1), channel_id=1, source_target_pairs={{0,16},{4,20},{8,24},{12,28},{16,0},{20,4},{24,8},{28,12},{1,17},{... | collective-permute-start | bytes 202760 | tf_op jit(solution)/shard_map/ppermute | solution.py:247
  21.3 3.1 %collective-permute-start.6 = (bf16[264,128]{1,0:T(8,128)(2,1)S(1)}, bf16[264,128]{1,0:T(8,128)(2,1)S(1)}, u32[]{:S(2)}, u32[]{:S(2)}) collective-permute-start(bf16[264,128]{1,0:T(8,128)(2,1)S(1)} %get-tuple-element.33), channel_id=1, source_target_pairs={{0,8},{4,12},{8,0},{12,4},{16,24},{20,28},{24,16},{28,20},{1,9},{5... | collective-permute-start | bytes 202760 | tf_op jit(solution)/shard_map/ppermute | solution.py:247

commit v18 on v17

--- a/solution.py
+++ b/solution.py
@@ -156,54 +156,70 @@
 
 def eliminate(gram):
     width = gram.shape[0]
-    block, per_group = 16, 2
-    lanes = lax.broadcasted_iota(jnp.int32, (block, width), 1)
-    subs = lax.broadcasted_iota(jnp.int32, (block, width), 0)
-
-    def column(strip, k):
-        return jnp.broadcast_to(strip[:, k : k + 1], (block, width))
-
-    def row(strip, k):
-        return jnp.broadcast_to(strip[k : k + 1, :], (block, width))
+    tall, block, per_group = 8, 16, 2
+    shape = (tall, width)
+    lanes = lax.broadcasted_iota(jnp.int32, shape, 1)
+    subs = lax.broadcasted_iota(jnp.int32, shape, 0)
+
+    def cut(strip):
+        return [strip[r : r + tall, :] for r in range(0, block, tall)]
+
+    def column(parts, k):
+        return [jnp.broadcast_to(part[:, k : k + 1], shape) for part in parts]
+
+    def row(parts, k):
+        part, k = parts[k // tall], k % tall
+        return jnp.broadcast_to(part[k : k + 1, :], shape)
 
     strips = [gram[r : r + block, :] for r in range(0, width, block)]
     finished = []
     for begin in range(0, len(strips), per_group):
-        group = strips[:per_group]
+        group = [cut(strip) for strip in strips[:per_group]]
         for at in range(per_group):
             first = (begin + at) * block
             panel = group[at]
             columns = [column(panel, first + j) for j in range(block)]
-            kept = panel
+            kept = list(panel)
             for j in range(0, block, 2):
-                here, there = subs == j, subs == j + 1
+                mine = j // tall
+                here, there = subs == j % tall, subs == j % tall + 1
                 both = here | there
                 lane, next_lane = lanes == first + j, lanes == first + j + 1
                 left, right = columns[j], columns[j + 1]
                 a, b, c = row(left, j), row(right, j), row(right, j + 1)
                 scale = 1.0 / (a * c - b * b)
-                by_top = jnp.where(here, -c, jnp.where(there, b, left * c - right * b))
-                by_bottom = jnp.where(here, b, jnp.where(there, -a, right * a - left * b))
+                by_top = [x * c - y * b for x, y in zip(left, right)]
+                by_bottom = [y * a - x * b for x, y in zip(left, right)]
+                by_top[mine] = jnp.where(here, -c, jnp.where(there, b, by_top[mine]))
+                by_bottom[mine] = jnp.where(here, b, jnp.where(there, -a, by_bottom[mine]))
+
+                def update(parts, up, down):
+                    rest = [jnp.where(both, 0.0, part) if k == mine else part for k, part in enumerate(parts)]
+                    return [x - (t * up + u * down) * scale for x, t, u in zip(rest, by_top, by_bottom)]
+
                 top, bottom = row(panel, j), row(panel, j + 1)
                 ratio = b / a
-                kept = jnp.where(here, top, jnp.where(there, bottom - ratio * jnp.where(lane, 1.0, top), kept))
-                kept = jnp.where(there & lane, -ratio, kept)
+                second = jnp.where(lane, -ratio, bottom - ratio * top)
+                kept[mine] = jnp.where(here, top, jnp.where(there, second, kept[mine]))
+                pair = lane | next_lane
                 top = jnp.where(lane, 1.0, jnp.where(next_lane, 0.0, top))
                 bottom = jnp.where(lane, 0.0, jnp.where(next_lane, 1.0, bottom))
-                panel = jnp.where(both | lane | next_lane, 0.0, panel) - (by_top * top + by_bottom * bottom) * scale
+                panel = update([jnp.where(pair, 0.0, part) for part in panel], top, bottom)
                 for m in range(j + 2, block):
-                    up, down = row(columns[m], j), row(columns[m], j + 1)
-                    columns[m] = jnp.where(both, 0.0, columns[m]) - (by_top * up + by_bottom * down) * scale
-            finished.append(kept)
+                    columns[m] = update(columns[m], row(columns[m], j), row(columns[m], j + 1))
+            finished += kept
             group[at] = panel
             rows = [row(panel, m) for m in range(block)]
             inside = (lanes >= first) & (lanes < first + block)
             for s in range(per_group):
                 if s != at:
-                    terms = [column(group[s], first + m) * rows[m] for m in range(block)]
-                    while len(terms) > 1:
-                        terms = [x + y for x, y in zip(terms[::2], terms[1::2])]
-                    group[s] = jnp.where(inside, 0.0, group[s]) - terms[0]
+                    factors = [column(group[s], first + m) for m in range(block)]
+                    for k in range(len(group[s])):
+                        terms = [factor[k] * value for factor, value in zip(factors, rows)]
+                        while len(terms) > 1:
+                            terms = [x + y for x, y in zip(terms[::2], terms[1::2])]
+                        group[s][k] = jnp.where(inside, 0.0, group[s][k]) - terms[0]
+        group = [jnp.concatenate(parts, axis=0) for parts in group]
         strips = strips[per_group:]
         if strips:
             first, last = begin * block, (begin + per_group) * block

time: 55.1 us -> 55.1 us (level)
  no operation moved by 1% of the time
where the time goes in v18:
time: 55.1 us; the launch traced here: 54.9 us
  blocking collectives  34.5 us (63%)
  starting transfers between devices  8.52 us (15%)
  Pallas kernels  7.38 us (13%)
  waiting for transfers between devices  3.05 us (6%)
  between operations  1.37 us (2%)
    all_to_all x1, blocking collectives, on_device(): lax.all_to_all(grams.reshape(devices, piece, width), everyone, split_axis...  14.8 us
    all_to_all x1, blocking collectives, on_device(): lax.all_to_all(copies, everyone, split_axis=0, concat_axis=0, tiled=True)  11 us
    all_gather x1, blocking collectives, on_device(): gathered = lax.all_gather(both, 'col', axis=0, tiled=True)  8.67 us
    ppermute x7, starting transfers between devices, exchange(): lax.ppermute(block, axis, [(i, i ^ step) for i in range(n)])  8.52 us
    pallas_call x1, Pallas kernels, on_device(): pl.pallas_call(functools.partial(final_kernel, total_rows), out_shape=(ja...  4.24 us
    ppermute x7, waiting for transfers between devices, exchange(): lax.ppermute(block, axis, [(i, i ^ step) for i in range(n)])  3.05 us
    pallas_call x1, Pallas kernels, on_device(): pl.pallas_call(functools.partial(tiles_kernel, n_row, n_col, total_rows),...  1.27 us
    pallas_call x1, Pallas kernels, on_device(): pl.pallas_call(prepare_kernel, out_shape=(jax.ShapeDtypeStruct((2 * rows_...  1.26 us
  transfers between devices with their start and end apart: 7, of which 4 were waited for; matrix products, arithmetic and copies ran while one was open for 0% of the time, Pallas kernels for 0%

profile of v18, /device:TPU:1, one launch (start us, length us, event | category | flops | bytes accessed | tf_op | source)
XLA Modules:
  0.0 54.9 jit_solution(5272761020117678849)
XLA Ops:
  0.6 1.3 %prepare.1 = (bf16[512,128]{1,0:T(8,128)(2,1)S(1)}, s32[1,1,16]{2,1,0:T(1,128)S(1)}, s32[1,1,16]{2,1,0:T(1,128)S(1)}, bf16[16,128,128]{2,1,0:T(8,128)(2,1)S(1)}) custom-call(f32[256,128]{1,0:T(8,128)} %now_ref.3, f32[256,128]{1,0:T(8,128)} %prev_hbm.1, s32[1,1,16]{2,1,0:T(1,128)} %rows_hbm.1, s32[1,1,16]{2,1,0:T(1,128)} %cols_hbm.1, ...), custom_call_target="tpu_custom_call" | custom-call | tf_op jit(solution)/shard_map/prepare/pallas_call | solution.py:278
  1.9 0.0 copy-start.2
  1.9 8.7 %all_gather.3.basis_ref = bf16[2048,128]{1,0:T(8,128)(2,1)S(1)} all-gather(bf16[512,128]{1,0:T(8,128)(2,1)S(1)} %get-tuple-element.23), channel_id=1, replica_groups=mesh['row'=8,'col'=4] {'col'}, dimensions={0}, use_global_device_ids=true | all-gather | bytes 655360 | tf_op jit(solution)/shard_map/all_gather | solution.py:296
  11.2 0.1 pad_add_fusion.me_ref
  11.3 0.0 copy-done.2
  11.3 1.3 %tile_products.1 = (bf16[264,128]{1,0:T(8,128)(2,1)S(1)}, bf16[264,128]{1,0:T(8,128)(2,1)S(1)}, bf16[264,128]{1,0:T(8,128)(2,1)S(1)}, bf16[264,128]{1,0:T(8,128)...) custom-call(s32[2]{0:T(128)S(1)} %pad_add_fusion.me_ref, ...), custom_call_target="tpu_custom_call" | custom-call | tf_op jit(solution)/shard_map/tile_products/pallas_call | solution.py:301
  12.6 1.3 %collective-permute-start.2 = (bf16[264,128]{1,0:T(8,128)(2,1)S(1)}, bf16[264,128]{1,0:T(8,128)(2,1)S(1)}, u32[]{:S(2)}, u32[]{:S(2)}) collective-permute-start(bf16[264,128]{1,0:T(8,128)(2,1)S(1)} %get-tuple-element.28), channel_id=1, source_target_pairs={{0,4},{4,0},{8,12},{12,8},{16,20},{20,16},{24,28},{28,24},{1,5},{5... | collective-permute-start | bytes 202760 | tf_op jit(solution)/shard_map/ppermute | solution.py:263
  13.9 1.3 %collective-permute-start.3 = (bf16[264,128]{1,0:T(8,128)(2,1)S(1)}, bf16[264,128]{1,0:T(8,128)(2,1)S(1)}, u32[]{:S(2)}, u32[]{:S(2)}) collective-permute-start(bf16[264,128]{1,0:T(8,128)(2,1)S(1)} %get-tuple-element.29), channel_id=1, source_target_pairs={{0,12},{4,8},{8,4},{12,0},{16,28},{20,24},{24,20},{28,16},{1,13},{... | collective-permute-start | bytes 202760 | tf_op jit(solution)/shard_map/ppermute | solution.py:263
  15.1 0.2 collective-permute-start.4
  15.3 1.2 %collective-permute-start = (bf16[264,128]{1,0:T(8,128)(2,1)S(1)}, bf16[264,128]{1,0:T(8,128)(2,1)S(1)}, u32[]{:S(2)}, u32[]{:S(2)}) collective-permute-start(bf16[264,128]{1,0:T(8,128)(2,1)S(1)} %get-tuple-element.25), channel_id=1, source_target_pairs={{0,4},{4,0},{8,12},{12,8},{16,20},{20,16},{24,28},{28,24},{1,5},{5... | collective-permute-start | bytes 202760 | tf_op jit(solution)/shard_map/ppermute | solution.py:263
  16.5 1.3 %collective-permute-start.1 = (bf16[264,128]{1,0:T(8,128)(2,1)S(1)}, bf16[264,128]{1,0:T(8,128)(2,1)S(1)}, u32[]{:S(2)}, u32[]{:S(2)}) collective-permute-start(bf16[264,128]{1,0:T(8,128)(2,1)S(1)} %get-tuple-element.26), channel_id=1, source_target_pairs={{0,12},{4,8},{8,4},{12,0},{16,28},{20,24},{24,20},{28,16},{1,13},{... | collective-permute-start | bytes 202760 | tf_op jit(solution)/shard_map/ppermute | solution.py:263
  17.8 0.0 collective-permute-done.2.refs_0_
  17.8 0.1 collective-permute-done.3.refs_1_
  17.9 1.0 %collective-permute-done.4.refs_2_ = bf16[264,128]{1,0:T(8,128)(2,1)S(1)} collective-permute-done((bf16[264,128]{1,0:T(8,128)(2,1)S(1)}, bf16[264,128]{1,0:T(8,128)(2,1)S(1)}, u32[]{:S(2)}, u32[]{:S(2)}) %collective-permute-start.4) | collective-permute-done | bytes 67616 | tf_op jit(solution)/shard_map/ppermute | solution.py:263
  18.9 0.0 copy-start.1
  18.9 0.0 copy-start
  19.0 2.4 %collective-permute-start.5 = (bf16[264,128]{1,0:T(8,128)(2,1)S(1)}, bf16[264,128]{1,0:T(8,128)(2,1)S(1)}, u32[]{:S(2)}, u32[]{:S(2)}) collective-permute-start(bf16[264,128]{1,0:T(8,128)(2,1)S(1)} %mirror_sum.1), channel_id=1, source_target_pairs={{0,16},{4,20},{8,24},{12,28},{16,0},{20,4},{24,8},{28,12},{1,17},{... | collective-permute-start | bytes 202760 | tf_op jit(solution)/shard_map/ppermute | solution.py:263
  21.3 1.0 %collective-permute-start.6 = (bf16[264,128]{1,0:T(8,128)(2,1)S(1)}, bf16[264,128]{1,0:T(8,128)(2,1)S(1)}, u32[]{:S(2)}, u32[]{:S(2)}) collective-permute-start(bf16[264,128]{1,0:T(8,128)(2,1)S(1)} %get-tuple-element.33), channel_id=1, source_target_pairs={{0,8},{4,12},{8,0},{12,4},{16,24},{20,28},{24,16},{28,20},{1,9},{5... | collective-permute-start | bytes 202760 | tf_op jit(solution)/shard_map/ppermute | solution.py:263
  22.3 0.0 copy-done.1
  22.3 0.2 shift_by_previous.1.shift_ref
  22.5 0.0 collective-permute-done.refs_0_
  22.5 0.0 collective-permute-done.1.refs_1_
  22.5 0.6 %collective-permute-done.5.refs_2_ = bf16[264,128]{1,0:T(8,128)(2,1)S(1)} collective-permute-done((bf16[264,128]{1,0:T(8,128)(2,1)S(1)}, bf16[264,128]{1,0:T(8,128)(2,1)S(1)}, u32[]{:S(2)}, u32[]{:S(2)}) %collective-permute-start.5) | collective-permute-done | bytes 67616 | tf_op jit(solution)/shard_map/ppermute | solution.py:263
  23.1 1.4 %collective-permute-done.6.refs_3_ = bf16[264,128]{1,0:T(8,128)(2,1)S(1)} collective-permute-done((bf16[264,128]{1,0:T(8,128)(2,1)S(1)}, bf16[264,128]{1,0:T(8,128)(2,1)S(1)}, u32[]{:S(2)}, u32[]{:S(2)}) %collective-permute-start.6) | collective-permute-done | bytes 67616 | tf_op jit(solution)/shard_map/ppermute | solution.py:263
  24.5 0.0 copy-done
  24.5 0.3 local_grams.1
  24.8 14.8 %all_to_all.10.parts_ref = f32[32,8,128]{2,1,0:T(8,128)S(1)} all-to-all(f32[32,8,128]{2,1,0:T(8,128)S(1)} %bitcast.4), channel_id=1, replica_groups=mesh['row'=8,'col'=4] {'row','col'}, dimensions={0} | all-to-all | bytes 262144 | tf_op jit(solution)/shard_map/all_to_all | solution.py:350
  39.5 0.1 sum_and_spread.1
  39.6 11.0 %all_to_all.11.pieces_ref = bf16[32,24,128]{2,1,0:T(8,128)(2,1)S(1)} all-to-all(bf16[32,24,128]{2,1,0:T(8,128)(2,1)S(1)} %sum_and_spread.1), channel_id=1, replica_groups=mesh['row'=8,'col'=4] {'row','col'}, dimensions={0} | all-to-all | bytes 393216 | tf_op jit(solution)/shard_map/all_to_all | solution.py:359
  50.6 4.2 %factor_and_basis.1 = (f32[256,128]{1,0:T(8,128)}, f32[128,128]{1,0:T(8,128)}, f32[128,128]{1,0:T(8,128)}) custom-call(bf16[32,24,128]{2,1,0:T(8,128)(2,1)S(1)} %all_to_all.11.pieces_ref, f32[256,128]{1,0:T(8,128)S(1)} %copy-done, f32[256,128]{1,0:T(8,128)S(1)} %get-tuple-element.36.shifted_ref), custom_call_target="tpu_custom_call" | custom-call | tf_op jit(solution)/shard_map/factor_and_basis/pallas_call | solution.py:360
  (1 shorter events, 0.0 us)
Async XLA Ops:
  1.9 9.4 %copy-start.2 = (f32[128,128]{1,0:T(8,128)S(1)}, f32[128,128]{1,0:T(8,128)}, u32[]{:S(2)}) copy-start(f32[128,128]{1,0:T(8,128)} %coupling_ref.3) | copy-start | bytes 196612
  12.6 5.2 %collective-permute-start.2 = (bf16[264,128]{1,0:T(8,128)(2,1)S(1)}, bf16[264,128]{1,0:T(8,128)(2,1)S(1)}, u32[]{:S(2)}, u32[]{:S(2)}) collective-permute-start(bf16[264,128]{1,0:T(8,128)(2,1)S(1)} %get-tuple-element.28), channel_id=1, source_target_pairs={{0,4},{4,0},{8,12},{12,8},{16,20},{20,16},{24,28},{28,24},{1,5},{5... | collective-permute-start | bytes 202760 | tf_op jit(solution)/shard_map/ppermute | solution.py:263
  13.9 4.1 %collective-permute-start.3 = (bf16[264,128]{1,0:T(8,128)(2,1)S(1)}, bf16[264,128]{1,0:T(8,128)(2,1)S(1)}, u32[]{:S(2)}, u32[]{:S(2)}) collective-permute-start(bf16[264,128]{1,0:T(8,128)(2,1)S(1)} %get-tuple-element.29), channel_id=1, source_target_pairs={{0,12},{4,8},{8,4},{12,0},{16,28},{20,24},{24,20},{28,16},{1,13},{... | collective-permute-start | bytes 202760 | tf_op jit(solution)/shard_map/ppermute | solution.py:263
  15.1 3.8 %collective-permute-start.4 = (bf16[264,128]{1,0:T(8,128)(2,1)S(1)}, bf16[264,128]{1,0:T(8,128)(2,1)S(1)}, u32[]{:S(2)}, u32[]{:S(2)}) collective-permute-start(bf16[264,128]{1,0:T(8,128)(2,1)S(1)} %get-tuple-element.30), channel_id=1, source_target_pairs={{0,8},{4,12},{8,0},{12,4},{16,24},{20,28},{24,16},{28,20},{1,9},{5... | collective-permute-start | bytes 202760 | tf_op jit(solution)/shard_map/ppermute | solution.py:263
  15.3 7.2 %collective-permute-start = (bf16[264,128]{1,0:T(8,128)(2,1)S(1)}, bf16[264,128]{1,0:T(8,128)(2,1)S(1)}, u32[]{:S(2)}, u32[]{:S(2)}) collective-permute-start(bf16[264,128]{1,0:T(8,128)(2,1)S(1)} %get-tuple-element.25), channel_id=1, source_target_pairs={{0,4},{4,0},{8,12},{12,8},{16,20},{20,16},{24,28},{28,24},{1,5},{5... | collective-permute-start | bytes 202760 | tf_op jit(solution)/shard_map/ppermute | solution.py:263
  16.5 6.0 %collective-permute-start.1 = (bf16[264,128]{1,0:T(8,128)(2,1)S(1)}, bf16[264,128]{1,0:T(8,128)(2,1)S(1)}, u32[]{:S(2)}, u32[]{:S(2)}) collective-permute-start(bf16[264,128]{1,0:T(8,128)(2,1)S(1)} %get-tuple-element.26), channel_id=1, source_target_pairs={{0,12},{4,8},{8,4},{12,0},{16,28},{20,24},{24,20},{28,16},{1,13},{... | collective-permute-start | bytes 202760 | tf_op jit(solution)/shard_map/ppermute | solution.py:263
  18.9 3.4 %copy-start.1 = (f32[256,128]{1,0:T(8,128)S(1)}, f32[256,128]{1,0:T(8,128)}, u32[]{:S(2)}) copy-start(f32[256,128]{1,0:T(8,128)} %prev_hbm.1) | copy-start | bytes 393220
  18.9 5.5 %copy-start = (f32[256,128]{1,0:T(8,128)S(1)}, f32[256,128]{1,0:T(8,128)}, u32[]{:S(2)}) copy-start(f32[256,128]{1,0:T(8,128)} %now_ref.3) | copy-start | bytes 393220
  19.0 4.1 %collective-permute-start.5 = (bf16[264,128]{1,0:T(8,128)(2,1)S(1)}, bf16[264,128]{1,0:T(8,128)(2,1)S(1)}, u32[]{:S(2)}, u32[]{:S(2)}) collective-permute-start(bf16[264,128]{1,0:T(8,128)(2,1)S(1)} %mirror_sum.1), channel_id=1, source_target_pairs={{0,16},{4,20},{8,24},{12,28},{16,0},{20,4},{24,8},{28,12},{1,17},{... | collective-permute-start | bytes 202760 | tf_op jit(solution)/shard_map/ppermute | solution.py:263
  21.3 3.1 %collective-permute-start.6 = (bf16[264,128]{1,0:T(8,128)(2,1)S(1)}, bf16[264,128]{1,0:T(8,128)(2,1)S(1)}, u32[]{:S(2)}, u32[]{:S(2)}) collective-permute-start(bf16[264,128]{1,0:T(8,128)(2,1)S(1)} %get-tuple-element.33), channel_id=1, source_target_pairs={{0,8},{4,12},{8,0},{12,4},{16,24},{20,28},{24,16},{28,20},{1,9},{5... | collective-permute-start | bytes 202760 | tf_op jit(solution)/shard_map/ppermute | solution.py:263

commit v19 on v18

--- a/solution.py
+++ b/solution.py
@@ -156,7 +156,7 @@
 
 def eliminate(gram):
     width = gram.shape[0]
-    tall, block, per_group = 8, 16, 2
+    tall, block = 8, 16
     shape = (tall, width)
     lanes = lax.broadcasted_iota(jnp.int32, shape, 1)
     subs = lax.broadcasted_iota(jnp.int32, shape, 0)
@@ -171,64 +171,56 @@
         part, k = parts[k // tall], k % tall
         return jnp.broadcast_to(part[k : k + 1, :], shape)
 
-    strips = [gram[r : r + block, :] for r in range(0, width, block)]
+    strips = [cut(gram[r : r + block, :]) for r in range(0, width, block)]
     finished = []
-    for begin in range(0, len(strips), per_group):
-        group = [cut(strip) for strip in strips[:per_group]]
-        for at in range(per_group):
-            first = (begin + at) * block
-            panel = group[at]
-            columns = [column(panel, first + j) for j in range(block)]
-            kept = list(panel)
-            for j in range(0, block, 2):
-                mine = j // tall
-                here, there = subs == j % tall, subs == j % tall + 1
-                both = here | there
-                lane, next_lane = lanes == first + j, lanes == first + j + 1
-                left, right = columns[j], columns[j + 1]
-                a, b, c = row(left, j), row(right, j), row(right, j + 1)
-                scale = 1.0 / (a * c - b * b)
-                by_top = [x * c - y * b for x, y in zip(left, right)]
-                by_bottom = [y * a - x * b for x, y in zip(left, right)]
-                by_top[mine] = jnp.where(here, -c, jnp.where(there, b, by_top[mine]))
-                by_bottom[mine] = jnp.where(here, b, jnp.where(there, -a, by_bottom[mine]))
-
-                def update(parts, up, down):
-                    rest = [jnp.where(both, 0.0, part) if k == mine else part for k, part in enumerate(parts)]
-                    return [x - (t * up + u * down) * scale for x, t, u in zip(rest, by_top, by_bottom)]
-
-                top, bottom = row(panel, j), row(panel, j + 1)
-                ratio = b / a
-                second = jnp.where(lane, -ratio, bottom - ratio * top)
-                kept[mine] = jnp.where(here, top, jnp.where(there, second, kept[mine]))
-                pair = lane | next_lane
-                top = jnp.where(lane, 1.0, jnp.where(next_lane, 0.0, top))
-                bottom = jnp.where(lane, 0.0, jnp.where(next_lane, 1.0, bottom))
-                panel = update([jnp.where(pair, 0.0, part) for part in panel], top, bottom)
-                for m in range(j + 2, block):
-                    columns[m] = update(columns[m], row(columns[m], j), row(columns[m], j + 1))
-            finished += kept
-            group[at] = panel
+    for first in range(0, width, block):
+        panel, *strips = strips
+        columns = [column(panel, first + j) for j in range(block)]
+        kept = list(panel)
+        for j in range(0, block, 2):
+            mine = j // tall
+            here, there = subs == j % tall, subs == j % tall + 1
+            both = here | there
+            lane, next_lane = lanes == first + j, lanes == first + j + 1
+            left, right = columns[j], columns[j + 1]
+            a, b, c = row(left, j), row(right, j), row(right, j + 1)
+            scale = 1.0 / (a * c - b * b)
+            by_top = [x * c - y * b for x, y in zip(left, right)]
+            by_bottom = [y * a - x * b for x, y in zip(left, right)]
+            by_top[mine] = jnp.where(here, -c, jnp.where(there, b, by_top[mine]))
+            by_bottom[mine] = jnp.where(here, b, jnp.where(there, -a, by_bottom[mine]))
+
+            def update(parts, up, down):
+                rest = [jnp.where(both, 0.0, part) if k == mine else part for k, part in enumerate(parts)]
+                return [x - (t * up + u * down) * scale for x, t, u in zip(rest, by_top, by_bottom)]
+
+            top, bottom = row(panel, j), row(panel, j + 1)
+            ratio = b / a
+            second = jnp.where(lane, -ratio, bottom - ratio * top)
+            kept[mine] = jnp.where(here, top, jnp.where(there, second, kept[mine]))
+            pair = lane | next_lane
+            top = jnp.where(lane, 1.0, jnp.where(next_lane, 0.0, top))
+            bottom = jnp.where(lane, 0.0, jnp.where(next_lane, 1.0, bottom))
+            panel = update([jnp.where(pair, 0.0, part) for part in panel], top, bottom)
+            for m in range(j + 2, block):
+                columns[m] = update(columns[m], row(columns[m], j), row(columns[m], j + 1))
+        finished += kept
+        if strips:
             rows = [row(panel, m) for m in range(block)]
             inside = (lanes >= first) & (lanes < first + block)
-            for s in range(per_group):
-                if s != at:
-                    factors = [column(group[s], first + m) for m in range(block)]
-                    for k in range(len(group[s])):
-                        terms = [factor[k] * value for factor, value in zip(factors, rows)]
-                        while len(terms) > 1:
-                            terms = [x + y for x, y in zip(terms[::2], terms[1::2])]
-                        group[s][k] = jnp.where(inside, 0.0, group[s][k]) - terms[0]
-        group = [jnp.concatenate(parts, axis=0) for parts in group]
-        strips = strips[per_group:]
-        if strips:
-            first, last = begin * block, (begin + per_group) * block
-            below = jnp.concatenate(strips, axis=0)
+            factors = [column(strips[0], first + m) for m in range(block)]
+            for k in range(len(panel)):
+                terms = [factor[k] * value for factor, value in zip(factors, rows)]
+                while len(terms) > 1:
+                    terms = [x + y for x, y in zip(terms[::2], terms[1::2])]
+                strips[0][k] = jnp.where(inside, 0.0, strips[0][k]) - terms[0]
+        if len(strips) > 1:
+            below = jnp.concatenate([part for strip in strips[1:] for part in strip], axis=0)
             solved = [jnp.zeros((first, width), F32)] if first else []
-            solved = jnp.concatenate(solved + group + [jnp.zeros((width - last, width), F32)], axis=0)
+            solved = jnp.concatenate(solved + panel + [jnp.zeros((width - first - block, width), F32)], axis=0)
             cols = lax.broadcasted_iota(jnp.int32, below.shape, 1)
-            below = jnp.where((cols >= first) & (cols < last), 0.0, below) - dot3(below, solved)
-            strips = [below[r : r + block, :] for r in range(0, below.shape[0], block)]
+            below = jnp.where((cols >= first) & (cols < first + block), 0.0, below) - dot3(below, solved)
+            strips[1:] = [cut(below[r : r + block, :]) for r in range(0, below.shape[0], block)]
     return jnp.concatenate(finished, axis=0)
 
 

time: 55.1 us -> 54.8 us (level)
  no operation moved by 1% of the time
where the time goes in v19:
time: 54.8 us; the launch traced here: 54.6 us
  blocking collectives  34.5 us (63%)
  starting transfers between devices  8.52 us (16%)
  Pallas kernels  7.05 us (13%)
  waiting for transfers between devices  3.05 us (6%)
  between operations  1.37 us (2%)
    all_to_all x1, blocking collectives, on_device(): lax.all_to_all(grams.reshape(devices, piece, width), everyone, split_axis...  14.8 us
    all_to_all x1, blocking collectives, on_device(): lax.all_to_all(copies, everyone, split_axis=0, concat_axis=0, tiled=True)  11 us
    all_gather x1, blocking collectives, on_device(): gathered = lax.all_gather(both, 'col', axis=0, tiled=True)  8.67 us
    ppermute x7, starting transfers between devices, exchange(): lax.ppermute(block, axis, [(i, i ^ step) for i in range(n)])  8.52 us
    pallas_call x1, Pallas kernels, on_device(): pl.pallas_call(functools.partial(final_kernel, total_rows), out_shape=(ja...  3.91 us
    ppermute x7, waiting for transfers between devices, exchange(): lax.ppermute(block, axis, [(i, i ^ step) for i in range(n)])  3.05 us
    pallas_call x1, Pallas kernels, on_device(): pl.pallas_call(functools.partial(tiles_kernel, n_row, n_col, total_rows),...  1.27 us
    pallas_call x1, Pallas kernels, on_device(): pl.pallas_call(prepare_kernel, out_shape=(jax.ShapeDtypeStruct((2 * rows_...  1.26 us
  transfers between devices with their start and end apart: 7, of which 4 were waited for; matrix products, arithmetic and copies ran while one was open for 0% of the time, Pallas kernels for 0%

profile of v19, /device:TPU:1, one launch (start us, length us, event | category | flops | bytes accessed | tf_op | source)
XLA Modules:
  0.0 54.6 jit_solution(14374857837609046244)
XLA Ops:
  0.6 1.3 %prepare.1 = (bf16[512,128]{1,0:T(8,128)(2,1)S(1)}, s32[1,1,16]{2,1,0:T(1,128)S(1)}, s32[1,1,16]{2,1,0:T(1,128)S(1)}, bf16[16,128,128]{2,1,0:T(8,128)(2,1)S(1)}) custom-call(f32[256,128]{1,0:T(8,128)} %now_ref.3, f32[256,128]{1,0:T(8,128)} %prev_hbm.1, s32[1,1,16]{2,1,0:T(1,128)} %rows_hbm.1, s32[1,1,16]{2,1,0:T(1,128)} %cols_hbm.1, ...), custom_call_target="tpu_custom_call" | custom-call | tf_op jit(solution)/shard_map/prepare/pallas_call | solution.py:270
  1.9 0.0 copy-start.2
  1.9 8.7 %all_gather.3.basis_ref = bf16[2048,128]{1,0:T(8,128)(2,1)S(1)} all-gather(bf16[512,128]{1,0:T(8,128)(2,1)S(1)} %get-tuple-element.23), channel_id=1, replica_groups=mesh['row'=8,'col'=4] {'col'}, dimensions={0}, use_global_device_ids=true | all-gather | bytes 655360 | tf_op jit(solution)/shard_map/all_gather | solution.py:288
  11.2 0.1 pad_add_fusion.me_ref
  11.3 0.0 copy-done.2
  11.3 1.3 %tile_products.1 = (bf16[264,128]{1,0:T(8,128)(2,1)S(1)}, bf16[264,128]{1,0:T(8,128)(2,1)S(1)}, bf16[264,128]{1,0:T(8,128)(2,1)S(1)}, bf16[264,128]{1,0:T(8,128)...) custom-call(s32[2]{0:T(128)S(1)} %pad_add_fusion.me_ref, ...), custom_call_target="tpu_custom_call" | custom-call | tf_op jit(solution)/shard_map/tile_products/pallas_call | solution.py:293
  12.6 1.3 %collective-permute-start.2 = (bf16[264,128]{1,0:T(8,128)(2,1)S(1)}, bf16[264,128]{1,0:T(8,128)(2,1)S(1)}, u32[]{:S(2)}, u32[]{:S(2)}) collective-permute-start(bf16[264,128]{1,0:T(8,128)(2,1)S(1)} %get-tuple-element.28), channel_id=1, source_target_pairs={{0,4},{4,0},{8,12},{12,8},{16,20},{20,16},{24,28},{28,24},{1,5},{5... | collective-permute-start | bytes 202760 | tf_op jit(solution)/shard_map/ppermute | solution.py:255
  13.9 1.3 %collective-permute-start.3 = (bf16[264,128]{1,0:T(8,128)(2,1)S(1)}, bf16[264,128]{1,0:T(8,128)(2,1)S(1)}, u32[]{:S(2)}, u32[]{:S(2)}) collective-permute-start(bf16[264,128]{1,0:T(8,128)(2,1)S(1)} %get-tuple-element.29), channel_id=1, source_target_pairs={{0,12},{4,8},{8,4},{12,0},{16,28},{20,24},{24,20},{28,16},{1,13},{... | collective-permute-start | bytes 202760 | tf_op jit(solution)/shard_map/ppermute | solution.py:255
  15.1 0.2 collective-permute-start.4
  15.3 1.2 %collective-permute-start = (bf16[264,128]{1,0:T(8,128)(2,1)S(1)}, bf16[264,128]{1,0:T(8,128)(2,1)S(1)}, u32[]{:S(2)}, u32[]{:S(2)}) collective-permute-start(bf16[264,128]{1,0:T(8,128)(2,1)S(1)} %get-tuple-element.25), channel_id=1, source_target_pairs={{0,4},{4,0},{8,12},{12,8},{16,20},{20,16},{24,28},{28,24},{1,5},{5... | collective-permute-start | bytes 202760 | tf_op jit(solution)/shard_map/ppermute | solution.py:255
  16.5 1.3 %collective-permute-start.1 = (bf16[264,128]{1,0:T(8,128)(2,1)S(1)}, bf16[264,128]{1,0:T(8,128)(2,1)S(1)}, u32[]{:S(2)}, u32[]{:S(2)}) collective-permute-start(bf16[264,128]{1,0:T(8,128)(2,1)S(1)} %get-tuple-element.26), channel_id=1, source_target_pairs={{0,12},{4,8},{8,4},{12,0},{16,28},{20,24},{24,20},{28,16},{1,13},{... | collective-permute-start | bytes 202760 | tf_op jit(solution)/shard_map/ppermute | solution.py:255
  17.8 0.0 collective-permute-done.2.refs_0_
  17.8 0.1 collective-permute-done.3.refs_1_
  17.9 1.0 %collective-permute-done.4.refs_2_ = bf16[264,128]{1,0:T(8,128)(2,1)S(1)} collective-permute-done((bf16[264,128]{1,0:T(8,128)(2,1)S(1)}, bf16[264,128]{1,0:T(8,128)(2,1)S(1)}, u32[]{:S(2)}, u32[]{:S(2)}) %collective-permute-start.4) | collective-permute-done | bytes 67616 | tf_op jit(solution)/shard_map/ppermute | solution.py:255
  18.9 0.0 copy-start.1
  18.9 0.0 copy-start
  19.0 2.4 %collective-permute-start.5 = (bf16[264,128]{1,0:T(8,128)(2,1)S(1)}, bf16[264,128]{1,0:T(8,128)(2,1)S(1)}, u32[]{:S(2)}, u32[]{:S(2)}) collective-permute-start(bf16[264,128]{1,0:T(8,128)(2,1)S(1)} %mirror_sum.1), channel_id=1, source_target_pairs={{0,16},{4,20},{8,24},{12,28},{16,0},{20,4},{24,8},{28,12},{1,17},{... | collective-permute-start | bytes 202760 | tf_op jit(solution)/shard_map/ppermute | solution.py:255
  21.3 1.0 %collective-permute-start.6 = (bf16[264,128]{1,0:T(8,128)(2,1)S(1)}, bf16[264,128]{1,0:T(8,128)(2,1)S(1)}, u32[]{:S(2)}, u32[]{:S(2)}) collective-permute-start(bf16[264,128]{1,0:T(8,128)(2,1)S(1)} %get-tuple-element.33), channel_id=1, source_target_pairs={{0,8},{4,12},{8,0},{12,4},{16,24},{20,28},{24,16},{28,20},{1,9},{5... | collective-permute-start | bytes 202760 | tf_op jit(solution)/shard_map/ppermute | solution.py:255
  22.3 0.0 copy-done.1
  22.3 0.2 shift_by_previous.1.shift_ref
  22.5 0.0 collective-permute-done.refs_0_
  22.5 0.0 collective-permute-done.1.refs_1_
  22.5 0.6 %collective-permute-done.5.refs_2_ = bf16[264,128]{1,0:T(8,128)(2,1)S(1)} collective-permute-done((bf16[264,128]{1,0:T(8,128)(2,1)S(1)}, bf16[264,128]{1,0:T(8,128)(2,1)S(1)}, u32[]{:S(2)}, u32[]{:S(2)}) %collective-permute-start.5) | collective-permute-done | bytes 67616 | tf_op jit(solution)/shard_map/ppermute | solution.py:255
  23.1 1.4 %collective-permute-done.6.refs_3_ = bf16[264,128]{1,0:T(8,128)(2,1)S(1)} collective-permute-done((bf16[264,128]{1,0:T(8,128)(2,1)S(1)}, bf16[264,128]{1,0:T(8,128)(2,1)S(1)}, u32[]{:S(2)}, u32[]{:S(2)}) %collective-permute-start.6) | collective-permute-done | bytes 67616 | tf_op jit(solution)/shard_map/ppermute | solution.py:255
  24.5 0.0 copy-done
  24.5 0.3 local_grams.1
  24.8 14.8 %all_to_all.10.parts_ref = f32[32,8,128]{2,1,0:T(8,128)S(1)} all-to-all(f32[32,8,128]{2,1,0:T(8,128)S(1)} %bitcast.4), channel_id=1, replica_groups=mesh['row'=8,'col'=4] {'row','col'}, dimensions={0} | all-to-all | bytes 262144 | tf_op jit(solution)/shard_map/all_to_all | solution.py:342
  39.5 0.1 sum_and_spread.1
  39.6 11.0 %all_to_all.11.pieces_ref = bf16[32,24,128]{2,1,0:T(8,128)(2,1)S(1)} all-to-all(bf16[32,24,128]{2,1,0:T(8,128)(2,1)S(1)} %sum_and_spread.1), channel_id=1, replica_groups=mesh['row'=8,'col'=4] {'row','col'}, dimensions={0} | all-to-all | bytes 393216 | tf_op jit(solution)/shard_map/all_to_all | solution.py:351
  50.6 3.9 %factor_and_basis.1 = (f32[256,128]{1,0:T(8,128)}, f32[128,128]{1,0:T(8,128)}, f32[128,128]{1,0:T(8,128)}) custom-call(bf16[32,24,128]{2,1,0:T(8,128)(2,1)S(1)} %all_to_all.11.pieces_ref, f32[256,128]{1,0:T(8,128)S(1)} %copy-done, f32[256,128]{1,0:T(8,128)S(1)} %get-tuple-element.36.shifted_ref), custom_call_target="tpu_custom_call" | custom-call | tf_op jit(solution)/shard_map/factor_and_basis/pallas_call | solution.py:352
  (1 shorter events, 0.0 us)
Async XLA Ops:
  1.9 9.4 %copy-start.2 = (f32[128,128]{1,0:T(8,128)S(1)}, f32[128,128]{1,0:T(8,128)}, u32[]{:S(2)}) copy-start(f32[128,128]{1,0:T(8,128)} %coupling_ref.3) | copy-start | bytes 196612
  12.6 5.2 %collective-permute-start.2 = (bf16[264,128]{1,0:T(8,128)(2,1)S(1)}, bf16[264,128]{1,0:T(8,128)(2,1)S(1)}, u32[]{:S(2)}, u32[]{:S(2)}) collective-permute-start(bf16[264,128]{1,0:T(8,128)(2,1)S(1)} %get-tuple-element.28), channel_id=1, source_target_pairs={{0,4},{4,0},{8,12},{12,8},{16,20},{20,16},{24,28},{28,24},{1,5},{5... | collective-permute-start | bytes 202760 | tf_op jit(solution)/shard_map/ppermute | solution.py:255
  13.9 4.1 %collective-permute-start.3 = (bf16[264,128]{1,0:T(8,128)(2,1)S(1)}, bf16[264,128]{1,0:T(8,128)(2,1)S(1)}, u32[]{:S(2)}, u32[]{:S(2)}) collective-permute-start(bf16[264,128]{1,0:T(8,128)(2,1)S(1)} %get-tuple-element.29), channel_id=1, source_target_pairs={{0,12},{4,8},{8,4},{12,0},{16,28},{20,24},{24,20},{28,16},{1,13},{... | collective-permute-start | bytes 202760 | tf_op jit(solution)/shard_map/ppermute | solution.py:255
  15.1 3.8 %collective-permute-start.4 = (bf16[264,128]{1,0:T(8,128)(2,1)S(1)}, bf16[264,128]{1,0:T(8,128)(2,1)S(1)}, u32[]{:S(2)}, u32[]{:S(2)}) collective-permute-start(bf16[264,128]{1,0:T(8,128)(2,1)S(1)} %get-tuple-element.30), channel_id=1, source_target_pairs={{0,8},{4,12},{8,0},{12,4},{16,24},{20,28},{24,16},{28,20},{1,9},{5... | collective-permute-start | bytes 202760 | tf_op jit(solution)/shard_map/ppermute | solution.py:255
  15.3 7.2 %collective-permute-start = (bf16[264,128]{1,0:T(8,128)(2,1)S(1)}, bf16[264,128]{1,0:T(8,128)(2,1)S(1)}, u32[]{:S(2)}, u32[]{:S(2)}) collective-permute-start(bf16[264,128]{1,0:T(8,128)(2,1)S(1)} %get-tuple-element.25), channel_id=1, source_target_pairs={{0,4},{4,0},{8,12},{12,8},{16,20},{20,16},{24,28},{28,24},{1,5},{5... | collective-permute-start | bytes 202760 | tf_op jit(solution)/shard_map/ppermute | solution.py:255
  16.5 6.0 %collective-permute-start.1 = (bf16[264,128]{1,0:T(8,128)(2,1)S(1)}, bf16[264,128]{1,0:T(8,128)(2,1)S(1)}, u32[]{:S(2)}, u32[]{:S(2)}) collective-permute-start(bf16[264,128]{1,0:T(8,128)(2,1)S(1)} %get-tuple-element.26), channel_id=1, source_target_pairs={{0,12},{4,8},{8,4},{12,0},{16,28},{20,24},{24,20},{28,16},{1,13},{... | collective-permute-start | bytes 202760 | tf_op jit(solution)/shard_map/ppermute | solution.py:255
  18.9 3.4 %copy-start.1 = (f32[256,128]{1,0:T(8,128)S(1)}, f32[256,128]{1,0:T(8,128)}, u32[]{:S(2)}) copy-start(f32[256,128]{1,0:T(8,128)} %prev_hbm.1) | copy-start | bytes 393220
  18.9 5.5 %copy-start = (f32[256,128]{1,0:T(8,128)S(1)}, f32[256,128]{1,0:T(8,128)}, u32[]{:S(2)}) copy-start(f32[256,128]{1,0:T(8,128)} %now_ref.3) | copy-start | bytes 393220
  19.0 4.1 %collective-permute-start.5 = (bf16[264,128]{1,0:T(8,128)(2,1)S(1)}, bf16[264,128]{1,0:T(8,128)(2,1)S(1)}, u32[]{:S(2)}, u32[]{:S(2)}) collective-permute-start(bf16[264,128]{1,0:T(8,128)(2,1)S(1)} %mirror_sum.1), channel_id=1, source_target_pairs={{0,16},{4,20},{8,24},{12,28},{16,0},{20,4},{24,8},{28,12},{1,17},{... | collective-permute-start | bytes 202760 | tf_op jit(solution)/shard_map/ppermute | solution.py:255
  21.3 3.1 %collective-permute-start.6 = (bf16[264,128]{1,0:T(8,128)(2,1)S(1)}, bf16[264,128]{1,0:T(8,128)(2,1)S(1)}, u32[]{:S(2)}, u32[]{:S(2)}) collective-permute-start(bf16[264,128]{1,0:T(8,128)(2,1)S(1)} %get-tuple-element.33), channel_id=1, source_target_pairs={{0,8},{4,12},{8,0},{12,4},{16,24},{20,28},{24,16},{28,20},{1,9},{5... | collective-permute-start | bytes 202760 | tf_op jit(solution)/shard_map/ppermute | solution.py:255

commit v20 on v19

--- a/solution.py
+++ b/solution.py
@@ -33,7 +33,7 @@
 
 
 def distances(n):
-    return [1, *range(n - 1, 1, -1)]
+    return [n - 1, *range(1, n - 1)]
 
 
 def high_and_low(value):
@@ -229,13 +229,16 @@
     piece = pieces_ref.shape[1] // 3
     pieces = pieces_ref[...]
     late = sum_high_and_low(pieces[:, : 2 * piece, :]).reshape(-1, width)
-    early = pieces[:, 2 * piece :, :].astype(F32).reshape(-1, width)
+    early = pieces[:, 2 * piece :, :].reshape(-1, width)
     now_product, square = late[:width], late[width : 2 * width]
     now_square, shift = early[:width], early[width : 2 * width]
     projection = now_product * total_rows**-0.5
     projection_ref[...] = projection
     scaled = now_product * (1.0 / total_rows)
-    half = shift - 0.5 * now_product + 0.5 * dot3(now_square, scaled)
+    scaled_high, scaled_low = split(scaled)
+    corrected = jnp.dot(now_square, scaled_low, preferred_element_type=F32)
+    corrected += jnp.dot(now_square, scaled_high, preferred_element_type=F32)
+    half = shift.astype(F32) - 0.5 * now_product + 0.5 * corrected
     mixed = dot3(scaled, half, TN)
     gram = square + mixed + mixed.T
     reduced = eliminate(gram * (1.0 / total_rows))

time: 54.8 us -> 53.8 us (0.982)
  blocking collectives: 34.5 us -> 33.4 us
  starting transfers between devices: 8.52 us -> 9.52 us
  waiting for transfers between devices: 3.05 us -> 2.21 us
    all_to_all x1, blocking collectives: 14.8 us -> 13.7 us  [on_device(): lax.all_to_all(grams.reshape(devices, piece, width), everyone, split_axis...]
    ppermute x7, starting transfers between devices: 8.52 us -> 9.52 us  [exchange(): lax.ppermute(block, axis, [(i, i ^ step) for i in range(n)])]
    ppermute x7, waiting for transfers between devices: 3.05 us -> 2.21 us  [exchange(): lax.ppermute(block, axis, [(i, i ^ step) for i in range(n)])]
  transfers between devices with their start and end apart: 7 -> 7, of which waited for: 4 -> 3; matrix products, arithmetic and copies ran while one was open for 0% -> 0% of each run, Pallas kernels for 0% -> 0%
where the time goes in v20:
time: 53.8 us; the launch traced here: 53.6 us
  blocking collectives  33.4 us (62%)
  starting transfers between devices  9.52 us (18%)
  Pallas kernels  7.01 us (13%)
  waiting for transfers between devices  2.21 us (4%)
  between operations  1.37 us (3%)
    all_to_all x1, blocking collectives, on_device(): lax.all_to_all(grams.reshape(devices, piece, width), everyone, split_axis...  13.7 us
    all_to_all x1, blocking collectives, on_device(): lax.all_to_all(copies, everyone, split_axis=0, concat_axis=0, tiled=True)  11 us
    ppermute x7, starting transfers between devices, exchange(): lax.ppermute(block, axis, [(i, i ^ step) for i in range(n)])  9.52 us
    all_gather x1, blocking collectives, on_device(): gathered = lax.all_gather(both, 'col', axis=0, tiled=True)  8.67 us
    pallas_call x1, Pallas kernels, on_device(): pl.pallas_call(functools.partial(final_kernel, total_rows), out_shape=(ja...  3.87 us
    ppermute x7, waiting for transfers between devices, exchange(): lax.ppermute(block, axis, [(i, i ^ step) for i in range(n)])  2.21 us
    pallas_call x1, Pallas kernels, on_device(): pl.pallas_call(functools.partial(tiles_kernel, n_row, n_col, total_rows),...  1.27 us
    pallas_call x1, Pallas kernels, on_device(): pl.pallas_call(prepare_kernel, out_shape=(jax.ShapeDtypeStruct((2 * rows_...  1.26 us
  transfers between devices with their start and end apart: 7, of which 3 were waited for; matrix products, arithmetic and copies ran while one was open for 0% of the time, Pallas kernels for 0%

profile of v20, /device:TPU:1, one launch (start us, length us, event | category | flops | bytes accessed | tf_op | source)
XLA Modules:
  0.0 53.6 jit_solution(10756531371670487063)
XLA Ops:
  0.6 1.3 %prepare.1 = (bf16[512,128]{1,0:T(8,128)(2,1)S(1)}, s32[1,1,16]{2,1,0:T(1,128)S(1)}, s32[1,1,16]{2,1,0:T(1,128)S(1)}, bf16[16,128,128]{2,1,0:T(8,128)(2,1)S(1)}) custom-call(f32[256,128]{1,0:T(8,128)} %now_ref.3, f32[256,128]{1,0:T(8,128)} %prev_hbm.1, s32[1,1,16]{2,1,0:T(1,128)} %rows_hbm.1, s32[1,1,16]{2,1,0:T(1,128)} %cols_hbm.1, ...), custom_call_target="tpu_custom_call" | custom-call | tf_op jit(solution)/shard_map/prepare/pallas_call | solution.py:273
  1.9 0.0 copy-start.2
  1.9 8.7 %all_gather.3.basis_ref = bf16[2048,128]{1,0:T(8,128)(2,1)S(1)} all-gather(bf16[512,128]{1,0:T(8,128)(2,1)S(1)} %get-tuple-element.23), channel_id=1, replica_groups=mesh['row'=8,'col'=4] {'col'}, dimensions={0}, use_global_device_ids=true | all-gather | bytes 655360 | tf_op jit(solution)/shard_map/all_gather | solution.py:291
  11.2 0.1 pad_add_fusion.me_ref
  11.3 0.0 copy-done.2
  11.3 1.3 %tile_products.1 = (bf16[264,128]{1,0:T(8,128)(2,1)S(1)}, bf16[264,128]{1,0:T(8,128)(2,1)S(1)}, bf16[264,128]{1,0:T(8,128)(2,1)S(1)}, bf16[264,128]{1,0:T(8,128)...) custom-call(s32[2]{0:T(128)S(1)} %pad_add_fusion.me_ref, ...), custom_call_target="tpu_custom_call" | custom-call | tf_op jit(solution)/shard_map/tile_products/pallas_call | solution.py:296
  12.6 2.3 %collective-permute-start.2 = (bf16[264,128]{1,0:T(8,128)(2,1)S(1)}, bf16[264,128]{1,0:T(8,128)(2,1)S(1)}, u32[]{:S(2)}, u32[]{:S(2)}) collective-permute-start(bf16[264,128]{1,0:T(8,128)(2,1)S(1)} %get-tuple-element.28), channel_id=1, source_target_pairs={{0,12},{4,8},{8,4},{12,0},{16,28},{20,24},{24,20},{28,16},{1,13},{... | collective-permute-start | bytes 202760 | tf_op jit(solution)/shard_map/ppermute | solution.py:258
  14.9 0.3 collective-permute-start.3
  15.1 0.2 collective-permute-start.4
  15.3 2.2 %collective-permute-start = (bf16[264,128]{1,0:T(8,128)(2,1)S(1)}, bf16[264,128]{1,0:T(8,128)(2,1)S(1)}, u32[]{:S(2)}, u32[]{:S(2)}) collective-permute-start(bf16[264,128]{1,0:T(8,128)(2,1)S(1)} %get-tuple-element.25), channel_id=1, source_target_pairs={{0,12},{4,8},{8,4},{12,0},{16,28},{20,24},{24,20},{28,16},{1,13},{... | collective-permute-start | bytes 202760 | tf_op jit(solution)/shard_map/ppermute | solution.py:258
  17.5 0.3 collective-permute-start.1
  17.8 0.0 collective-permute-done.2.refs_0_
  17.8 0.4 collective-permute-done.3.refs_1_
  18.1 0.4 collective-permute-done.4.refs_2_
  18.6 0.0 copy-start.1
  18.6 0.0 copy-start
  18.6 2.4 %collective-permute-start.5 = (bf16[264,128]{1,0:T(8,128)(2,1)S(1)}, bf16[264,128]{1,0:T(8,128)(2,1)S(1)}, u32[]{:S(2)}, u32[]{:S(2)}) collective-permute-start(bf16[264,128]{1,0:T(8,128)(2,1)S(1)} %mirror_sum.1), channel_id=1, source_target_pairs={{0,16},{4,20},{8,24},{12,28},{16,0},{20,4},{24,8},{28,12},{1,17},{... | collective-permute-start | bytes 202760 | tf_op jit(solution)/shard_map/ppermute | solution.py:258
  21.0 2.0 %collective-permute-start.6 = (bf16[264,128]{1,0:T(8,128)(2,1)S(1)}, bf16[264,128]{1,0:T(8,128)(2,1)S(1)}, u32[]{:S(2)}, u32[]{:S(2)}) collective-permute-start(bf16[264,128]{1,0:T(8,128)(2,1)S(1)} %get-tuple-element.33), channel_id=1, source_target_pairs={{0,8},{4,12},{8,0},{12,4},{16,24},{20,28},{24,16},{28,20},{1,9},{5... | collective-permute-start | bytes 202760 | tf_op jit(solution)/shard_map/ppermute | solution.py:258
  23.0 0.0 copy-done.1
  23.0 0.2 shift_by_previous.1.shift_ref
  23.2 0.0 collective-permute-done.refs_0_
  23.2 0.0 collective-permute-done.1.refs_1_
  23.2 0.0 collective-permute-done.5.refs_2_
  23.2 1.4 %collective-permute-done.6.refs_3_ = bf16[264,128]{1,0:T(8,128)(2,1)S(1)} collective-permute-done((bf16[264,128]{1,0:T(8,128)(2,1)S(1)}, bf16[264,128]{1,0:T(8,128)(2,1)S(1)}, u32[]{:S(2)}, u32[]{:S(2)}) %collective-permute-start.6) | collective-permute-done | bytes 67616 | tf_op jit(solution)/shard_map/ppermute | solution.py:258
  24.6 0.0 copy-done
  24.6 0.3 local_grams.1
  25.0 13.7 %all_to_all.10.parts_ref = f32[32,8,128]{2,1,0:T(8,128)S(1)} all-to-all(f32[32,8,128]{2,1,0:T(8,128)S(1)} %bitcast.4), channel_id=1, replica_groups=mesh['row'=8,'col'=4] {'row','col'}, dimensions={0} | all-to-all | bytes 262144 | tf_op jit(solution)/shard_map/all_to_all | solution.py:345
  38.6 0.1 sum_and_spread.1
  38.7 11.0 %all_to_all.11.pieces_ref = bf16[32,24,128]{2,1,0:T(8,128)(2,1)S(1)} all-to-all(bf16[32,24,128]{2,1,0:T(8,128)(2,1)S(1)} %sum_and_spread.1), channel_id=1, replica_groups=mesh['row'=8,'col'=4] {'row','col'}, dimensions={0} | all-to-all | bytes 393216 | tf_op jit(solution)/shard_map/all_to_all | solution.py:354
  49.7 3.9 %factor_and_basis.1 = (f32[256,128]{1,0:T(8,128)}, f32[128,128]{1,0:T(8,128)}, f32[128,128]{1,0:T(8,128)}) custom-call(bf16[32,24,128]{2,1,0:T(8,128)(2,1)S(1)} %all_to_all.11.pieces_ref, f32[256,128]{1,0:T(8,128)S(1)} %copy-done, f32[256,128]{1,0:T(8,128)S(1)} %get-tuple-element.36.shifted_ref), custom_call_target="tpu_custom_call" | custom-call | tf_op jit(solution)/shard_map/factor_and_basis/pallas_call | solution.py:355
  (1 shorter events, 0.0 us)
Async XLA Ops:
  1.9 9.4 %copy-start.2 = (f32[128,128]{1,0:T(8,128)S(1)}, f32[128,128]{1,0:T(8,128)}, u32[]{:S(2)}) copy-start(f32[128,128]{1,0:T(8,128)} %coupling_ref.3) | copy-start | bytes 196612
  12.6 5.2 %collective-permute-start.2 = (bf16[264,128]{1,0:T(8,128)(2,1)S(1)}, bf16[264,128]{1,0:T(8,128)(2,1)S(1)}, u32[]{:S(2)}, u32[]{:S(2)}) collective-permute-start(bf16[264,128]{1,0:T(8,128)(2,1)S(1)} %get-tuple-element.28), channel_id=1, source_target_pairs={{0,12},{4,8},{8,4},{12,0},{16,28},{20,24},{24,20},{28,16},{1,13},{... | collective-permute-start | bytes 202760 | tf_op jit(solution)/shard_map/ppermute | solution.py:258
  14.9 3.3 %collective-permute-start.3 = (bf16[264,128]{1,0:T(8,128)(2,1)S(1)}, bf16[264,128]{1,0:T(8,128)(2,1)S(1)}, u32[]{:S(2)}, u32[]{:S(2)}) collective-permute-start(bf16[264,128]{1,0:T(8,128)(2,1)S(1)} %get-tuple-element.29), channel_id=1, source_target_pairs={{0,4},{4,0},{8,12},{12,8},{16,20},{20,16},{24,28},{28,24},{1,5},{5... | collective-permute-start | bytes 202760 | tf_op jit(solution)/shard_map/ppermute | solution.py:258
  15.1 3.4 %collective-permute-start.4 = (bf16[264,128]{1,0:T(8,128)(2,1)S(1)}, bf16[264,128]{1,0:T(8,128)(2,1)S(1)}, u32[]{:S(2)}, u32[]{:S(2)}) collective-permute-start(bf16[264,128]{1,0:T(8,128)(2,1)S(1)} %get-tuple-element.30), channel_id=1, source_target_pairs={{0,8},{4,12},{8,0},{12,4},{16,24},{20,28},{24,16},{28,20},{1,9},{5... | collective-permute-start | bytes 202760 | tf_op jit(solution)/shard_map/ppermute | solution.py:258
  15.3 7.9 %collective-permute-start = (bf16[264,128]{1,0:T(8,128)(2,1)S(1)}, bf16[264,128]{1,0:T(8,128)(2,1)S(1)}, u32[]{:S(2)}, u32[]{:S(2)}) collective-permute-start(bf16[264,128]{1,0:T(8,128)(2,1)S(1)} %get-tuple-element.25), channel_id=1, source_target_pairs={{0,12},{4,8},{8,4},{12,0},{16,28},{20,24},{24,20},{28,16},{1,13},{... | collective-permute-start | bytes 202760 | tf_op jit(solution)/shard_map/ppermute | solution.py:258
  17.5 5.7 %collective-permute-start.1 = (bf16[264,128]{1,0:T(8,128)(2,1)S(1)}, bf16[264,128]{1,0:T(8,128)(2,1)S(1)}, u32[]{:S(2)}, u32[]{:S(2)}) collective-permute-start(bf16[264,128]{1,0:T(8,128)(2,1)S(1)} %get-tuple-element.26), channel_id=1, source_target_pairs={{0,4},{4,0},{8,12},{12,8},{16,20},{20,16},{24,28},{28,24},{1,5},{5... | collective-permute-start | bytes 202760 | tf_op jit(solution)/shard_map/ppermute | solution.py:258
  18.6 4.4 %copy-start.1 = (f32[256,128]{1,0:T(8,128)S(1)}, f32[256,128]{1,0:T(8,128)}, u32[]{:S(2)}) copy-start(f32[256,128]{1,0:T(8,128)} %prev_hbm.1) | copy-start | bytes 393220
  18.6 6.0 %copy-start = (f32[256,128]{1,0:T(8,128)S(1)}, f32[256,128]{1,0:T(8,128)}, u32[]{:S(2)}) copy-start(f32[256,128]{1,0:T(8,128)} %now_ref.3) | copy-start | bytes 393220
  18.6 4.6 %collective-permute-start.5 = (bf16[264,128]{1,0:T(8,128)(2,1)S(1)}, bf16[264,128]{1,0:T(8,128)(2,1)S(1)}, u32[]{:S(2)}, u32[]{:S(2)}) collective-permute-start(bf16[264,128]{1,0:T(8,128)(2,1)S(1)} %mirror_sum.1), channel_id=1, source_target_pairs={{0,16},{4,20},{8,24},{12,28},{16,0},{20,4},{24,8},{28,12},{1,17},{... | collective-permute-start | bytes 202760 | tf_op jit(solution)/shard_map/ppermute | solution.py:258
  21.0 3.6 %collective-permute-start.6 = (bf16[264,128]{1,0:T(8,128)(2,1)S(1)}, bf16[264,128]{1,0:T(8,128)(2,1)S(1)}, u32[]{:S(2)}, u32[]{:S(2)}) collective-permute-start(bf16[264,128]{1,0:T(8,128)(2,1)S(1)} %get-tuple-element.33), channel_id=1, source_target_pairs={{0,8},{4,12},{8,0},{12,4},{16,24},{20,28},{24,16},{28,20},{1,9},{5... | collective-permute-start | bytes 202760 | tf_op jit(solution)/shard_map/ppermute | solution.py:258

commit v21 on v20

--- a/solution.py
+++ b/solution.py
@@ -34,6 +34,10 @@
 
 def distances(n):
     return [n - 1, *range(1, n - 1)]
+
+
+def near_distances(n):
+    return [*range(2, n), 1]
 
 
 def high_and_low(value):
@@ -103,9 +107,10 @@
         slab = total_ref[pl.ds(pl.multiple_of(row * rows_dev, rows_dev), rows_dev), :]
         return slab, early_ref[pl.ds(pl.multiple_of((row * n_col + my_col) * piece, piece), piece), :]
 
-    for step, mirror_ref, near_ref in zip(distances(half), mirror_refs, near_refs):
-        write_block(mirror_ref, *parts_of(my_row ^ (step + half)))
-        write_block(near_ref, *parts_of(my_row ^ step))
+    for step, ref in zip(distances(half), mirror_refs):
+        write_block(ref, *parts_of(my_row ^ (step + half)))
+    for step, ref in zip(near_distances(half), near_refs):
+        write_block(ref, *parts_of(my_row ^ step))
     for row, ref in ((my_row ^ half, far_ref), (my_row, own_ref)):
         ref[:rows_dev, :], ref[rows_dev:, :] = parts_of(row)
 
@@ -305,8 +310,8 @@
         compiler_params=params,
         name="tile_products",
     )(me, rows, cols, tile_counts, tile_block, gathered, coupling)
-    steps = distances(half)
-    mirrors = exchange(blocks[: half - 1], "row", steps)
+    mirrors = exchange(blocks[: half - 1], "row", distances(half))
+    steps = near_distances(half)
     near = exchange(blocks[half - 1 : -1], "row", steps[:-1])
     mirror = pl.pallas_call(
         functools.partial(mirror_kernel, rows_dev),

time: 53.8 us -> 53.9 us (level)
  transfers between devices with their start and end apart: 7 -> 7, of which waited for: 3 -> 4; matrix products, arithmetic and copies ran while one was open for 0% -> 0% of each run, Pallas kernels for 0% -> 0%
where the time goes in v21:
time: 53.9 us; the launch traced here: 53.7 us
  blocking collectives  33.4 us (62%)
  starting transfers between devices  9.19 us (17%)
  Pallas kernels  7.02 us (13%)
  waiting for transfers between devices  2.6 us (5%)
  between operations  1.37 us (3%)
    all_to_all x1, blocking collectives, on_device(): lax.all_to_all(grams.reshape(devices, piece, width), everyone, split_axis...  13.7 us
    all_to_all x1, blocking collectives, on_device(): lax.all_to_all(copies, everyone, split_axis=0, concat_axis=0, tiled=True)  11 us
    ppermute x7, starting transfers between devices, exchange(): lax.ppermute(block, axis, [(i, i ^ step) for i in range(n)])  9.19 us
    all_gather x1, blocking collectives, on_device(): gathered = lax.all_gather(both, 'col', axis=0, tiled=True)  8.67 us
    pallas_call x1, Pallas kernels, on_device(): pl.pallas_call(functools.partial(final_kernel, total_rows), out_shape=(ja...  3.87 us
    ppermute x7, waiting for transfers between devices, exchange(): lax.ppermute(block, axis, [(i, i ^ step) for i in range(n)])  2.6 us
    pallas_call x1, Pallas kernels, on_device(): pl.pallas_call(functools.partial(tiles_kernel, n_row, n_col, total_rows),...  1.27 us
    pallas_call x1, Pallas kernels, on_device(): pl.pallas_call(prepare_kernel, out_shape=(jax.ShapeDtypeStruct((2 * rows_...  1.26 us
  transfers between devices with their start and end apart: 7, of which 4 were waited for; matrix products, arithmetic and copies ran while one was open for 0% of the time, Pallas kernels for 0%

profile of v21, /device:TPU:1, one launch (start us, length us, event | category | flops | bytes accessed | tf_op | source)
XLA Modules:
  0.0 53.7 jit_solution(18389968422759507663)
XLA Ops:
  0.6 1.3 %prepare.1 = (bf16[512,128]{1,0:T(8,128)(2,1)S(1)}, s32[1,1,16]{2,1,0:T(1,128)S(1)}, s32[1,1,16]{2,1,0:T(1,128)S(1)}, bf16[16,128,128]{2,1,0:T(8,128)(2,1)S(1)}) custom-call(f32[256,128]{1,0:T(8,128)} %now_ref.3, f32[256,128]{1,0:T(8,128)} %prev_hbm.1, s32[1,1,16]{2,1,0:T(1,128)} %rows_hbm.1, s32[1,1,16]{2,1,0:T(1,128)} %cols_hbm.1, ...), custom_call_target="tpu_custom_call" | custom-call | tf_op jit(solution)/shard_map/prepare/pallas_call | solution.py:278
  1.9 0.0 copy-start.2
  1.9 8.7 %all_gather.3.basis_ref = bf16[2048,128]{1,0:T(8,128)(2,1)S(1)} all-gather(bf16[512,128]{1,0:T(8,128)(2,1)S(1)} %get-tuple-element.23), channel_id=1, replica_groups=mesh['row'=8,'col'=4] {'col'}, dimensions={0}, use_global_device_ids=true | all-gather | bytes 655360 | tf_op jit(solution)/shard_map/all_gather | solution.py:296
  11.2 0.1 pad_add_fusion.me_ref
  11.3 0.0 copy-done.2
  11.3 1.3 %tile_products.1 = (bf16[264,128]{1,0:T(8,128)(2,1)S(1)}, bf16[264,128]{1,0:T(8,128)(2,1)S(1)}, bf16[264,128]{1,0:T(8,128)(2,1)S(1)}, bf16[264,128]{1,0:T(8,128)...) custom-call(s32[2]{0:T(128)S(1)} %pad_add_fusion.me_ref, ...), custom_call_target="tpu_custom_call" | custom-call | tf_op jit(solution)/shard_map/tile_products/pallas_call | solution.py:301
  12.6 2.3 %collective-permute-start.2 = (bf16[264,128]{1,0:T(8,128)(2,1)S(1)}, bf16[264,128]{1,0:T(8,128)(2,1)S(1)}, u32[]{:S(2)}, u32[]{:S(2)}) collective-permute-start(bf16[264,128]{1,0:T(8,128)(2,1)S(1)} %get-tuple-element.28), channel_id=1, source_target_pairs={{0,12},{4,8},{8,4},{12,0},{16,28},{20,24},{24,20},{28,16},{1,13},{... | collective-permute-start | bytes 202760 | tf_op jit(solution)/shard_map/ppermute | solution.py:263
  14.9 0.3 collective-permute-start.3
  15.1 0.2 collective-permute-start.4
  15.3 1.3 %collective-permute-start = (bf16[264,128]{1,0:T(8,128)(2,1)S(1)}, bf16[264,128]{1,0:T(8,128)(2,1)S(1)}, u32[]{:S(2)}, u32[]{:S(2)}) collective-permute-start(bf16[264,128]{1,0:T(8,128)(2,1)S(1)} %get-tuple-element.25), channel_id=1, source_target_pairs={{0,8},{4,12},{8,0},{12,4},{16,24},{20,28},{24,16},{28,20},{1,9},{5... | collective-permute-start | bytes 202760 | tf_op jit(solution)/shard_map/ppermute | solution.py:263
  16.6 1.1 %collective-permute-start.1 = (bf16[264,128]{1,0:T(8,128)(2,1)S(1)}, bf16[264,128]{1,0:T(8,128)(2,1)S(1)}, u32[]{:S(2)}, u32[]{:S(2)}) collective-permute-start(bf16[264,128]{1,0:T(8,128)(2,1)S(1)} %get-tuple-element.26), channel_id=1, source_target_pairs={{0,12},{4,8},{8,4},{12,0},{16,28},{20,24},{24,20},{28,16},{1,13},{... | collective-permute-start | bytes 202760 | tf_op jit(solution)/shard_map/ppermute | solution.py:263
  17.7 0.0 collective-permute-done.2.refs_0_
  17.7 0.4 collective-permute-done.3.refs_1_
  18.1 0.4 collective-permute-done.4.refs_2_
  18.6 0.0 copy-start.1
  18.6 0.0 copy-start
  18.6 2.4 %collective-permute-start.5 = (bf16[264,128]{1,0:T(8,128)(2,1)S(1)}, bf16[264,128]{1,0:T(8,128)(2,1)S(1)}, u32[]{:S(2)}, u32[]{:S(2)}) collective-permute-start(bf16[264,128]{1,0:T(8,128)(2,1)S(1)} %mirror_sum.1), channel_id=1, source_target_pairs={{0,16},{4,20},{8,24},{12,28},{16,0},{20,4},{24,8},{28,12},{1,17},{... | collective-permute-start | bytes 202760 | tf_op jit(solution)/shard_map/ppermute | solution.py:263
  21.0 1.7 %collective-permute-start.6 = (bf16[264,128]{1,0:T(8,128)(2,1)S(1)}, bf16[264,128]{1,0:T(8,128)(2,1)S(1)}, u32[]{:S(2)}, u32[]{:S(2)}) collective-permute-start(bf16[264,128]{1,0:T(8,128)(2,1)S(1)} %get-tuple-element.33), channel_id=1, source_target_pairs={{0,4},{4,0},{8,12},{12,8},{16,20},{20,16},{24,28},{28,24},{1,5},{5... | collective-permute-start | bytes 202760 | tf_op jit(solution)/shard_map/ppermute | solution.py:263
  22.7 0.0 copy-done.1
  22.7 0.2 shift_by_previous.1.shift_ref
  22.9 0.0 collective-permute-done.refs_0_
  23.0 0.0 collective-permute-done.1.refs_1_
  23.0 0.1 collective-permute-done.5.refs_2_
  23.0 1.7 %collective-permute-done.6.refs_3_ = bf16[264,128]{1,0:T(8,128)(2,1)S(1)} collective-permute-done((bf16[264,128]{1,0:T(8,128)(2,1)S(1)}, bf16[264,128]{1,0:T(8,128)(2,1)S(1)}, u32[]{:S(2)}, u32[]{:S(2)}) %collective-permute-start.6) | collective-permute-done | bytes 67616 | tf_op jit(solution)/shard_map/ppermute | solution.py:263
  24.7 0.0 copy-done
  24.7 0.3 local_grams.1
  25.0 13.7 %all_to_all.10.parts_ref = f32[32,8,128]{2,1,0:T(8,128)S(1)} all-to-all(f32[32,8,128]{2,1,0:T(8,128)S(1)} %bitcast.4), channel_id=1, replica_groups=mesh['row'=8,'col'=4] {'row','col'}, dimensions={0} | all-to-all | bytes 262144 | tf_op jit(solution)/shard_map/all_to_all | solution.py:350
  38.7 0.1 sum_and_spread.1
  38.8 11.0 %all_to_all.11.pieces_ref = bf16[32,24,128]{2,1,0:T(8,128)(2,1)S(1)} all-to-all(bf16[32,24,128]{2,1,0:T(8,128)(2,1)S(1)} %sum_and_spread.1), channel_id=1, replica_groups=mesh['row'=8,'col'=4] {'row','col'}, dimensions={0} | all-to-all | bytes 393216 | tf_op jit(solution)/shard_map/all_to_all | solution.py:359
  49.8 3.9 %factor_and_basis.1 = (f32[256,128]{1,0:T(8,128)}, f32[128,128]{1,0:T(8,128)}, f32[128,128]{1,0:T(8,128)}) custom-call(bf16[32,24,128]{2,1,0:T(8,128)(2,1)S(1)} %all_to_all.11.pieces_ref, f32[256,128]{1,0:T(8,128)S(1)} %copy-done, f32[256,128]{1,0:T(8,128)S(1)} %get-tuple-element.36.shifted_ref), custom_call_target="tpu_custom_call" | custom-call | tf_op jit(solution)/shard_map/factor_and_basis/pallas_call | solution.py:360
  (1 shorter events, 0.0 us)
Async XLA Ops:
  1.9 9.4 %copy-start.2 = (f32[128,128]{1,0:T(8,128)S(1)}, f32[128,128]{1,0:T(8,128)}, u32[]{:S(2)}) copy-start(f32[128,128]{1,0:T(8,128)} %coupling_ref.3) | copy-start | bytes 196612
  12.6 5.1 %collective-permute-start.2 = (bf16[264,128]{1,0:T(8,128)(2,1)S(1)}, bf16[264,128]{1,0:T(8,128)(2,1)S(1)}, u32[]{:S(2)}, u32[]{:S(2)}) collective-permute-start(bf16[264,128]{1,0:T(8,128)(2,1)S(1)} %get-tuple-element.28), channel_id=1, source_target_pairs={{0,12},{4,8},{8,4},{12,0},{16,28},{20,24},{24,20},{28,16},{1,13},{... | collective-permute-start | bytes 202760 | tf_op jit(solution)/shard_map/ppermute | solution.py:263
  14.9 3.3 %collective-permute-start.3 = (bf16[264,128]{1,0:T(8,128)(2,1)S(1)}, bf16[264,128]{1,0:T(8,128)(2,1)S(1)}, u32[]{:S(2)}, u32[]{:S(2)}) collective-permute-start(bf16[264,128]{1,0:T(8,128)(2,1)S(1)} %get-tuple-element.29), channel_id=1, source_target_pairs={{0,4},{4,0},{8,12},{12,8},{16,20},{20,16},{24,28},{28,24},{1,5},{5... | collective-permute-start | bytes 202760 | tf_op jit(solution)/shard_map/ppermute | solution.py:263
  15.1 3.4 %collective-permute-start.4 = (bf16[264,128]{1,0:T(8,128)(2,1)S(1)}, bf16[264,128]{1,0:T(8,128)(2,1)S(1)}, u32[]{:S(2)}, u32[]{:S(2)}) collective-permute-start(bf16[264,128]{1,0:T(8,128)(2,1)S(1)} %get-tuple-element.30), channel_id=1, source_target_pairs={{0,8},{4,12},{8,0},{12,4},{16,24},{20,28},{24,16},{28,20},{1,9},{5... | collective-permute-start | bytes 202760 | tf_op jit(solution)/shard_map/ppermute | solution.py:263
  15.3 7.6 %collective-permute-start = (bf16[264,128]{1,0:T(8,128)(2,1)S(1)}, bf16[264,128]{1,0:T(8,128)(2,1)S(1)}, u32[]{:S(2)}, u32[]{:S(2)}) collective-permute-start(bf16[264,128]{1,0:T(8,128)(2,1)S(1)} %get-tuple-element.25), channel_id=1, source_target_pairs={{0,8},{4,12},{8,0},{12,4},{16,24},{20,28},{24,16},{28,20},{1,9},{5... | collective-permute-start | bytes 202760 | tf_op jit(solution)/shard_map/ppermute | solution.py:263
  16.6 6.4 %collective-permute-start.1 = (bf16[264,128]{1,0:T(8,128)(2,1)S(1)}, bf16[264,128]{1,0:T(8,128)(2,1)S(1)}, u32[]{:S(2)}, u32[]{:S(2)}) collective-permute-start(bf16[264,128]{1,0:T(8,128)(2,1)S(1)} %get-tuple-element.26), channel_id=1, source_target_pairs={{0,12},{4,8},{8,4},{12,0},{16,28},{20,24},{24,20},{28,16},{1,13},{... | collective-permute-start | bytes 202760 | tf_op jit(solution)/shard_map/ppermute | solution.py:263
  18.6 4.1 %copy-start.1 = (f32[256,128]{1,0:T(8,128)S(1)}, f32[256,128]{1,0:T(8,128)}, u32[]{:S(2)}) copy-start(f32[256,128]{1,0:T(8,128)} %prev_hbm.1) | copy-start | bytes 393220
  18.6 6.1 %copy-start = (f32[256,128]{1,0:T(8,128)S(1)}, f32[256,128]{1,0:T(8,128)}, u32[]{:S(2)}) copy-start(f32[256,128]{1,0:T(8,128)} %now_ref.3) | copy-start | bytes 393220
  18.6 4.4 %collective-permute-start.5 = (bf16[264,128]{1,0:T(8,128)(2,1)S(1)}, bf16[264,128]{1,0:T(8,128)(2,1)S(1)}, u32[]{:S(2)}, u32[]{:S(2)}) collective-permute-start(bf16[264,128]{1,0:T(8,128)(2,1)S(1)} %mirror_sum.1), channel_id=1, source_target_pairs={{0,16},{4,20},{8,24},{12,28},{16,0},{20,4},{24,8},{28,12},{1,17},{... | collective-permute-start | bytes 202760 | tf_op jit(solution)/shard_map/ppermute | solution.py:263
  21.0 3.7 %collective-permute-start.6 = (bf16[264,128]{1,0:T(8,128)(2,1)S(1)}, bf16[264,128]{1,0:T(8,128)(2,1)S(1)}, u32[]{:S(2)}, u32[]{:S(2)}) collective-permute-start(bf16[264,128]{1,0:T(8,128)(2,1)S(1)} %get-tuple-element.33), channel_id=1, source_target_pairs={{0,4},{4,0},{8,12},{12,8},{16,20},{20,16},{24,28},{28,24},{1,5},{5... | collective-permute-start | bytes 202760 | tf_op jit(solution)/shard_map/ppermute | solution.py:263

commit v22 on v20

--- a/solution.py
+++ b/solution.py
@@ -224,7 +224,7 @@
     return jnp.concatenate(finished, axis=0)
 
 
-def final_kernel(total_rows, pieces_ref, now_ref, shifted_ref, basis_ref, projection_ref, rfactor_ref):
+def final_kernel(total_rows, pieces_ref, now_ref, shifted_ref, basis_out, projection_out, rfactor_out, basis_ref, projection_ref, rfactor_ref, sems):
     width = now_ref.shape[1]
     piece = pieces_ref.shape[1] // 3
     pieces = pieces_ref[...]
@@ -234,6 +234,8 @@
     now_square, shift = early[:width], early[width : 2 * width]
     projection = now_product * total_rows**-0.5
     projection_ref[...] = projection
+    copies = [pltpu.make_async_copy(projection_ref, projection_out, sems.at[0])]
+    copies[0].start()
     scaled = now_product * (1.0 / total_rows)
     scaled_high, scaled_low = split(scaled)
     corrected = jnp.dot(now_square, scaled_low, preferred_element_type=F32)
@@ -247,9 +249,18 @@
     diagonal = jnp.sum(jnp.where(rows == cols, reduced, 0.0), axis=1, keepdims=True)
     root = lax.rsqrt(diagonal)
     rfactor_ref[...] = jnp.where(rows <= cols, reduced, 0.0) * root
+    copies.append(pltpu.make_async_copy(rfactor_ref, rfactor_out, sems.at[1]))
+    copies[1].start()
     inverse = jnp.where(rows > cols, reduced, jnp.where(rows == cols, 1.0, 0.0)) * root
     residual = shifted_ref[...] - dot3(now_ref[...], scaled)
-    basis_ref[...] = dot3(residual, inverse, NT)
+    part = residual.shape[0] // 2
+    for k in range(2):
+        place = pl.ds(k * part, part)
+        basis_ref[place, :] = dot3(residual[k * part : (k + 1) * part], inverse, NT)
+        copies.append(pltpu.make_async_copy(basis_ref.at[place], basis_out.at[place], sems.at[2 + k]))
+        copies[-1].start()
+    for copy in copies:
+        copy.wait()
 
 
 def exchange(blocks, axis, steps):
@@ -360,7 +371,13 @@
             jax.ShapeDtypeStruct((width, width), F32),
         ),
         in_specs=[vmem] * 3,
-        out_specs=(vmem, vmem, vmem),
+        out_specs=[pl.BlockSpec(memory_space=pl.ANY)] * 3,
+        scratch_shapes=[
+            pltpu.VMEM((rows_dev, width), F32),
+            pltpu.VMEM((width, width), F32),
+            pltpu.VMEM((width, width), F32),
+            pltpu.SemaphoreType.DMA((4,)),
+        ],
         compiler_params=params,
         name="factor_and_basis",
     )(gathered_sums, basis_now, shifted)

time: 53.8 us -> 53.9 us (level)
  no operation moved by 1% of the time
where the time goes in v22:
time: 53.9 us; the launch traced here: 53.7 us
  blocking collectives  33.4 us (62%)
  starting transfers between devices  9.52 us (18%)
  Pallas kernels  7.08 us (13%)
  waiting for transfers between devices  2.21 us (4%)
  between operations  1.37 us (3%)
    all_to_all x1, blocking collectives, on_device(): lax.all_to_all(grams.reshape(devices, piece, width), everyone, split_axis...  13.7 us
    all_to_all x1, blocking collectives, on_device(): lax.all_to_all(copies, everyone, split_axis=0, concat_axis=0, tiled=True)  11 us
    ppermute x7, starting transfers between devices, exchange(): lax.ppermute(block, axis, [(i, i ^ step) for i in range(n)])  9.52 us
    all_gather x1, blocking collectives, on_device(): gathered = lax.all_gather(both, 'col', axis=0, tiled=True)  8.67 us
    pallas_call x1, Pallas kernels, on_device(): pl.pallas_call(functools.partial(final_kernel, total_rows), out_shape=(ja...  3.94 us
    ppermute x7, waiting for transfers between devices, exchange(): lax.ppermute(block, axis, [(i, i ^ step) for i in range(n)])  2.21 us
    pallas_call x1, Pallas kernels, on_device(): pl.pallas_call(functools.partial(tiles_kernel, n_row, n_col, total_rows),...  1.27 us
    pallas_call x1, Pallas kernels, on_device(): pl.pallas_call(prepare_kernel, out_shape=(jax.ShapeDtypeStruct((2 * rows_...  1.26 us
  transfers between devices with their start and end apart: 7, of which 3 were waited for; matrix products, arithmetic and copies ran while one was open for 0% of the time, Pallas kernels for 0%

profile of v22, /device:TPU:1, one launch (start us, length us, event | category | flops | bytes accessed | tf_op | source)
XLA Modules:
  0.0 53.7 jit_solution(6541042341448678335)
XLA Ops:
  0.6 1.3 %prepare.1 = (bf16[512,128]{1,0:T(8,128)(2,1)S(1)}, s32[1,1,16]{2,1,0:T(1,128)S(1)}, s32[1,1,16]{2,1,0:T(1,128)S(1)}, bf16[16,128,128]{2,1,0:T(8,128)(2,1)S(1)}) custom-call(f32[256,128]{1,0:T(8,128)} %now_ref.3, f32[256,128]{1,0:T(8,128)} %prev_hbm.1, s32[1,1,16]{2,1,0:T(1,128)} %rows_hbm.1, s32[1,1,16]{2,1,0:T(1,128)} %cols_hbm.1, ...), custom_call_target="tpu_custom_call" | custom-call | tf_op jit(solution)/shard_map/prepare/pallas_call | solution.py:284
  1.9 0.0 copy-start.2
  1.9 8.7 %all_gather.3.basis_ref = bf16[2048,128]{1,0:T(8,128)(2,1)S(1)} all-gather(bf16[512,128]{1,0:T(8,128)(2,1)S(1)} %get-tuple-element.23), channel_id=1, replica_groups=mesh['row'=8,'col'=4] {'col'}, dimensions={0}, use_global_device_ids=true | all-gather | bytes 655360 | tf_op jit(solution)/shard_map/all_gather | solution.py:302
  11.2 0.1 pad_add_fusion.me_ref
  11.3 0.0 copy-done.2
  11.3 1.3 %tile_products.1 = (bf16[264,128]{1,0:T(8,128)(2,1)S(1)}, bf16[264,128]{1,0:T(8,128)(2,1)S(1)}, bf16[264,128]{1,0:T(8,128)(2,1)S(1)}, bf16[264,128]{1,0:T(8,128)...) custom-call(s32[2]{0:T(128)S(1)} %pad_add_fusion.me_ref, ...), custom_call_target="tpu_custom_call" | custom-call | tf_op jit(solution)/shard_map/tile_products/pallas_call | solution.py:307
  12.6 2.3 %collective-permute-start.2 = (bf16[264,128]{1,0:T(8,128)(2,1)S(1)}, bf16[264,128]{1,0:T(8,128)(2,1)S(1)}, u32[]{:S(2)}, u32[]{:S(2)}) collective-permute-start(bf16[264,128]{1,0:T(8,128)(2,1)S(1)} %get-tuple-element.28), channel_id=1, source_target_pairs={{0,12},{4,8},{8,4},{12,0},{16,28},{20,24},{24,20},{28,16},{1,13},{... | collective-permute-start | bytes 202760 | tf_op jit(solution)/shard_map/ppermute | solution.py:269
  14.9 0.3 collective-permute-start.3
  15.1 0.2 collective-permute-start.4
  15.3 2.2 %collective-permute-start = (bf16[264,128]{1,0:T(8,128)(2,1)S(1)}, bf16[264,128]{1,0:T(8,128)(2,1)S(1)}, u32[]{:S(2)}, u32[]{:S(2)}) collective-permute-start(bf16[264,128]{1,0:T(8,128)(2,1)S(1)} %get-tuple-element.25), channel_id=1, source_target_pairs={{0,12},{4,8},{8,4},{12,0},{16,28},{20,24},{24,20},{28,16},{1,13},{... | collective-permute-start | bytes 202760 | tf_op jit(solution)/shard_map/ppermute | solution.py:269
  17.5 0.3 collective-permute-start.1
  17.8 0.0 collective-permute-done.2.refs_0_
  17.8 0.4 collective-permute-done.3.refs_1_
  18.1 0.4 collective-permute-done.4.refs_2_
  18.6 0.0 copy-start.1
  18.6 0.0 copy-start
  18.6 2.4 %collective-permute-start.5 = (bf16[264,128]{1,0:T(8,128)(2,1)S(1)}, bf16[264,128]{1,0:T(8,128)(2,1)S(1)}, u32[]{:S(2)}, u32[]{:S(2)}) collective-permute-start(bf16[264,128]{1,0:T(8,128)(2,1)S(1)} %mirror_sum.1), channel_id=1, source_target_pairs={{0,16},{4,20},{8,24},{12,28},{16,0},{20,4},{24,8},{28,12},{1,17},{... | collective-permute-start | bytes 202760 | tf_op jit(solution)/shard_map/ppermute | solution.py:269
  21.0 2.0 %collective-permute-start.6 = (bf16[264,128]{1,0:T(8,128)(2,1)S(1)}, bf16[264,128]{1,0:T(8,128)(2,1)S(1)}, u32[]{:S(2)}, u32[]{:S(2)}) collective-permute-start(bf16[264,128]{1,0:T(8,128)(2,1)S(1)} %get-tuple-element.33), channel_id=1, source_target_pairs={{0,8},{4,12},{8,0},{12,4},{16,24},{20,28},{24,16},{28,20},{1,9},{5... | collective-permute-start | bytes 202760 | tf_op jit(solution)/shard_map/ppermute | solution.py:269
  23.0 0.0 copy-done.1
  23.0 0.2 shift_by_previous.1.shift_ref
  23.2 0.0 collective-permute-done.refs_0_
  23.2 0.0 collective-permute-done.1.refs_1_
  23.2 0.0 collective-permute-done.5.refs_2_
  23.2 1.4 %collective-permute-done.6.refs_3_ = bf16[264,128]{1,0:T(8,128)(2,1)S(1)} collective-permute-done((bf16[264,128]{1,0:T(8,128)(2,1)S(1)}, bf16[264,128]{1,0:T(8,128)(2,1)S(1)}, u32[]{:S(2)}, u32[]{:S(2)}) %collective-permute-start.6) | collective-permute-done | bytes 67616 | tf_op jit(solution)/shard_map/ppermute | solution.py:269
  24.6 0.0 copy-done
  24.6 0.3 local_grams.1
  25.0 13.7 %all_to_all.10.parts_ref = f32[32,8,128]{2,1,0:T(8,128)S(1)} all-to-all(f32[32,8,128]{2,1,0:T(8,128)S(1)} %bitcast.4), channel_id=1, replica_groups=mesh['row'=8,'col'=4] {'row','col'}, dimensions={0} | all-to-all | bytes 262144 | tf_op jit(solution)/shard_map/all_to_all | solution.py:356
  38.6 0.1 sum_and_spread.1
  38.7 11.0 %all_to_all.11.pieces_ref = bf16[32,24,128]{2,1,0:T(8,128)(2,1)S(1)} all-to-all(bf16[32,24,128]{2,1,0:T(8,128)(2,1)S(1)} %sum_and_spread.1), channel_id=1, replica_groups=mesh['row'=8,'col'=4] {'row','col'}, dimensions={0} | all-to-all | bytes 393216 | tf_op jit(solution)/shard_map/all_to_all | solution.py:365
  49.7 3.9 %factor_and_basis.1 = (f32[256,128]{1,0:T(8,128)}, f32[128,128]{1,0:T(8,128)}, f32[128,128]{1,0:T(8,128)}) custom-call(bf16[32,24,128]{2,1,0:T(8,128)(2,1)S(1)} %all_to_all.11.pieces_ref, f32[256,128]{1,0:T(8,128)S(1)} %copy-done, f32[256,128]{1,0:T(8,128)S(1)} %get-tuple-element.36.shifted_ref), custom_call_target="tpu_custom_call" | custom-call | tf_op jit(solution)/shard_map/factor_and_basis/pallas_call | solution.py:366
  (1 shorter events, 0.0 us)
Async XLA Ops:
  1.9 9.4 %copy-start.2 = (f32[128,128]{1,0:T(8,128)S(1)}, f32[128,128]{1,0:T(8,128)}, u32[]{:S(2)}) copy-start(f32[128,128]{1,0:T(8,128)} %coupling_ref.3) | copy-start | bytes 196612
  12.6 5.2 %collective-permute-start.2 = (bf16[264,128]{1,0:T(8,128)(2,1)S(1)}, bf16[264,128]{1,0:T(8,128)(2,1)S(1)}, u32[]{:S(2)}, u32[]{:S(2)}) collective-permute-start(bf16[264,128]{1,0:T(8,128)(2,1)S(1)} %get-tuple-element.28), channel_id=1, source_target_pairs={{0,12},{4,8},{8,4},{12,0},{16,28},{20,24},{24,20},{28,16},{1,13},{... | collective-permute-start | bytes 202760 | tf_op jit(solution)/shard_map/ppermute | solution.py:269
  14.9 3.3 %collective-permute-start.3 = (bf16[264,128]{1,0:T(8,128)(2,1)S(1)}, bf16[264,128]{1,0:T(8,128)(2,1)S(1)}, u32[]{:S(2)}, u32[]{:S(2)}) collective-permute-start(bf16[264,128]{1,0:T(8,128)(2,1)S(1)} %get-tuple-element.29), channel_id=1, source_target_pairs={{0,4},{4,0},{8,12},{12,8},{16,20},{20,16},{24,28},{28,24},{1,5},{5... | collective-permute-start | bytes 202760 | tf_op jit(solution)/shard_map/ppermute | solution.py:269
  15.1 3.4 %collective-permute-start.4 = (bf16[264,128]{1,0:T(8,128)(2,1)S(1)}, bf16[264,128]{1,0:T(8,128)(2,1)S(1)}, u32[]{:S(2)}, u32[]{:S(2)}) collective-permute-start(bf16[264,128]{1,0:T(8,128)(2,1)S(1)} %get-tuple-element.30), channel_id=1, source_target_pairs={{0,8},{4,12},{8,0},{12,4},{16,24},{20,28},{24,16},{28,20},{1,9},{5... | collective-permute-start | bytes 202760 | tf_op jit(solution)/shard_map/ppermute | solution.py:269
  15.3 7.9 %collective-permute-start = (bf16[264,128]{1,0:T(8,128)(2,1)S(1)}, bf16[264,128]{1,0:T(8,128)(2,1)S(1)}, u32[]{:S(2)}, u32[]{:S(2)}) collective-permute-start(bf16[264,128]{1,0:T(8,128)(2,1)S(1)} %get-tuple-element.25), channel_id=1, source_target_pairs={{0,12},{4,8},{8,4},{12,0},{16,28},{20,24},{24,20},{28,16},{1,13},{... | collective-permute-start | bytes 202760 | tf_op jit(solution)/shard_map/ppermute | solution.py:269
  17.5 5.7 %collective-permute-start.1 = (bf16[264,128]{1,0:T(8,128)(2,1)S(1)}, bf16[264,128]{1,0:T(8,128)(2,1)S(1)}, u32[]{:S(2)}, u32[]{:S(2)}) collective-permute-start(bf16[264,128]{1,0:T(8,128)(2,1)S(1)} %get-tuple-element.26), channel_id=1, source_target_pairs={{0,4},{4,0},{8,12},{12,8},{16,20},{20,16},{24,28},{28,24},{1,5},{5... | collective-permute-start | bytes 202760 | tf_op jit(solution)/shard_map/ppermute | solution.py:269
  18.6 4.4 %copy-start.1 = (f32[256,128]{1,0:T(8,128)S(1)}, f32[256,128]{1,0:T(8,128)}, u32[]{:S(2)}) copy-start(f32[256,128]{1,0:T(8,128)} %prev_hbm.1) | copy-start | bytes 393220
  18.6 6.0 %copy-start = (f32[256,128]{1,0:T(8,128)S(1)}, f32[256,128]{1,0:T(8,128)}, u32[]{:S(2)}) copy-start(f32[256,128]{1,0:T(8,128)} %now_ref.3) | copy-start | bytes 393220
  18.6 4.6 %collective-permute-start.5 = (bf16[264,128]{1,0:T(8,128)(2,1)S(1)}, bf16[264,128]{1,0:T(8,128)(2,1)S(1)}, u32[]{:S(2)}, u32[]{:S(2)}) collective-permute-start(bf16[264,128]{1,0:T(8,128)(2,1)S(1)} %mirror_sum.1), channel_id=1, source_target_pairs={{0,16},{4,20},{8,24},{12,28},{16,0},{20,4},{24,8},{28,12},{1,17},{... | collective-permute-start | bytes 202760 | tf_op jit(solution)/shard_map/ppermute | solution.py:269
  21.0 3.6 %collective-permute-start.6 = (bf16[264,128]{1,0:T(8,128)(2,1)S(1)}, bf16[264,128]{1,0:T(8,128)(2,1)S(1)}, u32[]{:S(2)}, u32[]{:S(2)}) collective-permute-start(bf16[264,128]{1,0:T(8,128)(2,1)S(1)} %get-tuple-element.33), channel_id=1, source_target_pairs={{0,8},{4,12},{8,0},{12,4},{16,24},{20,28},{24,16},{28,20},{1,9},{5... | collective-permute-start | bytes 202760 | tf_op jit(solution)/shard_map/ppermute | solution.py:269
